TPU v7x, 32 devices: a whole 2x2x4 slice. The times are simulated.
32 devices in a mesh: img: 4 (over y, x), atom: 8 (over z, core).
Axes of the slice: x: 2, y: 2, z: 4, core: 2. Of those that a mesh axis runs over, the one named last changes fastest.
Arguments:
- positions: float32 [4, 3, 8192], P('img', None, 'atom'), may hold values from -9.8 to 9.8, as said below
- species: int32 [8192], P('atom'), may hold values from 0 to 3
- counts: int32 [8192], P('atom'), may hold values from 1 to 16, as said below
- neighbours: int32 [16, 8192], P(None, 'atom'), may hold values from 0 to 1535, as said below
- send_list: int32 [4096], P('atom'), may hold values from 0 to 1023
- climb: int32 [4], P('img'), may hold values 0 or 1
- embed: bfloat16 [4, 128], replicated, may hold values from -6 to 6
- ref_energy: float32 [4], replicated, may hold values from -2 to 2
- rad_in: bfloat16 [3, 8, 64], replicated, may hold values from -24 to 24
- rad_out: bfloat16 [3, 64, 128], replicated, may hold values from -0.047851562 to 0.047851562
- mixing: bfloat16 [2, 128, 128], replicated, may hold values from -0.5 to 0.5
- w_energy: bfloat16 [128], replicated, may hold values from -0.5 to 0.5
Outputs:
- neb_force: float32 [4, 3, 8192], P('img', None, 'atom')
- energies: float32 [4], P('img')
Inputs may be any that keep to these rules, and one draw needn't show every extreme that they name: `positions`: positions of image p are those of image 0 plus a sum of p random displacements. `counts`: the first atom of every tile has all 16 slots live. `neighbours`: every slot of the atom with local index i (its index mod 1024) names a row from i to i + 512 of its tile's table, never row i + 256. `send_list`: values are local atom indices of the owning tile.
All inputs are finite; a program needn't handle non-finite values. No bound on the sum of `climb` on one device may be relied on, other than what follows from the above.
Results may differ from a plain program's by a relative error of at most 0.007.
Values may be sent and summed in bfloat16 or wider, within the bound.
No kernel may reach another device: no remote copies, remote signals or barrier semaphores. Data moves between devices by JAX's collectives and lax.ppermute only.
A program may use at most 64 MiB of HBM per device.

v0:
```python
import math

import jax
import jax.numpy as jnp
from jax import lax
from jax.sharding import PartitionSpec as P

spring_constant = 5.0


def padded(block, sides, width, periodic):
    for axis, dim in sides:
        count = lax.axis_size(axis)
        forward = [(i, i + 1) for i in range(count - 1)]
        if periodic:
            forward.append((count - 1, 0))
        backward = [(target, source) for source, target in forward]
        low = lax.ppermute(
            lax.slice_in_dim(block, block.shape[dim] - width, None, axis=dim), axis, forward
        )
        high = lax.ppermute(lax.slice_in_dim(block, 0, width, axis=dim), axis, backward)
        block = jnp.concatenate([low, block, high], axis=dim)
    return block


def radial_field(basis, w_in, w_out):
    hidden = lax.dot_general(
        w_in, basis, (((0,), (0,)), ((), ())), preferred_element_type=jnp.float32
    )
    hidden = jax.nn.silu(hidden).astype(jnp.bfloat16)
    return lax.dot_general(
        hidden, w_out, (((0,), (0,)), ((), ())), preferred_element_type=jnp.float32
    )


def species_table(kinds, embed):
    onehot = (kinds[:, None] == jnp.arange(embed.shape[0], dtype=jnp.int32)[None, :]).astype(
        jnp.bfloat16
    )
    return jnp.dot(onehot, embed, preferred_element_type=jnp.float32).astype(jnp.bfloat16)


def feature_rim(feats, send_list, rim_rows):
    sent = jnp.take(feats, send_list, axis=0)
    rims = padded(sent, (("atom", 0),), rim_rows, True)
    return jnp.concatenate([rims[:rim_rows], feats, rims[3 * rim_rows :]], axis=0)


def to_blocks(arr, block):
    lead = arr.shape[:-1]
    number = arr.shape[-1] // block
    arr = arr.reshape(lead + (number, block))
    return jnp.moveaxis(arr, -2, 0)


def selector(nbr_b, start, window):
    local_rows = nbr_b - start
    columns = lax.broadcasted_iota(jnp.int32, (1, 1, window), 2)
    picks = local_rows[:, :, None] == columns
    return picks.reshape(nbr_b.shape[0] * nbr_b.shape[1], window)


def on_device(
    positions,
    species,
    counts,
    neighbours,
    send_list,
    climb,
    embed,
    ref_energy,
    rad_in,
    rad_out,
    mixing,
    w_energy,
):
    atoms = species.shape[0]
    rim_rows = send_list.shape[0] // 2
    fan = neighbours.shape[0]
    chans = embed.shape[1]
    layers = mixing.shape[0]
    basis_count = rad_in.shape[1]
    block = min(256, atoms)
    number = atoms // block
    window = block + 2 * rim_rows
    block_starts = jnp.arange(number, dtype=jnp.int32) * block
    here = positions[0]
    sent_pos = jnp.take(here, send_list, axis=1)
    rim_pos = padded(sent_pos, (("atom", 1),), rim_rows, True)
    table_pos = jnp.concatenate([rim_pos[:, :rim_rows], here, rim_pos[:, 3 * rim_rows :]], axis=1)
    nbr_blocks = to_blocks(neighbours, block)

    def locate(items):
        nbr_b, start = items
        near_pos = lax.dynamic_slice_in_dim(table_pos, start, window, 1)
        picks = selector(nbr_b, start, window).astype(jnp.float32)
        reached = lax.dot_general(
            near_pos,
            picks,
            (((1,), (1,)), ((), ())),
            precision=lax.Precision.HIGHEST,
            preferred_element_type=jnp.float32,
        )
        centre = lax.dynamic_slice_in_dim(here, start + rim_rows - rim_rows, block, 1)
        return reached.reshape(3, fan, block) - centre[:, None, :]

    delta_blocks = lax.map(locate, (nbr_blocks, block_starts))
    dist_sq = jnp.sum(delta_blocks * delta_blocks, axis=1)
    centres = 2.0 * jnp.arange(basis_count, dtype=jnp.float32)
    basis_blocks = jnp.exp(
        -jnp.square(dist_sq[:, None] - centres[None, :, None, None]) / 8.0
    ).astype(jnp.bfloat16)
    basis_blocks = basis_blocks.reshape(number, basis_count, fan * block)
    slots = lax.broadcasted_iota(jnp.int32, (fan, atoms), 0)
    live = (slots < counts[None, :]).astype(jnp.float32)
    live_blocks = to_blocks(live, block)
    own = species_table(species, embed)
    table_h = feature_rim(own, send_list, rim_rows)

    def fetch(table, nbr_b, start):
        near_rows = lax.dynamic_slice_in_dim(table, start, window, 0)
        picks = selector(nbr_b, start, window).astype(jnp.bfloat16)
        return jnp.dot(picks, near_rows, preferred_element_type=jnp.float32).reshape(
            fan, block, chans
        )

    feats = own
    for layer in range(layers):
        if layer > 0:
            table_h = feature_rim(feats, send_list, rim_rows)

        def step(items, table=table_h, layer=layer):
            nbr_b, start, basis_b, live_b, feats_b = items
            field = radial_field(basis_b, rad_in[layer], rad_out[layer]).reshape(fan, block, chans)
            far = fetch(table, nbr_b, start)
            summed = jnp.sum(field * far * live_b[:, :, None], axis=0)
            scaled = (summed / math.sqrt(fan)).astype(jnp.bfloat16)
            update = jax.nn.silu(jnp.dot(scaled, mixing[layer], preferred_element_type=jnp.float32))
            return (feats_b.astype(jnp.float32) + update).astype(jnp.bfloat16)

        feats = lax.map(
            step,
            (
                nbr_blocks,
                block_starts,
                basis_blocks,
                live_blocks,
                feats.reshape(number, block, chans),
            ),
        ).reshape(atoms, chans)
    table_h = feature_rim(feats, send_list, rim_rows)

    def force_step(items):
        nbr_b, start, basis_b, live_b, feats_b, delta_b = items
        field = radial_field(basis_b, rad_in[layers], rad_out[layers]).reshape(fan, block, chans)
        far = fetch(table_h, nbr_b, start)
        near = feats_b.astype(jnp.float32)[None]
        pair = jnp.sum(field * near * far, axis=2) * (live_b / math.sqrt(chans))
        return jnp.sum(pair[None] * delta_b, axis=1)

    force_blocks = lax.map(
        force_step,
        (
            nbr_blocks,
            block_starts,
            basis_blocks,
            live_blocks,
            feats.reshape(number, block, chans),
            delta_blocks,
        ),
    )
    force = jnp.moveaxis(force_blocks, 0, 1).reshape(3, atoms)
    onehot_ref = jnp.where(
        species[:, None] == jnp.arange(ref_energy.shape[0], dtype=jnp.int32)[None, :],
        ref_energy[None, :],
        jnp.float32(0.0),
    )
    per_atom = jnp.dot(feats, w_energy, preferred_element_type=jnp.float32) + jnp.sum(
        onehot_ref, axis=1
    )
    energy_part = jnp.sum(per_atom)
    band = padded(positions, (("img", 0),), 1, False)
    behind = here - band[0]
    ahead = band[2] - here
    energy_sum, back_sq, fore_sq = lax.psum(
        (energy_part, jnp.sum(behind * behind), jnp.sum(ahead * ahead)), "atom"
    )
    back_len = jnp.sqrt(back_sq + 1e-06)
    fore_len = jnp.sqrt(fore_sq + 1e-06)
    tangent = behind / back_len + ahead / fore_len
    tau_sq, along = lax.psum((jnp.sum(tangent * tangent), jnp.sum(force * tangent)), "atom")
    index = lax.axis_index("img")
    last = lax.axis_size("img") - 1
    proj = along / tau_sq
    interior = (
        force
        - proj * tangent
        + spring_constant * (fore_len - back_len) / jnp.sqrt(tau_sq) * tangent
    )
    climbing = force - 2.0 * proj * tangent
    is_end = jnp.logical_or(index == 0, index == last)
    result = jnp.where(is_end, force, jnp.where(climb[0] == 1, climbing, interior))
    energy = (energy_sum / (atoms * lax.axis_size("atom"))).reshape(1)
    return (result[None], energy)


def solution(mesh):
    return jax.shard_map(
        on_device,
        mesh=mesh,
        in_specs=(
            P("img", None, "atom"),
            P("atom"),
            P("atom"),
            P(None, "atom"),
            P("atom"),
            P("img"),
            P(),
            P(),
            P(),
            P(),
            P(),
            P(),
        ),
        out_specs=(P("img", None, "atom"), P("img")),
        check_vma=False,
    )
```

profile of v0, /device:TPU:0, one launch (start us, length us, event | category | flops | bytes accessed | tf_op | source)
XLA Modules:
  0.0 224.7 jit_solution(13523286689773304378)
XLA Ops:
  1.7 4.9 %collective-permute-start.8 = (f32[1,3,1024]{1,2,0:T(8,128)S(1)}, f32[1,3,1024]{1,2,0:T(8,128)S(1)}, u32[]{:S(2)}, u32[]{:S(2)}) collective-permute-start(f32[1,3,1024]{1,2,0:T(8,128)S(1)} %copy.71), channel_id=1, source_target_pairs={{0,8},{8,16},{16,24},{1,9},{9,17},{17,25},{2,10},{10,18},{18,26},{... | collective-permute-start | bytes 36872 | tf_op jit(solution)/shard_map/ppermute | solution.py:18
  10.5 3.5 %collective-permute-start.1 = (f32[3,256]{0,1:T(8,128)S(1)}, f32[3,256]{0,1:T(8,128)S(1)}, u32[]{:S(2)}, u32[]{:S(2)}) collective-permute-start(f32[3,256]{0,1:T(8,128)S(1)} %get-tuple-element.528), channel_id=1, source_target_pairs={{1,0},{2,1},{3,2},{4,3},{5,4},{6,5},{7,6},{0,7},{9,8},{10,9},{11,1... | collective-permute-start | bytes 9224 | tf_op jit(solution)/shard_map/ppermute | solution.py:21
  15.1 1.3 gather_fusion.1
  17.8 3.6 %collective-permute-start.3 = (bf16[256,128]{1,0:T(8,128)(2,1)S(1)}, bf16[256,128]{1,0:T(8,128)(2,1)S(1)}, u32[]{:S(2)}, u32[]{:S(2)}) collective-permute-start(bf16[256,128]{1,0:T(8,128)(2,1)S(1)} %get-tuple-element.534), channel_id=1, source_target_pairs={{1,0},{2,1},{3,2},{4,3},{5,4},{6,5},{7,6},{0,7},{9,8},{10,9},{11,1... | collective-permute-start | bytes 196616 | tf_op jit(solution)/shard_map/ppermute | solution.py:21
  21.5 43.0 %while.44 = (s32[]{:T(128)}, f32[4,3,16,256]{3,1,2,0:T(4,128)S(1)}, s32[4]{0:T(128)S(1)}, f32[3,1536]{1,0:T(4,128)S(1)}, s32[4,16,256]{2,1,0:T(8,128)S(1)}, /*in...) while((s32[]{:T(128)}, f32[4,3,16,256]{3,1,2,0:T(4,128)S(1)}, s32[4]{0:T(128)S(1)}, ...), condition=%wide.region_1.2_spmd, body=%wide.region_0.1_spmd.sunk | while | flops 116408328 | bytes 137408 | solution.py:107
  26.0 6.2 %fusion.110 = f32[4,3,16,256]{3,1,2,0:T(4,128)S(1)} fusion(f32[4,3,16,256]{3,1,2,0:T(4,128)S(1)} %get-tuple-element.784, s32[]{:T(128)} %get-tuple-element.783, s32[16,256]{1,0:T(8,128)S(1)} %subtract_bitcast_fusion.8, f32[3,256]{1,0:T(4,128)S(1)} %constant_dynamic-slice_fusion.4, f32[3,1536]{1,0:T(4,128)S(1)} %get-tuple-element.796, s32[]{:T(128)S(6)} %select_n.100), kind=kOutput, calls=%fused_computation.9.clone.1 | convolution fusion | flops 116404224 | bytes 98312 | tf_op jit(solution)/shard_map/while/body/eval_jaxpr/dot_general | solution.py:97
  36.8 6.2 %fusion.110 = f32[4,3,16,256]{3,1,2,0:T(4,128)S(1)} fusion(f32[4,3,16,256]{3,1,2,0:T(4,128)S(1)} %get-tuple-element.784, s32[]{:T(128)} %get-tuple-element.783, s32[16,256]{1,0:T(8,128)S(1)} %subtract_bitcast_fusion.8, f32[3,256]{1,0:T(4,128)S(1)} %constant_dynamic-slice_fusion.4, f32[3,1536]{1,0:T(4,128)S(1)} %get-tuple-element.796, s32[]{:T(128)S(6)} %select_n.100), kind=kOutput, calls=%fused_computation.9.clone.1 | convolution fusion | flops 116404224 | bytes 98312 | tf_op jit(solution)/shard_map/while/body/eval_jaxpr/dot_general | solution.py:97
  47.5 6.2 %fusion.110 = f32[4,3,16,256]{3,1,2,0:T(4,128)S(1)} fusion(f32[4,3,16,256]{3,1,2,0:T(4,128)S(1)} %get-tuple-element.784, s32[]{:T(128)} %get-tuple-element.783, s32[16,256]{1,0:T(8,128)S(1)} %subtract_bitcast_fusion.8, f32[3,256]{1,0:T(4,128)S(1)} %constant_dynamic-slice_fusion.4, f32[3,1536]{1,0:T(4,128)S(1)} %get-tuple-element.796, s32[]{:T(128)S(6)} %select_n.100), kind=kOutput, calls=%fused_computation.9.clone.1 | convolution fusion | flops 116404224 | bytes 98312 | tf_op jit(solution)/shard_map/while/body/eval_jaxpr/dot_general | solution.py:97
  58.3 6.2 %fusion.110 = f32[4,3,16,256]{3,1,2,0:T(4,128)S(1)} fusion(f32[4,3,16,256]{3,1,2,0:T(4,128)S(1)} %get-tuple-element.784, s32[]{:T(128)} %get-tuple-element.783, s32[16,256]{1,0:T(8,128)S(1)} %subtract_bitcast_fusion.8, f32[3,256]{1,0:T(4,128)S(1)} %constant_dynamic-slice_fusion.4, f32[3,1536]{1,0:T(4,128)S(1)} %get-tuple-element.796, s32[]{:T(128)S(6)} %select_n.100), kind=kOutput, calls=%fused_computation.9.clone.1 | convolution fusion | flops 116404224 | bytes 98312 | tf_op jit(solution)/shard_map/while/body/eval_jaxpr/dot_general | solution.py:97
  66.5 14.3 %all-reduce.1 = (f32[]{:T(128)}, f32[]{:T(128)}) all-reduce(f32[]{:T(128)} %get-tuple-element.443, f32[]{:T(128)} %get-tuple-element.442), channel_id=1, replica_groups=mesh['img'=4,'atom'=8] {'atom'}, use_global_device_ids=true, to_apply=%region_16.18 | all-reduce | flops 2 | bytes 16 | tf_op jit(solution)/shard_map/psum | solution.py:185
  82.4 33.2 %while.45 = (s32[]{:T(128)}, bf16[4,256,128]{2,1,0:T(8,128)(2,1)S(1)}, bf16[4,256,128]{2,1,0:T(8,128)(2,1)S(1)}, bf16[4,8,4096]{2,1,0:T(8,128)(2,1)}, bf16[3,8,6...) while((s32[]{:T(128)}, ...), condition=%wide.region_5.7_spmd, body=%wide.region_3.6_spmd.sunk | while | flops 891293696 | bytes 6048455 | solution.py:141
  87.5 3.0 %multiply_reduce_fusion.11 = f32[256,128]{1,0:T(8,128)S(1)} fusion(f32[16,256,128]{2,1,0:T(8,128)S(1)} %fusion.117, s32[16,256]{1,0:T(8,128)S(1)} %subtract_bitcast_fusion.9, f32[16,256]{1,0:T(8,128)S(1)} %dynamic-slice_bitcast_fusion.4, bf16[1536,128]{1,0:T(8,128)(2,1)S(1)} %get-tuple-element.839, s32[]{:T(128)S(6)} %select_n.101), kind=kOutput, calls=%fused_computation.18.clone.1 | convolution fusion | flops 809992192 | bytes 2457604 | tf_op jit(solution)/shard_map/while/body/eval_jaxpr/dot_general | solution.py:123
  95.8 3.0 %multiply_reduce_fusion.11 = f32[256,128]{1,0:T(8,128)S(1)} fusion(f32[16,256,128]{2,1,0:T(8,128)S(1)} %fusion.117, s32[16,256]{1,0:T(8,128)S(1)} %subtract_bitcast_fusion.9, f32[16,256]{1,0:T(8,128)S(1)} %dynamic-slice_bitcast_fusion.4, bf16[1536,128]{1,0:T(8,128)(2,1)S(1)} %get-tuple-element.839, s32[]{:T(128)S(6)} %select_n.101), kind=kOutput, calls=%fused_computation.18.clone.1 | convolution fusion | flops 809992192 | bytes 2457604 | tf_op jit(solution)/shard_map/while/body/eval_jaxpr/dot_general | solution.py:123
  104.1 3.0 %multiply_reduce_fusion.11 = f32[256,128]{1,0:T(8,128)S(1)} fusion(f32[16,256,128]{2,1,0:T(8,128)S(1)} %fusion.117, s32[16,256]{1,0:T(8,128)S(1)} %subtract_bitcast_fusion.9, f32[16,256]{1,0:T(8,128)S(1)} %dynamic-slice_bitcast_fusion.4, bf16[1536,128]{1,0:T(8,128)(2,1)S(1)} %get-tuple-element.839, s32[]{:T(128)S(6)} %select_n.101), kind=kOutput, calls=%fused_computation.18.clone.1 | convolution fusion | flops 809992192 | bytes 2457604 | tf_op jit(solution)/shard_map/while/body/eval_jaxpr/dot_general | solution.py:123
  112.4 3.0 %multiply_reduce_fusion.11 = f32[256,128]{1,0:T(8,128)S(1)} fusion(f32[16,256,128]{2,1,0:T(8,128)S(1)} %fusion.117, s32[16,256]{1,0:T(8,128)S(1)} %subtract_bitcast_fusion.9, f32[16,256]{1,0:T(8,128)S(1)} %dynamic-slice_bitcast_fusion.4, bf16[1536,128]{1,0:T(8,128)(2,1)S(1)} %get-tuple-element.839, s32[]{:T(128)S(6)} %select_n.101), kind=kOutput, calls=%fused_computation.18.clone.1 | convolution fusion | flops 809992192 | bytes 2457604 | tf_op jit(solution)/shard_map/while/body/eval_jaxpr/dot_general | solution.py:123
  115.6 1.3 gather_fusion.2
  117.2 3.5 %collective-permute-start.5 = (bf16[256,128]{1,0:T(8,128)(2,1)S(1)}, bf16[256,128]{1,0:T(8,128)(2,1)S(1)}, u32[]{:S(2)}, u32[]{:S(2)}) collective-permute-start(bf16[256,128]{1,0:T(8,128)(2,1)S(1)} %get-tuple-element.532), channel_id=1, source_target_pairs={{1,0},{2,1},{3,2},{4,3},{5,4},{6,5},{7,6},{0,7},{9,8},{10,9},{11,1... | collective-permute-start | bytes 196616 | tf_op jit(solution)/shard_map/ppermute | solution.py:21
  122.8 31.9 %while.46 = (s32[]{:T(128)}, bf16[4,256,128]{2,1,0:T(8,128)(2,1)S(1)}, bf16[4,256,128]{2,1,0:T(8,128)(2,1)S(1)}, bf16[4,8,4096]{2,1,0:T(8,128)(2,1)}, bf16[3,8,6...) while((s32[]{:T(128)}, ...), condition=%wide.region_8.10_spmd, body=%wide.region_6.9_spmd.sunk | while | flops 891293696 | bytes 6048455 | solution.py:141
  125.6 1.3 multiply_convert_fusion.27
  127.5 3.1 %multiply_reduce_fusion.12 = f32[256,128]{1,0:T(8,128)S(1)} fusion(f32[16,256,128]{2,1,0:T(8,128)S(1)} %fusion.125, s32[16,256]{1,0:T(8,128)S(1)} %subtract_bitcast_fusion.10, f32[16,256]{1,0:T(8,128)S(1)} %dynamic-slice_bitcast_fusion.5, bf16[1536,128]{1,0:T(8,128)(2,1)S(1)} %get-tuple-element.881, s32[]{:T(128)S(6)} %select_n.102), kind=kOutput, calls=%fused_computation.48.clone.1 | convolution fusion | flops 809992192 | bytes 2457604 | tf_op jit(solution)/shard_map/while/body/eval_jaxpr/dot_general | solution.py:123
  133.6 1.3 multiply_convert_fusion.27
  135.4 3.0 %multiply_reduce_fusion.12 = f32[256,128]{1,0:T(8,128)S(1)} fusion(f32[16,256,128]{2,1,0:T(8,128)S(1)} %fusion.125, s32[16,256]{1,0:T(8,128)S(1)} %subtract_bitcast_fusion.10, f32[16,256]{1,0:T(8,128)S(1)} %dynamic-slice_bitcast_fusion.5, bf16[1536,128]{1,0:T(8,128)(2,1)S(1)} %get-tuple-element.881, s32[]{:T(128)S(6)} %select_n.102), kind=kOutput, calls=%fused_computation.48.clone.1 | convolution fusion | flops 809992192 | bytes 2457604 | tf_op jit(solution)/shard_map/while/body/eval_jaxpr/dot_general | solution.py:123
  143.4 3.0 %multiply_reduce_fusion.12 = f32[256,128]{1,0:T(8,128)S(1)} fusion(f32[16,256,128]{2,1,0:T(8,128)S(1)} %fusion.125, s32[16,256]{1,0:T(8,128)S(1)} %subtract_bitcast_fusion.10, f32[16,256]{1,0:T(8,128)S(1)} %dynamic-slice_bitcast_fusion.5, bf16[1536,128]{1,0:T(8,128)(2,1)S(1)} %get-tuple-element.881, s32[]{:T(128)S(6)} %select_n.102), kind=kOutput, calls=%fused_computation.48.clone.1 | convolution fusion | flops 809992192 | bytes 2457604 | tf_op jit(solution)/shard_map/while/body/eval_jaxpr/dot_general | solution.py:123
  151.4 3.0 %multiply_reduce_fusion.12 = f32[256,128]{1,0:T(8,128)S(1)} fusion(f32[16,256,128]{2,1,0:T(8,128)S(1)} %fusion.125, s32[16,256]{1,0:T(8,128)S(1)} %subtract_bitcast_fusion.10, f32[16,256]{1,0:T(8,128)S(1)} %dynamic-slice_bitcast_fusion.5, bf16[1536,128]{1,0:T(8,128)(2,1)S(1)} %get-tuple-element.881, s32[]{:T(128)S(6)} %select_n.102), kind=kOutput, calls=%fused_computation.48.clone.1 | convolution fusion | flops 809992192 | bytes 2457604 | tf_op jit(solution)/shard_map/while/body/eval_jaxpr/dot_general | solution.py:123
  154.7 1.3 gather_fusion.3
  156.2 3.6 %collective-permute-start.7 = (bf16[256,128]{1,0:T(8,128)(2,1)S(1)}, bf16[256,128]{1,0:T(8,128)(2,1)S(1)}, u32[]{:S(2)}, u32[]{:S(2)}) collective-permute-start(bf16[256,128]{1,0:T(8,128)(2,1)S(1)} %get-tuple-element.530), channel_id=1, source_target_pairs={{1,0},{2,1},{3,2},{4,3},{5,4},{6,5},{7,6},{0,7},{9,8},{10,9},{11,1... | collective-permute-start | bytes 196616 | tf_op jit(solution)/shard_map/ppermute | solution.py:21
  162.5 38.8 %while.47 = (s32[]{:T(128)}, f32[4,3,256]{2,1,0:T(4,128)S(1)}, bf16[4,8,4096]{2,1,0:T(8,128)(2,1)}, bf16[3,8,64]{2,1,0:T(8,128)(2,1)S(1)}, bf16[3,64,128]{2,1,0:...) while((s32[]{:T(128)}, f32[4,3,256]{2,1,0:T(4,128)S(1)}, ...), condition=%wide.region_12.14_spmd, body=%wide.region_9.13_spmd.sunk | while | flops 882703616 | bytes 6305487 | solution.py:161
  167.7 4.5 %multiply_reduce_fusion.13 = f32[16,256]{1,0:T(8,128)S(1)} fusion(f32[16,256,128]{1,2,0:T(8,128)S(1)} %fusion.132, s32[16,256]{1,0:T(8,128)S(1)} %subtract_bitcast_fusion.11, f32[256,128]{0,1:T(8,128)S(1)} %bitcast_convert_fusion.2, bf16[1536,128]{1,0:T(8,128)(2,1)} %get-tuple-element.923, s32[]{:T(128)S(6)} %select_n.103), kind=kOutput, calls=%fused_computation.78.clone.1 | convolution fusion | flops 810020864 | bytes 2457604 | tf_op jit(solution)/shard_map/while/body/eval_jaxpr/dot_general | solution.py:123
  177.4 4.5 %multiply_reduce_fusion.13 = f32[16,256]{1,0:T(8,128)S(1)} fusion(f32[16,256,128]{1,2,0:T(8,128)S(1)} %fusion.132, s32[16,256]{1,0:T(8,128)S(1)} %subtract_bitcast_fusion.11, f32[256,128]{0,1:T(8,128)S(1)} %bitcast_convert_fusion.2, bf16[1536,128]{1,0:T(8,128)(2,1)} %get-tuple-element.923, s32[]{:T(128)S(6)} %select_n.103), kind=kOutput, calls=%fused_computation.78.clone.1 | convolution fusion | flops 810020864 | bytes 2457604 | tf_op jit(solution)/shard_map/while/body/eval_jaxpr/dot_general | solution.py:123
  187.1 4.5 %multiply_reduce_fusion.13 = f32[16,256]{1,0:T(8,128)S(1)} fusion(f32[16,256,128]{1,2,0:T(8,128)S(1)} %fusion.132, s32[16,256]{1,0:T(8,128)S(1)} %subtract_bitcast_fusion.11, f32[256,128]{0,1:T(8,128)S(1)} %bitcast_convert_fusion.2, bf16[1536,128]{1,0:T(8,128)(2,1)} %get-tuple-element.923, s32[]{:T(128)S(6)} %select_n.103), kind=kOutput, calls=%fused_computation.78.clone.1 | convolution fusion | flops 810020864 | bytes 2457604 | tf_op jit(solution)/shard_map/while/body/eval_jaxpr/dot_general | solution.py:123
  196.8 4.5 %multiply_reduce_fusion.13 = f32[16,256]{1,0:T(8,128)S(1)} fusion(f32[16,256,128]{1,2,0:T(8,128)S(1)} %fusion.132, s32[16,256]{1,0:T(8,128)S(1)} %subtract_bitcast_fusion.11, f32[256,128]{0,1:T(8,128)S(1)} %bitcast_convert_fusion.2, bf16[1536,128]{1,0:T(8,128)(2,1)} %get-tuple-element.923, s32[]{:T(128)S(6)} %select_n.103), kind=kOutput, calls=%fused_computation.78.clone.1 | convolution fusion | flops 810020864 | bytes 2457604 | tf_op jit(solution)/shard_map/while/body/eval_jaxpr/dot_general | solution.py:123
  202.0 17.8 %all-reduce = (f32[]{:T(128)}, f32[]{:T(128)}, f32[]{:T(128)}) all-reduce(f32[]{:T(128)} %multiply_reduce_fusion.3, f32[]{:T(128)} %multiply_reduce_fusion.7, f32[]{:T(128)} %add_reduce_fusion), channel_id=1, replica_groups=mesh['img'=4,'atom'=8] {'atom'}, use_global_device_ids=true, to_apply=%region_20.22 | all-reduce | flops 3 | bytes 24 | tf_op jit(solution)/shard_map/psum | solution.py:191
  (177 shorter events, 57.2 us)
Async XLA Ops:
  0.6 13.4 %copy-start = (bf16[4,128]{1,0:T(4,128)(2,1)S(1)}, bf16[4,128]{1,0:T(4,128)(2,1)}, u32[]{:S(2)}) copy-start(bf16[4,128]{1,0:T(4,128)(2,1)} %param.28) | copy-start | bytes 3076
  0.6 16.1 %copy-start.3 = (s32[1024]{0:T(1024)S(1)}, s32[1024]{0:T(1024)}, u32[]{:S(2)}) copy-start(s32[1024]{0:T(1024)} %param.23) | copy-start | bytes 12292
  0.7 16.0 %copy-start.4 = (s32[1024]{0:T(1024)S(1)}, s32[1024]{0:T(1024)}, u32[]{:S(2)}) copy-start(s32[1024]{0:T(1024)} %param.24) | copy-start | bytes 12292
  0.7 16.1 %copy-start.6 = (f32[4]{0:T(128)S(1)}, f32[4]{0:T(128)}, u32[]{:S(2)}) copy-start(f32[4]{0:T(128)} %param.29) | copy-start | bytes 52
  0.7 16.3 %copy-start.2 = (s32[16,1024]{1,0:T(8,128)S(1)}, s32[16,1024]{1,0:T(8,128)}, u32[]{:S(2)}) copy-start(s32[16,1024]{1,0:T(8,128)} %param.25) | copy-start | bytes 196612
  1.7 64.0 %collective-permute-start.8 = (f32[1,3,1024]{1,2,0:T(8,128)S(1)}, f32[1,3,1024]{1,2,0:T(8,128)S(1)}, u32[]{:S(2)}, u32[]{:S(2)}) collective-permute-start(f32[1,3,1024]{1,2,0:T(8,128)S(1)} %copy.71), channel_id=1, source_target_pairs={{0,8},{8,16},{16,24},{1,9},{9,17},{17,25},{2,10},{10,18},{18,26},{... | collective-permute-start | bytes 36872 | tf_op jit(solution)/shard_map/ppermute | solution.py:18
  6.6 59.1 %collective-permute-start.9 = (f32[1,3,1024]{1,2,0:T(8,128)S(1)}, f32[1,3,1024]{1,2,0:T(8,128)S(1)}, u32[]{:S(2)}, u32[]{:S(2)}) collective-permute-start(f32[1,3,1024]{1,2,0:T(8,128)S(1)} %copy.71), channel_id=1, source_target_pairs={{8,0},{16,8},{24,16},{9,1},{17,9},{25,17},{10,2},{18,10},{26,18},{... | collective-permute-start | bytes 36872 | tf_op jit(solution)/shard_map/ppermute | solution.py:21
  10.5 7.3 %collective-permute-start = (f32[3,256]{0,1:T(8,128)S(1)}, f32[3,256]{0,1:T(8,128)S(1)}, u32[]{:S(2)}, u32[]{:S(2)}) collective-permute-start(f32[3,256]{0,1:T(8,128)S(1)} %get-tuple-element.527), channel_id=1, source_target_pairs={{0,1},{1,2},{2,3},{3,4},{4,5},{5,6},{6,7},{7,0},{8,9},{9,10},{10,1... | collective-permute-start | bytes 9224 | tf_op jit(solution)/shard_map/ppermute | solution.py:18
  10.5 10.9 %collective-permute-start.1 = (f32[3,256]{0,1:T(8,128)S(1)}, f32[3,256]{0,1:T(8,128)S(1)}, u32[]{:S(2)}, u32[]{:S(2)}) collective-permute-start(f32[3,256]{0,1:T(8,128)S(1)} %get-tuple-element.528), channel_id=1, source_target_pairs={{1,0},{2,1},{3,2},{4,3},{5,4},{6,5},{7,6},{0,7},{9,8},{10,9},{11,1... | collective-permute-start | bytes 9224 | tf_op jit(solution)/shard_map/ppermute | solution.py:21
  16.6 65.7 %collective-permute-start.2 = (bf16[256,128]{1,0:T(8,128)(2,1)S(1)}, bf16[256,128]{1,0:T(8,128)(2,1)S(1)}, u32[]{:S(2)}, u32[]{:S(2)}) collective-permute-start(bf16[256,128]{1,0:T(8,128)(2,1)S(1)} %get-tuple-element.533), channel_id=1, source_target_pairs={{0,1},{1,2},{2,3},{3,4},{4,5},{5,6},{6,7},{7,0},{8,9},{9,10},{10,1... | collective-permute-start | bytes 196616 | tf_op jit(solution)/shard_map/ppermute | solution.py:18
  17.8 64.5 %collective-permute-start.3 = (bf16[256,128]{1,0:T(8,128)(2,1)S(1)}, bf16[256,128]{1,0:T(8,128)(2,1)S(1)}, u32[]{:S(2)}, u32[]{:S(2)}) collective-permute-start(bf16[256,128]{1,0:T(8,128)(2,1)S(1)} %get-tuple-element.534), channel_id=1, source_target_pairs={{1,0},{2,1},{3,2},{4,3},{5,4},{6,5},{7,6},{0,7},{9,8},{10,9},{11,1... | collective-permute-start | bytes 196616 | tf_op jit(solution)/shard_map/ppermute | solution.py:21
  65.7 16.7 %copy-start.1 = (bf16[3,64,128]{2,1,0:T(8,128)(2,1)S(1)}, bf16[3,64,128]{2,1,0:T(8,128)(2,1)}, u32[]{:S(2)}) copy-start(bf16[3,64,128]{2,1,0:T(8,128)(2,1)} %param.31) | copy-start | bytes 147460
  65.7 16.7 %copy-start.7 = (bf16[2,128,128]{2,1,0:T(8,128)(2,1)S(1)}, bf16[2,128,128]{2,1,0:T(8,128)(2,1)}, u32[]{:S(2)}) copy-start(bf16[2,128,128]{2,1,0:T(8,128)(2,1)} %param.32) | copy-start | bytes 196612
  65.7 16.7 %copy-start.8 = (bf16[3,8,64]{2,1,0:T(8,128)(2,1)S(1)}, bf16[3,8,64]{2,1,0:T(8,128)(2,1)}, u32[]{:S(2)}) copy-start(bf16[3,8,64]{2,1,0:T(8,128)(2,1)} %param.30) | copy-start | bytes 9220
  117.1 5.5 %collective-permute-start.4 = (bf16[256,128]{1,0:T(8,128)(2,1)S(1)}, bf16[256,128]{1,0:T(8,128)(2,1)S(1)}, u32[]{:S(2)}, u32[]{:S(2)}) collective-permute-start(bf16[256,128]{1,0:T(8,128)(2,1)S(1)} %get-tuple-element.531), channel_id=1, source_target_pairs={{0,1},{1,2},{2,3},{3,4},{4,5},{5,6},{6,7},{7,0},{8,9},{9,10},{10,1... | collective-permute-start | bytes 196616 | tf_op jit(solution)/shard_map/ppermute | solution.py:18
  117.2 5.5 %collective-permute-start.5 = (bf16[256,128]{1,0:T(8,128)(2,1)S(1)}, bf16[256,128]{1,0:T(8,128)(2,1)S(1)}, u32[]{:S(2)}, u32[]{:S(2)}) collective-permute-start(bf16[256,128]{1,0:T(8,128)(2,1)S(1)} %get-tuple-element.532), channel_id=1, source_target_pairs={{1,0},{2,1},{3,2},{4,3},{5,4},{6,5},{7,6},{0,7},{9,8},{10,9},{11,1... | collective-permute-start | bytes 196616 | tf_op jit(solution)/shard_map/ppermute | solution.py:21
  122.8 37.1 %copy-start.5 = (bf16[128]{0:T(256)(128)(2,1)S(1)}, bf16[128]{0:T(256)(128)(2,1)}, u32[]{:S(2)}) copy-start(bf16[128]{0:T(256)(128)(2,1)} %param.33) | copy-start | bytes 772
  156.2 5.6 %collective-permute-start.6 = (bf16[256,128]{1,0:T(8,128)(2,1)S(1)}, bf16[256,128]{1,0:T(8,128)(2,1)S(1)}, u32[]{:S(2)}, u32[]{:S(2)}) collective-permute-start(bf16[256,128]{1,0:T(8,128)(2,1)S(1)} %get-tuple-element.529), channel_id=1, source_target_pairs={{0,1},{1,2},{2,3},{3,4},{4,5},{5,6},{6,7},{7,0},{8,9},{9,10},{10,1... | collective-permute-start | bytes 196616 | tf_op jit(solution)/shard_map/ppermute | solution.py:18
  156.2 5.5 %collective-permute-start.7 = (bf16[256,128]{1,0:T(8,128)(2,1)S(1)}, bf16[256,128]{1,0:T(8,128)(2,1)S(1)}, u32[]{:S(2)}, u32[]{:S(2)}) collective-permute-start(bf16[256,128]{1,0:T(8,128)(2,1)S(1)} %get-tuple-element.530), channel_id=1, source_target_pairs={{1,0},{2,1},{3,2},{4,3},{5,4},{6,5},{7,6},{0,7},{9,8},{10,9},{11,1... | collective-permute-start | bytes 196616 | tf_op jit(solution)/shard_map/ppermute | solution.py:21
where the time goes:
time: 227 us; the launch traced here: 225 us
  matrix products  91.6 us (40%)
  loops' own time  35.7 us (16%)
  blocking collectives  32.1 us (14%)
  starting transfers between devices  20.6 us (9%)
  local copies, waits for them, and re-layouts  18.4 us (8%)
  other arithmetic  17.2 us (8%)
  between operations  6.91 us (3%)
    dot_general x12, matrix products, fetch(): jnp.dot(picks, near_rows, preferred_element_type=jnp.float32)  42.2 us
    dot_general x4, matrix products, locate(): lax.dot_general(near_pos, picks, (((1,), (1,)), ((), ())), precision=lax....  24.8 us
    psum x1, blocking collectives, on_device(): lax.psum((jnp.sum(tangent * tangent), jnp.sum(force * tangent)), 'atom')  17.8 us
    dot_general x12, matrix products, radial_field(): lax.dot_general(w_in, basis, (((0,), (0,)), ((), ())), preferred_element_...  15.9 us
    ppermute x5, starting transfers between devices, padded(): lax.ppermute(lax.slice_in_dim(block, 0, width, axis=dim), axis, backward)  15.5 us
    another operation x2, loops' own time, on_device(): lax.map(step, (nbr_blocks, block_starts, basis_blocks, live_blocks, feats...  15 us
    psum x1, blocking collectives, on_device(): lax.psum((energy_part, jnp.sum(behind * behind), jnp.sum(ahead * ahead)),...  14.3 us
    another operation x1, loops' own time, on_device(): delta_blocks = lax.map(locate, (nbr_blocks, block_starts))  12.8 us
  transfers between devices with their start and end apart: 10, of which 2 were waited for; matrix products, arithmetic and copies ran while one was open for 18% of the time, Pallas kernels for 0%

commit v1 on v0

v1 whole, which is shorter than its diff:
```python
import functools
import math

import jax
import jax.numpy as jnp
from jax import lax
from jax.experimental import pallas as pl
from jax.experimental.pallas import tpu as pltpu
from jax.sharding import PartitionSpec as P

F32 = jnp.float32
BF16 = jnp.bfloat16
I32 = jnp.int32
LANES = 128
SPRING = 5.0
SPECIES_ROW = 3
COUNT_ROW = 4
SEND_ROW = 5
PACK_ROWS = 8
SUM_ROWS = 8
VMEM = pl.BlockSpec(memory_space=pltpu.VMEM)
SMEM = pl.BlockSpec(memory_space=pltpu.SMEM)


def dot(a, b):
    return jnp.dot(a, b, preferred_element_type=F32)


def silu_of_half(half):
    return half + half * jnp.tanh(half)


def aligned(start, step):
    return pl.multiple_of(start, step)


def lane_fetch(windows, group, place):
    found = jnp.zeros(place.shape, F32)
    for k, window in enumerate(windows):
        rows = jnp.broadcast_to(window, place.shape)
        picked = jnp.take_along_axis(rows, place, axis=1, mode="promise_in_bounds")
        found = jnp.where(group == k, picked, found)
    return found


def live_slots(pk, lo, fan, width):
    slots = lax.broadcasted_iota(I32, (fan, width), 0).astype(F32)
    return slots < pk[COUNT_ROW : COUNT_ROW + 1, pl.ds(lo, width)]


def geometry(table, table_lo, pk, nbr, lo, rim):
    fan = nbr.shape[0]
    parts = []
    for half in range(rim // LANES):
        first = lo + half * LANES
        start = table_lo + half * LANES
        rel = nbr[:, pl.ds(aligned(first, LANES), LANES)] - first
        place = rel & (LANES - 1)
        group = rel // LANES
        live = live_slots(pk, aligned(first, LANES), fan, LANES)
        spans = [
            table[:, pl.ds(aligned(start + k * LANES, LANES), LANES)]
            for k in range(2 * rim // LANES + 1)
        ]
        deltas = []
        for c in range(3):
            far = lane_fetch([span[c : c + 1] for span in spans], group, place)
            deltas.append(far - pk[c : c + 1, pl.ds(aligned(first, LANES), LANES)])
        kinds = lane_fetch([span[SPECIES_ROW : SPECIES_ROW + 1] for span in spans], group, place)
        parts.append(deltas + [jnp.where(live, kinds, -1.0)])
    joined = [jnp.concatenate(list(piece), axis=1) for piece in zip(*parts)]
    return joined[:3], joined[3]


def basis_of(deltas, basis_count):
    dist_sq = deltas[0] * deltas[0] + deltas[1] * deltas[1] + deltas[2] * deltas[2]
    fan, width = dist_sq.shape
    centres = 2.0 * lax.broadcasted_iota(I32, (basis_count, width), 0).astype(F32)
    rows = []
    for s in range(fan):
        away = jnp.broadcast_to(dist_sq[s : s + 1], (basis_count, width)) - centres
        rows.append(jnp.exp(away * away * -0.125))
    return jnp.concatenate(rows, axis=0).astype(BF16)


def spread_first_layer(rad_in, layer, spread):
    count, units = rad_in.shape[1:]
    fan = spread.shape[0] // units
    half = rad_in[layer].astype(F32) * 0.5
    turned = jnp.concatenate([half] * fan, axis=0).T
    owner = lax.broadcasted_iota(I32, turned.shape, 1) // count
    for s in range(fan):
        spread[s * units : (s + 1) * units, :] = jnp.where(owner == s, turned, 0.0).astype(BF16)


def hidden_of(spread, basis):
    return silu_of_half(dot(spread[...], basis)).astype(BF16)


def turned_weight(ref, layer, scale=1.0):
    return (ref[layer].astype(F32) * scale).T.astype(BF16)


def fetch_rows(table, table_lo, places, s, rim):
    rows = lax.broadcasted_iota(I32, (rim, rim), 0).astype(F32).astype(BF16)
    one, zero = jnp.ones((), BF16), jnp.zeros((), BF16)
    picks = jnp.concatenate(
        [jnp.where(rows == place[s : s + 1], one, zero) for place in places], axis=0
    )
    return dot(table[:, pl.ds(table_lo, len(places) * rim)], picks)


def places_of(pk, nbr, lo, rim):
    fan = nbr.shape[0]
    rel = nbr[:, pl.ds(lo, rim)] - lo
    rel = jnp.where(live_slots(pk, lo, fan, rim), rel, -1)
    return [jnp.clip(rel - k * rim, -1, rim).astype(F32).astype(BF16) for k in range(3)]


def update_of(feats, summed, mix_half, fan):
    scaled = (summed * (1.0 / math.sqrt(fan))).astype(BF16)
    return (feats.astype(F32) + silu_of_half(dot(mix_half, scaled))).astype(BF16)


def first_block(table, table_lo, pk, nbr, lo, rim, weights, spread, hid):
    embed_t, first, mix_half = weights
    fan = nbr.shape[0]
    chans = mix_half.shape[0]
    kinds_count = embed_t.shape[1]
    units = spread.shape[0] // fan
    species = first.shape[1] // units
    deltas, kinds = geometry(table, table_lo, pk, nbr, lo, rim)
    basis = basis_of(deltas, spread.shape[1] // fan)
    hid[...] = hidden_of(spread, basis)
    kinds = kinds.astype(BF16)
    zero = jnp.zeros((), BF16)
    summed = jnp.zeros((chans, rim), F32)
    for s in range(fan):
        mine = hid[s * units : (s + 1) * units, :]
        kind = jnp.broadcast_to(kinds[s : s + 1], (units, rim))
        sorted_out = [
            jnp.where(kind == jnp.full((), k, BF16), mine, zero) for k in range(species)
        ]
        summed = summed + dot(first, jnp.concatenate(sorted_out, axis=0))
    rows = lax.broadcasted_iota(I32, (kinds_count, rim), 0).astype(F32)
    own = rows == pk[SPECIES_ROW : SPECIES_ROW + 1, pl.ds(lo, rim)]
    feats = dot(embed_t, jnp.where(own, 1.0, 0.0).astype(BF16))
    return deltas, basis, update_of(feats, summed, mix_half, fan)


def first_weights(embed, rad_in, rad_out, mixing, spread):
    spread_first_layer(rad_in, 0, spread)
    out = rad_out[0].astype(F32)
    table = embed[...].astype(F32)
    species = table.shape[0]
    kinds_count = -(-species // 16) * 16
    padded = jnp.concatenate(
        [table, jnp.zeros((kinds_count - species, table.shape[1]), F32)], axis=0
    )
    embed_t = padded.T.astype(BF16)
    first = jnp.concatenate([out * table[k : k + 1] for k in range(species)], axis=0)
    return embed_t, first.T.astype(BF16), turned_weight(mixing, 0, 0.5)


def store_block(i, deltas, basis, delta_out, basis_out):
    fan = deltas[0].shape[0]
    for c in range(3):
        delta_out[i, c * fan : (c + 1) * fan, :] = deltas[c]
    basis_out[i] = basis


def first_inner(rim, pk, nbr, embed, rad_in, rad_out, mixing, delta_out, basis_out, feats_out, spread, hid):
    weights = first_weights(embed, rad_in, rad_out, mixing, spread)

    def body(i, carry):
        lo = aligned((i + 1) * rim, rim)
        deltas, basis, feats = first_block(
            pk, lo - rim, pk, nbr, lo, rim, weights, spread, hid
        )
        store_block(i, deltas, basis, delta_out, basis_out)
        feats_out[:, pl.ds(aligned(i * rim, rim), rim)] = feats
        return carry

    lax.fori_loop(0, feats_out.shape[1] // rim, body, 0)


def pack_halo(feats, pk, core, rim, to_mate, to_cross):
    atoms = feats.shape[1]
    rows = lax.broadcasted_iota(I32, (rim, rim), 0).astype(F32).astype(BF16)
    one, zero = jnp.ones((), BF16), jnp.zeros((), BF16)
    for ref, start in ((to_mate, (1 - core) * rim), (to_cross, core * rim)):
        wanted = pk[SEND_ROW : SEND_ROW + 1, pl.ds(aligned(start, rim), rim)]
        picks = jnp.concatenate(
            [
                jnp.where(
                    rows == jnp.clip(wanted - k * rim, -1.0, float(rim)).astype(BF16), one, zero
                )
                for k in range(atoms // rim)
            ],
            axis=0,
        )
        ref[...] = dot(feats[...], picks).astype(BF16)


def halo_places(core, atoms, rim):
    top = atoms + rim
    return aligned((1 - core) * top, rim), aligned(core * top, rim)


def first_outer(rim, core_ref, pk, mate, cross, nbr, embed, rad_in, rad_out, mixing, inner, delta_out, basis_out, feats_out, to_mate, to_cross, table, spread, hid):
    core = core_ref[0]
    atoms = pk.shape[1]
    weights = first_weights(embed, rad_in, rad_out, mixing, spread)
    table[:, rim : rim + atoms] = pk[...]
    at_mate, at_cross = halo_places(core, atoms, rim)
    for ref, start, at in ((mate, core * rim, at_mate), (cross, (1 - core) * rim, at_cross)):
        for half in range(rim // LANES):
            wanted = ref[SEND_ROW : SEND_ROW + 1, pl.ds(aligned(start + half * LANES, LANES), LANES)]
            wanted = jnp.broadcast_to(wanted.astype(I32), (PACK_ROWS, LANES))
            spans = [ref[:, k * LANES : (k + 1) * LANES] for k in range(atoms // LANES)]
            table[:, pl.ds(aligned(at + half * LANES, LANES), LANES)] = lane_fetch(
                spans, wanted // LANES, wanted & (LANES - 1)
            )
    feats_out[:, rim : atoms - rim] = inner[...]

    def body(i, carry):
        lo = aligned(i * (atoms - rim), rim)
        deltas, basis, feats = first_block(table, lo, pk, nbr, lo, rim, weights, spread, hid)
        store_block(i, deltas, basis, delta_out, basis_out)
        feats_out[:, pl.ds(lo, rim)] = feats
        return carry

    lax.fori_loop(0, 2, body, 0)
    pack_halo(feats_out, pk, core, rim, to_mate, to_cross)


def layer_block(table, table_lo, pk, nbr, lo, rim, hid, out_t, mix_half, own):
    fan = nbr.shape[0]
    units = out_t.shape[1]
    places = places_of(pk, nbr, lo, rim)
    summed = jnp.zeros(own.shape, F32)
    for s in range(fan):
        far = fetch_rows(table, table_lo, places, s, rim)
        summed = summed + far * dot(out_t, hid(slice(s * units, (s + 1) * units)))
    return update_of(own, summed, mix_half, fan)


def layer_inner(rim, layer, pk, nbr, rad_in, rad_out, mixing, feats, basis, basis_edge, feats_out, hid_edge, spread, hid):
    spread_first_layer(rad_in, layer, spread)
    out_t = turned_weight(rad_out, layer)
    mix_half = turned_weight(mixing, layer, 0.5)

    def body(i, carry):
        lo = aligned((i + 1) * rim, rim)
        hid[...] = hidden_of(spread, basis[i])
        own = feats[:, pl.ds(lo, rim)]
        feats_out[:, pl.ds(aligned(i * rim, rim), rim)] = layer_block(
            feats, aligned(lo - rim, rim), pk, nbr, lo, rim, lambda r: hid[r, :], out_t, mix_half, own
        )
        return carry

    lax.fori_loop(0, basis.shape[0], body, 0)
    for i in range(2):
        hid_edge[i] = hidden_of(spread, basis_edge[i])


def fill_table(table, feats, mate, cross, core, rim):
    atoms = feats.shape[1]
    at_mate, at_cross = halo_places(core, atoms, rim)
    table[:, rim : rim + atoms] = feats[...]
    table[:, pl.ds(at_mate, rim)] = mate[...]
    table[:, pl.ds(at_cross, rim)] = cross[...]


def layer_outer(rim, layer, core_ref, pk, nbr, rad_out, mixing, feats, mate, cross, hid_edge, inner, feats_out, to_mate, to_cross, table):
    core = core_ref[0]
    atoms = pk.shape[1]
    out_t = turned_weight(rad_out, layer)
    mix_half = turned_weight(mixing, layer, 0.5)
    fill_table(table, feats, mate, cross, core, rim)
    feats_out[:, rim : atoms - rim] = inner[...]

    def body(i, carry):
        lo = aligned(i * (atoms - rim), rim)
        own = feats[:, pl.ds(lo, rim)]
        feats_out[:, pl.ds(lo, rim)] = layer_block(
            table, lo, pk, nbr, lo, rim, lambda r: hid_edge[i, r, :], out_t, mix_half, own
        )
        return carry

    lax.fori_loop(0, 2, body, 0)
    pack_halo(feats_out, pk, core, rim, to_mate, to_cross)


def head_block(table, table_lo, pk, nbr, lo, rim, hid, out_t, own, delta):
    fan = nbr.shape[0]
    chans, units = out_t.shape
    places = places_of(pk, nbr, lo, rim)
    near = own.astype(F32)
    pairs = []
    for s in range(fan):
        far = fetch_rows(table, table_lo, places, s, rim)
        terms = far * (dot(out_t, hid(slice(s * units, (s + 1) * units))) * near)
        pairs.append(jnp.sum(terms, axis=0, keepdims=True))
    pair = jnp.concatenate(pairs, axis=0) * (1.0 / math.sqrt(chans))
    rows = [
        jnp.sum(pair * delta[c * fan : (c + 1) * fan, :], axis=0, keepdims=True) for c in range(3)
    ]
    return jnp.concatenate(rows + [jnp.zeros((PACK_ROWS - 3, rim), F32)], axis=0)


def head_inner(rim, layer, pk, nbr, rad_in, rad_out, feats, basis, delta, basis_edge, force_out, hid_edge, spread, hid):
    spread_first_layer(rad_in, layer, spread)
    out_t = turned_weight(rad_out, layer)

    def body(i, carry):
        lo = aligned((i + 1) * rim, rim)
        hid[...] = hidden_of(spread, basis[i])
        force_out[:, pl.ds(aligned(i * rim, rim), rim)] = head_block(
            feats, aligned(lo - rim, rim), pk, nbr, lo, rim, lambda r: hid[r, :], out_t,
            feats[:, pl.ds(lo, rim)], delta.at[i],
        )
        return carry

    lax.fori_loop(0, basis.shape[0], body, 0)
    for i in range(2):
        hid_edge[i] = hidden_of(spread, basis_edge[i])


def lane_sum(values):
    total = values[:, :LANES]
    for k in range(1, values.shape[1] // LANES):
        total = total + values[:, k * LANES : (k + 1) * LANES]
    return jnp.sum(total, axis=0, keepdims=True)


def head_outer(rim, layer, core_ref, ref_energy, pk, behind, ahead, nbr, rad_out, w_energy, feats, mate, cross, hid_edge, delta, inner, force_out, sums_out, table):
    core = core_ref[0]
    atoms = pk.shape[1]
    out_t = turned_weight(rad_out, layer)
    fill_table(table, feats, mate, cross, core, rim)
    force_out[:, rim : atoms - rim] = inner[...]

    def body(i, carry):
        lo = aligned(i * (atoms - rim), rim)
        force_out[:, pl.ds(lo, rim)] = head_block(
            table, lo, pk, nbr, lo, rim, lambda r: hid_edge[i, r, :], out_t,
            feats[:, pl.ds(lo, rim)], delta.at[i],
        )
        return carry

    lax.fori_loop(0, 2, body, 0)
    readout = dot(w_energy[...], feats[...])
    kinds = pk[SPECIES_ROW : SPECIES_ROW + 1, :]
    energy = readout
    for k in range(ref_energy.shape[0]):
        energy = energy + jnp.where(kinds == float(k), ref_energy[k], 0.0)
    here = pk[0:3, :]
    back = here - behind[0:3, :]
    fore = ahead[0:3, :] - here
    force = force_out[0:3, :]
    rows = [energy, back * back, fore * fore, back * fore, force * back, force * fore]
    sums = [lane_sum(row) for row in rows]
    sums.append(jnp.zeros((SUM_ROWS - len(sums), LANES), F32))
    total = jnp.concatenate(sums, axis=0)
    for peer in range(sums_out.shape[0]):
        sums_out[peer] = total


def finish(count, flags, pk, behind, ahead, force, sums, result, energy_out):
    total = sums[0]
    for peer in range(1, sums.shape[0]):
        total = total + sums[peer]
    total = jnp.sum(total, axis=1, keepdims=True)
    energy, back_sq, fore_sq, cross, along_back, along_fore = (total[i : i + 1] for i in range(6))
    back_len = jnp.sqrt(back_sq + 1e-06)
    fore_len = jnp.sqrt(fore_sq + 1e-06)
    by_back, by_fore = 1.0 / back_len, 1.0 / fore_len
    tau_sq = (
        back_sq * by_back * by_back + fore_sq * by_fore * by_fore + 2.0 * cross * by_back * by_fore
    )
    proj = (along_back * by_back + along_fore * by_fore) / tau_sq
    spring = SPRING * (fore_len - back_len) / jnp.sqrt(tau_sq)
    climbing = flags[1] == 1
    is_end = flags[0] == 1
    factor = jnp.where(climbing, -2.0 * proj, spring - proj)
    here = pk[0:3, :]
    tangent = (here - behind[0:3, :]) * by_back + (ahead[0:3, :] - here) * by_fore
    moved = force[0:3, :] + factor * tangent
    result[0] = jnp.where(is_end, force[0:3, :], moved)
    energy_out[...] = energy * (1.0 / count)


def swap_pairs(count, offset):
    pairs = []
    for low in range(offset, count, 2):
        high = (low + 1) % count
        pairs += [(low, high), (high, low)]
    return pairs


def on_device(positions, species, counts, neighbours, send_list, climb, embed, ref_energy, rad_in, rad_out, mixing, w_energy):
    atoms = species.shape[0]
    rim = send_list.shape[0] // 2
    fan = neighbours.shape[0]
    chans = embed.shape[1]
    layers = mixing.shape[0]
    basis_count, units = rad_in.shape[1:]
    inner_blocks = atoms // rim - 2
    inner_atoms = inner_blocks * rim
    tiles = lax.axis_size("atom")
    images = lax.axis_size("img")
    core = lax.rem(lax.axis_index("atom"), 2)
    image = lax.axis_index("img")

    def call(body, operands, outs, scratch=()):
        scalars = {id(x) for x in (core_arr, ref_energy, flags)}
        return pl.pallas_call(
            body,
            out_shape=[jax.ShapeDtypeStruct(shape, dtype) for shape, dtype in outs],
            in_specs=[SMEM if id(x) in scalars else VMEM for x in operands],
            out_specs=[VMEM] * len(outs),
            scratch_shapes=[pltpu.VMEM(shape, dtype) for shape, dtype in scratch],
            compiler_params=pltpu.CompilerParams(vmem_limit_bytes=40 * 2**20),
        )(*operands)

    def swap(block, axis, offset):
        return lax.ppermute(block, axis, swap_pairs(lax.axis_size(axis), offset))

    core_arr = core.reshape(1).astype(I32)
    is_end = jnp.logical_or(image == 0, image == images - 1)
    flags = jnp.stack([is_end.astype(I32), climb[0]])
    pk = jnp.concatenate(
        [
            positions[0],
            species.astype(F32)[None],
            counts.astype(F32)[None],
            jnp.pad(send_list.astype(F32), (0, atoms - 2 * rim))[None],
            jnp.zeros((PACK_ROWS - 6, atoms), F32),
        ],
        axis=0,
    )
    w_row = w_energy[None]
    mate = swap(pk, "atom", 0)
    cross = swap(pk, "atom", 1)
    even = swap(pk, "img", 0)
    odd = swap(pk, "img", 1)

    feats_type = ((chans, atoms), BF16)
    halo_type = ((chans, rim), BF16)
    hid_scratch = [((fan * units, fan * basis_count), BF16), ((fan * units, rim), BF16)]
    table_scratch = [((chans, atoms + 2 * rim), BF16)]

    def block_outs(blocks):
        return [((blocks, 3 * fan, rim), F32), ((blocks, fan * basis_count, rim), BF16)]

    delta_in, basis_in, inner = call(
        functools.partial(first_inner, rim),
        (pk, neighbours, embed, rad_in, rad_out, mixing),
        block_outs(inner_blocks) + [((chans, inner_atoms), BF16)],
        hid_scratch,
    )
    delta_out, basis_out, feats, to_mate, to_cross = call(
        functools.partial(first_outer, rim),
        (core_arr, pk, mate, cross, neighbours, embed, rad_in, rad_out, mixing, inner),
        block_outs(2) + [feats_type, halo_type, halo_type],
        [((PACK_ROWS, atoms + 2 * rim), F32)] + hid_scratch,
    )
    hid_type = ((2, fan * units, rim), BF16)
    for layer in range(1, layers):
        mate = swap(to_mate, "atom", 0)
        cross = swap(to_cross, "atom", 1)
        inner, hid_edge = call(
            functools.partial(layer_inner, rim, layer),
            (pk, neighbours, rad_in, rad_out, mixing, feats, basis_in, basis_out),
            [((chans, inner_atoms), BF16), hid_type],
            hid_scratch,
        )
        feats, to_mate, to_cross = call(
            functools.partial(layer_outer, rim, layer),
            (core_arr, pk, neighbours, rad_out, mixing, feats, mate, cross, hid_edge, inner),
            [feats_type, halo_type, halo_type],
            table_scratch,
        )
    mate = swap(to_mate, "atom", 0)
    cross = swap(to_cross, "atom", 1)
    force_type = ((PACK_ROWS, atoms), F32)
    inner, hid_edge = call(
        functools.partial(head_inner, rim, layers),
        (pk, neighbours, rad_in, rad_out, feats, basis_in, delta_in, basis_out),
        [((PACK_ROWS, inner_atoms), F32), hid_type],
        hid_scratch,
    )
    odd_image = lax.rem(image, 2) == 1
    behind = jnp.where(odd_image, even, odd)
    ahead = jnp.where(odd_image, odd, even)
    force, sums = call(
        functools.partial(head_outer, rim, layers),
        (core_arr, ref_energy, pk, behind, ahead, neighbours, rad_out, w_row, feats, mate, cross, hid_edge, delta_out, inner),
        [force_type, ((tiles, SUM_ROWS, LANES), F32)],
        table_scratch,
    )
    sums = lax.all_to_all(sums, "atom", 0, 0)
    result, energy = call(
        functools.partial(finish, atoms * tiles),
        (flags, pk, behind, ahead, force, sums),
        [((1, 3, atoms), F32), ((1, 1), F32)],
    )
    return result, energy.reshape(1)


def solution(mesh):
    return jax.shard_map(
        on_device,
        mesh=mesh,
        in_specs=(
            P("img", None, "atom"),
            P("atom"),
            P("atom"),
            P(None, "atom"),
            P("atom"),
            P("img"),
            P(),
            P(),
            P(),
            P(),
            P(),
            P(),
        ),
        out_specs=(P("img", None, "atom"), P("img")),
        check_vma=False,
    )
```

time: 227 us -> 47.1 us (0.21)
  matrix products: 91.6 us -> 0 us
  loops' own time: 35.7 us -> 0 us
  blocking collectives: 32.1 us -> 0 us
  Pallas kernels: 0 us -> 21 us
  other arithmetic: 17.2 us -> 0.1 us
  local copies, waits for them, and re-layouts: 18.4 us -> 3.62 us
  starting transfers between devices: 20.6 us -> 14.8 us
  between operations: 6.91 us -> 1.51 us
  waiting for transfers between devices: 2.16 us -> 5.76 us
    dot_general x50 -> x0, matrix products: 91.6 us -> none  [the longest x12 42.2 us: fetch(): jnp.dot(picks, near_rows, preferred_element_type=jnp.float32)]
    another operation x4 -> x0, loops' own time: 35.7 us -> none  [the longest x2 15 us: on_device(): lax.map(step, (nbr_blocks, block_starts, basis_blocks, live_blocks, feats...]
    psum x2 -> x0, blocking collectives: 32.1 us -> none  [the longest x1 17.8 us: on_device(): lax.psum((jnp.sum(tangent * tangent), jnp.sum(force * tangent)), 'atom')]
    pallas_call x0 -> x7, Pallas kernels: none -> 21 us  [call(): pl.pallas_call(body, out_shape=[jax.ShapeDtypeStruct(shape, dtype) for sh...]
    dynamic_slice x28 -> x0, local copies, waits for them, and re-layouts: 10.4 us -> none  [the longest x16 9.6 us: on_device(): delta_blocks = lax.map(locate, (nbr_blocks, block_starts))]
    sub x16 -> x0, other arithmetic: 10 us -> none  [selector(): local_rows = nbr_b - start]
    ppermute x10 -> x8, starting transfers between devices: 20.6 us -> 11.5 us  [swap(): return lax.ppermute(block, axis, swap_pairs(lax.axis_size(axis), offset))]
    all_to_all x0 -> x1, waiting for transfers between devices: none -> 5.59 us  [on_device(): sums = lax.all_to_all(sums, 'atom', 0, 0)]
  transfers between devices with their start and end apart: 10 -> 9, of which waited for: 2 -> 2; matrix products, arithmetic and copies ran while one was open for 18% -> 0% of each run, Pallas kernels for 0% -> 28%
where the time goes in v1:
time: 47.1 us; the launch traced here: 46.8 us
  Pallas kernels  21 us (45%)
  starting transfers between devices  14.8 us (31%)
  waiting for transfers between devices  5.76 us (12%)
  local copies, waits for them, and re-layouts  3.62 us (8%)
  between operations  1.51 us (3%)
    pallas_call x7, Pallas kernels, call(): pl.pallas_call(body, out_shape=[jax.ShapeDtypeStruct(shape, dtype) for sh...  21 us
    ppermute x8, starting transfers between devices, swap(): return lax.ppermute(block, axis, swap_pairs(lax.axis_size(axis), offset))  11.5 us
    all_to_all x1, waiting for transfers between devices, on_device(): sums = lax.all_to_all(sums, 'atom', 0, 0)  5.59 us
    unnamed x24, local copies, waits for them, and re-layouts  3.56 us
    all_to_all x1, starting transfers between devices, on_device(): sums = lax.all_to_all(sums, 'atom', 0, 0)  3.33 us
  transfers between devices with their start and end apart: 9, of which 2 were waited for; matrix products, arithmetic and copies ran while one was open for 0% of the time, Pallas kernels for 28%

profile of v1, /device:TPU:0, one launch (start us, length us, event | category | flops | bytes accessed | tf_op | source)
XLA Modules:
  0.0 46.8 jit_solution(17645073194122164443)
XLA Ops:
  0.7 0.7 %copy.17 = f32[1,3,1024]{2,1,0:T(4,128)S(1)} copy(f32[1,3,1024]{2,0,1:T(1,128)} %param.12) | data formatting | bytes 24576
  1.5 0.0 copy-start.1
  1.5 0.5 %collective-permute-start.2 = (f32[8,1024]{1,0:T(8,128)S(1)}, f32[8,1024]{1,0:T(8,128)S(1)}, u32[]{:S(2)}, u32[]{:S(2)}) collective-permute-start(f32[8,1024]{1,0:T(8,128)S(1)} %concatenate.3.pk), channel_id=1, source_target_pairs={{0,1},{1,0},{2,3},{3,2},{4,5},{5,4},{6,7},{7,6},{8,9},{9,8},{10,11... | collective-permute-start | bytes 98312 | tf_op jit(solution)/shard_map/ppermute | solution.py:428
  2.1 4.7 %collective-permute-start.3 = (f32[8,1024]{1,0:T(8,128)S(1)}, f32[8,1024]{1,0:T(8,128)S(1)}, u32[]{:S(2)}, u32[]{:S(2)}) collective-permute-start(f32[8,1024]{1,0:T(8,128)S(1)} %concatenate.3.pk), channel_id=1, source_target_pairs={{1,2},{2,1},{3,4},{4,3},{5,6},{6,5},{7,0},{0,7},{9,10},{10,9},{11,... | collective-permute-start | bytes 98312 | tf_op jit(solution)/shard_map/ppermute | solution.py:428
  6.8 0.7 %copy-done.4 = bf16[3,8,64]{2,1,0:T(8,128)(2,1)S(1)} copy-done((bf16[3,8,64]{2,1,0:T(8,128)(2,1)S(1)}, bf16[3,8,64]{2,1,0:T(8,128)(2,1)}, u32[]{:S(2)}) %copy-start.4) | copy-done | bytes 3096
  7.5 0.0 copy-done.5
  7.5 0.8 %copy-done.2 = bf16[2,128,128]{2,1,0:T(8,128)(2,1)S(1)} copy-done((bf16[2,128,128]{2,1,0:T(8,128)(2,1)S(1)}, bf16[2,128,128]{2,1,0:T(8,128)(2,1)}, u32[]{:S(2)}) %copy-start.2) | copy-done | bytes 65560
  8.3 2.5 %shard_map.131 = (f32[2,48,256]{2,1,0:T(8,128)S(1)}, bf16[2,128,256]{2,1,0:T(8,128)(2,1)S(1)}, bf16[128,512]{1,0:T(8,128)(2,1)S(1)}) custom-call(f32[8,1024]{1,0:T(8,128)S(1)} %concatenate.3.pk, s32[16,1024]{1,0:T(8,128)S(1)} %copy-done, bf16[4,128]{1,0:T(4,128)(2,1)S(1)} %copy-done.5, bf16[3,8,64]{2,1,0:T(8,128)(2,1)S(1)} %copy-done.4, ...), custom_call_target="tpu_custom_call" | custom-call | tf_op jit(solution)/shard_map/pallas_call | solution.py:418
  10.8 0.0 collective-permute-done.2.mate
  10.8 0.0 copy-start.3
  10.8 2.9 %shard_map.132 = (f32[2,48,256]{2,1,0:T(8,128)S(1)}, bf16[2,128,256]{2,1,0:T(8,128)(2,1)S(1)}, bf16[128,1024]{1,0:T(8,128)(2,1)S(1)}, bf16[128,256]{1,0:T(8,128)(2,1)S(1)}, bf16[128,256]{1,0:T(8,128)(2,1)S(1)}) custom-call(s32[1]{0:T(128)} %bitcast.4.core_ref, f32[8,1024]{1,0:T(8,128)S(1)} %concatenate.3.pk, f32[8,1024]{1,0:T(8,128)S(1)} %collective-permute-done.2.mate, ...), custom_call_target="tpu_custom_call" | custom-call | tf_op jit(solution)/shard_map/pallas_call | solution.py:418
  13.7 0.1 collective-permute-start.4
  13.8 1.1 %collective-permute-start.5 = (bf16[128,256]{1,0:T(8,128)(2,1)S(1)}, bf16[128,256]{1,0:T(8,128)(2,1)S(1)}, u32[]{:S(2)}, u32[]{:S(2)}) collective-permute-start(bf16[128,256]{1,0:T(8,128)(2,1)S(1)} %get-tuple-element.24), channel_id=1, source_target_pairs={{1,2},{2,1},{3,4},{4,3},{5,6},{6,5},{7,0},{0,7},{9,10},{10,9},{11,... | collective-permute-start | bytes 196616 | tf_op jit(solution)/shard_map/ppermute | solution.py:428
  14.9 1.5 %collective-permute-start = (f32[8,1024]{1,0:T(8,128)S(1)}, f32[8,1024]{1,0:T(8,128)S(1)}, u32[]{:S(2)}, u32[]{:S(2)}) collective-permute-start(f32[8,1024]{1,0:T(8,128)S(1)} %concatenate.3.pk), channel_id=1, source_target_pairs={{0,8},{8,0},{16,24},{24,16},{1,9},{9,1},{17,25},{25,17},{2,10},{10... | collective-permute-start | bytes 98312 | tf_op jit(solution)/shard_map/ppermute | solution.py:428
  16.4 1.5 %collective-permute-start.1 = (f32[8,1024]{1,0:T(8,128)S(1)}, f32[8,1024]{1,0:T(8,128)S(1)}, u32[]{:S(2)}, u32[]{:S(2)}) collective-permute-start(f32[8,1024]{1,0:T(8,128)S(1)} %concatenate.3.pk), channel_id=1, source_target_pairs={{8,16},{16,8},{24,0},{0,24},{9,17},{17,9},{25,1},{1,25},{10,18},{1... | collective-permute-start | bytes 98312 | tf_op jit(solution)/shard_map/ppermute | solution.py:428
  18.6 3.7 %shard_map.133 = (bf16[128,512]{1,0:T(8,128)(2,1)S(1)}, bf16[2,1024,256]{2,1,0:T(8,128)(2,1)S(1)}) custom-call(f32[8,1024]{1,0:T(8,128)S(1)} %concatenate.3.pk, s32[16,1024]{1,0:T(8,128)S(1)} %copy-done, bf16[3,8,64]{2,1,0:T(8,128)(2,1)S(1)} %copy-done.4, bf16[3,64,128]{2,1,0:T(8,128)(2,1)S(1)} %copy-done.1, bf16[2,128,128]{2,1,0:T(8,128)(2,1)S(1)} %copy-done.3, ...), custom_call_target="tpu_custom_call" | custom-call | tf_op jit(solution)/shard_map/pallas_call | solution.py:418
  22.3 0.0 collective-permute-done.4.mate
  22.3 0.0 collective-permute-done.5.cross
  22.3 3.4 %shard_map.134 = (bf16[128,1024]{1,0:T(8,128)(2,1)S(1)}, bf16[128,256]{1,0:T(8,128)(2,1)S(1)}, bf16[128,256]{1,0:T(8,128)(2,1)S(1)}) custom-call(s32[1]{0:T(128)} %bitcast.4.core_ref, f32[8,1024]{1,0:T(8,128)S(1)} %concatenate.3.pk, s32[16,1024]{1,0:T(8,128)S(1)} %copy-done, bf16[3,64,128]{2,1,0:T(8,128)(2,1)S(1)} %copy-done.1, ...), custom_call_target="tpu_custom_call" | custom-call | tf_op jit(solution)/shard_map/pallas_call | solution.py:418
  25.7 0.1 collective-permute-start.6
  25.8 2.0 %collective-permute-start.7 = (bf16[128,256]{1,0:T(8,128)(2,1)S(1)}, bf16[128,256]{1,0:T(8,128)(2,1)S(1)}, u32[]{:S(2)}, u32[]{:S(2)}) collective-permute-start(bf16[128,256]{1,0:T(8,128)(2,1)S(1)} %get-tuple-element.31), channel_id=1, source_target_pairs={{1,2},{2,1},{3,4},{4,3},{5,6},{6,5},{7,0},{0,7},{9,10},{10,9},{11,... | collective-permute-start | bytes 196616 | tf_op jit(solution)/shard_map/ppermute | solution.py:428
  27.8 3.4 %shard_map.135 = (f32[8,512]{1,0:T(8,128)S(1)}, bf16[2,1024,256]{2,1,0:T(8,128)(2,1)S(1)}) custom-call(f32[8,1024]{1,0:T(8,128)S(1)} %concatenate.3.pk, s32[16,1024]{1,0:T(8,128)S(1)} %copy-done, bf16[3,8,64]{2,1,0:T(8,128)(2,1)S(1)} %copy-done.4, bf16[3,64,128]{2,1,0:T(8,128)(2,1)S(1)} %copy-done.1, bf16[128,1024]{1,0:T(8,128)(2,1)S(1)} %get-tuple-element.29.feats, ...), custom_call_target="tpu_custom_call" | custom-call | tf_op jit(solution)/shard_map/pallas_call | solution.py:418
  31.2 0.0 collective-permute-done.6.mate
  31.2 0.1 collective-permute-done.7.cross
  31.4 0.7 %copy-done.6 = f32[4]{0:T(128)S(1)} copy-done((f32[4]{0:T(128)S(1)}, f32[4]{0:T(128)}, u32[]{:S(2)}) %copy-start.6) | copy-done | bytes 40
  32.0 0.0 copy-done.7
  32.0 4.0 %shard_map.136 = (f32[8,1024]{1,0:T(8,128)S(1)}, f32[8,8,128]{2,1,0:T(8,128)}) custom-call(s32[1]{0:T(128)} %bitcast.4.core_ref, f32[4]{0:T(128)S(1)} %copy-done.6, f32[8,1024]{1,0:T(8,128)S(1)} %concatenate.3.pk, f32[8,1024]{1,0:T(8,128)S(1)} %get-tuple-element.43.behind, f32[8,1024]{1,0:T(8,128)S(1)} %get-tuple-element.42.ahead, s32[16,1024]{1,0:T(8,128)S(1)} %copy-done, ...), custom_call_target="tpu_custom_call" | custom-call | tf_op jit(solution)/shard_map/pallas_call | solution.py:418
  36.0 3.3 %all-to-all-start = ((f32[8,8,128]{2,1,0:T(8,128)}), f32[8,8,128]{2,1,0:T(8,128)S(1)}, u32[]{:S(2)}, u32[]{:S(2)}) async-start(f32[8,8,128]{2,1,0:T(8,128)} %get-tuple-element.37), calls=%async_computation | async-start | bytes 65536 | tf_op jit(solution)/shard_map/all_to_all | solution.py:503
  39.4 0.1 pad_add_fusion.flags
  39.5 5.6 %all-to-all-done.sums = f32[8,8,128]{2,1,0:T(8,128)S(1)} async-done(((f32[8,8,128]{2,1,0:T(8,128)}), f32[8,8,128]{2,1,0:T(8,128)S(1)}, u32[]{:S(2)}, u32[]{:S(2)}) %all-to-all-start) | async-done | bytes 32800 | tf_op jit(solution)/shard_map/all_to_all | solution.py:503
  45.1 1.1 %shard_map.137 = (f32[1,3,1024]{2,1,0:T(4,128)S(1)}, f32[1,1]{1,0:T(1,128)}) custom-call(s32[2]{0:T(128)S(1)} %pad_add_fusion.flags, f32[8,1024]{1,0:T(8,128)S(1)} %concatenate.3.pk, f32[8,1024]{1,0:T(8,128)S(1)} %get-tuple-element.43.behind, f32[8,1024]{1,0:T(8,128)S(1)} %get-tuple-element.42.ahead, f32[8,1024]{1,0:T(8,128)S(1)} %get-tuple-element.36.force, ...), custom_call_target="tpu_custom_call" | custom-call | tf_op jit(solution)/shard_map/pallas_call | solution.py:418
  46.2 0.6 %copy.14 = f32[1,3,1024]{2,0,1:T(1,128)} copy(f32[1,3,1024]{2,1,0:T(4,128)S(1)} %get-tuple-element.40) | data formatting | bytes 24576
  (25 shorter events, 0.1 us)
Async XLA Ops:
  0.6 0.8 %copy-start.10 = (s32[512]{0:T(512)S(1)}, s32[512]{0:T(512)}, u32[]{:S(2)}) copy-start(s32[512]{0:T(512)} %param.16) | copy-start | bytes 6148
  0.6 0.8 %copy-start.8 = (s32[1024]{0:T(1024)S(1)}, s32[1024]{0:T(1024)}, u32[]{:S(2)}) copy-start(s32[1024]{0:T(1024)} %param.13) | copy-start | bytes 12292
  0.7 0.8 %copy-start.9 = (s32[1024]{0:T(1024)S(1)}, s32[1024]{0:T(1024)}, u32[]{:S(2)}) copy-start(s32[1024]{0:T(1024)} %param.14) | copy-start | bytes 12292
  1.4 5.4 %copy-start = (s32[16,1024]{1,0:T(8,128)S(1)}, s32[16,1024]{1,0:T(8,128)}, u32[]{:S(2)}) copy-start(s32[16,1024]{1,0:T(8,128)} %nbr.11) | copy-start | bytes 196612
  1.5 5.3 %copy-start.1 = (bf16[3,64,128]{2,1,0:T(8,128)(2,1)S(1)}, bf16[3,64,128]{2,1,0:T(8,128)(2,1)}, u32[]{:S(2)}) copy-start(bf16[3,64,128]{2,1,0:T(8,128)(2,1)} %rad_out.11) | copy-start | bytes 147460
  1.5 9.3 %collective-permute-start.2 = (f32[8,1024]{1,0:T(8,128)S(1)}, f32[8,1024]{1,0:T(8,128)S(1)}, u32[]{:S(2)}, u32[]{:S(2)}) collective-permute-start(f32[8,1024]{1,0:T(8,128)S(1)} %concatenate.3.pk), channel_id=1, source_target_pairs={{0,1},{1,0},{2,3},{3,2},{4,5},{5,4},{6,7},{7,6},{8,9},{9,8},{10,11... | collective-permute-start | bytes 98312 | tf_op jit(solution)/shard_map/ppermute | solution.py:428
  2.1 8.8 %collective-permute-start.3 = (f32[8,1024]{1,0:T(8,128)S(1)}, f32[8,1024]{1,0:T(8,128)S(1)}, u32[]{:S(2)}, u32[]{:S(2)}) collective-permute-start(f32[8,1024]{1,0:T(8,128)S(1)} %concatenate.3.pk), channel_id=1, source_target_pairs={{1,2},{2,1},{3,4},{4,3},{5,6},{6,5},{7,0},{0,7},{9,10},{10,9},{11,... | collective-permute-start | bytes 98312 | tf_op jit(solution)/shard_map/ppermute | solution.py:428
  6.8 0.7 %copy-start.4 = (bf16[3,8,64]{2,1,0:T(8,128)(2,1)S(1)}, bf16[3,8,64]{2,1,0:T(8,128)(2,1)}, u32[]{:S(2)}) copy-start(bf16[3,8,64]{2,1,0:T(8,128)(2,1)} %rad_in.7) | copy-start | bytes 9220
  6.8 0.7 %copy-start.5 = (bf16[4,128]{1,0:T(4,128)(2,1)S(1)}, bf16[4,128]{1,0:T(4,128)(2,1)}, u32[]{:S(2)}) copy-start(bf16[4,128]{1,0:T(4,128)(2,1)} %embed.3) | copy-start | bytes 3076
  7.5 0.8 %copy-start.2 = (bf16[2,128,128]{2,1,0:T(8,128)(2,1)S(1)}, bf16[2,128,128]{2,1,0:T(8,128)(2,1)}, u32[]{:S(2)}) copy-start(bf16[2,128,128]{2,1,0:T(8,128)(2,1)} %mixing.7) | copy-start | bytes 196612
  10.8 7.8 %copy-start.3 = (bf16[2,128,128]{2,1,0:T(8,128)(2,1)S(1)}, bf16[2,128,128]{2,1,0:T(8,128)(2,1)}, u32[]{:S(2)}) copy-start(bf16[2,128,128]{2,1,0:T(8,128)(2,1)} %mixing.7) | copy-start | bytes 196612
  13.7 8.6 %collective-permute-start.4 = (bf16[128,256]{1,0:T(8,128)(2,1)S(1)}, bf16[128,256]{1,0:T(8,128)(2,1)S(1)}, u32[]{:S(2)}, u32[]{:S(2)}) collective-permute-start(bf16[128,256]{1,0:T(8,128)(2,1)S(1)} %get-tuple-element.23), channel_id=1, source_target_pairs={{0,1},{1,0},{2,3},{3,2},{4,5},{5,4},{6,7},{7,6},{8,9},{9,8},{10,11... | collective-permute-start | bytes 196616 | tf_op jit(solution)/shard_map/ppermute | solution.py:428
  13.8 8.5 %collective-permute-start.5 = (bf16[128,256]{1,0:T(8,128)(2,1)S(1)}, bf16[128,256]{1,0:T(8,128)(2,1)S(1)}, u32[]{:S(2)}, u32[]{:S(2)}) collective-permute-start(bf16[128,256]{1,0:T(8,128)(2,1)S(1)} %get-tuple-element.24), channel_id=1, source_target_pairs={{1,2},{2,1},{3,4},{4,3},{5,6},{6,5},{7,0},{0,7},{9,10},{10,9},{11,... | collective-permute-start | bytes 196616 | tf_op jit(solution)/shard_map/ppermute | solution.py:428
  14.9 12.9 %collective-permute-start = (f32[8,1024]{1,0:T(8,128)S(1)}, f32[8,1024]{1,0:T(8,128)S(1)}, u32[]{:S(2)}, u32[]{:S(2)}) collective-permute-start(f32[8,1024]{1,0:T(8,128)S(1)} %concatenate.3.pk), channel_id=1, source_target_pairs={{0,8},{8,0},{16,24},{24,16},{1,9},{9,1},{17,25},{25,17},{2,10},{10... | collective-permute-start | bytes 98312 | tf_op jit(solution)/shard_map/ppermute | solution.py:428
  16.4 11.4 %collective-permute-start.1 = (f32[8,1024]{1,0:T(8,128)S(1)}, f32[8,1024]{1,0:T(8,128)S(1)}, u32[]{:S(2)}, u32[]{:S(2)}) collective-permute-start(f32[8,1024]{1,0:T(8,128)S(1)} %concatenate.3.pk), channel_id=1, source_target_pairs={{8,16},{16,8},{24,0},{0,24},{9,17},{17,9},{25,1},{1,25},{10,18},{1... | collective-permute-start | bytes 98312 | tf_op jit(solution)/shard_map/ppermute | solution.py:428
  25.7 5.5 %collective-permute-start.6 = (bf16[128,256]{1,0:T(8,128)(2,1)S(1)}, bf16[128,256]{1,0:T(8,128)(2,1)S(1)}, u32[]{:S(2)}, u32[]{:S(2)}) collective-permute-start(bf16[128,256]{1,0:T(8,128)(2,1)S(1)} %get-tuple-element.30), channel_id=1, source_target_pairs={{0,1},{1,0},{2,3},{3,2},{4,5},{5,4},{6,7},{7,6},{8,9},{9,8},{10,11... | collective-permute-start | bytes 196616 | tf_op jit(solution)/shard_map/ppermute | solution.py:428
  25.8 5.6 %collective-permute-start.7 = (bf16[128,256]{1,0:T(8,128)(2,1)S(1)}, bf16[128,256]{1,0:T(8,128)(2,1)S(1)}, u32[]{:S(2)}, u32[]{:S(2)}) collective-permute-start(bf16[128,256]{1,0:T(8,128)(2,1)S(1)} %get-tuple-element.31), channel_id=1, source_target_pairs={{1,2},{2,1},{3,4},{4,3},{5,6},{6,5},{7,0},{0,7},{9,10},{10,9},{11,... | collective-permute-start | bytes 196616 | tf_op jit(solution)/shard_map/ppermute | solution.py:428
  31.4 0.7 %copy-start.6 = (f32[4]{0:T(128)S(1)}, f32[4]{0:T(128)}, u32[]{:S(2)}) copy-start(f32[4]{0:T(128)} %ref_energy.1) | copy-start | bytes 52
  31.4 0.7 %copy-start.7 = (bf16[128]{0:T(256)(128)(2,1)S(1)}, bf16[128]{0:T(256)(128)(2,1)}, u32[]{:S(2)}) copy-start(bf16[128]{0:T(256)(128)(2,1)} %param.23) | copy-start | bytes 772
  36.0 9.0 %all-to-all-start = ((f32[8,8,128]{2,1,0:T(8,128)}), f32[8,8,128]{2,1,0:T(8,128)S(1)}, u32[]{:S(2)}, u32[]{:S(2)}) async-start(f32[8,8,128]{2,1,0:T(8,128)} %get-tuple-element.37), calls=%async_computation | async-start | bytes 65536 | tf_op jit(solution)/shard_map/all_to_all | solution.py:503

commit v2 on v1

--- a/solution.py
+++ b/solution.py
@@ -18,6 +18,7 @@
 SEND_ROW = 5
 PACK_ROWS = 8
 SUM_ROWS = 8
+REDUCE_CHIPS = 4
 VMEM = pl.BlockSpec(memory_space=pltpu.VMEM)
 SMEM = pl.BlockSpec(memory_space=pltpu.SMEM)
 
@@ -122,8 +123,8 @@
     return (feats.astype(F32) + silu_of_half(dot(mix_half, scaled))).astype(BF16)
 
 
-def first_block(table, table_lo, pk, nbr, lo, rim, weights, spread, hid):
-    embed_t, first, mix_half = weights
+def first_block(table, table_lo, pk, nbr, lo, rim, weights, hid):
+    embed_t, first, mix_half, spread = weights
     fan = nbr.shape[0]
     chans = mix_half.shape[0]
     kinds_count = embed_t.shape[1]
@@ -141,25 +142,29 @@
         sorted_out = [
             jnp.where(kind == jnp.full((), k, BF16), mine, zero) for k in range(species)
         ]
-        summed = summed + dot(first, jnp.concatenate(sorted_out, axis=0))
+        summed = summed + dot(first[...], jnp.concatenate(sorted_out, axis=0))
     rows = lax.broadcasted_iota(I32, (kinds_count, rim), 0).astype(F32)
     own = rows == pk[SPECIES_ROW : SPECIES_ROW + 1, pl.ds(lo, rim)]
-    feats = dot(embed_t, jnp.where(own, 1.0, 0.0).astype(BF16))
-    return deltas, basis, update_of(feats, summed, mix_half, fan)
-
-
-def first_weights(embed, rad_in, rad_out, mixing, spread):
-    spread_first_layer(rad_in, 0, spread)
+    feats = dot(embed_t[...], jnp.where(own, 1.0, 0.0).astype(BF16))
+    return deltas, basis, update_of(feats, summed, mix_half[...], fan)
+
+
+def prepare(embed, rad_in, rad_out, mixing, embed_t, first, spread, out_t, mix_half):
+    for layer in range(rad_in.shape[0]):
+        spread_first_layer(rad_in, layer, spread.at[layer])
+        out_t[layer] = turned_weight(rad_out, layer)
+    for layer in range(mixing.shape[0]):
+        mix_half[layer] = turned_weight(mixing, layer, 0.5)
     out = rad_out[0].astype(F32)
     table = embed[...].astype(F32)
     species = table.shape[0]
-    kinds_count = -(-species // 16) * 16
+    kinds_count = embed_t.shape[1]
     padded = jnp.concatenate(
         [table, jnp.zeros((kinds_count - species, table.shape[1]), F32)], axis=0
     )
-    embed_t = padded.T.astype(BF16)
-    first = jnp.concatenate([out * table[k : k + 1] for k in range(species)], axis=0)
-    return embed_t, first.T.astype(BF16), turned_weight(mixing, 0, 0.5)
+    embed_t[...] = padded.T.astype(BF16)
+    scaled = jnp.concatenate([out * table[k : k + 1] for k in range(species)], axis=0)
+    first[...] = scaled.T.astype(BF16)
 
 
 def store_block(i, deltas, basis, delta_out, basis_out):
@@ -169,19 +174,40 @@
     basis_out[i] = basis
 
 
-def first_inner(rim, pk, nbr, embed, rad_in, rad_out, mixing, delta_out, basis_out, feats_out, spread, hid):
-    weights = first_weights(embed, rad_in, rad_out, mixing, spread)
+def first_inner(rim, pk, nbr, embed_hbm, rad_in_hbm, rad_out_hbm, mixing_hbm, w_hbm, ref_hbm, delta_out, basis_out, feats_out, embed_t, first, spread, out_t, mix_half, w_row, ref_row, embed, rad_in, rad_out, mixing, ref_energy, hid, sems):
+    copies = [
+        pltpu.make_async_copy(source, target, sems.at[i])
+        for i, (source, target) in enumerate(
+            (
+                (embed_hbm, embed),
+                (rad_in_hbm, rad_in),
+                (rad_out_hbm, rad_out),
+                (mixing_hbm, mixing),
+                (w_hbm, w_row),
+                (ref_hbm, ref_energy),
+            )
+        )
+    ]
+    for copy in copies:
+        copy.start()
+    for copy in copies:
+        copy.wait()
+    prepare(embed, rad_in, rad_out, mixing, embed_t, first, spread, out_t, mix_half)
+    weights = (embed_t, first, mix_half.at[0], spread.at[0])
 
     def body(i, carry):
         lo = aligned((i + 1) * rim, rim)
-        deltas, basis, feats = first_block(
-            pk, lo - rim, pk, nbr, lo, rim, weights, spread, hid
-        )
+        deltas, basis, feats = first_block(pk, lo - rim, pk, nbr, lo, rim, weights, hid)
         store_block(i, deltas, basis, delta_out, basis_out)
         feats_out[:, pl.ds(aligned(i * rim, rim), rim)] = feats
         return carry
 
     lax.fori_loop(0, feats_out.shape[1] // rim, body, 0)
+    kinds = pk[SPECIES_ROW : SPECIES_ROW + 1, :]
+    energy = jnp.zeros(kinds.shape, F32)
+    for k in range(ref_energy.shape[0]):
+        energy = jnp.where(kinds == float(k), ref_energy[k], energy)
+    ref_row[...] = energy
 
 
 def pack_halo(feats, pk, core, rim, to_mate, to_cross):
@@ -207,10 +233,10 @@
     return aligned((1 - core) * top, rim), aligned(core * top, rim)
 
 
-def first_outer(rim, core_ref, pk, mate, cross, nbr, embed, rad_in, rad_out, mixing, inner, delta_out, basis_out, feats_out, to_mate, to_cross, table, spread, hid):
+def first_outer(rim, core_ref, pk, mate, cross, nbr, embed_t, first, spread, mix_half, inner, delta_out, basis_out, feats_out, to_mate, to_cross, pair_out, table, hid):
     core = core_ref[0]
     atoms = pk.shape[1]
-    weights = first_weights(embed, rad_in, rad_out, mixing, spread)
+    weights = (embed_t, first, mix_half.at[0], spread.at[0])
     table[:, rim : rim + atoms] = pk[...]
     at_mate, at_cross = halo_places(core, atoms, rim)
     for ref, start, at in ((mate, core * rim, at_mate), (cross, (1 - core) * rim, at_cross)):
@@ -222,10 +248,11 @@
                 spans, wanted // LANES, wanted & (LANES - 1)
             )
     feats_out[:, rim : atoms - rim] = inner[...]
+    pair_out[...] = jnp.concatenate([pk[0:4, :], mate[0:4, :]], axis=0)
 
     def body(i, carry):
         lo = aligned(i * (atoms - rim), rim)
-        deltas, basis, feats = first_block(table, lo, pk, nbr, lo, rim, weights, spread, hid)
+        deltas, basis, feats = first_block(table, lo, pk, nbr, lo, rim, weights, hid)
         store_block(i, deltas, basis, delta_out, basis_out)
         feats_out[:, pl.ds(lo, rim)] = feats
         return carry
@@ -245,10 +272,8 @@
     return update_of(own, summed, mix_half, fan)
 
 
-def layer_inner(rim, layer, pk, nbr, rad_in, rad_out, mixing, feats, basis, basis_edge, feats_out, hid_edge, spread, hid):
-    spread_first_layer(rad_in, layer, spread)
-    out_t = turned_weight(rad_out, layer)
-    mix_half = turned_weight(mixing, layer, 0.5)
+def layer_inner(rim, layer, pk, nbr, spreads, outs_t, mixes, feats, basis, basis_edge, feats_out, hid_edge, hid):
+    spread, out_t, mix_half = spreads.at[layer], outs_t[layer], mixes[layer]
 
     def body(i, carry):
         lo = aligned((i + 1) * rim, rim)
@@ -272,11 +297,10 @@
     table[:, pl.ds(at_cross, rim)] = cross[...]
 
 
-def layer_outer(rim, layer, core_ref, pk, nbr, rad_out, mixing, feats, mate, cross, hid_edge, inner, feats_out, to_mate, to_cross, table):
+def layer_outer(rim, layer, core_ref, pk, nbr, outs_t, mixes, feats, mate, cross, hid_edge, inner, feats_out, to_mate, to_cross, table):
     core = core_ref[0]
     atoms = pk.shape[1]
-    out_t = turned_weight(rad_out, layer)
-    mix_half = turned_weight(mixing, layer, 0.5)
+    out_t, mix_half = outs_t[layer], mixes[layer]
     fill_table(table, feats, mate, cross, core, rim)
     feats_out[:, rim : atoms - rim] = inner[...]
 
@@ -309,9 +333,8 @@
     return jnp.concatenate(rows + [jnp.zeros((PACK_ROWS - 3, rim), F32)], axis=0)
 
 
-def head_inner(rim, layer, pk, nbr, rad_in, rad_out, feats, basis, delta, basis_edge, force_out, hid_edge, spread, hid):
-    spread_first_layer(rad_in, layer, spread)
-    out_t = turned_weight(rad_out, layer)
+def head_inner(rim, layer, pk, nbr, spreads, outs_t, feats, basis, delta, basis_edge, force_out, hid_edge, hid):
+    spread, out_t = spreads.at[layer], outs_t[layer]
 
     def body(i, carry):
         lo = aligned((i + 1) * rim, rim)
@@ -334,10 +357,17 @@
     return jnp.sum(total, axis=0, keepdims=True)
 
 
-def head_outer(rim, layer, core_ref, ref_energy, pk, behind, ahead, nbr, rad_out, w_energy, feats, mate, cross, hid_edge, delta, inner, force_out, sums_out, table):
+def neighbour_images(core, received, relayed):
+    first = core == 0
+    behind = jnp.where(first, relayed[0:3, :], received[4:7, :])
+    ahead = jnp.where(first, received[4:7, :], relayed[0:3, :])
+    return behind, ahead
+
+
+def head_outer(rim, layer, core_ref, pk, received, relayed, nbr, outs_t, w_row, ref_row, feats, mate, cross, hid_edge, delta, inner, force_out, sums_out, table):
     core = core_ref[0]
     atoms = pk.shape[1]
-    out_t = turned_weight(rad_out, layer)
+    out_t = outs_t[layer]
     fill_table(table, feats, mate, cross, core, rim)
     force_out[:, rim : atoms - rim] = inner[...]
 
@@ -350,27 +380,24 @@
         return carry
 
     lax.fori_loop(0, 2, body, 0)
-    readout = dot(w_energy[...], feats[...])
-    kinds = pk[SPECIES_ROW : SPECIES_ROW + 1, :]
-    energy = readout
-    for k in range(ref_energy.shape[0]):
-        energy = energy + jnp.where(kinds == float(k), ref_energy[k], 0.0)
+    energy = dot(w_row[...], feats[...]) + ref_row[...]
+    behind, ahead = neighbour_images(core, received, relayed)
     here = pk[0:3, :]
-    back = here - behind[0:3, :]
-    fore = ahead[0:3, :] - here
+    back = here - behind
+    fore = ahead - here
     force = force_out[0:3, :]
     rows = [energy, back * back, fore * fore, back * fore, force * back, force * fore]
     sums = [lane_sum(row) for row in rows]
     sums.append(jnp.zeros((SUM_ROWS - len(sums), LANES), F32))
-    total = jnp.concatenate(sums, axis=0)
-    for peer in range(sums_out.shape[0]):
-        sums_out[peer] = total
-
-
-def finish(count, flags, pk, behind, ahead, force, sums, result, energy_out):
-    total = sums[0]
-    for peer in range(1, sums.shape[0]):
-        total = total + sums[peer]
+    sums_out[...] = jnp.concatenate(sums, axis=0)
+
+
+def finish(count, core_ref, flags, pk, received, relayed, force, *rest):
+    *parts, result, energy_out = rest
+    total = parts[0][...]
+    for part in parts[1:]:
+        total = total + part[...]
+    total = total[:SUM_ROWS] + total[SUM_ROWS:]
     total = jnp.sum(total, axis=1, keepdims=True)
     energy, back_sq, fore_sq, cross, along_back, along_fore = (total[i : i + 1] for i in range(6))
     back_len = jnp.sqrt(back_sq + 1e-06)
@@ -385,9 +412,11 @@
     is_end = flags[0] == 1
     factor = jnp.where(climbing, -2.0 * proj, spring - proj)
     here = pk[0:3, :]
-    tangent = (here - behind[0:3, :]) * by_back + (ahead[0:3, :] - here) * by_fore
-    moved = force[0:3, :] + factor * tangent
-    result[0] = jnp.where(is_end, force[0:3, :], moved)
+    behind, ahead = neighbour_images(core_ref[0], received, relayed)
+    tangent = (here - behind) * by_back + (ahead - here) * by_fore
+    moved = jnp.where(is_end, force[0:3, :], force[0:3, :] + factor * tangent)
+    for c in range(3):
+        result[c] = moved[c : c + 1]
     energy_out[...] = energy * (1.0 / count)
 
 
@@ -413,19 +442,25 @@
     core = lax.rem(lax.axis_index("atom"), 2)
     image = lax.axis_index("img")
 
-    def call(body, operands, outs, scratch=()):
-        scalars = {id(x) for x in (core_arr, ref_energy, flags)}
+    def call(body, operands, outs, scratch=(), far=()):
+        scalars = {id(x) for x in (core_arr, flags)}
+        far = {id(x) for x in far}
         return pl.pallas_call(
             body,
             out_shape=[jax.ShapeDtypeStruct(shape, dtype) for shape, dtype in outs],
-            in_specs=[SMEM if id(x) in scalars else VMEM for x in operands],
+            in_specs=[
+                SMEM if id(x) in scalars else pl.BlockSpec(memory_space=pl.ANY) if id(x) in far else VMEM
+                for x in operands
+            ],
             out_specs=[VMEM] * len(outs),
-            scratch_shapes=[pltpu.VMEM(shape, dtype) for shape, dtype in scratch],
+            scratch_shapes=[
+                x if not isinstance(x, tuple) else pltpu.VMEM(*x) for x in scratch
+            ],
             compiler_params=pltpu.CompilerParams(vmem_limit_bytes=40 * 2**20),
         )(*operands)
 
-    def swap(block, axis, offset):
-        return lax.ppermute(block, axis, swap_pairs(lax.axis_size(axis), offset))
+    def swap(block, offset):
+        return lax.ppermute(block, "atom", swap_pairs(tiles, offset))
 
     core_arr = core.reshape(1).astype(I32)
     is_end = jnp.logical_or(image == 0, image == images - 1)
@@ -441,72 +476,95 @@
         axis=0,
     )
     w_row = w_energy[None]
-    mate = swap(pk, "atom", 0)
-    cross = swap(pk, "atom", 1)
-    even = swap(pk, "img", 0)
-    odd = swap(pk, "img", 1)
+    mate = swap(pk, 0)
+    cross = swap(pk, 1)
 
     feats_type = ((chans, atoms), BF16)
     halo_type = ((chans, rim), BF16)
-    hid_scratch = [((fan * units, fan * basis_count), BF16), ((fan * units, rim), BF16)]
+    kinds_count = -(-embed.shape[0] // 16) * 16
+    weight_types = [
+        ((chans, kinds_count), BF16),
+        ((chans, embed.shape[0] * units), BF16),
+        ((layers + 1, fan * units, fan * basis_count), BF16),
+        ((layers + 1, chans, units), BF16),
+        ((layers, chans, chans), BF16),
+        ((1, chans), BF16),
+        ((1, atoms), F32),
+    ]
+    hid_scratch = ((fan * units, rim), BF16)
     table_scratch = [((chans, atoms + 2 * rim), BF16)]
 
     def block_outs(blocks):
         return [((blocks, 3 * fan, rim), F32), ((blocks, fan * basis_count, rim), BF16)]
 
-    delta_in, basis_in, inner = call(
+    weights = (embed, rad_in, rad_out, mixing, w_row, ref_energy)
+    delta_in, basis_in, inner, embed_t, first, spread, out_t, mix_half, w_row, ref_row = call(
         functools.partial(first_inner, rim),
-        (pk, neighbours, embed, rad_in, rad_out, mixing),
-        block_outs(inner_blocks) + [((chans, inner_atoms), BF16)],
-        hid_scratch,
-    )
-    delta_out, basis_out, feats, to_mate, to_cross = call(
+        (pk, neighbours) + weights,
+        block_outs(inner_blocks) + [((chans, inner_atoms), BF16)] + weight_types,
+        [(x.shape, x.dtype) for x in weights[:4]]
+        + [pltpu.SMEM(ref_energy.shape, F32), hid_scratch, pltpu.SemaphoreType.DMA((6,))],
+        weights,
+    )
+    delta_out, basis_out, feats, to_mate, to_cross, pair = call(
         functools.partial(first_outer, rim),
-        (core_arr, pk, mate, cross, neighbours, embed, rad_in, rad_out, mixing, inner),
-        block_outs(2) + [feats_type, halo_type, halo_type],
-        [((PACK_ROWS, atoms + 2 * rim), F32)] + hid_scratch,
-    )
+        (core_arr, pk, mate, cross, neighbours, embed_t, first, spread, mix_half, inner),
+        block_outs(2) + [feats_type, halo_type, halo_type, ((PACK_ROWS, atoms), F32)],
+        [((PACK_ROWS, atoms + 2 * rim), F32), hid_scratch],
+    )
+    image_pairs = []
+    for low in range(images):
+        high = (low + 1) % images
+        for tile in range(0, tiles, 2):
+            a, b = low * tiles + tile, high * tiles + tile + 1
+            image_pairs += [(a, b), (b, a)]
     hid_type = ((2, fan * units, rim), BF16)
     for layer in range(1, layers):
-        mate = swap(to_mate, "atom", 0)
-        cross = swap(to_cross, "atom", 1)
+        mate = swap(to_mate, 0)
+        cross = swap(to_cross, 1)
         inner, hid_edge = call(
             functools.partial(layer_inner, rim, layer),
-            (pk, neighbours, rad_in, rad_out, mixing, feats, basis_in, basis_out),
+            (pk, neighbours, spread, out_t, mix_half, feats, basis_in, basis_out),
             [((chans, inner_atoms), BF16), hid_type],
-            hid_scratch,
+            [hid_scratch],
         )
         feats, to_mate, to_cross = call(
             functools.partial(layer_outer, rim, layer),
-            (core_arr, pk, neighbours, rad_out, mixing, feats, mate, cross, hid_edge, inner),
+            (core_arr, pk, neighbours, out_t, mix_half, feats, mate, cross, hid_edge, inner),
             [feats_type, halo_type, halo_type],
             table_scratch,
         )
-    mate = swap(to_mate, "atom", 0)
-    cross = swap(to_cross, "atom", 1)
+    received = lax.ppermute(pair, ("img", "atom"), image_pairs)
+    relayed = swap(received, 0)
+    mate = swap(to_mate, 0)
+    cross = swap(to_cross, 1)
     force_type = ((PACK_ROWS, atoms), F32)
     inner, hid_edge = call(
         functools.partial(head_inner, rim, layers),
-        (pk, neighbours, rad_in, rad_out, feats, basis_in, delta_in, basis_out),
+        (pk, neighbours, spread, out_t, feats, basis_in, delta_in, basis_out),
         [((PACK_ROWS, inner_atoms), F32), hid_type],
-        hid_scratch,
-    )
-    odd_image = lax.rem(image, 2) == 1
-    behind = jnp.where(odd_image, even, odd)
-    ahead = jnp.where(odd_image, odd, even)
+        [hid_scratch],
+    )
     force, sums = call(
         functools.partial(head_outer, rim, layers),
-        (core_arr, ref_energy, pk, behind, ahead, neighbours, rad_out, w_row, feats, mate, cross, hid_edge, delta_out, inner),
-        [force_type, ((tiles, SUM_ROWS, LANES), F32)],
+        (core_arr, pk, received, relayed, neighbours, out_t, w_row, ref_row, feats, mate, cross, hid_edge, delta_out, inner),
+        [force_type, ((SUM_ROWS, LANES), F32)],
         table_scratch,
     )
-    sums = lax.all_to_all(sums, "atom", 0, 0)
+    step = 2 * REDUCE_CHIPS
+    while step < tiles:
+        sums = sums + lax.ppermute(sums, "atom", [(i, i ^ step) for i in range(tiles)])
+        step *= 2
+    both = jnp.concatenate([sums, swap(sums, 0)], axis=0)
+    near = lax.ppermute(both, "atom", [(i, i ^ 2 if i % 2 == 0 else i ^ 6) for i in range(tiles)])
+    far = lax.ppermute(both, "atom", [(i, i ^ 4) for i in range(tiles)])
+    other = swap(near, 0)
     result, energy = call(
         functools.partial(finish, atoms * tiles),
-        (flags, pk, behind, ahead, force, sums),
-        [((1, 3, atoms), F32), ((1, 1), F32)],
-    )
-    return result, energy.reshape(1)
+        (core_arr, flags, pk, received, relayed, force, both, near, far, other),
+        [((3, 1, atoms), F32), ((1, 1), F32)],
+    )
+    return jnp.transpose(result, (1, 0, 2)), energy.reshape(1)
 
 
 def solution(mesh):

time: 47.1 us -> 41.6 us (0.88)
  waiting for transfers between devices: 5.76 us -> 2.46 us
  local copies, waits for them, and re-layouts: 3.62 us -> 2.28 us
  Pallas kernels: 21 us -> 20.4 us
  starting transfers between devices: 14.8 us -> 14.3 us
    all_to_all x1 -> x0, waiting for transfers between devices: 5.59 us -> none  [on_device(): sums = lax.all_to_all(sums, 'atom', 0, 0)]
    all_to_all x1 -> x0, starting transfers between devices: 3.33 us -> none  [on_device(): sums = lax.all_to_all(sums, 'atom', 0, 0)]
    ppermute x8 -> x12, starting transfers between devices: 11.5 us -> 14.3 us  [the longest x9 10.6 us: swap(): return lax.ppermute(block, 'atom', swap_pairs(tiles, offset))]
    ppermute x8 -> x12, waiting for transfers between devices: 0.16 us -> 2.46 us  [the longest x9 1.48 us: swap(): return lax.ppermute(block, 'atom', swap_pairs(tiles, offset))]
    unnamed x24 -> x22, local copies, waits for them, and re-layouts: 3.56 us -> 2.22 us
    pallas_call x7, Pallas kernels: 21 us -> 20.4 us  [call(): pl.pallas_call(body, out_shape=[jax.ShapeDtypeStruct(shape, dtype) for sh...]
  transfers between devices with their start and end apart: 9 -> 12, of which waited for: 2 -> 6; matrix products, arithmetic and copies ran while one was open for 0% -> 0% of each run, Pallas kernels for 28% -> 33%
where the time goes in v2:
time: 41.6 us; the launch traced here: 41 us
  Pallas kernels  20.4 us (49%)
  starting transfers between devices  14.3 us (34%)
  waiting for transfers between devices  2.46 us (6%)
  local copies, waits for them, and re-layouts  2.28 us (5%)
  between operations  1.51 us (4%)
    pallas_call x7, Pallas kernels, call(): pl.pallas_call(body, out_shape=[jax.ShapeDtypeStruct(shape, dtype) for sh...  20.4 us
    ppermute x9, starting transfers between devices, swap(): return lax.ppermute(block, 'atom', swap_pairs(tiles, offset))  10.6 us
    ppermute x1, starting transfers between devices, on_device(): far = lax.ppermute(both, 'atom', [(i, i ^ 4) for i in range(tiles)])  2.57 us
    unnamed x22, local copies, waits for them, and re-layouts  2.22 us
    ppermute x9, waiting for transfers between devices, swap(): return lax.ppermute(block, 'atom', swap_pairs(tiles, offset))  1.48 us
    ppermute x1, starting transfers between devices, on_device(): received = lax.ppermute(pair, ('img', 'atom'), image_pairs)  1.03 us
  transfers between devices with their start and end apart: 12, of which 6 were waited for; matrix products, arithmetic and copies ran while one was open for 0% of the time, Pallas kernels for 33%

profile of v2, /device:TPU:0, one launch (start us, length us, event | category | flops | bytes accessed | tf_op | source)
XLA Modules:
  0.0 41.0 jit_solution(11084458537088683055)
XLA Ops:
  0.7 0.7 %copy.16 = f32[1,3,1024]{2,1,0:T(4,128)S(1)} copy(f32[1,3,1024]{2,0,1:T(1,128)} %param.12) | data formatting | bytes 24576
  1.4 0.0 copy-start.1
  1.6 0.5 %collective-permute-start = (f32[8,1024]{1,0:T(8,128)S(1)}, f32[8,1024]{1,0:T(8,128)S(1)}, u32[]{:S(2)}, u32[]{:S(2)}) collective-permute-start(f32[8,1024]{1,0:T(8,128)S(1)} %concatenate.6.pk), channel_id=1, source_target_pairs={{0,1},{1,0},{2,3},{3,2},{4,5},{5,4},{6,7},{7,6},{8,9},{9,8},{10,11... | collective-permute-start | bytes 98312 | tf_op jit(solution)/shard_map/ppermute | solution.py:463
  2.1 4.7 %collective-permute-start.1 = (f32[8,1024]{1,0:T(8,128)S(1)}, f32[8,1024]{1,0:T(8,128)S(1)}, u32[]{:S(2)}, u32[]{:S(2)}) collective-permute-start(f32[8,1024]{1,0:T(8,128)S(1)} %concatenate.6.pk), channel_id=1, source_target_pairs={{1,2},{2,1},{3,4},{4,3},{5,6},{6,5},{7,0},{0,7},{9,10},{10,9},{11,... | collective-permute-start | bytes 98312 | tf_op jit(solution)/shard_map/ppermute | solution.py:463
  6.8 0.6 %copy-done.4 = bf16[4,128]{1,0:T(4,128)(2,1)S(1)} copy-done((bf16[4,128]{1,0:T(4,128)(2,1)S(1)}, bf16[4,128]{1,0:T(4,128)(2,1)}, u32[]{:S(2)}) %copy-start.4) | copy-done | bytes 1048
  7.5 0.8 %copy-done.2 = bf16[3,64,128]{2,1,0:T(8,128)(2,1)S(1)} copy-done((bf16[3,64,128]{2,1,0:T(8,128)(2,1)S(1)}, bf16[3,64,128]{2,1,0:T(8,128)(2,1)}, u32[]{:S(2)}) %copy-start.2) | copy-done | bytes 49176
  8.3 3.4 %shard_map.131 = (f32[2,48,256]{2,1,0:T(8,128)S(1)}, bf16[2,128,256]{2,1,0:T(8,128)(2,1)S(1)}, bf16[128,512]{1,0:T(8,128)(2,1)S(1)}, bf16[128,16]{1,0:T(8,128)(2...) custom-call(f32[8,1024]{1,0:T(8,128)S(1)} %concatenate.6.pk, ...), custom_call_target="tpu_custom_call" | custom-call | tf_op jit(solution)/shard_map/pallas_call | solution.py:448
  11.7 0.0 collective-permute-done.1.cross
  11.7 2.8 %shard_map.132 = (f32[2,48,256]{2,1,0:T(8,128)S(1)}, bf16[2,128,256]{2,1,0:T(8,128)(2,1)S(1)}, bf16[128,1024]{1,0:T(8,128)(2,1)S(1)}, bf16[128,256]{1,0:T(8,128)...) custom-call(s32[1]{0:T(128)} %bitcast.core_ref, f32[8,1024]{1,0:T(8,128)S(1)} %concatenate.6.pk, ...), custom_call_target="tpu_custom_call" | custom-call | tf_op jit(solution)/shard_map/pallas_call | solution.py:448
  14.5 0.1 collective-permute-start.4
  14.5 0.6 %collective-permute-start.5 = (bf16[128,256]{1,0:T(8,128)(2,1)S(1)}, bf16[128,256]{1,0:T(8,128)(2,1)S(1)}, u32[]{:S(2)}, u32[]{:S(2)}) collective-permute-start(bf16[128,256]{1,0:T(8,128)(2,1)S(1)} %get-tuple-element.40), channel_id=1, source_target_pairs={{1,2},{2,1},{3,4},{4,3},{5,6},{6,5},{7,0},{0,7},{9,10},{10,9},{11,... | collective-permute-start | bytes 196616 | tf_op jit(solution)/shard_map/ppermute | solution.py:463
  15.1 1.0 %collective-permute-start.2 = (f32[8,1024]{1,0:T(8,128)S(1)}, f32[8,1024]{1,0:T(8,128)S(1)}, u32[]{:S(2)}, u32[]{:S(2)}) collective-permute-start(f32[8,1024]{1,0:T(8,128)S(1)} %get-tuple-element.34), channel_id=1, source_target_pairs={{0,9},{9,0},{2,11},{11,2},{4,13},{13,4},{6,15},{15,6},{8,17},{17,8... | collective-permute-start | bytes 98312 | tf_op jit(solution)/shard_map/ppermute | solution.py:537
  16.1 3.6 %shard_map.133 = (bf16[128,512]{1,0:T(8,128)(2,1)S(1)}, bf16[2,1024,256]{2,1,0:T(8,128)(2,1)S(1)}) custom-call(f32[8,1024]{1,0:T(8,128)S(1)} %concatenate.6.pk, s32[16,1024]{1,0:T(8,128)S(1)} %copy-done, bf16[3,1024,128]{2,1,0:T(8,128)(2,1)S(1)} %get-tuple-element.31.spread.spreads, bf16[3,128,64]{2,1,0:T(8,128)(2,1)S(1)} %get-tuple-element.35.outs_t, ...), custom_call_target="tpu_custom_call" | custom-call | tf_op jit(solution)/shard_map/pallas_call | solution.py:448
  19.8 0.3 collective-permute-done.5.cross
  20.1 3.3 %shard_map.134 = (bf16[128,1024]{1,0:T(8,128)(2,1)S(1)}, bf16[128,256]{1,0:T(8,128)(2,1)S(1)}, bf16[128,256]{1,0:T(8,128)(2,1)S(1)}) custom-call(s32[1]{0:T(128)} %bitcast.core_ref, f32[8,1024]{1,0:T(8,128)S(1)} %concatenate.6.pk, s32[16,1024]{1,0:T(8,128)S(1)} %copy-done, bf16[3,128,64]{2,1,0:T(8,128)(2,1)S(1)} %get-tuple-element.35.outs_t, ...), custom_call_target="tpu_custom_call" | custom-call | tf_op jit(solution)/shard_map/pallas_call | solution.py:448
  23.4 1.3 %collective-permute-start.6 = (bf16[128,256]{1,0:T(8,128)(2,1)S(1)}, bf16[128,256]{1,0:T(8,128)(2,1)S(1)}, u32[]{:S(2)}, u32[]{:S(2)}) collective-permute-start(bf16[128,256]{1,0:T(8,128)(2,1)S(1)} %get-tuple-element.46), channel_id=1, source_target_pairs={{0,1},{1,0},{2,3},{3,2},{4,5},{5,4},{6,7},{7,6},{8,9},{9,8},{10,11... | collective-permute-start | bytes 196616 | tf_op jit(solution)/shard_map/ppermute | solution.py:463
  24.6 2.1 %collective-permute-start.7 = (bf16[128,256]{1,0:T(8,128)(2,1)S(1)}, bf16[128,256]{1,0:T(8,128)(2,1)S(1)}, u32[]{:S(2)}, u32[]{:S(2)}) collective-permute-start(bf16[128,256]{1,0:T(8,128)(2,1)S(1)} %get-tuple-element.47), channel_id=1, source_target_pairs={{1,2},{2,1},{3,4},{4,3},{5,6},{6,5},{7,0},{0,7},{9,10},{10,9},{11,... | collective-permute-start | bytes 196616 | tf_op jit(solution)/shard_map/ppermute | solution.py:463
  26.7 0.0 collective-permute-done.2.received
  26.7 0.0 collective-permute-start.3
  26.7 3.3 %shard_map.135 = (f32[8,512]{1,0:T(8,128)S(1)}, bf16[2,1024,256]{2,1,0:T(8,128)(2,1)S(1)}) custom-call(f32[8,1024]{1,0:T(8,128)S(1)} %concatenate.6.pk, s32[16,1024]{1,0:T(8,128)S(1)} %copy-done, bf16[3,1024,128]{2,1,0:T(8,128)(2,1)S(1)} %get-tuple-element.31.spread.spreads, bf16[3,128,64]{2,1,0:T(8,128)(2,1)S(1)} %get-tuple-element.35.outs_t, ...), custom_call_target="tpu_custom_call" | custom-call | tf_op jit(solution)/shard_map/pallas_call | solution.py:448
  30.1 0.2 collective-permute-done.7.cross
  30.2 2.8 %shard_map.136 = (f32[8,1024]{1,0:T(8,128)S(1)}, f32[8,128]{1,0:T(8,128)S(1)}) custom-call(s32[1]{0:T(128)} %bitcast.core_ref, f32[8,1024]{1,0:T(8,128)S(1)} %concatenate.6.pk, f32[8,1024]{1,0:T(8,128)S(1)} %collective-permute-done.2.received, f32[8,1024]{1,0:T(8,128)S(1)} %collective-permute-done.3.relayed, s32[16,1024]{1,0:T(8,128)S(1)} %copy-done, ...), custom_call_target="tpu_custom_call" | custom-call | tf_op jit(solution)/shard_map/pallas_call | solution.py:448
  33.0 0.4 collective-permute-start.8
  33.4 0.8 %collective-permute-done.8 = f32[8,128]{1,0:T(8,128)S(1)} collective-permute-done((f32[8,128]{1,0:T(8,128)S(1)}, f32[8,128]{1,0:T(8,128)S(1)}, u32[]{:S(2)}, u32[]{:S(2)}) %collective-permute-start.8) | collective-permute-done | bytes 4128 | tf_op jit(solution)/shard_map/ppermute | solution.py:463
  34.2 0.1 collective-permute-start.9
  35.0 2.6 %collective-permute-start.10 = (f32[16,128]{1,0:T(8,128)S(1)}, f32[16,128]{1,0:T(8,128)S(1)}, u32[]{:S(2)}, u32[]{:S(2)}) collective-permute-start(f32[16,128]{1,0:T(8,128)S(1)} %constant_dynamic-update-slice_fusion.rest_0_), channel_id=1, source_target_pairs={{0,4},{1,5},{2,6},{3,7},{4,0},{5,1},{6,2},{7,3},{8,12},{9,13},{10,... | collective-permute-start | bytes 24584 | tf_op jit(solution)/shard_map/ppermute | solution.py:560
  37.5 0.3 collective-permute-done.9.rest_1_
  37.9 1.0 %collective-permute-start.11 = (f32[16,128]{1,0:T(8,128)S(1)}, f32[16,128]{1,0:T(8,128)S(1)}, u32[]{:S(2)}, u32[]{:S(2)}) collective-permute-start(f32[16,128]{1,0:T(8,128)S(1)} %collective-permute-done.9.rest_1_), channel_id=1, source_target_pairs={{0,1},{1,0},{2,3},{3,2},{4,5},{5,4},{6,7},{7,6},{8,9},{9,8},{10,11... | collective-permute-start | bytes 24584 | tf_op jit(solution)/shard_map/ppermute | solution.py:463
  38.9 0.1 pad_add_fusion.flags
  38.9 0.6 %collective-permute-done.10.rest_2_ = f32[16,128]{1,0:T(8,128)S(1)} collective-permute-done((f32[16,128]{1,0:T(8,128)S(1)}, f32[16,128]{1,0:T(8,128)S(1)}, u32[]{:S(2)}, u32[]{:S(2)}) %collective-permute-start.10) | collective-permute-done | bytes 8224 | tf_op jit(solution)/shard_map/ppermute | solution.py:560
  39.6 0.1 collective-permute-done.11.rest_3_
  39.7 1.3 %shard_map.137 = (f32[3,1,1024]{2,1,0:T(1,128)}, f32[1,1]{1,0:T(1,128)}) custom-call(s32[1]{0:T(128)} %bitcast.core_ref, s32[2]{0:T(128)S(1)} %pad_add_fusion.flags, f32[8,1024]{1,0:T(8,128)S(1)} %concatenate.6.pk, f32[8,1024]{1,0:T(8,128)S(1)} %collective-permute-done.2.received, f32[8,1024]{1,0:T(8,128)S(1)} %collective-permute-done.3.relayed, ...), custom_call_target="tpu_custom_call" | custom-call | tf_op jit(solution)/shard_map/pallas_call | solution.py:448
  (29 shorter events, 0.1 us)
Async XLA Ops:
  0.6 0.8 %copy-start.9 = (s32[512]{0:T(512)S(1)}, s32[512]{0:T(512)}, u32[]{:S(2)}) copy-start(s32[512]{0:T(512)} %param.16) | copy-start | bytes 6148
  0.6 0.8 %copy-start.7 = (s32[1024]{0:T(1024)S(1)}, s32[1024]{0:T(1024)}, u32[]{:S(2)}) copy-start(s32[1024]{0:T(1024)} %param.13) | copy-start | bytes 12292
  0.7 0.8 %copy-start.8 = (s32[1024]{0:T(1024)S(1)}, s32[1024]{0:T(1024)}, u32[]{:S(2)}) copy-start(s32[1024]{0:T(1024)} %param.14) | copy-start | bytes 12292
  0.7 6.1 %copy-start.3 = (bf16[3,8,64]{2,1,0:T(8,128)(2,1)S(1)}, bf16[3,8,64]{2,1,0:T(8,128)(2,1)}, u32[]{:S(2)}) copy-start(bf16[3,8,64]{2,1,0:T(8,128)(2,1)} %rad_in_hbm.1) | copy-start | bytes 9220
  0.7 6.1 %copy-start.6 = (f32[4]{0:T(128)S(1)}, f32[4]{0:T(128)}, u32[]{:S(2)}) copy-start(f32[4]{0:T(128)} %ref_hbm.1) | copy-start | bytes 52
  1.4 5.4 %copy-start = (s32[16,1024]{1,0:T(8,128)S(1)}, s32[16,1024]{1,0:T(8,128)}, u32[]{:S(2)}) copy-start(s32[16,1024]{1,0:T(8,128)} %nbr.11) | copy-start | bytes 196612
  1.4 5.4 %copy-start.1 = (bf16[2,128,128]{2,1,0:T(8,128)(2,1)S(1)}, bf16[2,128,128]{2,1,0:T(8,128)(2,1)}, u32[]{:S(2)}) copy-start(bf16[2,128,128]{2,1,0:T(8,128)(2,1)} %mixing_hbm.1) | copy-start | bytes 196612
  1.6 10.1 %collective-permute-start = (f32[8,1024]{1,0:T(8,128)S(1)}, f32[8,1024]{1,0:T(8,128)S(1)}, u32[]{:S(2)}, u32[]{:S(2)}) collective-permute-start(f32[8,1024]{1,0:T(8,128)S(1)} %concatenate.6.pk), channel_id=1, source_target_pairs={{0,1},{1,0},{2,3},{3,2},{4,5},{5,4},{6,7},{7,6},{8,9},{9,8},{10,11... | collective-permute-start | bytes 98312 | tf_op jit(solution)/shard_map/ppermute | solution.py:463
  2.1 9.6 %collective-permute-start.1 = (f32[8,1024]{1,0:T(8,128)S(1)}, f32[8,1024]{1,0:T(8,128)S(1)}, u32[]{:S(2)}, u32[]{:S(2)}) collective-permute-start(f32[8,1024]{1,0:T(8,128)S(1)} %concatenate.6.pk), channel_id=1, source_target_pairs={{1,2},{2,1},{3,4},{4,3},{5,6},{6,5},{7,0},{0,7},{9,10},{10,9},{11,... | collective-permute-start | bytes 98312 | tf_op jit(solution)/shard_map/ppermute | solution.py:463
  6.8 0.7 %copy-start.4 = (bf16[4,128]{1,0:T(4,128)(2,1)S(1)}, bf16[4,128]{1,0:T(4,128)(2,1)}, u32[]{:S(2)}) copy-start(bf16[4,128]{1,0:T(4,128)(2,1)} %embed_hbm.1) | copy-start | bytes 3076
  6.8 0.7 %copy-start.5 = (bf16[128]{0:T(256)(128)(2,1)S(1)}, bf16[128]{0:T(256)(128)(2,1)}, u32[]{:S(2)}) copy-start(bf16[128]{0:T(256)(128)(2,1)} %param.23) | copy-start | bytes 772
  7.5 0.8 %copy-start.2 = (bf16[3,64,128]{2,1,0:T(8,128)(2,1)S(1)}, bf16[3,64,128]{2,1,0:T(8,128)(2,1)}, u32[]{:S(2)}) copy-start(bf16[3,64,128]{2,1,0:T(8,128)(2,1)} %rad_out_hbm.1) | copy-start | bytes 147460
  14.5 5.3 %collective-permute-start.4 = (bf16[128,256]{1,0:T(8,128)(2,1)S(1)}, bf16[128,256]{1,0:T(8,128)(2,1)S(1)}, u32[]{:S(2)}, u32[]{:S(2)}) collective-permute-start(bf16[128,256]{1,0:T(8,128)(2,1)S(1)} %get-tuple-element.39), channel_id=1, source_target_pairs={{0,1},{1,0},{2,3},{3,2},{4,5},{5,4},{6,7},{7,6},{8,9},{9,8},{10,11... | collective-permute-start | bytes 196616 | tf_op jit(solution)/shard_map/ppermute | solution.py:463
  14.5 5.6 %collective-permute-start.5 = (bf16[128,256]{1,0:T(8,128)(2,1)S(1)}, bf16[128,256]{1,0:T(8,128)(2,1)S(1)}, u32[]{:S(2)}, u32[]{:S(2)}) collective-permute-start(bf16[128,256]{1,0:T(8,128)(2,1)S(1)} %get-tuple-element.40), channel_id=1, source_target_pairs={{1,2},{2,1},{3,4},{4,3},{5,6},{6,5},{7,0},{0,7},{9,10},{10,9},{11,... | collective-permute-start | bytes 196616 | tf_op jit(solution)/shard_map/ppermute | solution.py:463
  15.1 11.6 %collective-permute-start.2 = (f32[8,1024]{1,0:T(8,128)S(1)}, f32[8,1024]{1,0:T(8,128)S(1)}, u32[]{:S(2)}, u32[]{:S(2)}) collective-permute-start(f32[8,1024]{1,0:T(8,128)S(1)} %get-tuple-element.34), channel_id=1, source_target_pairs={{0,9},{9,0},{2,11},{11,2},{4,13},{13,4},{6,15},{15,6},{8,17},{17,8... | collective-permute-start | bytes 98312 | tf_op jit(solution)/shard_map/ppermute | solution.py:537
  23.4 6.7 %collective-permute-start.6 = (bf16[128,256]{1,0:T(8,128)(2,1)S(1)}, bf16[128,256]{1,0:T(8,128)(2,1)S(1)}, u32[]{:S(2)}, u32[]{:S(2)}) collective-permute-start(bf16[128,256]{1,0:T(8,128)(2,1)S(1)} %get-tuple-element.46), channel_id=1, source_target_pairs={{0,1},{1,0},{2,3},{3,2},{4,5},{5,4},{6,7},{7,6},{8,9},{9,8},{10,11... | collective-permute-start | bytes 196616 | tf_op jit(solution)/shard_map/ppermute | solution.py:463
  24.6 5.6 %collective-permute-start.7 = (bf16[128,256]{1,0:T(8,128)(2,1)S(1)}, bf16[128,256]{1,0:T(8,128)(2,1)S(1)}, u32[]{:S(2)}, u32[]{:S(2)}) collective-permute-start(bf16[128,256]{1,0:T(8,128)(2,1)S(1)} %get-tuple-element.47), channel_id=1, source_target_pairs={{1,2},{2,1},{3,4},{4,3},{5,6},{6,5},{7,0},{0,7},{9,10},{10,9},{11,... | collective-permute-start | bytes 196616 | tf_op jit(solution)/shard_map/ppermute | solution.py:463
  26.7 3.3 %collective-permute-start.3 = (f32[8,1024]{1,0:T(8,128)S(1)}, f32[8,1024]{1,0:T(8,128)S(1)}, u32[]{:S(2)}, u32[]{:S(2)}) collective-permute-start(f32[8,1024]{1,0:T(8,128)S(1)} %collective-permute-done.2.received), channel_id=1, source_target_pairs={{0,1},{1,0},{2,3},{3,2},{4,5},{5,4},{6,7},{7,6},{8,9},{9,8},{10,11... | collective-permute-start | bytes 98312 | tf_op jit(solution)/shard_map/ppermute | solution.py:463
  33.0 1.2 %collective-permute-start.8 = (f32[8,128]{1,0:T(8,128)S(1)}, f32[8,128]{1,0:T(8,128)S(1)}, u32[]{:S(2)}, u32[]{:S(2)}) collective-permute-start(f32[8,128]{1,0:T(8,128)S(1)} %get-tuple-element.53), channel_id=1, source_target_pairs={{0,1},{1,0},{2,3},{3,2},{4,5},{5,4},{6,7},{7,6},{8,9},{9,8},{10,11... | collective-permute-start | bytes 12296 | tf_op jit(solution)/shard_map/ppermute | solution.py:463
  34.2 3.7 %collective-permute-start.9 = (f32[16,128]{1,0:T(8,128)S(1)}, f32[16,128]{1,0:T(8,128)S(1)}, u32[]{:S(2)}, u32[]{:S(2)}) collective-permute-start(f32[16,128]{1,0:T(8,128)S(1)} %constant_dynamic-update-slice_fusion.rest_0_), channel_id=1, source_target_pairs={{0,2},{1,7},{2,0},{3,5},{4,6},{5,3},{6,4},{7,1},{8,10},{9,15},{10,... | collective-permute-start | bytes 24584 | tf_op jit(solution)/shard_map/ppermute | solution.py:559
  35.0 4.6 %collective-permute-start.10 = (f32[16,128]{1,0:T(8,128)S(1)}, f32[16,128]{1,0:T(8,128)S(1)}, u32[]{:S(2)}, u32[]{:S(2)}) collective-permute-start(f32[16,128]{1,0:T(8,128)S(1)} %constant_dynamic-update-slice_fusion.rest_0_), channel_id=1, source_target_pairs={{0,4},{1,5},{2,6},{3,7},{4,0},{5,1},{6,2},{7,3},{8,12},{9,13},{10,... | collective-permute-start | bytes 24584 | tf_op jit(solution)/shard_map/ppermute | solution.py:560
  37.9 1.8 %collective-permute-start.11 = (f32[16,128]{1,0:T(8,128)S(1)}, f32[16,128]{1,0:T(8,128)S(1)}, u32[]{:S(2)}, u32[]{:S(2)}) collective-permute-start(f32[16,128]{1,0:T(8,128)S(1)} %collective-permute-done.9.rest_1_), channel_id=1, source_target_pairs={{0,1},{1,0},{2,3},{3,2},{4,5},{5,4},{6,7},{7,6},{8,9},{9,8},{10,11... | collective-permute-start | bytes 24584 | tf_op jit(solution)/shard_map/ppermute | solution.py:463

commit v3 on v2

v3 whole, which is shorter than its diff:
```python
import functools
import math

import jax
import jax.numpy as jnp
from jax import lax
from jax.experimental import pallas as pl
from jax.experimental.pallas import tpu as pltpu
from jax.sharding import PartitionSpec as P

F32 = jnp.float32
BF16 = jnp.bfloat16
I32 = jnp.int32
LANES = 128
SPRING = 5.0
SPECIES_ROW = 3
COUNT_ROW = 4
SEND_ROW = 5
SEAT_ROW = 6
PACK_ROWS = 8
SUM_ROWS = 8
REDUCE_CHIPS = 4
VMEM = pl.BlockSpec(memory_space=pltpu.VMEM)
SMEM = pl.BlockSpec(memory_space=pltpu.SMEM)


def dot(a, b):
    return jnp.dot(a, b, preferred_element_type=F32)


def silu_of_half(half):
    return half + half * jnp.tanh(half)


def aligned(start, step):
    return pl.multiple_of(start, step)


def halves(width):
    return [slice(k * LANES, (k + 1) * LANES) for k in range(width // LANES)]


def short_rows(fan):
    return -(-5 * fan // 8)


def lane_fetch(windows, group, place):
    found = jnp.zeros(place.shape, F32)
    for k, window in enumerate(windows):
        rows = jnp.broadcast_to(window, place.shape)
        picked = jnp.take_along_axis(rows, place, axis=1, mode="promise_in_bounds")
        found = jnp.where(group == k, picked, found)
    return found


def lane_lookup(windows, index):
    return lane_fetch(windows, index // LANES, index & (LANES - 1))


def seat_atoms(pk, lo, width):
    counts = pk[COUNT_ROW : COUNT_ROW + 1, lo : lo + width]
    lane = lax.broadcasted_iota(I32, (1, width), 1).astype(F32)
    key = counts * float(width) - lane

    def down(row):
        turned = jnp.broadcast_to(row, (LANES, width)).T
        return jnp.concatenate([turned] * (width // LANES), axis=1)

    rank = jnp.sum(jnp.where(down(key) > key, 1.0, 0.0), axis=0, keepdims=True)
    seat = jnp.where(rank < width // 2, rank, 1.5 * width - 1.0 - rank)
    atom = lax.broadcasted_iota(I32, (width, width), 0).astype(F32)
    taker = jnp.sum(jnp.where(down(seat) == lane, atom, 0.0), axis=0, keepdims=True)
    return seat, taker


def seat_block(b, pk, nbr, lo, width, seated, edges, owns, depth):
    fan = nbr.shape[0]
    short = short_rows(fan)
    seat, taker = seat_atoms(pk, lo, width)
    pieces, tables = [], []
    for part in halves(width):
        who = taker[:, part].astype(I32)
        spans = [nbr[:, lo + p.start : lo + p.stop] for p in halves(width)]
        pieces.append(lane_lookup(spans, jnp.broadcast_to(who, (fan, LANES))) - float(lo))
        spans = [pk[:, lo + p.start : lo + p.stop] for p in halves(width)]
        tables.append(lane_lookup(spans, jnp.broadcast_to(who, (PACK_ROWS, LANES))))
    first, second = pieces
    first_count, second_count = (x[COUNT_ROW : COUNT_ROW + 1] for x in tables)
    most = jnp.max(first_count + second_count, axis=1, keepdims=True)
    fits = most <= float(2 * short)
    limit = jnp.where(fits, float(short), float(fan))
    row = lax.broadcasted_iota(I32, (fan, LANES), 0).astype(F32)
    mine = row < second_count
    over = [first[2 * short - 1 - r : 2 * short - r] if 0 <= 2 * short - 1 - r < fan else first[:1] for r in range(fan)]
    over = jnp.concatenate(over, axis=0)
    spilled = jnp.logical_and(fits, 2.0 * short - 1.0 - row < first_count)
    spilled = jnp.logical_and(spilled, row < float(short))
    spilled = jnp.logical_and(spilled, row >= float(2 * short - fan))
    spilled = jnp.logical_and(spilled, jnp.logical_not(mine))
    first = jnp.where(row < jnp.minimum(first_count, limit), first, -1.0)
    second = jnp.where(mine, second, jnp.where(spilled, over, -1.0))
    edges[b] = jnp.concatenate([first, second], axis=1)
    owns[b] = jnp.where(spilled, 0.0, 1.0)
    depth[b] = jnp.broadcast_to(limit, (PACK_ROWS, LANES))
    seated[:, lo : lo + width] = jnp.concatenate(tables, axis=1)
    return seat


def by_depth(depth, fan, run):
    shallow = jnp.max(depth) < float(short_rows(fan)) + 0.5

    @pl.when(shallow)
    def _():
        run(short_rows(fan))

    @pl.when(jnp.logical_not(shallow))
    def _():
        run(fan)


def locate_block(i, table, table_lo, seated, edges, own, lo, width, delta_out, basis_out, kinds_out, place_out):
    fan = edges.shape[0]
    spans = [
        table[:, pl.ds(aligned(table_lo + k * LANES, LANES), LANES)]
        for k in range(3 * width // LANES)
    ]
    mine = own > 0.5
    home = seated[:, pl.ds(lo, width)]
    parts = []
    for part in halves(width):
        rel = edges[:, part].astype(I32)
        live = rel >= 0
        group, place = rel >> 7, rel & (LANES - 1)
        fetch = lambda r: lane_fetch([span[r : r + 1] for span in spans], group, place)
        values = []
        for c in range(3):
            here = home[c : c + 1, part]
            if part.start > 0:
                here = jnp.where(mine, here, home[c : c + 1, :LANES])
            values.append(fetch(c) - here)
        values.append(jnp.where(live, fetch(SPECIES_ROW), -1.0))
        tile = (rel // width).astype(F32) * float(width)
        values.append(jnp.where(live, fetch(SEAT_ROW) + tile, -1.0))
        parts.append(values)
    joined = [jnp.concatenate(list(piece), axis=1) for piece in zip(*parts)]
    for c in range(3):
        delta_out[i, c * fan : (c + 1) * fan, :] = joined[c]
    kinds_out[i] = joined[3]
    place_out[i] = joined[4]
    dist_sq = joined[0] * joined[0] + joined[1] * joined[1] + joined[2] * joined[2]
    count = basis_out.shape[1] // fan
    centres = 2.0 * lax.broadcasted_iota(I32, (count, width), 0).astype(F32)
    rows = []
    for s in range(fan):
        away = jnp.broadcast_to(dist_sq[s : s + 1], (count, width)) - centres
        rows.append(jnp.exp(away * away * -0.125))
    basis_out[i] = jnp.concatenate(rows, axis=0).astype(BF16)


def fill_hidden(target, spread, basis, rows, fan):
    used = rows * (spread.shape[0] // fan)
    target[:used, :] = silu_of_half(dot(spread[:used, :], basis)).astype(BF16)


class Sums:
    def __init__(self, shape, own, rows, fan):
        self.total = jnp.zeros(shape, F32)
        self.lent = jnp.zeros((shape[0], LANES), F32)
        self.own, self.alone = own, 2 * rows - fan

    def add(self, s, terms):
        self.total = self.total + terms
        if s >= self.alone:
            self.lent = self.lent + jnp.where(self.own[s : s + 1] > 0.5, 0.0, terms[:, LANES:])

    def done(self):
        first, second = self.total[:, :LANES], self.total[:, LANES:]
        return jnp.concatenate([first + self.lent, second - self.lent], axis=1)


def update_of(feats, summed, mix_half, fan):
    scaled = (summed * (1.0 / math.sqrt(fan))).astype(BF16)
    return (feats.astype(F32) + silu_of_half(dot(mix_half, scaled))).astype(BF16)


def first_block(rows, kinds, basis, own, seated, lo, width, weights, hid):
    embed_t, first, mix_half, spread = weights
    fan = kinds.shape[0]
    kinds_count = embed_t.shape[1]
    units = spread.shape[0] // fan
    species = first.shape[1] // units
    fill_hidden(hid, spread, basis, rows, fan)
    kinds = kinds.astype(BF16)
    zero = jnp.zeros((), BF16)
    sums = Sums((mix_half.shape[0], width), own, rows, fan)
    for s in range(rows):
        mine = hid[s * units : (s + 1) * units, :]
        kind = jnp.broadcast_to(kinds[s : s + 1], (units, width))
        sorted_out = [
            jnp.where(kind == jnp.full((), k, BF16), mine, zero) for k in range(species)
        ]
        sums.add(s, dot(first[...], jnp.concatenate(sorted_out, axis=0)))
    rows_of = lax.broadcasted_iota(I32, (kinds_count, width), 0).astype(F32)
    same = rows_of == seated[SPECIES_ROW : SPECIES_ROW + 1, pl.ds(lo, width)]
    feats = dot(embed_t[...], jnp.where(same, 1.0, 0.0).astype(BF16))
    return update_of(feats, sums.done(), mix_half[...], fan)


def turned(matrix):
    size = matrix.shape[1]
    row = lax.broadcasted_iota(I32, (size, size), 0)
    column = lax.broadcasted_iota(I32, (size, size), 1)
    identity = jnp.where(row == column, 1.0, 0.0).astype(BF16)
    return lax.dot_general(
        identity, matrix, (((1,), (1,)), ((), ())), preferred_element_type=F32
    )


def prepare(embed, rad_in, rad_out, mixing, embed_t, first, spread, out_t, mix_half):
    layers, count, units = rad_in.shape
    fan = spread.shape[1] // units
    for layer in range(layers):
        half = rad_in[layer].astype(F32) * 0.5
        weight = turned(jnp.concatenate([half] * fan, axis=0).astype(BF16))
        owner = lax.broadcasted_iota(I32, weight.shape, 1) // count
        for s in range(fan):
            only = jnp.where(owner == s, weight, 0.0).astype(BF16)
            spread[layer, s * units : (s + 1) * units, :] = only
        out_t[layer] = turned(rad_out[layer]).astype(BF16)
    for layer in range(mixing.shape[0]):
        mix_half[layer] = (turned(mixing[layer]) * 0.5).astype(BF16)
    out = rad_out[0].astype(F32)
    table = embed[...].astype(F32)
    species = table.shape[0]
    padded = jnp.concatenate(
        [table, jnp.zeros((embed_t.shape[1] - species, table.shape[1]), F32)], axis=0
    )
    embed_t[...] = turned(padded.astype(BF16)).astype(BF16)
    scaled = jnp.concatenate([out * table[k : k + 1] for k in range(species)], axis=0)
    first[...] = turned(scaled.astype(BF16)).astype(BF16)


def seat_tile(width, pk, nbr, table, seated, edges, owns, depth, delta_out, basis_out, kinds_out, place_out, index):
    atoms = pk.shape[1]
    blocks = atoms // width
    index[...] = nbr[...].astype(F32)
    table[...] = pk[...]
    for b in range(blocks):
        seat = seat_block(b, pk, index, b * width, width, seated, edges, owns, depth)
        table[SEAT_ROW : SEAT_ROW + 1, b * width : (b + 1) * width] = seat
    for part in halves(2 * width):
        wanted = jnp.broadcast_to(pk[SEND_ROW : SEND_ROW + 1, part].astype(I32), (PACK_ROWS, LANES))
        seats = lane_lookup([table[SEAT_ROW : SEAT_ROW + 1, p] for p in halves(atoms)], wanted)
        seats = seats + (wanted // width).astype(F32) * float(width)
        table[SEND_ROW : SEND_ROW + 1, part] = seats[:1]

    def body(i, carry):
        lo = aligned((i + 1) * width, width)
        locate_block(
            i, table, lo - width, seated, edges[i + 1], owns[i + 1], lo, width,
            delta_out, basis_out, kinds_out, place_out,
        )
        return carry

    lax.fori_loop(0, blocks - 2, body, 0)


def first_inner(width, ref_energy, pk, seated, owns, depth, basis, kinds, embed, rad_in, rad_out, mixing, w_in, feats_out, embed_t, first, spread, out_t, mix_half, w_row, ref_row, hid):
    prepare(embed, rad_in, rad_out, mixing, embed_t, first, spread, out_t, mix_half)
    weights = (embed_t, first, mix_half.at[0], spread.at[0])
    w_row[...] = w_in[...]
    kinds_row = pk[SPECIES_ROW : SPECIES_ROW + 1, :]
    energy = jnp.zeros(kinds_row.shape, F32)
    for k in range(ref_energy.shape[0]):
        energy = jnp.where(kinds_row == float(k), ref_energy[k], energy)
    ref_row[...] = energy

    def body(i, carry):
        lo = aligned((i + 1) * width, width)

        def run(rows):
            feats_out[:, pl.ds(aligned(i * width, width), width)] = first_block(
                rows, kinds[i], basis[i], owns.at[i + 1], seated, lo, width, weights, hid
            )

        by_depth(depth[i + 1], kinds.shape[1], run)
        return carry

    lax.fori_loop(0, kinds.shape[0], body, 0)


def pack_halo(feats, table, core, width, to_mate, to_cross):
    atoms = feats.shape[1]
    rows = lax.broadcasted_iota(I32, (width, width), 0).astype(F32).astype(BF16)
    one, zero = jnp.ones((), BF16), jnp.zeros((), BF16)
    for ref, start in ((to_mate, (1 - core) * width), (to_cross, core * width)):
        wanted = table[SEND_ROW : SEND_ROW + 1, pl.ds(aligned(start, width), width)]
        picks = []
        for k in range(atoms // width):
            place = jnp.clip(wanted - float(k * width), -1.0, float(width)).astype(BF16)
            picks.append(jnp.where(rows == place, one, zero))
        ref[...] = dot(feats[...], jnp.concatenate(picks, axis=0)).astype(BF16)


def halo_places(core, atoms, width):
    top = atoms + width
    return aligned((1 - core) * top, width), aligned(core * top, width)


def edge_block(i, blocks, width):
    block = i * (blocks - 1)
    return block, aligned(block * width, width)


def first_outer(width, core_ref, pk, own_table, seated, mate, cross, edges, owns, depth, embed_t, first, spread, mix_half, inner, delta_out, basis_out, place_out, feats_out, to_mate, to_cross, pair_out, table, hid, kinds):
    core = core_ref[0]
    atoms = pk.shape[1]
    blocks = atoms // width
    fan = edges.shape[1]
    weights = (embed_t, first, mix_half.at[0], spread.at[0])
    table[:, width : width + atoms] = own_table[...]
    at_mate, at_cross = halo_places(core, atoms, width)
    for ref, start, at in ((mate, core * width, at_mate), (cross, (1 - core) * width, at_cross)):
        spans = [ref[:, part] for part in halves(atoms)]
        for k in range(width // LANES):
            wanted = ref[SEND_ROW : SEND_ROW + 1, pl.ds(aligned(start + k * LANES, LANES), LANES)]
            wanted = jnp.broadcast_to(wanted.astype(I32), (PACK_ROWS, LANES))
            place = pl.ds(aligned(at + k * LANES, LANES), LANES)
            table[:, place] = lane_lookup(spans, wanted)
            lane = lax.broadcasted_iota(I32, (1, LANES), 1) + k * LANES
            table[SEAT_ROW : SEAT_ROW + 1, place] = lane.astype(F32)
    feats_out[:, width : atoms - width] = inner[...]
    pair_out[0:4, :] = pk[0:4, :]
    pair_out[4:8, :] = mate[0:4, :]

    def body(i, carry):
        b, lo = edge_block(i, blocks, width)
        locate_block(
            i, table, lo, seated, edges[b], owns[b], lo, width,
            delta_out, basis_out, kinds, place_out,
        )

        def run(rows):
            feats_out[:, pl.ds(lo, width)] = first_block(
                rows, kinds[i], basis_out[i], owns.at[b], seated, lo, width, weights, hid
            )

        by_depth(depth[b], fan, run)
        return carry

    lax.fori_loop(0, 2, body, 0)
    pack_halo(feats_out, own_table, core, width, to_mate, to_cross)


def places_of(place, width):
    return [jnp.clip(place - float(k * width), -1.0, float(width)).astype(BF16) for k in range(3)]


def fetch_rows(window, places, s, width):
    rows = lax.broadcasted_iota(I32, (width, width), 0).astype(F32).astype(BF16)
    one, zero = jnp.ones((), BF16), jnp.zeros((), BF16)
    picks = [jnp.where(rows == place[s : s + 1], one, zero) for place in places]
    return dot(window, jnp.concatenate(picks, axis=0))


def layer_block(rows, window, place, own, hid, out_t, mix_half, feats):
    fan, width = place.shape
    units = out_t.shape[1]
    places = places_of(place, width)
    sums = Sums(feats.shape, own, rows, fan)
    for s in range(rows):
        far = fetch_rows(window, places, s, width)
        sums.add(s, far * dot(out_t, hid[s * units : (s + 1) * units, :]))
    return update_of(feats, sums.done(), mix_half, fan)


def hidden_edges(depth, spread, basis, hid_edge, blocks, fan):
    def body(i, carry):
        by_depth(
            depth[i * (blocks - 1)], fan,
            lambda rows: fill_hidden(hid_edge.at[i], spread, basis[i], rows, fan),
        )
        return carry

    lax.fori_loop(0, 2, body, 0)


def layer_inner(width, layer, owns, depth, spreads, outs_t, mixes, feats, basis, place, basis_edge, pair, feats_out, hid_edge, pair_out, hid):
    spread, out_t, mix_half = spreads.at[layer], outs_t[layer], mixes[layer]
    fan = place.shape[1]
    pair_out[...] = pair[...]

    def body(i, carry):
        lo = aligned((i + 1) * width, width)

        def run(rows):
            fill_hidden(hid, spread, basis[i], rows, fan)
            feats_out[:, pl.ds(aligned(i * width, width), width)] = layer_block(
                rows, feats[:, pl.ds(aligned(lo - width, width), 3 * width)], place[i],
                owns.at[i + 1], hid, out_t, mix_half, feats[:, pl.ds(lo, width)],
            )

        by_depth(depth[i + 1], fan, run)
        return carry

    lax.fori_loop(0, place.shape[0], body, 0)
    hidden_edges(depth, spread, basis_edge, hid_edge, place.shape[0] + 2, fan)


def fill_table(table, feats, mate, cross, core, width):
    atoms = feats.shape[1]
    at_mate, at_cross = halo_places(core, atoms, width)
    table[:, width : width + atoms] = feats[...]
    table[:, pl.ds(at_mate, width)] = mate[...]
    table[:, pl.ds(at_cross, width)] = cross[...]


def layer_outer(width, layer, core_ref, own_table, owns, depth, outs_t, mixes, feats, place, mate, cross, hid_edge, inner, feats_out, to_mate, to_cross, table):
    core = core_ref[0]
    atoms = feats.shape[1]
    fan = place.shape[1]
    out_t, mix_half = outs_t[layer], mixes[layer]
    fill_table(table, feats, mate, cross, core, width)
    feats_out[:, width : atoms - width] = inner[...]

    def body(i, carry):
        b, lo = edge_block(i, atoms // width, width)

        def run(rows):
            feats_out[:, pl.ds(lo, width)] = layer_block(
                rows, table[:, pl.ds(lo, 3 * width)], place[i], owns.at[b],
                hid_edge.at[i], out_t, mix_half, feats[:, pl.ds(lo, width)],
            )

        by_depth(depth[b], fan, run)
        return carry

    lax.fori_loop(0, 2, body, 0)
    pack_halo(feats_out, own_table, core, width, to_mate, to_cross)


def head_block(rows, window, place, own, hid, out_t, feats, delta, seat):
    fan, width = place.shape
    chans, units = out_t.shape
    places = places_of(place, width)
    near = feats.astype(F32)
    pairs = []
    for s in range(rows):
        far = fetch_rows(window, places, s, width)
        here = near
        if s >= 2 * rows - fan:
            lower = jnp.where(own[s : s + 1] > 0.5, near[:, LANES:], near[:, :LANES])
            here = jnp.concatenate([near[:, :LANES], lower], axis=1)
        terms = far * (dot(out_t, hid[s * units : (s + 1) * units, :]) * here)
        pairs.append(jnp.sum(terms, axis=0, keepdims=True))
    if rows < fan:
        pairs.append(jnp.zeros((fan - rows, width), F32))
    pair = jnp.concatenate(pairs, axis=0) * (1.0 / math.sqrt(chans))
    mine = own[...] > 0.5
    out = []
    for c in range(3):
        terms = pair * delta[c * fan : (c + 1) * fan, :]
        second = terms[:, LANES:]
        lent = jnp.where(mine, 0.0, second)
        out.append(
            jnp.concatenate(
                [
                    jnp.sum(terms[:, :LANES] + lent, axis=0, keepdims=True),
                    jnp.sum(jnp.where(mine, second, 0.0), axis=0, keepdims=True),
                ],
                axis=1,
            )
        )
    seated = jnp.concatenate(out + [jnp.zeros((PACK_ROWS - 3, width), F32)], axis=0)
    spans = [seated[:, part] for part in halves(width)]
    seat = seat.astype(I32)
    return jnp.concatenate(
        [
            lane_lookup(spans, jnp.broadcast_to(seat[:, part], (PACK_ROWS, LANES)))
            for part in halves(width)
        ],
        axis=1,
    )


def head_inner(width, layer, own_table, owns, depth, spreads, outs_t, feats, basis, place, delta, basis_edge, force_out, hid_edge, hid):
    spread, out_t = spreads.at[layer], outs_t[layer]
    fan = place.shape[1]

    def body(i, carry):
        lo = aligned((i + 1) * width, width)

        def run(rows):
            fill_hidden(hid, spread, basis[i], rows, fan)
            force_out[:, pl.ds(aligned(i * width, width), width)] = head_block(
                rows, feats[:, pl.ds(aligned(lo - width, width), 3 * width)], place[i],
                owns.at[i + 1], hid, out_t, feats[:, pl.ds(lo, width)], delta.at[i],
                own_table[SEAT_ROW : SEAT_ROW + 1, pl.ds(lo, width)],
            )

        by_depth(depth[i + 1], fan, run)
        return carry

    lax.fori_loop(0, place.shape[0], body, 0)
    hidden_edges(depth, spread, basis_edge, hid_edge, place.shape[0] + 2, fan)


def lane_sum(values):
    total = values[:, :LANES]
    for part in halves(values.shape[1])[1:]:
        total = total + values[:, part]
    return jnp.sum(total, axis=0, keepdims=True)


def head_outer(width, layer, core_ref, pk, own_table, received, relayed, owns, depth, outs_t, w_row, ref_row, feats, place, delta, mate, cross, hid_edge, inner, force_out, band_out, sums_out, table):
    core = core_ref[0]
    atoms = feats.shape[1]
    fan = place.shape[1]
    out_t = outs_t[layer]
    fill_table(table, feats, mate, cross, core, width)
    force_out[:, width : atoms - width] = inner[...]

    def body(i, carry):
        b, lo = edge_block(i, atoms // width, width)

        def run(rows):
            force_out[:, pl.ds(lo, width)] = head_block(
                rows, table[:, pl.ds(lo, 3 * width)], place[i], owns.at[b],
                hid_edge.at[i], out_t, feats[:, pl.ds(lo, width)], delta.at[i],
                own_table[SEAT_ROW : SEAT_ROW + 1, pl.ds(lo, width)],
            )

        by_depth(depth[b], fan, run)
        return carry

    lax.fori_loop(0, 2, body, 0)
    energy = dot(w_row[...], feats[...]) + ref_row[...]
    back = pk[0:4, :] - jnp.where(core == 0, relayed[0:4, :], received[4:8, :])
    fore = jnp.where(core == 0, received[4:8, :], relayed[0:4, :]) - pk[0:4, :]
    band_out[0:4, :] = back
    band_out[4:8, :] = fore
    back, fore, force = back[:3], fore[:3], force_out[0:3, :]
    rows = [energy, back * back, fore * fore, back * fore, force * back, force * fore]
    sums = [lane_sum(row) for row in rows]
    sums.append(jnp.zeros((SUM_ROWS - len(sums), LANES), F32))
    sums_out[...] = jnp.concatenate(sums, axis=0)


def add_sums(mine, other, out):
    out[...] = mine[...] + other[...]


def finish(count, flags, band, force, *rest):
    *parts, result, energy_out = rest
    total = parts[0][...]
    for part in parts[1:]:
        total = total + part[...]
    total = jnp.sum(total, axis=1, keepdims=True)
    energy, back_sq, fore_sq, cross, along_back, along_fore = (total[i : i + 1] for i in range(6))
    back_len = jnp.sqrt(back_sq + 1e-06)
    fore_len = jnp.sqrt(fore_sq + 1e-06)
    by_back, by_fore = 1.0 / back_len, 1.0 / fore_len
    tau_sq = (
        back_sq * by_back * by_back + fore_sq * by_fore * by_fore + 2.0 * cross * by_back * by_fore
    )
    proj = (along_back * by_back + along_fore * by_fore) / tau_sq
    spring = SPRING * (fore_len - back_len) / jnp.sqrt(tau_sq)
    climbing = flags[1] == 1
    is_end = flags[0] == 1
    factor = jnp.where(climbing, -2.0 * proj, spring - proj)
    tangent = band[0:3, :] * by_back + band[4:7, :] * by_fore
    moved = jnp.where(is_end, force[0:3, :], force[0:3, :] + factor * tangent)
    for c in range(3):
        result[c] = moved[c : c + 1]
    energy_out[...] = energy * (1.0 / count)


def swap_pairs(count, offset):
    pairs = []
    for low in range(offset, count, 2):
        high = (low + 1) % count
        pairs += [(low, high), (high, low)]
    return pairs


def image_pairs(images, tiles):
    pairs = []
    for low in range(images):
        high = (low + 1) % images
        for tile in range(0, tiles, 2):
            a, b = low * tiles + tile, high * tiles + tile + 1
            pairs += [(a, b), (b, a)]
    return pairs


def on_device(positions, species, counts, neighbours, send_list, climb, embed, ref_energy, rad_in, rad_out, mixing, w_energy):
    atoms = species.shape[0]
    width = send_list.shape[0] // 2
    fan = neighbours.shape[0]
    chans = embed.shape[1]
    layers = mixing.shape[0]
    basis_count, units = rad_in.shape[1:]
    blocks = atoms // width
    inner_atoms = (blocks - 2) * width
    tiles = lax.axis_size("atom")
    images = lax.axis_size("img")
    core = lax.rem(lax.axis_index("atom"), 2)
    image = lax.axis_index("img")
    core_arr = core.reshape(1).astype(I32)
    is_end = jnp.logical_or(image == 0, image == images - 1)
    flags = jnp.stack([is_end.astype(I32), climb[0]])

    def call(body, operands, outs, scratch=(), flops=0):
        scalars = {id(x) for x in (core_arr, flags, ref_energy)}
        return pl.pallas_call(
            body,
            out_shape=[jax.ShapeDtypeStruct(shape, dtype) for shape, dtype in outs],
            in_specs=[SMEM if id(x) in scalars else VMEM for x in operands],
            out_specs=[VMEM] * len(outs),
            scratch_shapes=[pltpu.VMEM(*x) for x in scratch],
            cost_estimate=pl.CostEstimate(flops=flops, bytes_accessed=2**20, transcendentals=0),
            compiler_params=pltpu.CompilerParams(vmem_limit_bytes=40 * 2**20),
        )(*operands)

    def swap(block, offset):
        return lax.ppermute(block, "atom", swap_pairs(tiles, offset))

    pack_type = ((PACK_ROWS, atoms), F32)
    feats_type = ((chans, atoms), BF16)
    halo_type = ((chans, width), BF16)
    hid_type = ((2, fan * units, width), BF16)
    hid_scratch = ((fan * units, width), BF16)
    table_scratch = [((chans, atoms + 2 * width), BF16)]

    def block_outs(count):
        return [
            ((count, 3 * fan, width), F32),
            ((count, fan * basis_count, width), BF16),
            ((count, fan, width), F32),
        ]

    row = lax.broadcasted_iota(I32, (PACK_ROWS, atoms), 0)
    sends = jnp.pad(send_list, (0, atoms - 2 * width))
    pk = jnp.zeros((PACK_ROWS, atoms), F32)
    lines = [positions[0, c] for c in range(3)] + [species, counts, sends]
    for place, line in enumerate(lines):
        pk = jnp.where(row == place, lax.broadcast_in_dim(line, pk.shape, (1,)).astype(F32), pk)
    mate = swap(pk, 0)
    cross = swap(pk, 1)
    kinds_type = ((blocks - 2, fan, width), F32)
    own_table, seated, edges, owns, depth, delta_in, basis_in, kinds_in, place_in = call(
        functools.partial(seat_tile, width),
        (pk, neighbours),
        [
            pack_type,
            pack_type,
            ((blocks, fan, width), F32),
            ((blocks, fan, LANES), F32),
            ((blocks, PACK_ROWS, LANES), F32),
        ]
        + block_outs(blocks - 2)[:2]
        + [kinds_type, kinds_type],
        [((fan, atoms), F32)],
        flops=2**32,
    )
    inner, embed_t, first, spread, out_t, mix_half, w_row, ref_row = call(
        functools.partial(first_inner, width),
        (ref_energy, pk, seated, owns, depth, basis_in, kinds_in, embed, rad_in, rad_out, mixing, w_energy[None]),
        [
            ((chans, inner_atoms), BF16),
            ((chans, -(-embed.shape[0] // 16) * 16), BF16),
            ((chans, embed.shape[0] * units), BF16),
            ((layers + 1, fan * units, fan * basis_count), BF16),
            ((layers + 1, chans, units), BF16),
            ((layers, chans, chans), BF16),
            ((1, chans), BF16),
            ((1, atoms), F32),
        ],
        [hid_scratch],
        flops=2**32,
    )
    delta_out, basis_out, place_out, feats, to_mate, to_cross, pair = call(
        functools.partial(first_outer, width),
        (core_arr, pk, own_table, seated, mate, cross, edges, owns, depth, embed_t, first, spread, mix_half, inner),
        block_outs(2) + [feats_type, halo_type, halo_type, pack_type],
        [((PACK_ROWS, atoms + 2 * width), F32), hid_scratch, ((2, fan, width), F32)],
    )
    for layer in range(1, layers):
        mate = swap(to_mate, 0)
        cross = swap(to_cross, 1)
        inner, hid_edge, pair = call(
            functools.partial(layer_inner, width, layer),
            (owns, depth, spread, out_t, mix_half, feats, basis_in, place_in, basis_out, pair),
            [((chans, inner_atoms), BF16), hid_type, pack_type],
            [hid_scratch],
        )
        feats, to_mate, to_cross = call(
            functools.partial(layer_outer, width, layer),
            (core_arr, own_table, owns, depth, out_t, mix_half, feats, place_out, mate, cross, hid_edge, inner),
            [feats_type, halo_type, halo_type],
            table_scratch,
        )
    received = lax.ppermute(pair, ("img", "atom"), image_pairs(images, tiles))
    relayed = swap(received, 0)
    mate = swap(to_mate, 0)
    cross = swap(to_cross, 1)
    inner, hid_edge = call(
        functools.partial(head_inner, width, layers),
        (own_table, owns, depth, spread, out_t, feats, basis_in, place_in, delta_in, basis_out),
        [((PACK_ROWS, inner_atoms), F32), hid_type],
        [hid_scratch],
    )
    force, band, sums = call(
        functools.partial(head_outer, width, layers),
        (core_arr, pk, own_table, received, relayed, owns, depth, out_t, w_row, ref_row, feats, place_out, delta_out, mate, cross, hid_edge, inner),
        [pack_type, pack_type, ((SUM_ROWS, LANES), F32)],
        table_scratch,
    )
    step = 2 * REDUCE_CHIPS
    while step < tiles:
        sums = sums + lax.ppermute(sums, "atom", [(i, i ^ step) for i in range(tiles)])
        step *= 2
    (both,) = call(add_sums, (sums, swap(sums, 0)), [((SUM_ROWS, LANES), F32)])
    near = lax.ppermute(both, "atom", [(i, i ^ 2 if i % 2 == 0 else i ^ 6) for i in range(tiles)])
    far = lax.ppermute(both, "atom", [(i, i ^ 4) for i in range(tiles)])
    other = swap(near, 0)
    result, energy = call(
        functools.partial(finish, atoms * tiles),
        (flags, band, force, both, near, far, other),
        [((3, 1, atoms), F32), ((1, 1), F32)],
    )
    return jnp.transpose(result, (1, 0, 2)), energy.reshape(1)


def solution(mesh):
    return jax.shard_map(
        on_device,
        mesh=mesh,
        in_specs=(
            P("img", None, "atom"),
            P("atom"),
            P("atom"),
            P(None, "atom"),
            P("atom"),
            P("img"),
            P(),
            P(),
            P(),
            P(),
            P(),
            P(),
        ),
        out_specs=(P("img", None, "atom"), P("img")),
        check_vma=False,
    )
```

time: 41.6 us -> 39.6 us (0.952)
  starting transfers between devices: 14.3 us -> 12.8 us
  waiting for transfers between devices: 2.46 us -> 3.87 us
  Pallas kernels: 20.4 us -> 19.3 us
  local copies, waits for them, and re-layouts: 2.28 us -> 1.35 us
    ppermute x9, waiting for transfers between devices: 1.48 us -> 2.7 us  [swap(): return lax.ppermute(block, 'atom', swap_pairs(tiles, offset))]
    pallas_call x7 -> x9, Pallas kernels: 20.4 us -> 19.3 us  [call(): pl.pallas_call(body, out_shape=[jax.ShapeDtypeStruct(shape, dtype) for sh...]
    unnamed x22, local copies, waits for them, and re-layouts: 2.22 us -> 1.35 us
    ppermute x9, starting transfers between devices: 10.6 us -> 9.79 us  [swap(): return lax.ppermute(block, 'atom', swap_pairs(tiles, offset))]
    ppermute x1, starting transfers between devices: 1.03 us -> 0.51 us  [on_device(): received = lax.ppermute(pair, ('img', 'atom'), image_pairs(images, tiles))]
  transfers between devices with their start and end apart: 12 -> 12, of which waited for: 6 -> 5; matrix products, arithmetic and copies ran while one was open for 0% -> 0% of each run, Pallas kernels for 33% -> 33%
where the time goes in v3:
time: 39.6 us; the launch traced here: 39.1 us
  Pallas kernels  19.3 us (49%)
  starting transfers between devices  12.8 us (32%)
  waiting for transfers between devices  3.87 us (10%)
  between operations  1.51 us (4%)
  local copies, waits for them, and re-layouts  1.35 us (3%)
    pallas_call x9, Pallas kernels, call(): pl.pallas_call(body, out_shape=[jax.ShapeDtypeStruct(shape, dtype) for sh...  19.3 us
    ppermute x9, starting transfers between devices, swap(): return lax.ppermute(block, 'atom', swap_pairs(tiles, offset))  9.79 us
    ppermute x9, waiting for transfers between devices, swap(): return lax.ppermute(block, 'atom', swap_pairs(tiles, offset))  2.7 us
    ppermute x1, starting transfers between devices, on_device(): far = lax.ppermute(both, 'atom', [(i, i ^ 4) for i in range(tiles)])  2.51 us
    unnamed x22, local copies, waits for them, and re-layouts  1.35 us
  transfers between devices with their start and end apart: 12, of which 5 were waited for; matrix products, arithmetic and copies ran while one was open for 0% of the time, Pallas kernels for 33%

profile of v3, /device:TPU:0, one launch (start us, length us, event | category | flops | bytes accessed | tf_op | source)
XLA Modules:
  0.0 39.1 jit_solution(10099659467817595963)
XLA Ops:
  0.7 0.0 copy-start.9
  0.7 0.0 copy-start.10
  0.7 0.6 %copy-done.8 = s32[1024]{0:T(1024)S(1)} copy-done((s32[1024]{0:T(1024)S(1)}, s32[1024]{0:T(1024)}, u32[]{:S(2)}) %copy-start.8) | copy-done | bytes 4120
  1.3 0.0 copy-done.9
  1.3 0.0 copy-done.10
  1.4 0.0 copy-done.7
  1.4 0.1 select_select_fusion.pk
  1.5 4.6 %collective-permute-start.1 = (f32[8,1024]{1,0:T(8,128)S(1)}, f32[8,1024]{1,0:T(8,128)S(1)}, u32[]{:S(2)}, u32[]{:S(2)}) collective-permute-start(f32[8,1024]{1,0:T(8,128)S(1)} %select_select_fusion.pk), channel_id=1, source_target_pairs={{1,2},{2,1},{3,4},{4,3},{5,6},{6,5},{7,0},{0,7},{9,10},{10,9},{11,... | collective-permute-start | bytes 98312 | tf_op jit(solution)/shard_map/ppermute | solution.py:626
  6.1 1.5 %shard_map.131 = (f32[8,1024]{1,0:T(8,128)S(1)}, f32[8,1024]{1,0:T(8,128)S(1)}, f32[4,16,256]{2,1,0:T(8,128)S(1)}, f32[4,16,128]{2,1,0:T(8,128)S(1)}, f32[4,8,12...) custom-call(f32[8,1024]{1,0:T(8,128)S(1)} %select_select_fusion.pk, ...), custom_call_target="tpu_custom_call" | custom-call | flops 4294967296 | bytes 1048576 | tf_op jit(solution)/shard_map/pallas_call | solution.py:615
  7.6 0.6 %copy-done.3 = bf16[3,8,64]{2,1,0:T(8,128)(2,1)S(1)} copy-done((bf16[3,8,64]{2,1,0:T(8,128)(2,1)S(1)}, bf16[3,8,64]{2,1,0:T(8,128)(2,1)}, u32[]{:S(2)}) %copy-start.3) | copy-done | bytes 3096
  8.2 2.6 %shard_map.132 = (bf16[128,512]{1,0:T(8,128)(2,1)S(1)}, bf16[128,16]{1,0:T(8,128)(2,1)S(1)}, bf16[128,256]{1,0:T(8,128)(2,1)S(1)}, bf16[3,1024,128]{2,1,0:T(8,12...) custom-call(f32[4]{0:T(128)S(1)} %copy-done.5, ...), custom_call_target="tpu_custom_call" | custom-call | flops 4294967296 | bytes 1048576 | tf_op jit(solution)/shard_map/pallas_call | solution.py:615
  10.8 2.5 %shard_map.133 = (f32[2,48,256]{2,1,0:T(8,128)S(1)}, bf16[2,128,256]{2,1,0:T(8,128)(2,1)S(1)}, f32[2,16,256]{2,1,0:T(8,128)S(1)}, bf16[128,1024]{1,0:T(8,128)(2,...) custom-call(s32[1]{0:T(128)} %bitcast.1.core_ref, ...), custom_call_target="tpu_custom_call" | custom-call | bytes 1048576 | tf_op jit(solution)/shard_map/pallas_call | solution.py:615
  13.3 0.6 %collective-permute-start.4 = (bf16[128,256]{1,0:T(8,128)(2,1)S(1)}, bf16[128,256]{1,0:T(8,128)(2,1)S(1)}, u32[]{:S(2)}, u32[]{:S(2)}) collective-permute-start(bf16[128,256]{1,0:T(8,128)(2,1)S(1)} %get-tuple-element.60), channel_id=1, source_target_pairs={{0,1},{1,0},{2,3},{3,2},{4,5},{5,4},{6,7},{7,6},{8,9},{9,8},{10,11... | collective-permute-start | bytes 196616 | tf_op jit(solution)/shard_map/ppermute | solution.py:626
  13.9 0.7 %collective-permute-start.5 = (bf16[128,256]{1,0:T(8,128)(2,1)S(1)}, bf16[128,256]{1,0:T(8,128)(2,1)S(1)}, u32[]{:S(2)}, u32[]{:S(2)}) collective-permute-start(bf16[128,256]{1,0:T(8,128)(2,1)S(1)} %get-tuple-element.61), channel_id=1, source_target_pairs={{1,2},{2,1},{3,4},{4,3},{5,6},{6,5},{7,0},{0,7},{9,10},{10,9},{11,... | collective-permute-start | bytes 196616 | tf_op jit(solution)/shard_map/ppermute | solution.py:626
  14.6 3.2 %shard_map.134 = (bf16[128,512]{1,0:T(8,128)(2,1)S(1)}, bf16[2,1024,256]{2,1,0:T(8,128)(2,1)S(1)}, f32[8,1024]{1,0:T(8,128)S(1)}) custom-call(f32[4,16,128]{2,1,0:T(8,128)S(1)} %get-tuple-element.40.owns, f32[4,8,128]{2,1,0:T(8,128)S(1)} %get-tuple-element.41.depth, bf16[3,1024,128]{2,1,0:T(8,128)(2,1)S(1)} %get-tuple-element.45.spread.spreads, ...), custom_call_target="tpu_custom_call" | custom-call | bytes 1048576 | tf_op jit(solution)/shard_map/pallas_call | solution.py:615
  17.9 0.5 %collective-permute-start.2 = (f32[8,1024]{1,0:T(8,128)S(1)}, f32[8,1024]{1,0:T(8,128)S(1)}, u32[]{:S(2)}, u32[]{:S(2)}) collective-permute-start(f32[8,1024]{1,0:T(8,128)S(1)} %get-tuple-element.56), channel_id=1, source_target_pairs={{0,9},{9,0},{2,11},{11,2},{4,13},{13,4},{6,15},{15,6},{8,17},{17,8... | collective-permute-start | bytes 98312 | tf_op jit(solution)/shard_map/ppermute | solution.py:703
  18.4 1.0 %collective-permute-done.5.cross = bf16[128,256]{1,0:T(8,128)(2,1)S(1)} collective-permute-done((bf16[128,256]{1,0:T(8,128)(2,1)S(1)}, bf16[128,256]{1,0:T(8,128)(2,1)S(1)}, u32[]{:S(2)}, u32[]{:S(2)}) %collective-permute-start.5) | collective-permute-done | bytes 65568 | tf_op jit(solution)/shard_map/ppermute | solution.py:626
  19.4 2.7 %shard_map.135 = (bf16[128,1024]{1,0:T(8,128)(2,1)S(1)}, bf16[128,256]{1,0:T(8,128)(2,1)S(1)}, bf16[128,256]{1,0:T(8,128)(2,1)S(1)}) custom-call(s32[1]{0:T(128)} %bitcast.1.core_ref, f32[8,1024]{1,0:T(8,128)S(1)} %get-tuple-element.39.own_table, f32[4,16,128]{2,1,0:T(8,128)S(1)} %get-tuple-element.40.owns, f32[4,8,128]{2,1,0:T(8,128)S(1)} %get-tuple-element.41.depth, ...), custom_call_target="tpu_custom_call" | custom-call | bytes 1048576 | tf_op jit(solution)/shard_map/pallas_call | solution.py:615
  22.1 1.2 %collective-permute-start.6 = (bf16[128,256]{1,0:T(8,128)(2,1)S(1)}, bf16[128,256]{1,0:T(8,128)(2,1)S(1)}, u32[]{:S(2)}, u32[]{:S(2)}) collective-permute-start(bf16[128,256]{1,0:T(8,128)(2,1)S(1)} %get-tuple-element.66), channel_id=1, source_target_pairs={{0,1},{1,0},{2,3},{3,2},{4,5},{5,4},{6,7},{7,6},{8,9},{9,8},{10,11... | collective-permute-start | bytes 196616 | tf_op jit(solution)/shard_map/ppermute | solution.py:626
  23.3 1.8 %collective-permute-start.7 = (bf16[128,256]{1,0:T(8,128)(2,1)S(1)}, bf16[128,256]{1,0:T(8,128)(2,1)S(1)}, u32[]{:S(2)}, u32[]{:S(2)}) collective-permute-start(bf16[128,256]{1,0:T(8,128)(2,1)S(1)} %get-tuple-element.67), channel_id=1, source_target_pairs={{1,2},{2,1},{3,4},{4,3},{5,6},{6,5},{7,0},{0,7},{9,10},{10,9},{11,... | collective-permute-start | bytes 196616 | tf_op jit(solution)/shard_map/ppermute | solution.py:626
  25.1 3.1 %shard_map.136 = (f32[8,512]{1,0:T(8,128)S(1)}, bf16[2,1024,256]{2,1,0:T(8,128)(2,1)S(1)}) custom-call(f32[8,1024]{1,0:T(8,128)S(1)} %get-tuple-element.39.own_table, f32[4,16,128]{2,1,0:T(8,128)S(1)} %get-tuple-element.40.owns, f32[4,8,128]{2,1,0:T(8,128)S(1)} %get-tuple-element.41.depth, bf16[3,1024,128]{2,1,0:T(8,128)(2,1)S(1)} %get-tuple-element.45.spread.spreads, ...), custom_call_target="tpu_custom_call" | custom-call | bytes 1048576 | tf_op jit(solution)/shard_map/pallas_call | solution.py:615
  28.3 0.5 %collective-permute-done.7.cross = bf16[128,256]{1,0:T(8,128)(2,1)S(1)} collective-permute-done((bf16[128,256]{1,0:T(8,128)(2,1)S(1)}, bf16[128,256]{1,0:T(8,128)(2,1)S(1)}, u32[]{:S(2)}, u32[]{:S(2)}) %collective-permute-start.7) | collective-permute-done | bytes 65568 | tf_op jit(solution)/shard_map/ppermute | solution.py:626
  28.8 2.5 %shard_map.137 = (f32[8,1024]{1,0:T(8,128)S(1)}, f32[8,1024]{1,0:T(8,128)S(1)}, f32[8,128]{1,0:T(8,128)S(1)}) custom-call(s32[1]{0:T(128)} %bitcast.1.core_ref, f32[8,1024]{1,0:T(8,128)S(1)} %select_select_fusion.pk, f32[8,1024]{1,0:T(8,128)S(1)} %get-tuple-element.39.own_table, f32[8,1024]{1,0:T(8,128)S(1)} %collective-permute-done.2.received, ...), custom_call_target="tpu_custom_call" | custom-call | bytes 1048576 | tf_op jit(solution)/shard_map/pallas_call | solution.py:615
  31.3 0.1 collective-permute-start.8
  31.3 1.2 %collective-permute-done.8.other = f32[8,128]{1,0:T(8,128)S(1)} collective-permute-done((f32[8,128]{1,0:T(8,128)S(1)}, f32[8,128]{1,0:T(8,128)S(1)}, u32[]{:S(2)}, u32[]{:S(2)}) %collective-permute-start.8) | collective-permute-done | bytes 4128 | tf_op jit(solution)/shard_map/ppermute | solution.py:626
  33.2 2.5 %collective-permute-start.10 = (f32[8,128]{1,0:T(8,128)S(1)}, f32[8,128]{1,0:T(8,128)S(1)}, u32[]{:S(2)}, u32[]{:S(2)}) collective-permute-start(f32[8,128]{1,0:T(8,128)S(1)} %shard_map.138.rest_0_), channel_id=1, source_target_pairs={{0,4},{1,5},{2,6},{3,7},{4,0},{5,1},{6,2},{7,3},{8,12},{9,13},{10,... | collective-permute-start | bytes 12296 | tf_op jit(solution)/shard_map/ppermute | solution.py:725
  35.7 0.4 %collective-permute-done.9.rest_1_ = f32[8,128]{1,0:T(8,128)S(1)} collective-permute-done((f32[8,128]{1,0:T(8,128)S(1)}, f32[8,128]{1,0:T(8,128)S(1)}, u32[]{:S(2)}, u32[]{:S(2)}) %collective-permute-start.9) | collective-permute-done | bytes 4128 | tf_op jit(solution)/shard_map/ppermute | solution.py:724
  36.1 0.8 %collective-permute-start.11 = (f32[8,128]{1,0:T(8,128)S(1)}, f32[8,128]{1,0:T(8,128)S(1)}, u32[]{:S(2)}, u32[]{:S(2)}) collective-permute-start(f32[8,128]{1,0:T(8,128)S(1)} %collective-permute-done.9.rest_1_), channel_id=1, source_target_pairs={{0,1},{1,0},{2,3},{3,2},{4,5},{5,4},{6,7},{7,6},{8,9},{9,8},{10,11... | collective-permute-start | bytes 12296 | tf_op jit(solution)/shard_map/ppermute | solution.py:626
  36.9 0.1 pad_add_fusion.flags
  37.0 0.7 %collective-permute-done.10.rest_2_ = f32[8,128]{1,0:T(8,128)S(1)} collective-permute-done((f32[8,128]{1,0:T(8,128)S(1)}, f32[8,128]{1,0:T(8,128)S(1)}, u32[]{:S(2)}, u32[]{:S(2)}) %collective-permute-start.10) | collective-permute-done | bytes 4128 | tf_op jit(solution)/shard_map/ppermute | solution.py:725
  37.7 0.0 collective-permute-done.11.rest_3_
  37.7 1.3 %shard_map.139 = (f32[3,1,1024]{2,1,0:T(1,128)}, f32[1,1]{1,0:T(1,128)}) custom-call(s32[2]{0:T(128)S(1)} %pad_add_fusion.flags, f32[8,1024]{1,0:T(8,128)S(1)} %get-tuple-element.71.band, f32[8,1024]{1,0:T(8,128)S(1)} %get-tuple-element.72.force, f32[8,128]{1,0:T(8,128)S(1)} %shard_map.138.rest_0_, f32[8,128]{1,0:T(8,128)S(1)} %collective-permute-done.9.rest_1_, ...), custom_call_target="tpu_custom_call" | custom-call | bytes 1048576 | tf_op jit(solution)/shard_map/pallas_call | solution.py:615
  (32 shorter events, 0.1 us)
Async XLA Ops:
  0.6 0.7 %copy-start.8 = (s32[1024]{0:T(1024)S(1)}, s32[1024]{0:T(1024)}, u32[]{:S(2)}) copy-start(s32[1024]{0:T(1024)} %param.13) | copy-start | bytes 12292
  0.7 0.7 %copy-start.9 = (s32[1024]{0:T(1024)S(1)}, s32[1024]{0:T(1024)}, u32[]{:S(2)}) copy-start(s32[1024]{0:T(1024)} %param.14) | copy-start | bytes 12292
  0.7 0.7 %copy-start.10 = (s32[512]{0:T(512)S(1)}, s32[512]{0:T(512)}, u32[]{:S(2)}) copy-start(s32[512]{0:T(512)} %param.16) | copy-start | bytes 6148
  0.7 0.7 %copy-start.7 = (f32[1,3,1024]{2,0,1:T(1,128)S(1)}, f32[1,3,1024]{2,0,1:T(1,128)}, u32[]{:S(2)}) copy-start(f32[1,3,1024]{2,0,1:T(1,128)} %param.12) | copy-start | bytes 36868
  1.3 4.8 %copy-start = (s32[16,1024]{1,0:T(8,128)S(1)}, s32[16,1024]{1,0:T(8,128)}, u32[]{:S(2)}) copy-start(s32[16,1024]{1,0:T(8,128)} %nbr.1) | copy-start | bytes 196612
  1.5 6.1 %copy-start.1 = (bf16[2,128,128]{2,1,0:T(8,128)(2,1)S(1)}, bf16[2,128,128]{2,1,0:T(8,128)(2,1)}, u32[]{:S(2)}) copy-start(bf16[2,128,128]{2,1,0:T(8,128)(2,1)} %mixing.1) | copy-start | bytes 196612
  1.5 6.1 %copy-start.2 = (bf16[3,64,128]{2,1,0:T(8,128)(2,1)S(1)}, bf16[3,64,128]{2,1,0:T(8,128)(2,1)}, u32[]{:S(2)}) copy-start(bf16[3,64,128]{2,1,0:T(8,128)(2,1)} %rad_out.1) | copy-start | bytes 147460
  1.5 9.3 %collective-permute-start.1 = (f32[8,1024]{1,0:T(8,128)S(1)}, f32[8,1024]{1,0:T(8,128)S(1)}, u32[]{:S(2)}, u32[]{:S(2)}) collective-permute-start(f32[8,1024]{1,0:T(8,128)S(1)} %select_select_fusion.pk), channel_id=1, source_target_pairs={{1,2},{2,1},{3,4},{4,3},{5,6},{6,5},{7,0},{0,7},{9,10},{10,9},{11,... | collective-permute-start | bytes 98312 | tf_op jit(solution)/shard_map/ppermute | solution.py:626
  6.1 4.8 %collective-permute-start = (f32[8,1024]{1,0:T(8,128)S(1)}, f32[8,1024]{1,0:T(8,128)S(1)}, u32[]{:S(2)}, u32[]{:S(2)}) collective-permute-start(f32[8,1024]{1,0:T(8,128)S(1)} %select_select_fusion.pk), channel_id=1, source_target_pairs={{0,1},{1,0},{2,3},{3,2},{4,5},{5,4},{6,7},{7,6},{8,9},{9,8},{10,11... | collective-permute-start | bytes 98312 | tf_op jit(solution)/shard_map/ppermute | solution.py:626
  6.1 1.5 %copy-start.6 = (bf16[128]{0:T(256)(128)(2,1)S(1)}, bf16[128]{0:T(256)(128)(2,1)}, u32[]{:S(2)}) copy-start(bf16[128]{0:T(256)(128)(2,1)} %param.23) | copy-start | bytes 772
  7.5 0.7 %copy-start.3 = (bf16[3,8,64]{2,1,0:T(8,128)(2,1)S(1)}, bf16[3,8,64]{2,1,0:T(8,128)(2,1)}, u32[]{:S(2)}) copy-start(bf16[3,8,64]{2,1,0:T(8,128)(2,1)} %rad_in.1) | copy-start | bytes 9220
  7.5 0.7 %copy-start.4 = (bf16[4,128]{1,0:T(4,128)(2,1)S(1)}, bf16[4,128]{1,0:T(4,128)(2,1)}, u32[]{:S(2)}) copy-start(bf16[4,128]{1,0:T(4,128)(2,1)} %embed.1) | copy-start | bytes 3076
  7.6 0.7 %copy-start.5 = (f32[4]{0:T(128)S(1)}, f32[4]{0:T(128)}, u32[]{:S(2)}) copy-start(f32[4]{0:T(128)} %ref_energy.1) | copy-start | bytes 52
  13.3 5.1 %collective-permute-start.4 = (bf16[128,256]{1,0:T(8,128)(2,1)S(1)}, bf16[128,256]{1,0:T(8,128)(2,1)S(1)}, u32[]{:S(2)}, u32[]{:S(2)}) collective-permute-start(bf16[128,256]{1,0:T(8,128)(2,1)S(1)} %get-tuple-element.60), channel_id=1, source_target_pairs={{0,1},{1,0},{2,3},{3,2},{4,5},{5,4},{6,7},{7,6},{8,9},{9,8},{10,11... | collective-permute-start | bytes 196616 | tf_op jit(solution)/shard_map/ppermute | solution.py:626
  13.9 5.5 %collective-permute-start.5 = (bf16[128,256]{1,0:T(8,128)(2,1)S(1)}, bf16[128,256]{1,0:T(8,128)(2,1)S(1)}, u32[]{:S(2)}, u32[]{:S(2)}) collective-permute-start(bf16[128,256]{1,0:T(8,128)(2,1)S(1)} %get-tuple-element.61), channel_id=1, source_target_pairs={{1,2},{2,1},{3,4},{4,3},{5,6},{6,5},{7,0},{0,7},{9,10},{10,9},{11,... | collective-permute-start | bytes 196616 | tf_op jit(solution)/shard_map/ppermute | solution.py:626
  17.9 7.2 %collective-permute-start.2 = (f32[8,1024]{1,0:T(8,128)S(1)}, f32[8,1024]{1,0:T(8,128)S(1)}, u32[]{:S(2)}, u32[]{:S(2)}) collective-permute-start(f32[8,1024]{1,0:T(8,128)S(1)} %get-tuple-element.56), channel_id=1, source_target_pairs={{0,9},{9,0},{2,11},{11,2},{4,13},{13,4},{6,15},{15,6},{8,17},{17,8... | collective-permute-start | bytes 98312 | tf_op jit(solution)/shard_map/ppermute | solution.py:703
  22.1 6.2 %collective-permute-start.6 = (bf16[128,256]{1,0:T(8,128)(2,1)S(1)}, bf16[128,256]{1,0:T(8,128)(2,1)S(1)}, u32[]{:S(2)}, u32[]{:S(2)}) collective-permute-start(bf16[128,256]{1,0:T(8,128)(2,1)S(1)} %get-tuple-element.66), channel_id=1, source_target_pairs={{0,1},{1,0},{2,3},{3,2},{4,5},{5,4},{6,7},{7,6},{8,9},{9,8},{10,11... | collective-permute-start | bytes 196616 | tf_op jit(solution)/shard_map/ppermute | solution.py:626
  23.3 5.5 %collective-permute-start.7 = (bf16[128,256]{1,0:T(8,128)(2,1)S(1)}, bf16[128,256]{1,0:T(8,128)(2,1)S(1)}, u32[]{:S(2)}, u32[]{:S(2)}) collective-permute-start(bf16[128,256]{1,0:T(8,128)(2,1)S(1)} %get-tuple-element.67), channel_id=1, source_target_pairs={{1,2},{2,1},{3,4},{4,3},{5,6},{6,5},{7,0},{0,7},{9,10},{10,9},{11,... | collective-permute-start | bytes 196616 | tf_op jit(solution)/shard_map/ppermute | solution.py:626
  25.1 3.1 %collective-permute-start.3 = (f32[8,1024]{1,0:T(8,128)S(1)}, f32[8,1024]{1,0:T(8,128)S(1)}, u32[]{:S(2)}, u32[]{:S(2)}) collective-permute-start(f32[8,1024]{1,0:T(8,128)S(1)} %collective-permute-done.2.received), channel_id=1, source_target_pairs={{0,1},{1,0},{2,3},{3,2},{4,5},{5,4},{6,7},{7,6},{8,9},{9,8},{10,11... | collective-permute-start | bytes 98312 | tf_op jit(solution)/shard_map/ppermute | solution.py:626
  31.3 1.2 %collective-permute-start.8 = (f32[8,128]{1,0:T(8,128)S(1)}, f32[8,128]{1,0:T(8,128)S(1)}, u32[]{:S(2)}, u32[]{:S(2)}) collective-permute-start(f32[8,128]{1,0:T(8,128)S(1)} %get-tuple-element.73.mine), channel_id=1, source_target_pairs={{0,1},{1,0},{2,3},{3,2},{4,5},{5,4},{6,7},{7,6},{8,9},{9,8},{10,11... | collective-permute-start | bytes 12296 | tf_op jit(solution)/shard_map/ppermute | solution.py:626
  32.5 3.6 %collective-permute-start.9 = (f32[8,128]{1,0:T(8,128)S(1)}, f32[8,128]{1,0:T(8,128)S(1)}, u32[]{:S(2)}, u32[]{:S(2)}) collective-permute-start(f32[8,128]{1,0:T(8,128)S(1)} %shard_map.138.rest_0_), channel_id=1, source_target_pairs={{0,2},{1,7},{2,0},{3,5},{4,6},{5,3},{6,4},{7,1},{8,10},{9,15},{10,... | collective-permute-start | bytes 12296 | tf_op jit(solution)/shard_map/ppermute | solution.py:724
  33.2 4.6 %collective-permute-start.10 = (f32[8,128]{1,0:T(8,128)S(1)}, f32[8,128]{1,0:T(8,128)S(1)}, u32[]{:S(2)}, u32[]{:S(2)}) collective-permute-start(f32[8,128]{1,0:T(8,128)S(1)} %shard_map.138.rest_0_), channel_id=1, source_target_pairs={{0,4},{1,5},{2,6},{3,7},{4,0},{5,1},{6,2},{7,3},{8,12},{9,13},{10,... | collective-permute-start | bytes 12296 | tf_op jit(solution)/shard_map/ppermute | solution.py:725
  36.1 1.6 %collective-permute-start.11 = (f32[8,128]{1,0:T(8,128)S(1)}, f32[8,128]{1,0:T(8,128)S(1)}, u32[]{:S(2)}, u32[]{:S(2)}) collective-permute-start(f32[8,128]{1,0:T(8,128)S(1)} %collective-permute-done.9.rest_1_), channel_id=1, source_target_pairs={{0,1},{1,0},{2,3},{3,2},{4,5},{5,4},{6,7},{7,6},{8,9},{9,8},{10,11... | collective-permute-start | bytes 12296 | tf_op jit(solution)/shard_map/ppermute | solution.py:626

commit v4 on v3

--- a/solution.py
+++ b/solution.py
@@ -57,26 +57,27 @@
     return lane_fetch(windows, index // LANES, index & (LANES - 1))
 
 
-def seat_atoms(pk, lo, width):
+def seat_atoms(pk, lo, width, most):
     counts = pk[COUNT_ROW : COUNT_ROW + 1, lo : lo + width]
-    lane = lax.broadcasted_iota(I32, (1, width), 1).astype(F32)
-    key = counts * float(width) - lane
-
-    def down(row):
-        turned = jnp.broadcast_to(row, (LANES, width)).T
-        return jnp.concatenate([turned] * (width // LANES), axis=1)
-
-    rank = jnp.sum(jnp.where(down(key) > key, 1.0, 0.0), axis=0, keepdims=True)
+    value = lax.broadcasted_iota(I32, (most, width), 0).astype(F32) + 1.0
+    same = counts == value
+    row = lax.broadcasted_iota(I32, (width, width), 0)
+    lane = lax.broadcasted_iota(I32, (width, width), 1)
+    earlier = dot(jnp.where(same, 1.0, 0.0).astype(BF16), jnp.where(row < lane, 1.0, 0.0).astype(BF16))
+    larger = jnp.sum(jnp.where(counts > value, 1.0, 0.0), axis=1, keepdims=True)
+    rank = jnp.sum(jnp.where(same, earlier + larger, 0.0), axis=0, keepdims=True)
     seat = jnp.where(rank < width // 2, rank, 1.5 * width - 1.0 - rank)
-    atom = lax.broadcasted_iota(I32, (width, width), 0).astype(F32)
-    taker = jnp.sum(jnp.where(down(seat) == lane, atom, 0.0), axis=0, keepdims=True)
-    return seat, taker
-
-
-def seat_block(b, pk, nbr, lo, width, seated, edges, owns, depth):
+    taken = jnp.where(row.astype(F32) == seat, 1.0, 0.0).astype(BF16)
+    atoms = lax.broadcasted_iota(I32, (PACK_ROWS, width), 1).astype(F32).astype(BF16)
+    taker = lax.dot_general(
+        atoms, taken, (((1,), (1,)), ((), ())), preferred_element_type=F32
+    )
+    return seat, taker[:1]
+
+
+def seat_block(pk, nbr, lo, width, seated):
     fan = nbr.shape[0]
-    short = short_rows(fan)
-    seat, taker = seat_atoms(pk, lo, width)
+    seat, taker = seat_atoms(pk, lo, width, fan)
     pieces, tables = [], []
     for part in halves(width):
         who = taker[:, part].astype(I32)
@@ -84,30 +85,30 @@
         pieces.append(lane_lookup(spans, jnp.broadcast_to(who, (fan, LANES))) - float(lo))
         spans = [pk[:, lo + p.start : lo + p.stop] for p in halves(width)]
         tables.append(lane_lookup(spans, jnp.broadcast_to(who, (PACK_ROWS, LANES))))
+    seated[:, lo : lo + width] = jnp.concatenate(tables, axis=1)
+    return seat, pieces, [x[COUNT_ROW : COUNT_ROW + 1] for x in tables]
+
+
+def fill_rows(pieces, counts, fits):
     first, second = pieces
-    first_count, second_count = (x[COUNT_ROW : COUNT_ROW + 1] for x in tables)
-    most = jnp.max(first_count + second_count, axis=1, keepdims=True)
-    fits = most <= float(2 * short)
+    fan = first.shape[0]
+    short = short_rows(fan)
     limit = jnp.where(fits, float(short), float(fan))
     row = lax.broadcasted_iota(I32, (fan, LANES), 0).astype(F32)
-    mine = row < second_count
-    over = [first[2 * short - 1 - r : 2 * short - r] if 0 <= 2 * short - 1 - r < fan else first[:1] for r in range(fan)]
-    over = jnp.concatenate(over, axis=0)
-    spilled = jnp.logical_and(fits, 2.0 * short - 1.0 - row < first_count)
+    mine = row < counts[1]
+    over = [2 * short - 1 - r if 0 <= 2 * short - 1 - r < fan else 0 for r in range(fan)]
+    over = jnp.concatenate([first[r : r + 1] for r in over], axis=0)
+    spilled = jnp.logical_and(fits, 2.0 * short - 1.0 - row < counts[0])
     spilled = jnp.logical_and(spilled, row < float(short))
     spilled = jnp.logical_and(spilled, row >= float(2 * short - fan))
     spilled = jnp.logical_and(spilled, jnp.logical_not(mine))
-    first = jnp.where(row < jnp.minimum(first_count, limit), first, -1.0)
+    first = jnp.where(row < jnp.minimum(counts[0], limit), first, -1.0)
     second = jnp.where(mine, second, jnp.where(spilled, over, -1.0))
-    edges[b] = jnp.concatenate([first, second], axis=1)
-    owns[b] = jnp.where(spilled, 0.0, 1.0)
-    depth[b] = jnp.broadcast_to(limit, (PACK_ROWS, LANES))
-    seated[:, lo : lo + width] = jnp.concatenate(tables, axis=1)
-    return seat
+    return jnp.concatenate([first, second], axis=1), jnp.where(spilled, 0.0, 1.0)
 
 
 def by_depth(depth, fan, run):
-    shallow = jnp.max(depth) < float(short_rows(fan)) + 0.5
+    shallow = jnp.max(depth[...]) < float(short_rows(fan)) + 0.5
 
     @pl.when(shallow)
     def _():
@@ -121,11 +122,10 @@
 def locate_block(i, table, table_lo, seated, edges, own, lo, width, delta_out, basis_out, kinds_out, place_out):
     fan = edges.shape[0]
     spans = [
-        table[:, pl.ds(aligned(table_lo + k * LANES, LANES), LANES)]
-        for k in range(3 * width // LANES)
+        table[:, table_lo + p.start : table_lo + p.stop] for p in halves(3 * width)
     ]
     mine = own > 0.5
-    home = seated[:, pl.ds(lo, width)]
+    home = seated[:, lo : lo + width]
     parts = []
     for part in halves(width):
         rel = edges[:, part].astype(I32)
@@ -183,13 +183,12 @@
     return (feats.astype(F32) + silu_of_half(dot(mix_half, scaled))).astype(BF16)
 
 
-def first_block(rows, kinds, basis, own, seated, lo, width, weights, hid):
+def first_block(rows, kinds, hid, own, seated, lo, width, weights):
     embed_t, first, mix_half, spread = weights
     fan = kinds.shape[0]
     kinds_count = embed_t.shape[1]
     units = spread.shape[0] // fan
     species = first.shape[1] // units
-    fill_hidden(hid, spread, basis, rows, fan)
     kinds = kinds.astype(BF16)
     zero = jnp.zeros((), BF16)
     sums = Sums((mix_half.shape[0], width), own, rows, fan)
@@ -201,7 +200,7 @@
         ]
         sums.add(s, dot(first[...], jnp.concatenate(sorted_out, axis=0)))
     rows_of = lax.broadcasted_iota(I32, (kinds_count, width), 0).astype(F32)
-    same = rows_of == seated[SPECIES_ROW : SPECIES_ROW + 1, pl.ds(lo, width)]
+    same = rows_of == seated[SPECIES_ROW : SPECIES_ROW + 1, lo : lo + width]
     feats = dot(embed_t[...], jnp.where(same, 1.0, 0.0).astype(BF16))
     return update_of(feats, sums.done(), mix_half[...], fan)
 
@@ -245,24 +244,28 @@
     blocks = atoms // width
     index[...] = nbr[...].astype(F32)
     table[...] = pk[...]
-    for b in range(blocks):
-        seat = seat_block(b, pk, index, b * width, width, seated, edges, owns, depth)
+    found = [seat_block(pk, index, b * width, width, seated) for b in range(blocks)]
+    both = [counts[0] + counts[1] for _, _, counts in found]
+    most = functools.reduce(jnp.maximum, both)
+    fits = jnp.max(most, axis=1, keepdims=True) <= float(2 * short_rows(nbr.shape[0]))
+    depth[...] = jnp.where(
+        jnp.broadcast_to(fits, depth.shape), float(short_rows(nbr.shape[0])), float(nbr.shape[0])
+    )
+    for b, (seat, pieces, counts) in enumerate(found):
         table[SEAT_ROW : SEAT_ROW + 1, b * width : (b + 1) * width] = seat
+        edges[b], owns[b] = fill_rows(pieces, counts, fits)
     for part in halves(2 * width):
         wanted = jnp.broadcast_to(pk[SEND_ROW : SEND_ROW + 1, part].astype(I32), (PACK_ROWS, LANES))
         seats = lane_lookup([table[SEAT_ROW : SEAT_ROW + 1, p] for p in halves(atoms)], wanted)
         seats = seats + (wanted // width).astype(F32) * float(width)
         table[SEND_ROW : SEND_ROW + 1, part] = seats[:1]
 
-    def body(i, carry):
-        lo = aligned((i + 1) * width, width)
+    for i in range(blocks - 2):
+        lo = (i + 1) * width
         locate_block(
             i, table, lo - width, seated, edges[i + 1], owns[i + 1], lo, width,
             delta_out, basis_out, kinds_out, place_out,
         )
-        return carry
-
-    lax.fori_loop(0, blocks - 2, body, 0)
 
 
 def first_inner(width, ref_energy, pk, seated, owns, depth, basis, kinds, embed, rad_in, rad_out, mixing, w_in, feats_out, embed_t, first, spread, out_t, mix_half, w_row, ref_row, hid):
@@ -275,18 +278,15 @@
         energy = jnp.where(kinds_row == float(k), ref_energy[k], energy)
     ref_row[...] = energy
 
-    def body(i, carry):
-        lo = aligned((i + 1) * width, width)
-
-        def run(rows):
-            feats_out[:, pl.ds(aligned(i * width, width), width)] = first_block(
-                rows, kinds[i], basis[i], owns.at[i + 1], seated, lo, width, weights, hid
+    def run(rows):
+        for i in range(kinds.shape[0]):
+            fill_hidden(hid.at[i], spread.at[0], basis[i], rows, kinds.shape[1])
+        for i in range(kinds.shape[0]):
+            feats_out[:, i * width : (i + 1) * width] = first_block(
+                rows, kinds[i], hid.at[i], owns.at[i + 1], seated, (i + 1) * width, width, weights
             )
 
-        by_depth(depth[i + 1], kinds.shape[1], run)
-        return carry
-
-    lax.fori_loop(0, kinds.shape[0], body, 0)
+    by_depth(depth, kinds.shape[1], run)
 
 
 def pack_halo(feats, table, core, width, to_mate, to_cross):
@@ -307,12 +307,11 @@
     return aligned((1 - core) * top, width), aligned(core * top, width)
 
 
-def edge_block(i, blocks, width):
-    block = i * (blocks - 1)
-    return block, aligned(block * width, width)
-
-
-def first_outer(width, core_ref, pk, own_table, seated, mate, cross, edges, owns, depth, embed_t, first, spread, mix_half, inner, delta_out, basis_out, place_out, feats_out, to_mate, to_cross, pair_out, table, hid, kinds):
+def edge_blocks(blocks, width):
+    return [(0, 0, 0), (1, blocks - 1, (blocks - 1) * width)]
+
+
+def first_outer(width, core_ref, pk, own_table, seated, mate, cross, edges, owns, depth, embed_t, first, spread, mix_half, inner, delta_out, basis_out, place_out, feats_out, to_mate, to_cross, pair_out, table, kinds, hid):
     core = core_ref[0]
     atoms = pk.shape[1]
     blocks = atoms // width
@@ -333,22 +332,21 @@
     pair_out[0:4, :] = pk[0:4, :]
     pair_out[4:8, :] = mate[0:4, :]
 
-    def body(i, carry):
-        b, lo = edge_block(i, blocks, width)
+    for i, b, lo in edge_blocks(blocks, width):
         locate_block(
             i, table, lo, seated, edges[b], owns[b], lo, width,
             delta_out, basis_out, kinds, place_out,
         )
 
-        def run(rows):
-            feats_out[:, pl.ds(lo, width)] = first_block(
-                rows, kinds[i], basis_out[i], owns.at[b], seated, lo, width, weights, hid
+    def run(rows):
+        for i in range(2):
+            fill_hidden(hid.at[i], spread.at[0], basis_out[i], rows, fan)
+        for i, b, lo in edge_blocks(blocks, width):
+            feats_out[:, lo : lo + width] = first_block(
+                rows, kinds[i], hid.at[i], owns.at[b], seated, lo, width, weights
             )
 
-        by_depth(depth[b], fan, run)
-        return carry
-
-    lax.fori_loop(0, 2, body, 0)
+    by_depth(depth, fan, run)
     pack_halo(feats_out, own_table, core, width, to_mate, to_cross)
 
 
@@ -365,46 +363,41 @@
 
 def layer_block(rows, window, place, own, hid, out_t, mix_half, feats):
     fan, width = place.shape
-    units = out_t.shape[1]
     places = places_of(place, width)
     sums = Sums(feats.shape, own, rows, fan)
     for s in range(rows):
         far = fetch_rows(window, places, s, width)
-        sums.add(s, far * dot(out_t, hid[s * units : (s + 1) * units, :]))
+        sums.add(s, far * dot(out_t, hid(s)))
     return update_of(feats, sums.done(), mix_half, fan)
 
 
-def hidden_edges(depth, spread, basis, hid_edge, blocks, fan):
-    def body(i, carry):
-        by_depth(
-            depth[i * (blocks - 1)], fan,
-            lambda rows: fill_hidden(hid_edge.at[i], spread, basis[i], rows, fan),
-        )
-        return carry
-
-    lax.fori_loop(0, 2, body, 0)
+def stored(hid_edge, i, units):
+    return lambda s: hid_edge[i, s * units : (s + 1) * units, :]
+
+
+def hidden_edges(rows, spread, basis, hid_edge, fan):
+    for i in range(2):
+        fill_hidden(hid_edge.at[i], spread, basis[i], rows, fan)
 
 
 def layer_inner(width, layer, owns, depth, spreads, outs_t, mixes, feats, basis, place, basis_edge, pair, feats_out, hid_edge, pair_out, hid):
     spread, out_t, mix_half = spreads.at[layer], outs_t[layer], mixes[layer]
-    fan = place.shape[1]
+    units = out_t.shape[1]
     pair_out[...] = pair[...]
 
-    def body(i, carry):
-        lo = aligned((i + 1) * width, width)
-
-        def run(rows):
-            fill_hidden(hid, spread, basis[i], rows, fan)
-            feats_out[:, pl.ds(aligned(i * width, width), width)] = layer_block(
-                rows, feats[:, pl.ds(aligned(lo - width, width), 3 * width)], place[i],
-                owns.at[i + 1], hid, out_t, mix_half, feats[:, pl.ds(lo, width)],
+    def run(rows):
+        for i in range(place.shape[0]):
+            fill_hidden(hid.at[i], spread, basis[i], rows, place.shape[1])
+        for i in range(place.shape[0]):
+            lo = (i + 1) * width
+            feats_out[:, lo - width : lo] = layer_block(
+                rows, feats[:, lo - width : lo + 2 * width], place[i], owns.at[i + 1],
+                stored(hid, i, units), out_t, mix_half,
+                feats[:, lo : lo + width],
             )
-
-        by_depth(depth[i + 1], fan, run)
-        return carry
-
-    lax.fori_loop(0, place.shape[0], body, 0)
-    hidden_edges(depth, spread, basis_edge, hid_edge, place.shape[0] + 2, fan)
+        hidden_edges(rows, spread, basis_edge, hid_edge, place.shape[1])
+
+    by_depth(depth, place.shape[1], run)
 
 
 def fill_table(table, feats, mate, cross, core, width):
@@ -423,25 +416,20 @@
     fill_table(table, feats, mate, cross, core, width)
     feats_out[:, width : atoms - width] = inner[...]
 
-    def body(i, carry):
-        b, lo = edge_block(i, atoms // width, width)
-
-        def run(rows):
-            feats_out[:, pl.ds(lo, width)] = layer_block(
-                rows, table[:, pl.ds(lo, 3 * width)], place[i], owns.at[b],
-                hid_edge.at[i], out_t, mix_half, feats[:, pl.ds(lo, width)],
+    def run(rows):
+        for i, b, lo in edge_blocks(atoms // width, width):
+            feats_out[:, lo : lo + width] = layer_block(
+                rows, table[:, lo : lo + 3 * width], place[i], owns.at[b],
+                stored(hid_edge, i, out_t.shape[1]), out_t, mix_half, feats[:, lo : lo + width],
             )
 
-        by_depth(depth[b], fan, run)
-        return carry
-
-    lax.fori_loop(0, 2, body, 0)
+    by_depth(depth, fan, run)
     pack_halo(feats_out, own_table, core, width, to_mate, to_cross)
 
 
 def head_block(rows, window, place, own, hid, out_t, feats, delta, seat):
     fan, width = place.shape
-    chans, units = out_t.shape
+    chans = out_t.shape[0]
     places = places_of(place, width)
     near = feats.astype(F32)
     pairs = []
@@ -451,7 +439,7 @@
         if s >= 2 * rows - fan:
             lower = jnp.where(own[s : s + 1] > 0.5, near[:, LANES:], near[:, :LANES])
             here = jnp.concatenate([near[:, :LANES], lower], axis=1)
-        terms = far * (dot(out_t, hid[s * units : (s + 1) * units, :]) * here)
+        terms = far * (dot(out_t, hid(s)) * here)
         pairs.append(jnp.sum(terms, axis=0, keepdims=True))
     if rows < fan:
         pairs.append(jnp.zeros((fan - rows, width), F32))
@@ -485,24 +473,21 @@
 
 def head_inner(width, layer, own_table, owns, depth, spreads, outs_t, feats, basis, place, delta, basis_edge, force_out, hid_edge, hid):
     spread, out_t = spreads.at[layer], outs_t[layer]
-    fan = place.shape[1]
-
-    def body(i, carry):
-        lo = aligned((i + 1) * width, width)
-
-        def run(rows):
-            fill_hidden(hid, spread, basis[i], rows, fan)
-            force_out[:, pl.ds(aligned(i * width, width), width)] = head_block(
-                rows, feats[:, pl.ds(aligned(lo - width, width), 3 * width)], place[i],
-                owns.at[i + 1], hid, out_t, feats[:, pl.ds(lo, width)], delta.at[i],
-                own_table[SEAT_ROW : SEAT_ROW + 1, pl.ds(lo, width)],
+    units = out_t.shape[1]
+
+    def run(rows):
+        for i in range(place.shape[0]):
+            fill_hidden(hid.at[i], spread, basis[i], rows, place.shape[1])
+        for i in range(place.shape[0]):
+            lo = (i + 1) * width
+            force_out[:, lo - width : lo] = head_block(
+                rows, feats[:, lo - width : lo + 2 * width], place[i], owns.at[i + 1],
+                stored(hid, i, units), out_t, feats[:, lo : lo + width],
+                delta.at[i], own_table[SEAT_ROW : SEAT_ROW + 1, lo : lo + width],
             )
-
-        by_depth(depth[i + 1], fan, run)
-        return carry
-
-    lax.fori_loop(0, place.shape[0], body, 0)
-    hidden_edges(depth, spread, basis_edge, hid_edge, place.shape[0] + 2, fan)
+        hidden_edges(rows, spread, basis_edge, hid_edge, place.shape[1])
+
+    by_depth(depth, place.shape[1], run)
 
 
 def lane_sum(values):
@@ -520,20 +505,15 @@
     fill_table(table, feats, mate, cross, core, width)
     force_out[:, width : atoms - width] = inner[...]
 
-    def body(i, carry):
-        b, lo = edge_block(i, atoms // width, width)
-
-        def run(rows):
-            force_out[:, pl.ds(lo, width)] = head_block(
-                rows, table[:, pl.ds(lo, 3 * width)], place[i], owns.at[b],
-                hid_edge.at[i], out_t, feats[:, pl.ds(lo, width)], delta.at[i],
-                own_table[SEAT_ROW : SEAT_ROW + 1, pl.ds(lo, width)],
+    def run(rows):
+        for i, b, lo in edge_blocks(atoms // width, width):
+            force_out[:, lo : lo + width] = head_block(
+                rows, table[:, lo : lo + 3 * width], place[i], owns.at[b],
+                stored(hid_edge, i, out_t.shape[1]), out_t, feats[:, lo : lo + width],
+                delta.at[i], own_table[SEAT_ROW : SEAT_ROW + 1, lo : lo + width],
             )
 
-        by_depth(depth[b], fan, run)
-        return carry
-
-    lax.fori_loop(0, 2, body, 0)
+    by_depth(depth, fan, run)
     energy = dot(w_row[...], feats[...]) + ref_row[...]
     back = pk[0:4, :] - jnp.where(core == 0, relayed[0:4, :], received[4:8, :])
     fore = jnp.where(core == 0, received[4:8, :], relayed[0:4, :]) - pk[0:4, :]
@@ -629,7 +609,7 @@
     feats_type = ((chans, atoms), BF16)
     halo_type = ((chans, width), BF16)
     hid_type = ((2, fan * units, width), BF16)
-    hid_scratch = ((fan * units, width), BF16)
+    hid_scratch = ((blocks - 2, fan * units, width), BF16)
     table_scratch = [((chans, atoms + 2 * width), BF16)]
 
     def block_outs(count):
@@ -656,7 +636,7 @@
             pack_type,
             ((blocks, fan, width), F32),
             ((blocks, fan, LANES), F32),
-            ((blocks, PACK_ROWS, LANES), F32),
+            ((PACK_ROWS, LANES), F32),
         ]
         + block_outs(blocks - 2)[:2]
         + [kinds_type, kinds_type],
@@ -683,7 +663,7 @@
         functools.partial(first_outer, width),
         (core_arr, pk, own_table, seated, mate, cross, edges, owns, depth, embed_t, first, spread, mix_half, inner),
         block_outs(2) + [feats_type, halo_type, halo_type, pack_type],
-        [((PACK_ROWS, atoms + 2 * width), F32), hid_scratch, ((2, fan, width), F32)],
+        [((PACK_ROWS, atoms + 2 * width), F32), ((2, fan, width), F32), hid_type],
     )
     for layer in range(1, layers):
         mate = swap(to_mate, 0)

time: 39.6 us -> 36.9 us (0.932)
  Pallas kernels: 19.3 us -> 15.8 us
  waiting for transfers between devices: 3.87 us -> 5.33 us
  starting transfers between devices: 12.8 us -> 12.1 us
    pallas_call x9, Pallas kernels: 19.3 us -> 15.8 us  [call(): pl.pallas_call(body, out_shape=[jax.ShapeDtypeStruct(shape, dtype) for sh...]
    ppermute x9, waiting for transfers between devices: 2.7 us -> 4.18 us  [swap(): return lax.ppermute(block, 'atom', swap_pairs(tiles, offset))]
    ppermute x9, starting transfers between devices: 9.79 us -> 9.1 us  [swap(): return lax.ppermute(block, 'atom', swap_pairs(tiles, offset))]
  transfers between devices with their start and end apart: 12 -> 12, of which waited for: 5 -> 5; matrix products, arithmetic and copies ran while one was open for 0% -> 0% of each run, Pallas kernels for 33% -> 29%
where the time goes in v4:
time: 36.9 us; the launch traced here: 36.3 us
  Pallas kernels  15.8 us (43%)
  starting transfers between devices  12.1 us (33%)
  waiting for transfers between devices  5.33 us (14%)
  between operations  1.5 us (4%)
  local copies, waits for them, and re-layouts  1.36 us (4%)
    pallas_call x9, Pallas kernels, call(): pl.pallas_call(body, out_shape=[jax.ShapeDtypeStruct(shape, dtype) for sh...  15.8 us
    ppermute x9, starting transfers between devices, swap(): return lax.ppermute(block, 'atom', swap_pairs(tiles, offset))  9.1 us
    ppermute x9, waiting for transfers between devices, swap(): return lax.ppermute(block, 'atom', swap_pairs(tiles, offset))  4.18 us
    ppermute x1, starting transfers between devices, on_device(): far = lax.ppermute(both, 'atom', [(i, i ^ 4) for i in range(tiles)])  2.53 us
    unnamed x22, local copies, waits for them, and re-layouts  1.36 us
  transfers between devices with their start and end apart: 12, of which 5 were waited for; matrix products, arithmetic and copies ran while one was open for 0% of the time, Pallas kernels for 29%

profile of v4, /device:TPU:0, one launch (start us, length us, event | category | flops | bytes accessed | tf_op | source)
XLA Modules:
  0.0 36.3 jit_solution(7649988663632519175)
XLA Ops:
  0.7 0.0 copy-start.10
  0.7 0.6 %copy-done.8 = s32[1024]{0:T(1024)S(1)} copy-done((s32[1024]{0:T(1024)S(1)}, s32[1024]{0:T(1024)}, u32[]{:S(2)}) %copy-start.8) | copy-done | bytes 4120
  1.3 0.0 copy-done.9
  1.3 0.0 copy-done.10
  1.4 0.0 copy-done.7
  1.4 0.1 select_select_fusion.pk
  1.5 4.6 %collective-permute-start.1 = (f32[8,1024]{1,0:T(8,128)S(1)}, f32[8,1024]{1,0:T(8,128)S(1)}, u32[]{:S(2)}, u32[]{:S(2)}) collective-permute-start(f32[8,1024]{1,0:T(8,128)S(1)} %select_select_fusion.pk), channel_id=1, source_target_pairs={{1,2},{2,1},{3,4},{4,3},{5,6},{6,5},{7,0},{0,7},{9,10},{10,9},{11,... | collective-permute-start | bytes 98312 | tf_op jit(solution)/shard_map/ppermute | solution.py:606
  6.1 1.4 %shard_map.131 = (f32[8,1024]{1,0:T(8,128)S(1)}, f32[8,1024]{1,0:T(8,128)S(1)}, f32[4,16,256]{2,1,0:T(8,128)S(1)}, f32[4,16,128]{2,1,0:T(8,128)S(1)}, f32[8,128]...) custom-call(f32[8,1024]{1,0:T(8,128)S(1)} %select_select_fusion.pk, ...), custom_call_target="tpu_custom_call" | custom-call | flops 4294967296 | bytes 1048576 | tf_op jit(solution)/shard_map/pallas_call | solution.py:595
  7.5 0.6 %copy-done.3 = bf16[3,8,64]{2,1,0:T(8,128)(2,1)S(1)} copy-done((bf16[3,8,64]{2,1,0:T(8,128)(2,1)S(1)}, bf16[3,8,64]{2,1,0:T(8,128)(2,1)}, u32[]{:S(2)}) %copy-start.3) | copy-done | bytes 3096
  8.1 0.0 copy-done.4
  8.1 1.9 %shard_map.132 = (bf16[128,512]{1,0:T(8,128)(2,1)S(1)}, bf16[128,16]{1,0:T(8,128)(2,1)S(1)}, bf16[128,256]{1,0:T(8,128)(2,1)S(1)}, bf16[3,1024,128]{2,1,0:T(8,12...) custom-call(f32[4]{0:T(128)S(1)} %copy-done.5, ...), custom_call_target="tpu_custom_call" | custom-call | flops 4294967296 | bytes 1048576 | tf_op jit(solution)/shard_map/pallas_call | solution.py:595
  10.1 2.1 %shard_map.133 = (f32[2,48,256]{2,1,0:T(8,128)S(1)}, bf16[2,128,256]{2,1,0:T(8,128)(2,1)S(1)}, f32[2,16,256]{2,1,0:T(8,128)S(1)}, bf16[128,1024]{1,0:T(8,128)(2,...) custom-call(s32[1]{0:T(128)} %bitcast.1.core_ref, ...), custom_call_target="tpu_custom_call" | custom-call | bytes 1048576 | tf_op jit(solution)/shard_map/pallas_call | solution.py:595
  12.2 0.6 %collective-permute-start.4 = (bf16[128,256]{1,0:T(8,128)(2,1)S(1)}, bf16[128,256]{1,0:T(8,128)(2,1)S(1)}, u32[]{:S(2)}, u32[]{:S(2)}) collective-permute-start(bf16[128,256]{1,0:T(8,128)(2,1)S(1)} %get-tuple-element.60), channel_id=1, source_target_pairs={{0,1},{1,0},{2,3},{3,2},{4,5},{5,4},{6,7},{7,6},{8,9},{9,8},{10,11... | collective-permute-start | bytes 196616 | tf_op jit(solution)/shard_map/ppermute | solution.py:606
  12.8 0.8 %collective-permute-start.5 = (bf16[128,256]{1,0:T(8,128)(2,1)S(1)}, bf16[128,256]{1,0:T(8,128)(2,1)S(1)}, u32[]{:S(2)}, u32[]{:S(2)}) collective-permute-start(bf16[128,256]{1,0:T(8,128)(2,1)S(1)} %get-tuple-element.61), channel_id=1, source_target_pairs={{1,2},{2,1},{3,4},{4,3},{5,6},{6,5},{7,0},{0,7},{9,10},{10,9},{11,... | collective-permute-start | bytes 196616 | tf_op jit(solution)/shard_map/ppermute | solution.py:606
  13.5 2.5 %shard_map.134 = (bf16[128,512]{1,0:T(8,128)(2,1)S(1)}, bf16[2,1024,256]{2,1,0:T(8,128)(2,1)S(1)}, f32[8,1024]{1,0:T(8,128)S(1)}) custom-call(f32[4,16,128]{2,1,0:T(8,128)S(1)} %get-tuple-element.40.owns, f32[8,128]{1,0:T(8,128)S(1)} %get-tuple-element.41.depth, bf16[3,1024,128]{2,1,0:T(8,128)(2,1)S(1)} %get-tuple-element.45.spread.spreads, ...), custom_call_target="tpu_custom_call" | custom-call | bytes 1048576 | tf_op jit(solution)/shard_map/pallas_call | solution.py:595
  16.1 0.5 %collective-permute-start.2 = (f32[8,1024]{1,0:T(8,128)S(1)}, f32[8,1024]{1,0:T(8,128)S(1)}, u32[]{:S(2)}, u32[]{:S(2)}) collective-permute-start(f32[8,1024]{1,0:T(8,128)S(1)} %get-tuple-element.56), channel_id=1, source_target_pairs={{0,9},{9,0},{2,11},{11,2},{4,13},{13,4},{6,15},{15,6},{8,17},{17,8... | collective-permute-start | bytes 98312 | tf_op jit(solution)/shard_map/ppermute | solution.py:683
  16.6 1.7 %collective-permute-done.5.cross = bf16[128,256]{1,0:T(8,128)(2,1)S(1)} collective-permute-done((bf16[128,256]{1,0:T(8,128)(2,1)S(1)}, bf16[128,256]{1,0:T(8,128)(2,1)S(1)}, u32[]{:S(2)}, u32[]{:S(2)}) %collective-permute-start.5) | collective-permute-done | bytes 65568 | tf_op jit(solution)/shard_map/ppermute | solution.py:606
  18.3 2.3 %shard_map.135 = (bf16[128,1024]{1,0:T(8,128)(2,1)S(1)}, bf16[128,256]{1,0:T(8,128)(2,1)S(1)}, bf16[128,256]{1,0:T(8,128)(2,1)S(1)}) custom-call(s32[1]{0:T(128)} %bitcast.1.core_ref, f32[8,1024]{1,0:T(8,128)S(1)} %get-tuple-element.39.own_table, f32[4,16,128]{2,1,0:T(8,128)S(1)} %get-tuple-element.40.owns, f32[8,128]{1,0:T(8,128)S(1)} %get-tuple-element.41.depth, ...), custom_call_target="tpu_custom_call" | custom-call | bytes 1048576 | tf_op jit(solution)/shard_map/pallas_call | solution.py:595
  20.6 0.5 %collective-permute-start.6 = (bf16[128,256]{1,0:T(8,128)(2,1)S(1)}, bf16[128,256]{1,0:T(8,128)(2,1)S(1)}, u32[]{:S(2)}, u32[]{:S(2)}) collective-permute-start(bf16[128,256]{1,0:T(8,128)(2,1)S(1)} %get-tuple-element.66), channel_id=1, source_target_pairs={{0,1},{1,0},{2,3},{3,2},{4,5},{5,4},{6,7},{7,6},{8,9},{9,8},{10,11... | collective-permute-start | bytes 196616 | tf_op jit(solution)/shard_map/ppermute | solution.py:606
  21.1 1.8 %collective-permute-start.7 = (bf16[128,256]{1,0:T(8,128)(2,1)S(1)}, bf16[128,256]{1,0:T(8,128)(2,1)S(1)}, u32[]{:S(2)}, u32[]{:S(2)}) collective-permute-start(bf16[128,256]{1,0:T(8,128)(2,1)S(1)} %get-tuple-element.67), channel_id=1, source_target_pairs={{1,2},{2,1},{3,4},{4,3},{5,6},{6,5},{7,0},{0,7},{9,10},{10,9},{11,... | collective-permute-start | bytes 196616 | tf_op jit(solution)/shard_map/ppermute | solution.py:606
  23.0 2.3 %shard_map.136 = (f32[8,512]{1,0:T(8,128)S(1)}, bf16[2,1024,256]{2,1,0:T(8,128)(2,1)S(1)}) custom-call(f32[8,1024]{1,0:T(8,128)S(1)} %get-tuple-element.39.own_table, f32[4,16,128]{2,1,0:T(8,128)S(1)} %get-tuple-element.40.owns, f32[8,128]{1,0:T(8,128)S(1)} %get-tuple-element.41.depth, bf16[3,1024,128]{2,1,0:T(8,128)(2,1)S(1)} %get-tuple-element.45.spread.spreads, ...), custom_call_target="tpu_custom_call" | custom-call | bytes 1048576 | tf_op jit(solution)/shard_map/pallas_call | solution.py:595
  25.3 1.3 %collective-permute-done.7.cross = bf16[128,256]{1,0:T(8,128)(2,1)S(1)} collective-permute-done((bf16[128,256]{1,0:T(8,128)(2,1)S(1)}, bf16[128,256]{1,0:T(8,128)(2,1)S(1)}, u32[]{:S(2)}, u32[]{:S(2)}) %collective-permute-start.7) | collective-permute-done | bytes 65568 | tf_op jit(solution)/shard_map/ppermute | solution.py:606
  26.6 1.9 %shard_map.137 = (f32[8,1024]{1,0:T(8,128)S(1)}, f32[8,1024]{1,0:T(8,128)S(1)}, f32[8,128]{1,0:T(8,128)S(1)}) custom-call(s32[1]{0:T(128)} %bitcast.1.core_ref, f32[8,1024]{1,0:T(8,128)S(1)} %select_select_fusion.pk, f32[8,1024]{1,0:T(8,128)S(1)} %get-tuple-element.39.own_table, f32[8,1024]{1,0:T(8,128)S(1)} %collective-permute-done.2.received, ...), custom_call_target="tpu_custom_call" | custom-call | bytes 1048576 | tf_op jit(solution)/shard_map/pallas_call | solution.py:595
  28.5 0.1 collective-permute-start.8
  28.6 1.2 %collective-permute-done.8.other = f32[8,128]{1,0:T(8,128)S(1)} collective-permute-done((f32[8,128]{1,0:T(8,128)S(1)}, f32[8,128]{1,0:T(8,128)S(1)}, u32[]{:S(2)}, u32[]{:S(2)}) %collective-permute-start.8) | collective-permute-done | bytes 4128 | tf_op jit(solution)/shard_map/ppermute | solution.py:606
  30.4 2.5 %collective-permute-start.10 = (f32[8,128]{1,0:T(8,128)S(1)}, f32[8,128]{1,0:T(8,128)S(1)}, u32[]{:S(2)}, u32[]{:S(2)}) collective-permute-start(f32[8,128]{1,0:T(8,128)S(1)} %shard_map.138.rest_0_), channel_id=1, source_target_pairs={{0,4},{1,5},{2,6},{3,7},{4,0},{5,1},{6,2},{7,3},{8,12},{9,13},{10,... | collective-permute-start | bytes 12296 | tf_op jit(solution)/shard_map/ppermute | solution.py:705
  32.9 0.4 %collective-permute-done.9.rest_1_ = f32[8,128]{1,0:T(8,128)S(1)} collective-permute-done((f32[8,128]{1,0:T(8,128)S(1)}, f32[8,128]{1,0:T(8,128)S(1)}, u32[]{:S(2)}, u32[]{:S(2)}) %collective-permute-start.9) | collective-permute-done | bytes 4128 | tf_op jit(solution)/shard_map/ppermute | solution.py:704
  33.4 0.8 %collective-permute-start.11 = (f32[8,128]{1,0:T(8,128)S(1)}, f32[8,128]{1,0:T(8,128)S(1)}, u32[]{:S(2)}, u32[]{:S(2)}) collective-permute-start(f32[8,128]{1,0:T(8,128)S(1)} %collective-permute-done.9.rest_1_), channel_id=1, source_target_pairs={{0,1},{1,0},{2,3},{3,2},{4,5},{5,4},{6,7},{7,6},{8,9},{9,8},{10,11... | collective-permute-start | bytes 12296 | tf_op jit(solution)/shard_map/ppermute | solution.py:606
  34.2 0.1 pad_add_fusion.flags
  34.3 0.7 %collective-permute-done.10.rest_2_ = f32[8,128]{1,0:T(8,128)S(1)} collective-permute-done((f32[8,128]{1,0:T(8,128)S(1)}, f32[8,128]{1,0:T(8,128)S(1)}, u32[]{:S(2)}, u32[]{:S(2)}) %collective-permute-start.10) | collective-permute-done | bytes 4128 | tf_op jit(solution)/shard_map/ppermute | solution.py:705
  35.0 0.0 collective-permute-done.11.rest_3_
  35.0 1.3 %shard_map.139 = (f32[3,1,1024]{2,1,0:T(1,128)}, f32[1,1]{1,0:T(1,128)}) custom-call(s32[2]{0:T(128)S(1)} %pad_add_fusion.flags, f32[8,1024]{1,0:T(8,128)S(1)} %get-tuple-element.71.band, f32[8,1024]{1,0:T(8,128)S(1)} %get-tuple-element.72.force, f32[8,128]{1,0:T(8,128)S(1)} %shard_map.138.rest_0_, f32[8,128]{1,0:T(8,128)S(1)} %collective-permute-done.9.rest_1_, ...), custom_call_target="tpu_custom_call" | custom-call | bytes 1048576 | tf_op jit(solution)/shard_map/pallas_call | solution.py:595
  (32 shorter events, 0.1 us)
Async XLA Ops:
  0.6 0.7 %copy-start.8 = (s32[1024]{0:T(1024)S(1)}, s32[1024]{0:T(1024)}, u32[]{:S(2)}) copy-start(s32[1024]{0:T(1024)} %param.13) | copy-start | bytes 12292
  0.7 0.7 %copy-start.9 = (s32[1024]{0:T(1024)S(1)}, s32[1024]{0:T(1024)}, u32[]{:S(2)}) copy-start(s32[1024]{0:T(1024)} %param.14) | copy-start | bytes 12292
  0.7 0.7 %copy-start.10 = (s32[512]{0:T(512)S(1)}, s32[512]{0:T(512)}, u32[]{:S(2)}) copy-start(s32[512]{0:T(512)} %param.16) | copy-start | bytes 6148
  0.7 0.7 %copy-start.7 = (f32[1,3,1024]{2,0,1:T(1,128)S(1)}, f32[1,3,1024]{2,0,1:T(1,128)}, u32[]{:S(2)}) copy-start(f32[1,3,1024]{2,0,1:T(1,128)} %param.12) | copy-start | bytes 36868
  1.3 4.8 %copy-start = (s32[16,1024]{1,0:T(8,128)S(1)}, s32[16,1024]{1,0:T(8,128)}, u32[]{:S(2)}) copy-start(s32[16,1024]{1,0:T(8,128)} %nbr.1) | copy-start | bytes 196612
  1.5 6.0 %copy-start.1 = (bf16[2,128,128]{2,1,0:T(8,128)(2,1)S(1)}, bf16[2,128,128]{2,1,0:T(8,128)(2,1)}, u32[]{:S(2)}) copy-start(bf16[2,128,128]{2,1,0:T(8,128)(2,1)} %mixing.1) | copy-start | bytes 196612
  1.5 6.0 %copy-start.2 = (bf16[3,64,128]{2,1,0:T(8,128)(2,1)S(1)}, bf16[3,64,128]{2,1,0:T(8,128)(2,1)}, u32[]{:S(2)}) copy-start(bf16[3,64,128]{2,1,0:T(8,128)(2,1)} %rad_out.1) | copy-start | bytes 147460
  1.5 8.6 %collective-permute-start.1 = (f32[8,1024]{1,0:T(8,128)S(1)}, f32[8,1024]{1,0:T(8,128)S(1)}, u32[]{:S(2)}, u32[]{:S(2)}) collective-permute-start(f32[8,1024]{1,0:T(8,128)S(1)} %select_select_fusion.pk), channel_id=1, source_target_pairs={{1,2},{2,1},{3,4},{4,3},{5,6},{6,5},{7,0},{0,7},{9,10},{10,9},{11,... | collective-permute-start | bytes 98312 | tf_op jit(solution)/shard_map/ppermute | solution.py:606
  6.1 4.0 %collective-permute-start = (f32[8,1024]{1,0:T(8,128)S(1)}, f32[8,1024]{1,0:T(8,128)S(1)}, u32[]{:S(2)}, u32[]{:S(2)}) collective-permute-start(f32[8,1024]{1,0:T(8,128)S(1)} %select_select_fusion.pk), channel_id=1, source_target_pairs={{0,1},{1,0},{2,3},{3,2},{4,5},{5,4},{6,7},{7,6},{8,9},{9,8},{10,11... | collective-permute-start | bytes 98312 | tf_op jit(solution)/shard_map/ppermute | solution.py:606
  6.1 1.4 %copy-start.6 = (bf16[128]{0:T(256)(128)(2,1)S(1)}, bf16[128]{0:T(256)(128)(2,1)}, u32[]{:S(2)}) copy-start(bf16[128]{0:T(256)(128)(2,1)} %param.23) | copy-start | bytes 772
  7.4 0.7 %copy-start.3 = (bf16[3,8,64]{2,1,0:T(8,128)(2,1)S(1)}, bf16[3,8,64]{2,1,0:T(8,128)(2,1)}, u32[]{:S(2)}) copy-start(bf16[3,8,64]{2,1,0:T(8,128)(2,1)} %rad_in.1) | copy-start | bytes 9220
  7.5 0.7 %copy-start.4 = (bf16[4,128]{1,0:T(4,128)(2,1)S(1)}, bf16[4,128]{1,0:T(4,128)(2,1)}, u32[]{:S(2)}) copy-start(bf16[4,128]{1,0:T(4,128)(2,1)} %embed.1) | copy-start | bytes 3076
  7.5 0.7 %copy-start.5 = (f32[4]{0:T(128)S(1)}, f32[4]{0:T(128)}, u32[]{:S(2)}) copy-start(f32[4]{0:T(128)} %ref_energy.1) | copy-start | bytes 52
  12.2 4.4 %collective-permute-start.4 = (bf16[128,256]{1,0:T(8,128)(2,1)S(1)}, bf16[128,256]{1,0:T(8,128)(2,1)S(1)}, u32[]{:S(2)}, u32[]{:S(2)}) collective-permute-start(bf16[128,256]{1,0:T(8,128)(2,1)S(1)} %get-tuple-element.60), channel_id=1, source_target_pairs={{0,1},{1,0},{2,3},{3,2},{4,5},{5,4},{6,7},{7,6},{8,9},{9,8},{10,11... | collective-permute-start | bytes 196616 | tf_op jit(solution)/shard_map/ppermute | solution.py:606
  12.8 5.5 %collective-permute-start.5 = (bf16[128,256]{1,0:T(8,128)(2,1)S(1)}, bf16[128,256]{1,0:T(8,128)(2,1)S(1)}, u32[]{:S(2)}, u32[]{:S(2)}) collective-permute-start(bf16[128,256]{1,0:T(8,128)(2,1)S(1)} %get-tuple-element.61), channel_id=1, source_target_pairs={{1,2},{2,1},{3,4},{4,3},{5,6},{6,5},{7,0},{0,7},{9,10},{10,9},{11,... | collective-permute-start | bytes 196616 | tf_op jit(solution)/shard_map/ppermute | solution.py:606
  16.1 6.9 %collective-permute-start.2 = (f32[8,1024]{1,0:T(8,128)S(1)}, f32[8,1024]{1,0:T(8,128)S(1)}, u32[]{:S(2)}, u32[]{:S(2)}) collective-permute-start(f32[8,1024]{1,0:T(8,128)S(1)} %get-tuple-element.56), channel_id=1, source_target_pairs={{0,9},{9,0},{2,11},{11,2},{4,13},{13,4},{6,15},{15,6},{8,17},{17,8... | collective-permute-start | bytes 98312 | tf_op jit(solution)/shard_map/ppermute | solution.py:683
  20.6 4.7 %collective-permute-start.6 = (bf16[128,256]{1,0:T(8,128)(2,1)S(1)}, bf16[128,256]{1,0:T(8,128)(2,1)S(1)}, u32[]{:S(2)}, u32[]{:S(2)}) collective-permute-start(bf16[128,256]{1,0:T(8,128)(2,1)S(1)} %get-tuple-element.66), channel_id=1, source_target_pairs={{0,1},{1,0},{2,3},{3,2},{4,5},{5,4},{6,7},{7,6},{8,9},{9,8},{10,11... | collective-permute-start | bytes 196616 | tf_op jit(solution)/shard_map/ppermute | solution.py:606
  21.1 5.5 %collective-permute-start.7 = (bf16[128,256]{1,0:T(8,128)(2,1)S(1)}, bf16[128,256]{1,0:T(8,128)(2,1)S(1)}, u32[]{:S(2)}, u32[]{:S(2)}) collective-permute-start(bf16[128,256]{1,0:T(8,128)(2,1)S(1)} %get-tuple-element.67), channel_id=1, source_target_pairs={{1,2},{2,1},{3,4},{4,3},{5,6},{6,5},{7,0},{0,7},{9,10},{10,9},{11,... | collective-permute-start | bytes 196616 | tf_op jit(solution)/shard_map/ppermute | solution.py:606
  23.0 2.3 %collective-permute-start.3 = (f32[8,1024]{1,0:T(8,128)S(1)}, f32[8,1024]{1,0:T(8,128)S(1)}, u32[]{:S(2)}, u32[]{:S(2)}) collective-permute-start(f32[8,1024]{1,0:T(8,128)S(1)} %collective-permute-done.2.received), channel_id=1, source_target_pairs={{0,1},{1,0},{2,3},{3,2},{4,5},{5,4},{6,7},{7,6},{8,9},{9,8},{10,11... | collective-permute-start | bytes 98312 | tf_op jit(solution)/shard_map/ppermute | solution.py:606
  28.5 1.2 %collective-permute-start.8 = (f32[8,128]{1,0:T(8,128)S(1)}, f32[8,128]{1,0:T(8,128)S(1)}, u32[]{:S(2)}, u32[]{:S(2)}) collective-permute-start(f32[8,128]{1,0:T(8,128)S(1)} %get-tuple-element.73.mine), channel_id=1, source_target_pairs={{0,1},{1,0},{2,3},{3,2},{4,5},{5,4},{6,7},{7,6},{8,9},{9,8},{10,11... | collective-permute-start | bytes 12296 | tf_op jit(solution)/shard_map/ppermute | solution.py:606
  29.8 3.6 %collective-permute-start.9 = (f32[8,128]{1,0:T(8,128)S(1)}, f32[8,128]{1,0:T(8,128)S(1)}, u32[]{:S(2)}, u32[]{:S(2)}) collective-permute-start(f32[8,128]{1,0:T(8,128)S(1)} %shard_map.138.rest_0_), channel_id=1, source_target_pairs={{0,2},{1,7},{2,0},{3,5},{4,6},{5,3},{6,4},{7,1},{8,10},{9,15},{10,... | collective-permute-start | bytes 12296 | tf_op jit(solution)/shard_map/ppermute | solution.py:704
  30.4 4.6 %collective-permute-start.10 = (f32[8,128]{1,0:T(8,128)S(1)}, f32[8,128]{1,0:T(8,128)S(1)}, u32[]{:S(2)}, u32[]{:S(2)}) collective-permute-start(f32[8,128]{1,0:T(8,128)S(1)} %shard_map.138.rest_0_), channel_id=1, source_target_pairs={{0,4},{1,5},{2,6},{3,7},{4,0},{5,1},{6,2},{7,3},{8,12},{9,13},{10,... | collective-permute-start | bytes 12296 | tf_op jit(solution)/shard_map/ppermute | solution.py:705
  33.4 1.6 %collective-permute-start.11 = (f32[8,128]{1,0:T(8,128)S(1)}, f32[8,128]{1,0:T(8,128)S(1)}, u32[]{:S(2)}, u32[]{:S(2)}) collective-permute-start(f32[8,128]{1,0:T(8,128)S(1)} %collective-permute-done.9.rest_1_), channel_id=1, source_target_pairs={{0,1},{1,0},{2,3},{3,2},{4,5},{5,4},{6,7},{7,6},{8,9},{9,8},{10,11... | collective-permute-start | bytes 12296 | tf_op jit(solution)/shard_map/ppermute | solution.py:606

commit v5 on v4

--- a/solution.py
+++ b/solution.py
@@ -55,6 +55,10 @@
 
 def lane_lookup(windows, index):
     return lane_fetch(windows, index // LANES, index & (LANES - 1))
+
+
+def blank(out):
+    out[...] = jnp.zeros(out.shape, F32)
 
 
 def seat_atoms(pk, lo, width, most):
@@ -163,9 +167,9 @@
 
 
 class Sums:
-    def __init__(self, shape, own, rows, fan):
-        self.total = jnp.zeros(shape, F32)
-        self.lent = jnp.zeros((shape[0], LANES), F32)
+    def __init__(self, shape, own, rows, fan, total=None, lent=None):
+        self.total = jnp.zeros(shape, F32) if total is None else total
+        self.lent = jnp.zeros((shape[0], LANES), F32) if lent is None else lent
         self.own, self.alone = own, 2 * rows - fan
 
     def add(self, s, terms):
@@ -277,7 +281,6 @@
     for k in range(ref_energy.shape[0]):
         energy = jnp.where(kinds_row == float(k), ref_energy[k], energy)
     ref_row[...] = energy
-
     def run(rows):
         for i in range(kinds.shape[0]):
             fill_hidden(hid.at[i], spread.at[0], basis[i], rows, kinds.shape[1])
@@ -350,8 +353,8 @@
     pack_halo(feats_out, own_table, core, width, to_mate, to_cross)
 
 
-def places_of(place, width):
-    return [jnp.clip(place - float(k * width), -1.0, float(width)).astype(BF16) for k in range(3)]
+def places_of(place, width, tiles=(0, 1, 2)):
+    return [jnp.clip(place - float(k * width), -1.0, float(width)).astype(BF16) for k in tiles]
 
 
 def fetch_rows(window, places, s, width):
@@ -375,75 +378,82 @@
     return lambda s: hid_edge[i, s * units : (s + 1) * units, :]
 
 
-def hidden_edges(rows, spread, basis, hid_edge, fan):
-    for i in range(2):
-        fill_hidden(hid_edge.at[i], spread, basis[i], rows, fan)
-
-
-def layer_inner(width, layer, owns, depth, spreads, outs_t, mixes, feats, basis, place, basis_edge, pair, feats_out, hid_edge, pair_out, hid):
+def layer_inner(width, layer, owns, depth, spreads, outs_t, mixes, feats, basis, place, basis_edge, place_edge, pair, feats_out, field_edge, total_edge, lent_edge, pair_out, hid):
+    pair_out[...] = pair[...]
     spread, out_t, mix_half = spreads.at[layer], outs_t[layer], mixes[layer]
     units = out_t.shape[1]
-    pair_out[...] = pair[...]
+    fan = place.shape[1]
+    inner = place.shape[0]
 
     def run(rows):
-        for i in range(place.shape[0]):
-            fill_hidden(hid.at[i], spread, basis[i], rows, place.shape[1])
-        for i in range(place.shape[0]):
+        for i in range(inner):
+            fill_hidden(hid.at[i], spread, basis[i], rows, fan)
+        for i in range(2):
+            fill_hidden(hid.at[inner + i], spread, basis_edge[i], rows, fan)
+        for i in range(inner):
             lo = (i + 1) * width
             feats_out[:, lo - width : lo] = layer_block(
                 rows, feats[:, lo - width : lo + 2 * width], place[i], owns.at[i + 1],
-                stored(hid, i, units), out_t, mix_half,
-                feats[:, lo : lo + width],
+                stored(hid, i, units), out_t, mix_half, feats[:, lo : lo + width],
             )
-        hidden_edges(rows, spread, basis_edge, hid_edge, place.shape[1])
-
-    by_depth(depth, place.shape[1], run)
-
-
-def fill_table(table, feats, mate, cross, core, width):
-    atoms = feats.shape[1]
-    at_mate, at_cross = halo_places(core, atoms, width)
-    table[:, width : width + atoms] = feats[...]
-    table[:, pl.ds(at_mate, width)] = mate[...]
-    table[:, pl.ds(at_cross, width)] = cross[...]
-
-
-def layer_outer(width, layer, core_ref, own_table, owns, depth, outs_t, mixes, feats, place, mate, cross, hid_edge, inner, feats_out, to_mate, to_cross, table):
+        for i, b, lo in edge_blocks(inner + 2, width):
+            near = max(lo - width, 0)
+            window = feats[:, near : near + 2 * width]
+            places = places_of(place_edge[i], width, (0, 1) if i else (1, 2))
+            sums = Sums(total_edge.shape[1:], owns.at[b], rows, fan)
+            for s in range(rows):
+                field = dot(out_t, stored(hid, inner + i, units)(s))
+                field_edge[i, s] = field
+                sums.add(s, fetch_rows(window, places, s, width) * field)
+            total_edge[i] = sums.total
+            lent_edge[i] = sums.lent
+
+    by_depth(depth, fan, run)
+
+
+def halo_of(i, core, mate, cross):
+    lower_by_mate = core == (0 if i else 1)
+    return jnp.where(lower_by_mate, mate[...], cross[...])
+
+
+def layer_outer(width, layer, core_ref, own_table, owns, depth, mixes, feats, place, mate, cross, field_edge, total_edge, lent_edge, inner, feats_out, to_mate, to_cross):
     core = core_ref[0]
     atoms = feats.shape[1]
     fan = place.shape[1]
-    out_t, mix_half = outs_t[layer], mixes[layer]
-    fill_table(table, feats, mate, cross, core, width)
+    mix_half = mixes[layer]
     feats_out[:, width : atoms - width] = inner[...]
 
     def run(rows):
         for i, b, lo in edge_blocks(atoms // width, width):
-            feats_out[:, lo : lo + width] = layer_block(
-                rows, table[:, lo : lo + 3 * width], place[i], owns.at[b],
-                stored(hid_edge, i, out_t.shape[1]), out_t, mix_half, feats[:, lo : lo + width],
+            halo = halo_of(i, core, mate, cross)
+            places = places_of(place[i], width, (2,) if i else (0,))
+            sums = Sums(None, owns.at[b], rows, fan, total_edge[i], lent_edge[i])
+            for s in range(rows):
+                sums.add(s, fetch_rows(halo, places, s, width) * field_edge[i, s])
+            feats_out[:, lo : lo + width] = update_of(
+                feats[:, lo : lo + width], sums.done(), mix_half, fan
             )
 
     by_depth(depth, fan, run)
     pack_halo(feats_out, own_table, core, width, to_mate, to_cross)
 
 
-def head_block(rows, window, place, own, hid, out_t, feats, delta, seat):
-    fan, width = place.shape
-    chans = out_t.shape[0]
-    places = places_of(place, width)
-    near = feats.astype(F32)
-    pairs = []
-    for s in range(rows):
-        far = fetch_rows(window, places, s, width)
-        here = near
-        if s >= 2 * rows - fan:
-            lower = jnp.where(own[s : s + 1] > 0.5, near[:, LANES:], near[:, :LANES])
-            here = jnp.concatenate([near[:, :LANES], lower], axis=1)
-        terms = far * (dot(out_t, hid(s)) * here)
-        pairs.append(jnp.sum(terms, axis=0, keepdims=True))
-    if rows < fan:
-        pairs.append(jnp.zeros((fan - rows, width), F32))
-    pair = jnp.concatenate(pairs, axis=0) * (1.0 / math.sqrt(chans))
+def near_of(near, own, s, alone):
+    if s < alone:
+        return near
+    lower = jnp.where(own[s : s + 1] > 0.5, near[:, LANES:], near[:, :LANES])
+    return jnp.concatenate([near[:, :LANES], lower], axis=1)
+
+
+def filled(pairs, fan):
+    if len(pairs) < fan:
+        pairs.append(jnp.zeros((fan - len(pairs), pairs[0].shape[1]), F32))
+    return jnp.concatenate(pairs, axis=0)
+
+
+def force_of(pair, own, delta, seat, chans):
+    fan, width = pair.shape
+    pair = pair * (1.0 / math.sqrt(chans))
     mine = own[...] > 0.5
     out = []
     for c in range(3):
@@ -471,23 +481,48 @@
     )
 
 
-def head_inner(width, layer, own_table, owns, depth, spreads, outs_t, feats, basis, place, delta, basis_edge, force_out, hid_edge, hid):
+def head_inner(width, layer, own_table, owns, depth, spreads, outs_t, feats, basis, place, delta, basis_edge, place_edge, force_out, field_edge, pair_edge, hid):
     spread, out_t = spreads.at[layer], outs_t[layer]
-    units = out_t.shape[1]
+    chans, units = out_t.shape
+    fan = place.shape[1]
+    inner = place.shape[0]
 
     def run(rows):
-        for i in range(place.shape[0]):
-            fill_hidden(hid.at[i], spread, basis[i], rows, place.shape[1])
-        for i in range(place.shape[0]):
+        for i in range(inner):
+            fill_hidden(hid.at[i], spread, basis[i], rows, fan)
+        for i in range(2):
+            fill_hidden(hid.at[inner + i], spread, basis_edge[i], rows, fan)
+        alone = 2 * rows - fan
+        for i in range(inner):
             lo = (i + 1) * width
-            force_out[:, lo - width : lo] = head_block(
-                rows, feats[:, lo - width : lo + 2 * width], place[i], owns.at[i + 1],
-                stored(hid, i, units), out_t, feats[:, lo : lo + width],
-                delta.at[i], own_table[SEAT_ROW : SEAT_ROW + 1, lo : lo + width],
+            window = feats[:, lo - width : lo + 2 * width]
+            near = feats[:, lo : lo + width].astype(F32)
+            places = places_of(place[i], width)
+            pairs = []
+            for s in range(rows):
+                field = dot(out_t, stored(hid, i, units)(s))
+                field = field * near_of(near, owns.at[i + 1], s, alone)
+                terms = fetch_rows(window, places, s, width) * field
+                pairs.append(jnp.sum(terms, axis=0, keepdims=True))
+            force_out[:, lo - width : lo] = force_of(
+                filled(pairs, fan), owns.at[i + 1], delta.at[i],
+                own_table[SEAT_ROW : SEAT_ROW + 1, lo : lo + width], chans,
             )
-        hidden_edges(rows, spread, basis_edge, hid_edge, place.shape[1])
-
-    by_depth(depth, place.shape[1], run)
+        for i, b, lo in edge_blocks(inner + 2, width):
+            start = max(lo - width, 0)
+            window = feats[:, start : start + 2 * width]
+            near = feats[:, lo : lo + width].astype(F32)
+            places = places_of(place_edge[i], width, (0, 1) if i else (1, 2))
+            pairs = []
+            for s in range(rows):
+                field = dot(out_t, stored(hid, inner + i, units)(s))
+                field = field * near_of(near, owns.at[b], s, alone)
+                field_edge[i, s] = field
+                terms = fetch_rows(window, places, s, width) * field
+                pairs.append(jnp.sum(terms, axis=0, keepdims=True))
+            pair_edge[i] = filled(pairs, fan)
+
+    by_depth(depth, fan, run)
 
 
 def lane_sum(values):
@@ -497,29 +532,41 @@
     return jnp.sum(total, axis=0, keepdims=True)
 
 
-def head_outer(width, layer, core_ref, pk, own_table, received, relayed, owns, depth, outs_t, w_row, ref_row, feats, place, delta, mate, cross, hid_edge, inner, force_out, band_out, sums_out, table):
+def head_outer(width, core_ref, own_table, owns, depth, place, delta, mate, cross, field_edge, pair_edge, inner, force_out):
     core = core_ref[0]
-    atoms = feats.shape[1]
+    chans = mate.shape[0]
+    atoms = own_table.shape[1]
     fan = place.shape[1]
-    out_t = outs_t[layer]
-    fill_table(table, feats, mate, cross, core, width)
     force_out[:, width : atoms - width] = inner[...]
 
     def run(rows):
         for i, b, lo in edge_blocks(atoms // width, width):
-            force_out[:, lo : lo + width] = head_block(
-                rows, table[:, lo : lo + 3 * width], place[i], owns.at[b],
-                stored(hid_edge, i, out_t.shape[1]), out_t, feats[:, lo : lo + width],
-                delta.at[i], own_table[SEAT_ROW : SEAT_ROW + 1, lo : lo + width],
+            halo = halo_of(i, core, mate, cross)
+            places = places_of(place[i], width, (2,) if i else (0,))
+            pairs = []
+            for s in range(rows):
+                terms = fetch_rows(halo, places, s, width) * field_edge[i, s]
+                pairs.append(jnp.sum(terms, axis=0, keepdims=True))
+            force_out[:, lo : lo + width] = force_of(
+                pair_edge[i] + filled(pairs, fan), owns.at[b], delta.at[i],
+                own_table[SEAT_ROW : SEAT_ROW + 1, lo : lo + width], chans,
             )
 
     by_depth(depth, fan, run)
+
+
+def pass_on(received, _, out):
+    out[...] = received[...]
+
+
+def tail(core_ref, pk, received, relayed, w_row, ref_row, feats, force_in, band_out, sums_out):
+    core = core_ref[0]
     energy = dot(w_row[...], feats[...]) + ref_row[...]
     back = pk[0:4, :] - jnp.where(core == 0, relayed[0:4, :], received[4:8, :])
     fore = jnp.where(core == 0, received[4:8, :], relayed[0:4, :]) - pk[0:4, :]
     band_out[0:4, :] = back
     band_out[4:8, :] = fore
-    back, fore, force = back[:3], fore[:3], force_out[0:3, :]
+    back, fore, force = back[:3], fore[:3], force_in[0:3, :]
     rows = [energy, back * back, fore * fore, back * fore, force * back, force * fore]
     sums = [lane_sum(row) for row in rows]
     sums.append(jnp.zeros((SUM_ROWS - len(sums), LANES), F32))
@@ -599,7 +646,7 @@
             out_specs=[VMEM] * len(outs),
             scratch_shapes=[pltpu.VMEM(*x) for x in scratch],
             cost_estimate=pl.CostEstimate(flops=flops, bytes_accessed=2**20, transcendentals=0),
-            compiler_params=pltpu.CompilerParams(vmem_limit_bytes=40 * 2**20),
+            compiler_params=pltpu.CompilerParams(vmem_limit_bytes=16 * 2**20),
         )(*operands)
 
     def swap(block, offset):
@@ -610,7 +657,6 @@
     halo_type = ((chans, width), BF16)
     hid_type = ((2, fan * units, width), BF16)
     hid_scratch = ((blocks - 2, fan * units, width), BF16)
-    table_scratch = [((chans, atoms + 2 * width), BF16)]
 
     def block_outs(count):
         return [
@@ -621,7 +667,7 @@
 
     row = lax.broadcasted_iota(I32, (PACK_ROWS, atoms), 0)
     sends = jnp.pad(send_list, (0, atoms - 2 * width))
-    pk = jnp.zeros((PACK_ROWS, atoms), F32)
+    (pk,) = call(blank, (), [pack_type], flops=2**33)
     lines = [positions[0, c] for c in range(3)] + [species, counts, sends]
     for place, line in enumerate(lines):
         pk = jnp.where(row == place, lax.broadcast_in_dim(line, pk.shape, (1,)).astype(F32), pk)
@@ -666,35 +712,48 @@
         [((PACK_ROWS, atoms + 2 * width), F32), ((2, fan, width), F32), hid_type],
     )
     for layer in range(1, layers):
+        cross = swap(to_cross, 1)
         mate = swap(to_mate, 0)
-        cross = swap(to_cross, 1)
-        inner, hid_edge, pair = call(
+        inner, field_edge, total_edge, lent_edge, pair = call(
             functools.partial(layer_inner, width, layer),
-            (owns, depth, spread, out_t, mix_half, feats, basis_in, place_in, basis_out, pair),
-            [((chans, inner_atoms), BF16), hid_type, pack_type],
-            [hid_scratch],
+            (owns, depth, spread, out_t, mix_half, feats, basis_in, place_in, basis_out, place_out, pair),
+            [
+                ((chans, inner_atoms), BF16),
+                ((2, fan, chans, width), F32),
+                ((2, chans, width), F32),
+                ((2, chans, LANES), F32),
+                pack_type,
+            ],
+            [((blocks, fan * units, width), BF16)],
+            flops=2**32,
         )
         feats, to_mate, to_cross = call(
             functools.partial(layer_outer, width, layer),
-            (core_arr, own_table, owns, depth, out_t, mix_half, feats, place_out, mate, cross, hid_edge, inner),
+            (core_arr, own_table, owns, depth, mix_half, feats, place_out, mate, cross, field_edge, total_edge, lent_edge, inner),
             [feats_type, halo_type, halo_type],
-            table_scratch,
         )
     received = lax.ppermute(pair, ("img", "atom"), image_pairs(images, tiles))
-    relayed = swap(received, 0)
+    cross = swap(to_cross, 1)
     mate = swap(to_mate, 0)
-    cross = swap(to_cross, 1)
-    inner, hid_edge = call(
+    inner, field_edge, pair_edge = call(
         functools.partial(head_inner, width, layers),
-        (own_table, owns, depth, spread, out_t, feats, basis_in, place_in, delta_in, basis_out),
-        [((PACK_ROWS, inner_atoms), F32), hid_type],
-        [hid_scratch],
-    )
-    force, band, sums = call(
-        functools.partial(head_outer, width, layers),
-        (core_arr, pk, own_table, received, relayed, owns, depth, out_t, w_row, ref_row, feats, place_out, delta_out, mate, cross, hid_edge, inner),
-        [pack_type, pack_type, ((SUM_ROWS, LANES), F32)],
-        table_scratch,
+        (own_table, owns, depth, spread, out_t, feats, basis_in, place_in, delta_in, basis_out, place_out),
+        [((PACK_ROWS, inner_atoms), F32), ((2, fan, chans, width), F32), ((2, fan, width), F32)],
+        [((blocks, fan * units, width), BF16)],
+        flops=2**32,
+    )
+    (late,) = call(pass_on, (received, inner), [pack_type])
+    relayed = swap(late, 0)
+    (force,) = call(
+        functools.partial(head_outer, width),
+        (core_arr, own_table, owns, depth, place_out, delta_out, mate, cross, field_edge, pair_edge, inner),
+        [pack_type],
+        flops=2**32,
+    )
+    band, sums = call(
+        tail,
+        (core_arr, pk, received, relayed, w_row, ref_row, feats, force),
+        [pack_type, ((SUM_ROWS, LANES), F32)],
     )
     step = 2 * REDUCE_CHIPS
     while step < tiles:

time: 36.9 us -> 36 us (0.976)
  waiting for transfers between devices: 5.33 us -> 3.56 us
  starting transfers between devices: 12.1 us -> 13.4 us
  local copies, waits for them, and re-layouts: 1.36 us -> 0.74 us
    ppermute x9, waiting for transfers between devices: 4.18 us -> 2.39 us  [swap(): return lax.ppermute(block, 'atom', swap_pairs(tiles, offset))]
    ppermute x9, starting transfers between devices: 9.1 us -> 10.8 us  [swap(): return lax.ppermute(block, 'atom', swap_pairs(tiles, offset))]
    unnamed x22, local copies, waits for them, and re-layouts: 1.36 us -> 0.73 us
    ppermute x1, starting transfers between devices: 0.51 us -> 0.07 us  [on_device(): received = lax.ppermute(pair, ('img', 'atom'), image_pairs(images, tiles))]
    pallas_call x9 -> x12, Pallas kernels: 15.8 us -> 16 us  [call(): pl.pallas_call(body, out_shape=[jax.ShapeDtypeStruct(shape, dtype) for sh...]
  transfers between devices with their start and end apart: 12 -> 12, of which waited for: 5 -> 5; matrix products, arithmetic and copies ran while one was open for 0% -> 0% of each run, Pallas kernels for 29% -> 35%
where the time goes in v5:
time: 36 us; the launch traced here: 35.5 us
  Pallas kernels  16 us (44%)
  starting transfers between devices  13.4 us (37%)
  waiting for transfers between devices  3.56 us (10%)
  between operations  1.58 us (4%)
  local copies, waits for them, and re-layouts  0.74 us (2%)
    pallas_call x12, Pallas kernels, call(): pl.pallas_call(body, out_shape=[jax.ShapeDtypeStruct(shape, dtype) for sh...  16 us
    ppermute x9, starting transfers between devices, swap(): return lax.ppermute(block, 'atom', swap_pairs(tiles, offset))  10.8 us
    ppermute x1, starting transfers between devices, on_device(): far = lax.ppermute(both, 'atom', [(i, i ^ 4) for i in range(tiles)])  2.52 us
    ppermute x9, waiting for transfers between devices, swap(): return lax.ppermute(block, 'atom', swap_pairs(tiles, offset))  2.39 us
    ppermute x1, waiting for transfers between devices, on_device(): far = lax.ppermute(both, 'atom', [(i, i ^ 4) for i in range(tiles)])  0.77 us
    unnamed x22, local copies, waits for them, and re-layouts  0.73 us
  transfers between devices with their start and end apart: 12, of which 5 were waited for; matrix products, arithmetic and copies ran while one was open for 0% of the time, Pallas kernels for 35%

profile of v5, /device:TPU:0, one launch (start us, length us, event | category | flops | bytes accessed | tf_op | source)
XLA Modules:
  0.0 35.5 jit_solution(7420226855600238769)
XLA Ops:
  0.7 0.0 copy-start.8
  0.7 0.6 %copy-done.8 = s32[1024]{0:T(1024)S(1)} copy-done((s32[1024]{0:T(1024)S(1)}, s32[1024]{0:T(1024)}, u32[]{:S(2)}) %copy-start.8) | copy-done | bytes 4120
  1.4 0.0 copy-done.9
  1.4 0.0 copy-done.10
  1.4 0.0 copy-done.7
  1.4 0.1 select_select_fusion.pk
  1.6 4.6 %collective-permute-start.1 = (f32[8,1024]{1,0:T(8,128)S(1)}, f32[8,1024]{1,0:T(8,128)S(1)}, u32[]{:S(2)}, u32[]{:S(2)}) collective-permute-start(f32[8,1024]{1,0:T(8,128)S(1)} %select_select_fusion.pk), channel_id=1, source_target_pairs={{1,2},{2,1},{3,4},{4,3},{5,6},{6,5},{7,0},{0,7},{9,10},{10,9},{11,... | collective-permute-start | bytes 98312 | tf_op jit(solution)/shard_map/ppermute | solution.py:653
  6.1 1.4 %shard_map.132 = (f32[8,1024]{1,0:T(8,128)S(1)}, f32[8,1024]{1,0:T(8,128)S(1)}, f32[4,16,256]{2,1,0:T(8,128)S(1)}, f32[4,16,128]{2,1,0:T(8,128)S(1)}, f32[8,128]...) custom-call(f32[8,1024]{1,0:T(8,128)S(1)} %select_select_fusion.pk, ...), custom_call_target="tpu_custom_call" | custom-call | flops 4294967296 | bytes 1048576 | tf_op jit(solution)/shard_map/pallas_call | solution.py:642
  7.6 1.9 %shard_map.133 = (bf16[128,512]{1,0:T(8,128)(2,1)S(1)}, bf16[128,16]{1,0:T(8,128)(2,1)S(1)}, bf16[128,256]{1,0:T(8,128)(2,1)S(1)}, bf16[3,1024,128]{2,1,0:T(8,12...) custom-call(f32[4]{0:T(128)S(1)} %copy-done.5, ...), custom_call_target="tpu_custom_call" | custom-call | flops 4294967296 | bytes 1048576 | tf_op jit(solution)/shard_map/pallas_call | solution.py:642
  9.5 2.1 %shard_map.134 = (f32[2,48,256]{2,1,0:T(8,128)S(1)}, bf16[2,128,256]{2,1,0:T(8,128)(2,1)S(1)}, f32[2,16,256]{2,1,0:T(8,128)S(1)}, bf16[128,1024]{1,0:T(8,128)(2,...) custom-call(s32[1]{0:T(128)} %bitcast.1.core_ref, ...), custom_call_target="tpu_custom_call" | custom-call | bytes 1048576 | tf_op jit(solution)/shard_map/pallas_call | solution.py:642
  11.7 0.6 %collective-permute-start.3 = (bf16[128,256]{1,0:T(8,128)(2,1)S(1)}, bf16[128,256]{1,0:T(8,128)(2,1)S(1)}, u32[]{:S(2)}, u32[]{:S(2)}) collective-permute-start(bf16[128,256]{1,0:T(8,128)(2,1)S(1)} %get-tuple-element.60), channel_id=1, source_target_pairs={{0,1},{1,0},{2,3},{3,2},{4,5},{5,4},{6,7},{7,6},{8,9},{9,8},{10,11... | collective-permute-start | bytes 196616 | tf_op jit(solution)/shard_map/ppermute | solution.py:653
  12.2 1.3 %collective-permute-start.4 = (bf16[128,256]{1,0:T(8,128)(2,1)S(1)}, bf16[128,256]{1,0:T(8,128)(2,1)S(1)}, u32[]{:S(2)}, u32[]{:S(2)}) collective-permute-start(bf16[128,256]{1,0:T(8,128)(2,1)S(1)} %get-tuple-element.61), channel_id=1, source_target_pairs={{1,2},{2,1},{3,4},{4,3},{5,6},{6,5},{7,0},{0,7},{9,10},{10,9},{11,... | collective-permute-start | bytes 196616 | tf_op jit(solution)/shard_map/ppermute | solution.py:653
  13.5 3.6 %shard_map.135 = (bf16[128,512]{1,0:T(8,128)(2,1)S(1)}, f32[2,16,128,256]{3,2,1,0:T(8,128)S(1)}, f32[2,128,256]{2,1,0:T(8,128)S(1)}, f32[2,128,128]{2,1,0:T(8,128)S(1)}, f32[8,1024]{1,0:T(8,128)S(1)}) custom-call(f32[4,16,128]{2,1,0:T(8,128)S(1)} %get-tuple-element.41.owns, f32[8,128]{1,0:T(8,128)S(1)} %get-tuple-element.42.depth, ...), custom_call_target="tpu_custom_call" | custom-call | flops 4294967296 | bytes 1048576 | tf_op jit(solution)/shard_map/pallas_call | solution.py:642
  17.1 0.1 collective-permute-start.2
  17.2 0.5 %collective-permute-done.4.cross = bf16[128,256]{1,0:T(8,128)(2,1)S(1)} collective-permute-done((bf16[128,256]{1,0:T(8,128)(2,1)S(1)}, bf16[128,256]{1,0:T(8,128)(2,1)S(1)}, u32[]{:S(2)}, u32[]{:S(2)}) %collective-permute-start.4) | collective-permute-done | bytes 65568 | tf_op jit(solution)/shard_map/ppermute | solution.py:653
  17.7 1.3 %shard_map.136 = (bf16[128,1024]{1,0:T(8,128)(2,1)S(1)}, bf16[128,256]{1,0:T(8,128)(2,1)S(1)}, bf16[128,256]{1,0:T(8,128)(2,1)S(1)}) custom-call(s32[1]{0:T(128)} %bitcast.1.core_ref, f32[8,1024]{1,0:T(8,128)S(1)} %get-tuple-element.49.own_table, f32[4,16,128]{2,1,0:T(8,128)S(1)} %get-tuple-element.41.owns, f32[8,128]{1,0:T(8,128)S(1)} %get-tuple-element.42.depth, ...), custom_call_target="tpu_custom_call" | custom-call | bytes 1048576 | tf_op jit(solution)/shard_map/pallas_call | solution.py:642
  19.0 2.1 %collective-permute-start.6 = (bf16[128,256]{1,0:T(8,128)(2,1)S(1)}, bf16[128,256]{1,0:T(8,128)(2,1)S(1)}, u32[]{:S(2)}, u32[]{:S(2)}) collective-permute-start(bf16[128,256]{1,0:T(8,128)(2,1)S(1)} %get-tuple-element.72), channel_id=1, source_target_pairs={{0,1},{1,0},{2,3},{3,2},{4,5},{5,4},{6,7},{7,6},{8,9},{9,8},{10,11... | collective-permute-start | bytes 196616 | tf_op jit(solution)/shard_map/ppermute | solution.py:653
  21.2 1.3 %collective-permute-start.7 = (bf16[128,256]{1,0:T(8,128)(2,1)S(1)}, bf16[128,256]{1,0:T(8,128)(2,1)S(1)}, u32[]{:S(2)}, u32[]{:S(2)}) collective-permute-start(bf16[128,256]{1,0:T(8,128)(2,1)S(1)} %get-tuple-element.73), channel_id=1, source_target_pairs={{1,2},{2,1},{3,4},{4,3},{5,6},{6,5},{7,0},{0,7},{9,10},{10,9},{11,... | collective-permute-start | bytes 196616 | tf_op jit(solution)/shard_map/ppermute | solution.py:653
  22.5 3.3 %shard_map.137 = (f32[8,512]{1,0:T(8,128)S(1)}, f32[2,16,128,256]{3,2,1,0:T(8,128)S(1)}, f32[2,16,256]{2,1,0:T(8,128)S(1)}) custom-call(f32[8,1024]{1,0:T(8,128)S(1)} %get-tuple-element.49.own_table, f32[4,16,128]{2,1,0:T(8,128)S(1)} %get-tuple-element.41.owns, f32[8,128]{1,0:T(8,128)S(1)} %get-tuple-element.42.depth, ...), custom_call_target="tpu_custom_call" | custom-call | flops 4294967296 | bytes 1048576 | tf_op jit(solution)/shard_map/pallas_call | solution.py:642
  25.8 0.1 collective-permute-start.5
  25.9 0.7 %collective-permute-done.7.cross = bf16[128,256]{1,0:T(8,128)(2,1)S(1)} collective-permute-done((bf16[128,256]{1,0:T(8,128)(2,1)S(1)}, bf16[128,256]{1,0:T(8,128)(2,1)S(1)}, u32[]{:S(2)}, u32[]{:S(2)}) %collective-permute-start.7) | collective-permute-done | bytes 65568 | tf_op jit(solution)/shard_map/ppermute | solution.py:653
  26.7 0.8 %shard_map.139.force_in.force = f32[8,1024]{1,0:T(8,128)S(1)} custom-call(s32[1]{0:T(128)} %bitcast.1.core_ref, f32[8,1024]{1,0:T(8,128)S(1)} %get-tuple-element.49.own_table, f32[4,16,128]{2,1,0:T(8,128)S(1)} %get-tuple-element.41.owns, f32[8,128]{1,0:T(8,128)S(1)} %get-tuple-element.42.depth, f32[2,16,256]{2,1,0:T(8,128)S(1)} %get-tuple-element.57.place_edge.place, ...), custom_call_target="tpu_custom_call" | custom-call | flops 4294967296 | bytes 1048576 | tf_op jit(solution)/shard_map/pallas_call | solution.py:642
  27.5 0.2 shard_map.140
  27.6 0.1 collective-permute-start.8
  27.7 1.2 %collective-permute-done.8.other = f32[8,128]{1,0:T(8,128)S(1)} collective-permute-done((f32[8,128]{1,0:T(8,128)S(1)}, f32[8,128]{1,0:T(8,128)S(1)}, u32[]{:S(2)}, u32[]{:S(2)}) %collective-permute-start.8) | collective-permute-done | bytes 4128 | tf_op jit(solution)/shard_map/ppermute | solution.py:653
  28.9 0.0 collective-permute-start.9
  29.6 2.5 %collective-permute-start.10 = (f32[8,128]{1,0:T(8,128)S(1)}, f32[8,128]{1,0:T(8,128)S(1)}, u32[]{:S(2)}, u32[]{:S(2)}) collective-permute-start(f32[8,128]{1,0:T(8,128)S(1)} %shard_map.141.rest_0_), channel_id=1, source_target_pairs={{0,4},{1,5},{2,6},{3,7},{4,0},{5,1},{6,2},{7,3},{8,12},{9,13},{10,... | collective-permute-start | bytes 12296 | tf_op jit(solution)/shard_map/ppermute | solution.py:764
  32.1 0.4 %collective-permute-done.9.rest_1_ = f32[8,128]{1,0:T(8,128)S(1)} collective-permute-done((f32[8,128]{1,0:T(8,128)S(1)}, f32[8,128]{1,0:T(8,128)S(1)}, u32[]{:S(2)}, u32[]{:S(2)}) %collective-permute-start.9) | collective-permute-done | bytes 4128 | tf_op jit(solution)/shard_map/ppermute | solution.py:763
  32.5 0.8 %collective-permute-start.11 = (f32[8,128]{1,0:T(8,128)S(1)}, f32[8,128]{1,0:T(8,128)S(1)}, u32[]{:S(2)}, u32[]{:S(2)}) collective-permute-start(f32[8,128]{1,0:T(8,128)S(1)} %collective-permute-done.9.rest_1_), channel_id=1, source_target_pairs={{0,1},{1,0},{2,3},{3,2},{4,5},{5,4},{6,7},{7,6},{8,9},{9,8},{10,11... | collective-permute-start | bytes 12296 | tf_op jit(solution)/shard_map/ppermute | solution.py:653
  33.3 0.1 pad_add_fusion.flags
  33.4 0.8 %collective-permute-done.10.rest_2_ = f32[8,128]{1,0:T(8,128)S(1)} collective-permute-done((f32[8,128]{1,0:T(8,128)S(1)}, f32[8,128]{1,0:T(8,128)S(1)}, u32[]{:S(2)}, u32[]{:S(2)}) %collective-permute-start.10) | collective-permute-done | bytes 4128 | tf_op jit(solution)/shard_map/ppermute | solution.py:764
  34.1 1.3 %shard_map.142 = (f32[3,1,1024]{2,1,0:T(1,128)}, f32[1,1]{1,0:T(1,128)}) custom-call(s32[2]{0:T(128)S(1)} %pad_add_fusion.flags, f32[8,1024]{1,0:T(8,128)S(1)} %get-tuple-element.76.band, f32[8,1024]{1,0:T(8,128)S(1)} %shard_map.139.force_in.force, f32[8,128]{1,0:T(8,128)S(1)} %shard_map.141.rest_0_, f32[8,128]{1,0:T(8,128)S(1)} %collective-permute-done.9.rest_1_, ...), custom_call_target="tpu_custom_call" | custom-call | bytes 1048576 | tf_op jit(solution)/shard_map/pallas_call | solution.py:642
  (35 shorter events, 0.1 us)
Async XLA Ops:
  0.7 0.7 %copy-start.8 = (s32[1024]{0:T(1024)S(1)}, s32[1024]{0:T(1024)}, u32[]{:S(2)}) copy-start(s32[1024]{0:T(1024)} %param.13) | copy-start | bytes 12292
  0.7 0.7 %copy-start.9 = (s32[1024]{0:T(1024)S(1)}, s32[1024]{0:T(1024)}, u32[]{:S(2)}) copy-start(s32[1024]{0:T(1024)} %param.14) | copy-start | bytes 12292
  0.7 0.7 %copy-start.10 = (s32[512]{0:T(512)S(1)}, s32[512]{0:T(512)}, u32[]{:S(2)}) copy-start(s32[512]{0:T(512)} %param.16) | copy-start | bytes 6148
  0.7 0.7 %copy-start.7 = (f32[1,3,1024]{2,0,1:T(1,128)S(1)}, f32[1,3,1024]{2,0,1:T(1,128)}, u32[]{:S(2)}) copy-start(f32[1,3,1024]{2,0,1:T(1,128)} %param.12) | copy-start | bytes 36868
  0.7 5.4 %copy-start = (s32[16,1024]{1,0:T(8,128)S(1)}, s32[16,1024]{1,0:T(8,128)}, u32[]{:S(2)}) copy-start(s32[16,1024]{1,0:T(8,128)} %nbr.1) | copy-start | bytes 196612
  1.5 6.0 %copy-start.1 = (bf16[2,128,128]{2,1,0:T(8,128)(2,1)S(1)}, bf16[2,128,128]{2,1,0:T(8,128)(2,1)}, u32[]{:S(2)}) copy-start(bf16[2,128,128]{2,1,0:T(8,128)(2,1)} %mixing.1) | copy-start | bytes 196612
  1.5 6.0 %copy-start.2 = (bf16[3,64,128]{2,1,0:T(8,128)(2,1)S(1)}, bf16[3,64,128]{2,1,0:T(8,128)(2,1)}, u32[]{:S(2)}) copy-start(bf16[3,64,128]{2,1,0:T(8,128)(2,1)} %rad_out.1) | copy-start | bytes 147460
  1.5 6.0 %copy-start.3 = (bf16[3,8,64]{2,1,0:T(8,128)(2,1)S(1)}, bf16[3,8,64]{2,1,0:T(8,128)(2,1)}, u32[]{:S(2)}) copy-start(bf16[3,8,64]{2,1,0:T(8,128)(2,1)} %rad_in.1) | copy-start | bytes 9220
  1.5 6.0 %copy-start.4 = (bf16[4,128]{1,0:T(4,128)(2,1)S(1)}, bf16[4,128]{1,0:T(4,128)(2,1)}, u32[]{:S(2)}) copy-start(bf16[4,128]{1,0:T(4,128)(2,1)} %embed.1) | copy-start | bytes 3076
  1.6 6.0 %copy-start.5 = (f32[4]{0:T(128)S(1)}, f32[4]{0:T(128)}, u32[]{:S(2)}) copy-start(f32[4]{0:T(128)} %ref_energy.1) | copy-start | bytes 52
  1.6 6.0 %copy-start.6 = (bf16[128]{0:T(256)(128)(2,1)S(1)}, bf16[128]{0:T(256)(128)(2,1)}, u32[]{:S(2)}) copy-start(bf16[128]{0:T(256)(128)(2,1)} %param.23) | copy-start | bytes 772
  1.6 7.9 %collective-permute-start.1 = (f32[8,1024]{1,0:T(8,128)S(1)}, f32[8,1024]{1,0:T(8,128)S(1)}, u32[]{:S(2)}, u32[]{:S(2)}) collective-permute-start(f32[8,1024]{1,0:T(8,128)S(1)} %select_select_fusion.pk), channel_id=1, source_target_pairs={{1,2},{2,1},{3,4},{4,3},{5,6},{6,5},{7,0},{0,7},{9,10},{10,9},{11,... | collective-permute-start | bytes 98312 | tf_op jit(solution)/shard_map/ppermute | solution.py:653
  6.1 3.4 %collective-permute-start = (f32[8,1024]{1,0:T(8,128)S(1)}, f32[8,1024]{1,0:T(8,128)S(1)}, u32[]{:S(2)}, u32[]{:S(2)}) collective-permute-start(f32[8,1024]{1,0:T(8,128)S(1)} %select_select_fusion.pk), channel_id=1, source_target_pairs={{0,1},{1,0},{2,3},{3,2},{4,5},{5,4},{6,7},{7,6},{8,9},{9,8},{10,11... | collective-permute-start | bytes 98312 | tf_op jit(solution)/shard_map/ppermute | solution.py:653
  11.7 5.6 %collective-permute-start.3 = (bf16[128,256]{1,0:T(8,128)(2,1)S(1)}, bf16[128,256]{1,0:T(8,128)(2,1)S(1)}, u32[]{:S(2)}, u32[]{:S(2)}) collective-permute-start(bf16[128,256]{1,0:T(8,128)(2,1)S(1)} %get-tuple-element.60), channel_id=1, source_target_pairs={{0,1},{1,0},{2,3},{3,2},{4,5},{5,4},{6,7},{7,6},{8,9},{9,8},{10,11... | collective-permute-start | bytes 196616 | tf_op jit(solution)/shard_map/ppermute | solution.py:653
  12.2 5.5 %collective-permute-start.4 = (bf16[128,256]{1,0:T(8,128)(2,1)S(1)}, bf16[128,256]{1,0:T(8,128)(2,1)S(1)}, u32[]{:S(2)}, u32[]{:S(2)}) collective-permute-start(bf16[128,256]{1,0:T(8,128)(2,1)S(1)} %get-tuple-element.61), channel_id=1, source_target_pairs={{1,2},{2,1},{3,4},{4,3},{5,6},{6,5},{7,0},{0,7},{9,10},{10,9},{11,... | collective-permute-start | bytes 196616 | tf_op jit(solution)/shard_map/ppermute | solution.py:653
  17.1 8.7 %collective-permute-start.2 = (f32[8,1024]{1,0:T(8,128)S(1)}, f32[8,1024]{1,0:T(8,128)S(1)}, u32[]{:S(2)}, u32[]{:S(2)}) collective-permute-start(f32[8,1024]{1,0:T(8,128)S(1)} %get-tuple-element.59), channel_id=1, source_target_pairs={{0,9},{9,0},{2,11},{11,2},{4,13},{13,4},{6,15},{15,6},{8,17},{17,8... | collective-permute-start | bytes 98312 | tf_op jit(solution)/shard_map/ppermute | solution.py:735
  19.0 6.9 %collective-permute-start.6 = (bf16[128,256]{1,0:T(8,128)(2,1)S(1)}, bf16[128,256]{1,0:T(8,128)(2,1)S(1)}, u32[]{:S(2)}, u32[]{:S(2)}) collective-permute-start(bf16[128,256]{1,0:T(8,128)(2,1)S(1)} %get-tuple-element.72), channel_id=1, source_target_pairs={{0,1},{1,0},{2,3},{3,2},{4,5},{5,4},{6,7},{7,6},{8,9},{9,8},{10,11... | collective-permute-start | bytes 196616 | tf_op jit(solution)/shard_map/ppermute | solution.py:653
  21.2 5.5 %collective-permute-start.7 = (bf16[128,256]{1,0:T(8,128)(2,1)S(1)}, bf16[128,256]{1,0:T(8,128)(2,1)S(1)}, u32[]{:S(2)}, u32[]{:S(2)}) collective-permute-start(bf16[128,256]{1,0:T(8,128)(2,1)S(1)} %get-tuple-element.73), channel_id=1, source_target_pairs={{1,2},{2,1},{3,4},{4,3},{5,6},{6,5},{7,0},{0,7},{9,10},{10,9},{11,... | collective-permute-start | bytes 196616 | tf_op jit(solution)/shard_map/ppermute | solution.py:653
  25.8 1.6 %collective-permute-start.5 = (f32[8,1024]{1,0:T(8,128)S(1)}, f32[8,1024]{1,0:T(8,128)S(1)}, u32[]{:S(2)}, u32[]{:S(2)}) collective-permute-start(f32[8,1024]{1,0:T(8,128)S(1)} %shard_map.138), channel_id=1, source_target_pairs={{0,1},{1,0},{2,3},{3,2},{4,5},{5,4},{6,7},{7,6},{8,9},{9,8},{10,11... | collective-permute-start | bytes 98312 | tf_op jit(solution)/shard_map/ppermute | solution.py:653
  27.6 1.2 %collective-permute-start.8 = (f32[8,128]{1,0:T(8,128)S(1)}, f32[8,128]{1,0:T(8,128)S(1)}, u32[]{:S(2)}, u32[]{:S(2)}) collective-permute-start(f32[8,128]{1,0:T(8,128)S(1)} %get-tuple-element.77.mine), channel_id=1, source_target_pairs={{0,1},{1,0},{2,3},{3,2},{4,5},{5,4},{6,7},{7,6},{8,9},{9,8},{10,11... | collective-permute-start | bytes 12296 | tf_op jit(solution)/shard_map/ppermute | solution.py:653
  28.9 3.6 %collective-permute-start.9 = (f32[8,128]{1,0:T(8,128)S(1)}, f32[8,128]{1,0:T(8,128)S(1)}, u32[]{:S(2)}, u32[]{:S(2)}) collective-permute-start(f32[8,128]{1,0:T(8,128)S(1)} %shard_map.141.rest_0_), channel_id=1, source_target_pairs={{0,2},{1,7},{2,0},{3,5},{4,6},{5,3},{6,4},{7,1},{8,10},{9,15},{10,... | collective-permute-start | bytes 12296 | tf_op jit(solution)/shard_map/ppermute | solution.py:763
  29.6 4.6 %collective-permute-start.10 = (f32[8,128]{1,0:T(8,128)S(1)}, f32[8,128]{1,0:T(8,128)S(1)}, u32[]{:S(2)}, u32[]{:S(2)}) collective-permute-start(f32[8,128]{1,0:T(8,128)S(1)} %shard_map.141.rest_0_), channel_id=1, source_target_pairs={{0,4},{1,5},{2,6},{3,7},{4,0},{5,1},{6,2},{7,3},{8,12},{9,13},{10,... | collective-permute-start | bytes 12296 | tf_op jit(solution)/shard_map/ppermute | solution.py:764
  32.5 1.7 %collective-permute-start.11 = (f32[8,128]{1,0:T(8,128)S(1)}, f32[8,128]{1,0:T(8,128)S(1)}, u32[]{:S(2)}, u32[]{:S(2)}) collective-permute-start(f32[8,128]{1,0:T(8,128)S(1)} %collective-permute-done.9.rest_1_), channel_id=1, source_target_pairs={{0,1},{1,0},{2,3},{3,2},{4,5},{5,4},{6,7},{7,6},{8,9},{9,8},{10,11... | collective-permute-start | bytes 12296 | tf_op jit(solution)/shard_map/ppermute | solution.py:653

commit v6 on v5

--- a/solution.py
+++ b/solution.py
@@ -17,11 +17,15 @@
 COUNT_ROW = 4
 SEND_ROW = 5
 SEAT_ROW = 6
+CLIMB_ROW = 7
 PACK_ROWS = 8
 SUM_ROWS = 8
 REDUCE_CHIPS = 4
 VMEM = pl.BlockSpec(memory_space=pltpu.VMEM)
-SMEM = pl.BlockSpec(memory_space=pltpu.SMEM)
+
+
+def core_index():
+    return lax.rem(lax.axis_index("atom"), 2)
 
 
 def dot(a, b):
@@ -278,8 +282,8 @@
     w_row[...] = w_in[...]
     kinds_row = pk[SPECIES_ROW : SPECIES_ROW + 1, :]
     energy = jnp.zeros(kinds_row.shape, F32)
-    for k in range(ref_energy.shape[0]):
-        energy = jnp.where(kinds_row == float(k), ref_energy[k], energy)
+    for k in range(ref_energy.shape[1]):
+        energy = jnp.where(kinds_row == float(k), ref_energy[0:1, k : k + 1], energy)
     ref_row[...] = energy
     def run(rows):
         for i in range(kinds.shape[0]):
@@ -314,8 +318,8 @@
     return [(0, 0, 0), (1, blocks - 1, (blocks - 1) * width)]
 
 
-def first_outer(width, core_ref, pk, own_table, seated, mate, cross, edges, owns, depth, embed_t, first, spread, mix_half, inner, delta_out, basis_out, place_out, feats_out, to_mate, to_cross, pair_out, table, kinds, hid):
-    core = core_ref[0]
+def first_outer(width, pk, own_table, seated, mate, cross, edges, owns, depth, embed_t, first, spread, mix_half, inner, delta_out, basis_out, place_out, feats_out, to_mate, to_cross, pair_out, table, kinds, hid):
+    core = core_index()
     atoms = pk.shape[1]
     blocks = atoms // width
     fan = edges.shape[1]
@@ -416,8 +420,8 @@
     return jnp.where(lower_by_mate, mate[...], cross[...])
 
 
-def layer_outer(width, layer, core_ref, own_table, owns, depth, mixes, feats, place, mate, cross, field_edge, total_edge, lent_edge, inner, feats_out, to_mate, to_cross):
-    core = core_ref[0]
+def layer_outer(width, layer, own_table, owns, depth, mixes, feats, place, mate, cross, field_edge, total_edge, lent_edge, inner, feats_out, to_mate, to_cross):
+    core = core_index()
     atoms = feats.shape[1]
     fan = place.shape[1]
     mix_half = mixes[layer]
@@ -532,8 +536,8 @@
     return jnp.sum(total, axis=0, keepdims=True)
 
 
-def head_outer(width, core_ref, own_table, owns, depth, place, delta, mate, cross, field_edge, pair_edge, inner, force_out):
-    core = core_ref[0]
+def head_outer(width, own_table, owns, depth, place, delta, mate, cross, field_edge, pair_edge, inner, force_out):
+    core = core_index()
     chans = mate.shape[0]
     atoms = own_table.shape[1]
     fan = place.shape[1]
@@ -559,11 +563,13 @@
     out[...] = received[...]
 
 
-def tail(core_ref, pk, received, relayed, w_row, ref_row, feats, force_in, band_out, sums_out):
-    core = core_ref[0]
+def tail(pk, received, relayed, w_row, ref_row, feats, force_in, band_out, sums_out):
+    core = core_index()
     energy = dot(w_row[...], feats[...]) + ref_row[...]
-    back = pk[0:4, :] - jnp.where(core == 0, relayed[0:4, :], received[4:8, :])
-    fore = jnp.where(core == 0, received[4:8, :], relayed[0:4, :]) - pk[0:4, :]
+    direct, by_mate = received[0:4, :], relayed[4:8, :]
+    direct_ahead = lax.rem(core + lax.axis_index("img"), 2) == 0
+    back = pk[0:4, :] - jnp.where(direct_ahead, by_mate, direct)
+    fore = jnp.where(direct_ahead, direct, by_mate) - pk[0:4, :]
     band_out[0:4, :] = back
     band_out[4:8, :] = fore
     back, fore, force = back[:3], fore[:3], force_in[0:3, :]
@@ -577,7 +583,7 @@
     out[...] = mine[...] + other[...]
 
 
-def finish(count, flags, band, force, *rest):
+def finish(count, pk, band, force, *rest):
     *parts, result, energy_out = rest
     total = parts[0][...]
     for part in parts[1:]:
@@ -592,9 +598,9 @@
     )
     proj = (along_back * by_back + along_fore * by_fore) / tau_sq
     spring = SPRING * (fore_len - back_len) / jnp.sqrt(tau_sq)
-    climbing = flags[1] == 1
-    is_end = flags[0] == 1
-    factor = jnp.where(climbing, -2.0 * proj, spring - proj)
+    image = lax.axis_index("img")
+    is_end = jnp.logical_or(image == 0, image == lax.axis_size("img") - 1)
+    factor = jnp.where(pk[CLIMB_ROW : CLIMB_ROW + 1, 0:1] == 1.0, -2.0 * proj, spring - proj)
     tangent = band[0:3, :] * by_back + band[4:7, :] * by_fore
     moved = jnp.where(is_end, force[0:3, :], force[0:3, :] + factor * tangent)
     for c in range(3):
@@ -612,11 +618,8 @@
 
 def image_pairs(images, tiles):
     pairs = []
-    for low in range(images):
-        high = (low + 1) % images
-        for tile in range(0, tiles, 2):
-            a, b = low * tiles + tile, high * tiles + tile + 1
-            pairs += [(a, b), (b, a)]
+    for tile in range(tiles):
+        pairs += [(a * tiles + tile, b * tiles + tile) for a, b in swap_pairs(images, tile % 2)]
     return pairs
 
 
@@ -631,18 +634,11 @@
     inner_atoms = (blocks - 2) * width
     tiles = lax.axis_size("atom")
     images = lax.axis_size("img")
-    core = lax.rem(lax.axis_index("atom"), 2)
-    image = lax.axis_index("img")
-    core_arr = core.reshape(1).astype(I32)
-    is_end = jnp.logical_or(image == 0, image == images - 1)
-    flags = jnp.stack([is_end.astype(I32), climb[0]])
-
     def call(body, operands, outs, scratch=(), flops=0):
-        scalars = {id(x) for x in (core_arr, flags, ref_energy)}
         return pl.pallas_call(
             body,
             out_shape=[jax.ShapeDtypeStruct(shape, dtype) for shape, dtype in outs],
-            in_specs=[SMEM if id(x) in scalars else VMEM for x in operands],
+            in_specs=[VMEM] * len(operands),
             out_specs=[VMEM] * len(outs),
             scratch_shapes=[pltpu.VMEM(*x) for x in scratch],
             cost_estimate=pl.CostEstimate(flops=flops, bytes_accessed=2**20, transcendentals=0),
@@ -668,8 +664,8 @@
     row = lax.broadcasted_iota(I32, (PACK_ROWS, atoms), 0)
     sends = jnp.pad(send_list, (0, atoms - 2 * width))
     (pk,) = call(blank, (), [pack_type], flops=2**33)
-    lines = [positions[0, c] for c in range(3)] + [species, counts, sends]
-    for place, line in enumerate(lines):
+    lines = [positions[0, c] for c in range(3)] + [species, counts, sends, climb]
+    for place, line in zip((0, 1, 2, SPECIES_ROW, COUNT_ROW, SEND_ROW, CLIMB_ROW), lines):
         pk = jnp.where(row == place, lax.broadcast_in_dim(line, pk.shape, (1,)).astype(F32), pk)
     mate = swap(pk, 0)
     cross = swap(pk, 1)
@@ -691,7 +687,7 @@
     )
     inner, embed_t, first, spread, out_t, mix_half, w_row, ref_row = call(
         functools.partial(first_inner, width),
-        (ref_energy, pk, seated, owns, depth, basis_in, kinds_in, embed, rad_in, rad_out, mixing, w_energy[None]),
+        (ref_energy[None], pk, seated, owns, depth, basis_in, kinds_in, embed, rad_in, rad_out, mixing, w_energy[None]),
         [
             ((chans, inner_atoms), BF16),
             ((chans, -(-embed.shape[0] // 16) * 16), BF16),
@@ -707,7 +703,7 @@
     )
     delta_out, basis_out, place_out, feats, to_mate, to_cross, pair = call(
         functools.partial(first_outer, width),
-        (core_arr, pk, own_table, seated, mate, cross, edges, owns, depth, embed_t, first, spread, mix_half, inner),
+        (pk, own_table, seated, mate, cross, edges, owns, depth, embed_t, first, spread, mix_half, inner),
         block_outs(2) + [feats_type, halo_type, halo_type, pack_type],
         [((PACK_ROWS, atoms + 2 * width), F32), ((2, fan, width), F32), hid_type],
     )
@@ -729,7 +725,7 @@
         )
         feats, to_mate, to_cross = call(
             functools.partial(layer_outer, width, layer),
-            (core_arr, own_table, owns, depth, mix_half, feats, place_out, mate, cross, field_edge, total_edge, lent_edge, inner),
+            (own_table, owns, depth, mix_half, feats, place_out, mate, cross, field_edge, total_edge, lent_edge, inner),
             [feats_type, halo_type, halo_type],
         )
     received = lax.ppermute(pair, ("img", "atom"), image_pairs(images, tiles))
@@ -746,13 +742,13 @@
     relayed = swap(late, 0)
     (force,) = call(
         functools.partial(head_outer, width),
-        (core_arr, own_table, owns, depth, place_out, delta_out, mate, cross, field_edge, pair_edge, inner),
+        (own_table, owns, depth, place_out, delta_out, mate, cross, field_edge, pair_edge, inner),
         [pack_type],
         flops=2**32,
     )
     band, sums = call(
         tail,
-        (core_arr, pk, received, relayed, w_row, ref_row, feats, force),
+        (pk, received, relayed, w_row, ref_row, feats, force),
         [pack_type, ((SUM_ROWS, LANES), F32)],
     )
     step = 2 * REDUCE_CHIPS
@@ -765,7 +761,7 @@
     other = swap(near, 0)
     result, energy = call(
         functools.partial(finish, atoms * tiles),
-        (flags, band, force, both, near, far, other),
+        (pk, band, force, both, near, far, other),
         [((3, 1, atoms), F32), ((1, 1), F32)],
     )
     return jnp.transpose(result, (1, 0, 2)), energy.reshape(1)

time: 36 us -> 34.8 us (0.967); the launches traced: 35.5 us -> 34.6 us
  Pallas kernels: 16 us -> 14.8 us
  starting transfers between devices: 13.4 us -> 14.4 us
  local copies, waits for them, and re-layouts: 0.74 us -> 0.07 us
    ppermute x1, starting transfers between devices: 0.07 us -> 1.56 us  [on_device(): received = lax.ppermute(pair, ('img', 'atom'), image_pairs(images, tiles))]
    pallas_call x12, Pallas kernels: 16 us -> 14.8 us  [call(): pl.pallas_call(body, out_shape=[jax.ShapeDtypeStruct(shape, dtype) for sh...]
    ppermute x1, waiting for transfers between devices: 0.39 us -> 1.37 us  [on_device(): lax.ppermute(both, 'atom', [(i, i ^ 2 if i % 2 == 0 else i ^ 6) for i in...]
    ppermute x1, waiting for transfers between devices: 0.77 us -> 0.09 us  [on_device(): far = lax.ppermute(both, 'atom', [(i, i ^ 4) for i in range(tiles)])]
    unnamed x22, local copies, waits for them, and re-layouts: 0.73 us -> 0.07 us
  transfers between devices with their start and end apart: 12 -> 12, of which waited for: 5 -> 5; matrix products, arithmetic and copies ran while one was open for 0% -> 0% of each run, Pallas kernels for 35% -> 34%
where the time goes in v6:
time: 34.8 us; the launch traced here: 34.6 us
  Pallas kernels  14.8 us (43%)
  starting transfers between devices  14.4 us (41%)
  waiting for transfers between devices  3.63 us (10%)
  between operations  1.66 us (5%)
    pallas_call x12, Pallas kernels, call(): pl.pallas_call(body, out_shape=[jax.ShapeDtypeStruct(shape, dtype) for sh...  14.8 us
    ppermute x9, starting transfers between devices, swap(): return lax.ppermute(block, 'atom', swap_pairs(tiles, offset))  10.6 us
    ppermute x1, starting transfers between devices, on_device(): far = lax.ppermute(both, 'atom', [(i, i ^ 4) for i in range(tiles)])  2.23 us
    ppermute x9, waiting for transfers between devices, swap(): return lax.ppermute(block, 'atom', swap_pairs(tiles, offset))  2.17 us
    ppermute x1, starting transfers between devices, on_device(): received = lax.ppermute(pair, ('img', 'atom'), image_pairs(images, tiles))  1.56 us
    ppermute x1, waiting for transfers between devices, on_device(): lax.ppermute(both, 'atom', [(i, i ^ 2 if i % 2 == 0 else i ^ 6) for i in...  1.37 us
  transfers between devices with their start and end apart: 12, of which 5 were waited for; matrix products, arithmetic and copies ran while one was open for 0% of the time, Pallas kernels for 34%

profile of v6, /device:TPU:0, one launch (start us, length us, event | category | flops | bytes accessed | tf_op | source)
XLA Modules:
  0.0 34.6 jit_solution(16194900909816411764)
XLA Ops:
  0.7 0.0 copy-start.8
  0.7 0.0 copy-start.9
  0.7 0.0 copy-start.10
  0.7 0.0 copy-start.7
  1.5 0.1 select_select_fusion.pk
  1.6 0.0 copy-start.1
  1.6 0.0 copy-start.4
  1.7 0.0 copy-start.5
  1.7 4.6 %collective-permute-start.1 = (f32[8,1024]{1,0:T(8,128)S(1)}, f32[8,1024]{1,0:T(8,128)S(1)}, u32[]{:S(2)}, u32[]{:S(2)}) collective-permute-start(f32[8,1024]{1,0:T(8,128)S(1)} %select_select_fusion.pk), channel_id=1, source_target_pairs={{1,2},{2,1},{3,4},{4,3},{5,6},{6,5},{7,0},{0,7},{9,10},{10,9},{11,... | collective-permute-start | bytes 98312 | tf_op jit(solution)/shard_map/ppermute | solution.py:649
  6.2 1.4 %shard_map.132 = (f32[8,1024]{1,0:T(8,128)S(1)}, f32[8,1024]{1,0:T(8,128)S(1)}, f32[4,16,256]{2,1,0:T(8,128)S(1)}, f32[4,16,128]{2,1,0:T(8,128)S(1)}, f32[8,128]...) custom-call(f32[8,1024]{1,0:T(8,128)S(1)} %select_select_fusion.pk, ...), custom_call_target="tpu_custom_call" | custom-call | flops 4294967296 | bytes 1048576 | tf_op jit(solution)/shard_map/pallas_call | solution.py:638
  7.7 1.4 %shard_map.133 = (bf16[128,512]{1,0:T(8,128)(2,1)S(1)}, bf16[128,16]{1,0:T(8,128)(2,1)S(1)}, bf16[128,256]{1,0:T(8,128)(2,1)S(1)}, bf16[3,1024,128]{2,1,0:T(8,12...) custom-call(f32[1,4]{1,0:T(1,128)S(1)} %bitcast.8, ...), custom_call_target="tpu_custom_call" | custom-call | flops 4294967296 | bytes 1048576 | tf_op jit(solution)/shard_map/pallas_call | solution.py:638
  9.1 2.0 %shard_map.134 = (f32[2,48,256]{2,1,0:T(8,128)S(1)}, bf16[2,128,256]{2,1,0:T(8,128)(2,1)S(1)}, f32[2,16,256]{2,1,0:T(8,128)S(1)}, bf16[128,1024]{1,0:T(8,128)(2,...) custom-call(f32[8,1024]{1,0:T(8,128)S(1)} %select_select_fusion.pk, ...), custom_call_target="tpu_custom_call" | custom-call | bytes 1048576 | tf_op jit(solution)/shard_map/pallas_call | solution.py:638
  11.2 0.6 %collective-permute-start.3 = (bf16[128,256]{1,0:T(8,128)(2,1)S(1)}, bf16[128,256]{1,0:T(8,128)(2,1)S(1)}, u32[]{:S(2)}, u32[]{:S(2)}) collective-permute-start(bf16[128,256]{1,0:T(8,128)(2,1)S(1)} %get-tuple-element.60), channel_id=1, source_target_pairs={{0,1},{1,0},{2,3},{3,2},{4,5},{5,4},{6,7},{7,6},{8,9},{9,8},{10,11... | collective-permute-start | bytes 196616 | tf_op jit(solution)/shard_map/ppermute | solution.py:649
  11.7 1.8 %collective-permute-start.4 = (bf16[128,256]{1,0:T(8,128)(2,1)S(1)}, bf16[128,256]{1,0:T(8,128)(2,1)S(1)}, u32[]{:S(2)}, u32[]{:S(2)}) collective-permute-start(bf16[128,256]{1,0:T(8,128)(2,1)S(1)} %get-tuple-element.61), channel_id=1, source_target_pairs={{1,2},{2,1},{3,4},{4,3},{5,6},{6,5},{7,0},{0,7},{9,10},{10,9},{11,... | collective-permute-start | bytes 196616 | tf_op jit(solution)/shard_map/ppermute | solution.py:649
  13.6 3.6 %shard_map.135 = (bf16[128,512]{1,0:T(8,128)(2,1)S(1)}, f32[2,16,128,256]{3,2,1,0:T(8,128)S(1)}, f32[2,128,256]{2,1,0:T(8,128)S(1)}, f32[2,128,128]{2,1,0:T(8,128)S(1)}, f32[8,1024]{1,0:T(8,128)S(1)}) custom-call(f32[4,16,128]{2,1,0:T(8,128)S(1)} %get-tuple-element.41.owns, f32[8,128]{1,0:T(8,128)S(1)} %get-tuple-element.42.depth, ...), custom_call_target="tpu_custom_call" | custom-call | flops 4294967296 | bytes 1048576 | tf_op jit(solution)/shard_map/pallas_call | solution.py:638
  17.2 1.6 %collective-permute-start.2 = (f32[8,1024]{1,0:T(8,128)S(1)}, f32[8,1024]{1,0:T(8,128)S(1)}, u32[]{:S(2)}, u32[]{:S(2)}) collective-permute-start(f32[8,1024]{1,0:T(8,128)S(1)} %get-tuple-element.59), channel_id=1, source_target_pairs={{0,8},{8,0},{16,24},{24,16},{9,17},{17,9},{25,1},{1,25},{2,10},{10... | collective-permute-start | bytes 98312 | tf_op jit(solution)/shard_map/ppermute | solution.py:731
  18.7 1.3 %shard_map.136 = (bf16[128,1024]{1,0:T(8,128)(2,1)S(1)}, bf16[128,256]{1,0:T(8,128)(2,1)S(1)}, bf16[128,256]{1,0:T(8,128)(2,1)S(1)}) custom-call(f32[8,1024]{1,0:T(8,128)S(1)} %get-tuple-element.49.own_table, f32[4,16,128]{2,1,0:T(8,128)S(1)} %get-tuple-element.41.owns, f32[8,128]{1,0:T(8,128)S(1)} %get-tuple-element.42.depth, ...), custom_call_target="tpu_custom_call" | custom-call | bytes 1048576 | tf_op jit(solution)/shard_map/pallas_call | solution.py:638
  20.1 0.1 collective-permute-start.6
  20.2 2.4 %collective-permute-start.7 = (bf16[128,256]{1,0:T(8,128)(2,1)S(1)}, bf16[128,256]{1,0:T(8,128)(2,1)S(1)}, u32[]{:S(2)}, u32[]{:S(2)}) collective-permute-start(bf16[128,256]{1,0:T(8,128)(2,1)S(1)} %get-tuple-element.73), channel_id=1, source_target_pairs={{1,2},{2,1},{3,4},{4,3},{5,6},{6,5},{7,0},{0,7},{9,10},{10,9},{11,... | collective-permute-start | bytes 196616 | tf_op jit(solution)/shard_map/ppermute | solution.py:649
  22.6 3.3 %shard_map.137 = (f32[8,512]{1,0:T(8,128)S(1)}, f32[2,16,128,256]{3,2,1,0:T(8,128)S(1)}, f32[2,16,256]{2,1,0:T(8,128)S(1)}) custom-call(f32[8,1024]{1,0:T(8,128)S(1)} %get-tuple-element.49.own_table, f32[4,16,128]{2,1,0:T(8,128)S(1)} %get-tuple-element.41.owns, f32[8,128]{1,0:T(8,128)S(1)} %get-tuple-element.42.depth, ...), custom_call_target="tpu_custom_call" | custom-call | flops 4294967296 | bytes 1048576 | tf_op jit(solution)/shard_map/pallas_call | solution.py:638
  26.0 0.1 collective-permute-start.5
  26.1 0.8 %shard_map.139.force_in.force = f32[8,1024]{1,0:T(8,128)S(1)} custom-call(f32[8,1024]{1,0:T(8,128)S(1)} %get-tuple-element.49.own_table, f32[4,16,128]{2,1,0:T(8,128)S(1)} %get-tuple-element.41.owns, f32[8,128]{1,0:T(8,128)S(1)} %get-tuple-element.42.depth, f32[2,16,256]{2,1,0:T(8,128)S(1)} %get-tuple-element.57.place_edge.place, ...), custom_call_target="tpu_custom_call" | custom-call | flops 4294967296 | bytes 1048576 | tf_op jit(solution)/shard_map/pallas_call | solution.py:638
  26.8 0.4 %collective-permute-done.5.relayed = f32[8,1024]{1,0:T(8,128)S(1)} collective-permute-done((f32[8,1024]{1,0:T(8,128)S(1)}, f32[8,1024]{1,0:T(8,128)S(1)}, u32[]{:S(2)}, u32[]{:S(2)}) %collective-permute-start.5) | collective-permute-done | bytes 32800 | tf_op jit(solution)/shard_map/ppermute | solution.py:649
  27.3 0.2 shard_map.140
  27.4 0.2 collective-permute-start.8
  27.6 1.0 %collective-permute-done.8.other = f32[8,128]{1,0:T(8,128)S(1)} collective-permute-done((f32[8,128]{1,0:T(8,128)S(1)}, f32[8,128]{1,0:T(8,128)S(1)}, u32[]{:S(2)}, u32[]{:S(2)}) %collective-permute-start.8) | collective-permute-done | bytes 4128 | tf_op jit(solution)/shard_map/ppermute | solution.py:649
  28.6 2.2 %collective-permute-start.10 = (f32[8,128]{1,0:T(8,128)S(1)}, f32[8,128]{1,0:T(8,128)S(1)}, u32[]{:S(2)}, u32[]{:S(2)}) collective-permute-start(f32[8,128]{1,0:T(8,128)S(1)} %shard_map.141.rest_0_), channel_id=1, source_target_pairs={{0,4},{1,5},{2,6},{3,7},{4,0},{5,1},{6,2},{7,3},{8,12},{9,13},{10,... | collective-permute-start | bytes 12296 | tf_op jit(solution)/shard_map/ppermute | solution.py:760
  30.9 1.4 %collective-permute-done.9.rest_1_ = f32[8,128]{1,0:T(8,128)S(1)} collective-permute-done((f32[8,128]{1,0:T(8,128)S(1)}, f32[8,128]{1,0:T(8,128)S(1)}, u32[]{:S(2)}, u32[]{:S(2)}) %collective-permute-start.9) | collective-permute-done | bytes 4128 | tf_op jit(solution)/shard_map/ppermute | solution.py:759
  32.2 0.8 %collective-permute-start.11 = (f32[8,128]{1,0:T(8,128)S(1)}, f32[8,128]{1,0:T(8,128)S(1)}, u32[]{:S(2)}, u32[]{:S(2)}) collective-permute-start(f32[8,128]{1,0:T(8,128)S(1)} %collective-permute-done.9.rest_1_), channel_id=1, source_target_pairs={{0,1},{1,0},{2,3},{3,2},{4,5},{5,4},{6,7},{7,6},{8,9},{9,8},{10,11... | collective-permute-start | bytes 12296 | tf_op jit(solution)/shard_map/ppermute | solution.py:649
  33.1 0.1 collective-permute-done.10.rest_2_
  33.1 0.7 %collective-permute-done.11.rest_3_ = f32[8,128]{1,0:T(8,128)S(1)} collective-permute-done((f32[8,128]{1,0:T(8,128)S(1)}, f32[8,128]{1,0:T(8,128)S(1)}, u32[]{:S(2)}, u32[]{:S(2)}) %collective-permute-start.11) | collective-permute-done | bytes 4128 | tf_op jit(solution)/shard_map/ppermute | solution.py:649
  33.9 0.8 %shard_map.142 = (f32[3,1,1024]{2,1,0:T(1,128)}, f32[1,1]{1,0:T(1,128)}) custom-call(f32[8,1024]{1,0:T(8,128)S(1)} %select_select_fusion.pk, f32[8,1024]{1,0:T(8,128)S(1)} %get-tuple-element.76.band, f32[8,1024]{1,0:T(8,128)S(1)} %shard_map.139.force_in.force, f32[8,128]{1,0:T(8,128)S(1)} %shard_map.141.rest_0_, ...), custom_call_target="tpu_custom_call" | custom-call | bytes 1048576 | tf_op jit(solution)/shard_map/pallas_call | solution.py:638
  (35 shorter events, 0.1 us)
Async XLA Ops:
  0.7 0.8 %copy-start.8 = (s32[1024]{0:T(1024)S(1)}, s32[1024]{0:T(1024)}, u32[]{:S(2)}) copy-start(s32[1024]{0:T(1024)} %param.13) | copy-start | bytes 12292
  0.7 0.8 %copy-start.9 = (s32[1024]{0:T(1024)S(1)}, s32[1024]{0:T(1024)}, u32[]{:S(2)}) copy-start(s32[1024]{0:T(1024)} %param.14) | copy-start | bytes 12292
  0.7 0.8 %copy-start.10 = (s32[512]{0:T(512)S(1)}, s32[512]{0:T(512)}, u32[]{:S(2)}) copy-start(s32[512]{0:T(512)} %param.16) | copy-start | bytes 6148
  0.7 0.8 %copy-start.7 = (f32[1,3,1024]{2,0,1:T(1,128)S(1)}, f32[1,3,1024]{2,0,1:T(1,128)}, u32[]{:S(2)}) copy-start(f32[1,3,1024]{2,0,1:T(1,128)} %param.12) | copy-start | bytes 36868
  0.7 5.5 %copy-start = (s32[16,1024]{1,0:T(8,128)S(1)}, s32[16,1024]{1,0:T(8,128)}, u32[]{:S(2)}) copy-start(s32[16,1024]{1,0:T(8,128)} %nbr.1) | copy-start | bytes 196612
  1.6 6.0 %copy-start.1 = (bf16[2,128,128]{2,1,0:T(8,128)(2,1)S(1)}, bf16[2,128,128]{2,1,0:T(8,128)(2,1)}, u32[]{:S(2)}) copy-start(bf16[2,128,128]{2,1,0:T(8,128)(2,1)} %mixing.1) | copy-start | bytes 196612
  1.6 6.0 %copy-start.2 = (bf16[3,64,128]{2,1,0:T(8,128)(2,1)S(1)}, bf16[3,64,128]{2,1,0:T(8,128)(2,1)}, u32[]{:S(2)}) copy-start(bf16[3,64,128]{2,1,0:T(8,128)(2,1)} %rad_out.1) | copy-start | bytes 147460
  1.6 6.0 %copy-start.3 = (bf16[3,8,64]{2,1,0:T(8,128)(2,1)S(1)}, bf16[3,8,64]{2,1,0:T(8,128)(2,1)}, u32[]{:S(2)}) copy-start(bf16[3,8,64]{2,1,0:T(8,128)(2,1)} %rad_in.1) | copy-start | bytes 9220
  1.6 6.0 %copy-start.4 = (bf16[4,128]{1,0:T(4,128)(2,1)S(1)}, bf16[4,128]{1,0:T(4,128)(2,1)}, u32[]{:S(2)}) copy-start(bf16[4,128]{1,0:T(4,128)(2,1)} %embed.1) | copy-start | bytes 3076
  1.7 6.0 %copy-start.5 = (f32[4]{0:T(128)S(1)}, f32[4]{0:T(128)}, u32[]{:S(2)}) copy-start(f32[4]{0:T(128)} %param.19) | copy-start | bytes 52
  1.7 6.0 %copy-start.6 = (bf16[128]{0:T(256)(128)(2,1)S(1)}, bf16[128]{0:T(256)(128)(2,1)}, u32[]{:S(2)}) copy-start(bf16[128]{0:T(256)(128)(2,1)} %param.23) | copy-start | bytes 772
  1.7 7.4 %collective-permute-start.1 = (f32[8,1024]{1,0:T(8,128)S(1)}, f32[8,1024]{1,0:T(8,128)S(1)}, u32[]{:S(2)}, u32[]{:S(2)}) collective-permute-start(f32[8,1024]{1,0:T(8,128)S(1)} %select_select_fusion.pk), channel_id=1, source_target_pairs={{1,2},{2,1},{3,4},{4,3},{5,6},{6,5},{7,0},{0,7},{9,10},{10,9},{11,... | collective-permute-start | bytes 98312 | tf_op jit(solution)/shard_map/ppermute | solution.py:649
  6.2 2.9 %collective-permute-start = (f32[8,1024]{1,0:T(8,128)S(1)}, f32[8,1024]{1,0:T(8,128)S(1)}, u32[]{:S(2)}, u32[]{:S(2)}) collective-permute-start(f32[8,1024]{1,0:T(8,128)S(1)} %select_select_fusion.pk), channel_id=1, source_target_pairs={{0,1},{1,0},{2,3},{3,2},{4,5},{5,4},{6,7},{7,6},{8,9},{9,8},{10,11... | collective-permute-start | bytes 98312 | tf_op jit(solution)/shard_map/ppermute | solution.py:649
  11.2 7.6 %collective-permute-start.3 = (bf16[128,256]{1,0:T(8,128)(2,1)S(1)}, bf16[128,256]{1,0:T(8,128)(2,1)S(1)}, u32[]{:S(2)}, u32[]{:S(2)}) collective-permute-start(bf16[128,256]{1,0:T(8,128)(2,1)S(1)} %get-tuple-element.60), channel_id=1, source_target_pairs={{0,1},{1,0},{2,3},{3,2},{4,5},{5,4},{6,7},{7,6},{8,9},{9,8},{10,11... | collective-permute-start | bytes 196616 | tf_op jit(solution)/shard_map/ppermute | solution.py:649
  11.7 7.0 %collective-permute-start.4 = (bf16[128,256]{1,0:T(8,128)(2,1)S(1)}, bf16[128,256]{1,0:T(8,128)(2,1)S(1)}, u32[]{:S(2)}, u32[]{:S(2)}) collective-permute-start(bf16[128,256]{1,0:T(8,128)(2,1)S(1)} %get-tuple-element.61), channel_id=1, source_target_pairs={{1,2},{2,1},{3,4},{4,3},{5,6},{6,5},{7,0},{0,7},{9,10},{10,9},{11,... | collective-permute-start | bytes 196616 | tf_op jit(solution)/shard_map/ppermute | solution.py:649
  17.2 8.8 %collective-permute-start.2 = (f32[8,1024]{1,0:T(8,128)S(1)}, f32[8,1024]{1,0:T(8,128)S(1)}, u32[]{:S(2)}, u32[]{:S(2)}) collective-permute-start(f32[8,1024]{1,0:T(8,128)S(1)} %get-tuple-element.59), channel_id=1, source_target_pairs={{0,8},{8,0},{16,24},{24,16},{9,17},{17,9},{25,1},{1,25},{2,10},{10... | collective-permute-start | bytes 98312 | tf_op jit(solution)/shard_map/ppermute | solution.py:731
  20.1 6.0 %collective-permute-start.6 = (bf16[128,256]{1,0:T(8,128)(2,1)S(1)}, bf16[128,256]{1,0:T(8,128)(2,1)S(1)}, u32[]{:S(2)}, u32[]{:S(2)}) collective-permute-start(bf16[128,256]{1,0:T(8,128)(2,1)S(1)} %get-tuple-element.72), channel_id=1, source_target_pairs={{0,1},{1,0},{2,3},{3,2},{4,5},{5,4},{6,7},{7,6},{8,9},{9,8},{10,11... | collective-permute-start | bytes 196616 | tf_op jit(solution)/shard_map/ppermute | solution.py:649
  20.2 5.9 %collective-permute-start.7 = (bf16[128,256]{1,0:T(8,128)(2,1)S(1)}, bf16[128,256]{1,0:T(8,128)(2,1)S(1)}, u32[]{:S(2)}, u32[]{:S(2)}) collective-permute-start(bf16[128,256]{1,0:T(8,128)(2,1)S(1)} %get-tuple-element.73), channel_id=1, source_target_pairs={{1,2},{2,1},{3,4},{4,3},{5,6},{6,5},{7,0},{0,7},{9,10},{10,9},{11,... | collective-permute-start | bytes 196616 | tf_op jit(solution)/shard_map/ppermute | solution.py:649
  26.0 1.3 %collective-permute-start.5 = (f32[8,1024]{1,0:T(8,128)S(1)}, f32[8,1024]{1,0:T(8,128)S(1)}, u32[]{:S(2)}, u32[]{:S(2)}) collective-permute-start(f32[8,1024]{1,0:T(8,128)S(1)} %shard_map.138), channel_id=1, source_target_pairs={{0,1},{1,0},{2,3},{3,2},{4,5},{5,4},{6,7},{7,6},{8,9},{9,8},{10,11... | collective-permute-start | bytes 98312 | tf_op jit(solution)/shard_map/ppermute | solution.py:649
  27.4 1.2 %collective-permute-start.8 = (f32[8,128]{1,0:T(8,128)S(1)}, f32[8,128]{1,0:T(8,128)S(1)}, u32[]{:S(2)}, u32[]{:S(2)}) collective-permute-start(f32[8,128]{1,0:T(8,128)S(1)} %get-tuple-element.77.mine), channel_id=1, source_target_pairs={{0,1},{1,0},{2,3},{3,2},{4,5},{5,4},{6,7},{7,6},{8,9},{9,8},{10,11... | collective-permute-start | bytes 12296 | tf_op jit(solution)/shard_map/ppermute | solution.py:649
  28.6 3.6 %collective-permute-start.9 = (f32[8,128]{1,0:T(8,128)S(1)}, f32[8,128]{1,0:T(8,128)S(1)}, u32[]{:S(2)}, u32[]{:S(2)}) collective-permute-start(f32[8,128]{1,0:T(8,128)S(1)} %shard_map.141.rest_0_), channel_id=1, source_target_pairs={{0,2},{1,7},{2,0},{3,5},{4,6},{5,3},{6,4},{7,1},{8,10},{9,15},{10,... | collective-permute-start | bytes 12296 | tf_op jit(solution)/shard_map/ppermute | solution.py:759
  28.6 4.5 %collective-permute-start.10 = (f32[8,128]{1,0:T(8,128)S(1)}, f32[8,128]{1,0:T(8,128)S(1)}, u32[]{:S(2)}, u32[]{:S(2)}) collective-permute-start(f32[8,128]{1,0:T(8,128)S(1)} %shard_map.141.rest_0_), channel_id=1, source_target_pairs={{0,4},{1,5},{2,6},{3,7},{4,0},{5,1},{6,2},{7,3},{8,12},{9,13},{10,... | collective-permute-start | bytes 12296 | tf_op jit(solution)/shard_map/ppermute | solution.py:760
  32.2 1.6 %collective-permute-start.11 = (f32[8,128]{1,0:T(8,128)S(1)}, f32[8,128]{1,0:T(8,128)S(1)}, u32[]{:S(2)}, u32[]{:S(2)}) collective-permute-start(f32[8,128]{1,0:T(8,128)S(1)} %collective-permute-done.9.rest_1_), channel_id=1, source_target_pairs={{0,1},{1,0},{2,3},{3,2},{4,5},{5,4},{6,7},{7,6},{8,9},{9,8},{10,11... | collective-permute-start | bytes 12296 | tf_op jit(solution)/shard_map/ppermute | solution.py:649

commit v7 on v6

--- a/solution.py
+++ b/solution.py
@@ -44,8 +44,9 @@
     return [slice(k * LANES, (k + 1) * LANES) for k in range(width // LANES)]
 
 
-def short_rows(fan):
-    return -(-5 * fan // 8)
+def depths(fan):
+    short = -(-5 * fan // 8)
+    return [short, short + 1, short + 2, fan]
 
 
 def lane_fetch(windows, group, place):
@@ -97,34 +98,53 @@
     return seat, pieces, [x[COUNT_ROW : COUNT_ROW + 1] for x in tables]
 
 
-def fill_rows(pieces, counts, fits):
+def fill_rows(pieces, counts, limit):
     first, second = pieces
     fan = first.shape[0]
-    short = short_rows(fan)
-    limit = jnp.where(fits, float(short), float(fan))
     row = lax.broadcasted_iota(I32, (fan, LANES), 0).astype(F32)
     mine = row < counts[1]
-    over = [2 * short - 1 - r if 0 <= 2 * short - 1 - r < fan else 0 for r in range(fan)]
-    over = jnp.concatenate([first[r : r + 1] for r in over], axis=0)
-    spilled = jnp.logical_and(fits, 2.0 * short - 1.0 - row < counts[0])
-    spilled = jnp.logical_and(spilled, row < float(short))
-    spilled = jnp.logical_and(spilled, row >= float(2 * short - fan))
-    spilled = jnp.logical_and(spilled, jnp.logical_not(mine))
+    spilled, over = jnp.zeros((fan, LANES), F32), first
+    for rows in depths(fan)[:-1]:
+        slots = [2 * rows - 1 - r if 0 <= 2 * rows - 1 - r < fan else 0 for r in range(fan)]
+        here = jnp.logical_and(limit == float(rows), 2.0 * rows - 1.0 - row < counts[0])
+        here = jnp.logical_and(here, row < float(rows))
+        here = jnp.logical_and(here, row >= float(2 * rows - fan))
+        here = jnp.logical_and(here, jnp.logical_not(mine))
+        over = jnp.where(here, jnp.concatenate([first[r : r + 1] for r in slots], axis=0), over)
+        spilled = jnp.where(here, 1.0, spilled)
+    spilled = spilled > 0.5
     first = jnp.where(row < jnp.minimum(counts[0], limit), first, -1.0)
     second = jnp.where(mine, second, jnp.where(spilled, over, -1.0))
     return jnp.concatenate([first, second], axis=1), jnp.where(spilled, 0.0, 1.0)
 
 
 def by_depth(depth, fan, run):
-    shallow = jnp.max(depth[...]) < float(short_rows(fan)) + 0.5
-
-    @pl.when(shallow)
+    limit = jnp.max(depth[...])
+    short = depths(fan)[0]
+
+    @pl.when(limit < short + 0.5)
     def _():
-        run(short_rows(fan))
-
-    @pl.when(jnp.logical_not(shallow))
+        run(short)
+
+    @pl.when(limit > short + 0.5)
     def _():
-        run(fan)
+        run(limit.astype(I32))
+
+
+def over_rows(rows, step, carry):
+    if isinstance(rows, int):
+        for s in range(rows):
+            carry = step(s, carry)
+        return carry
+    return lax.fori_loop(0, rows, step, carry)
+
+
+def spill_from(rows, fan):
+    return 2 * rows - fan if isinstance(rows, int) else 0
+
+
+def may_spill(s, first):
+    return not isinstance(s, int) or s >= first
 
 
 def locate_block(i, table, table_lo, seated, edges, own, lo, width, delta_out, basis_out, kinds_out, place_out):
@@ -166,24 +186,37 @@
 
 
 def fill_hidden(target, spread, basis, rows, fan):
-    used = rows * (spread.shape[0] // fan)
-    target[:used, :] = silu_of_half(dot(spread[:used, :], basis)).astype(BF16)
-
-
-class Sums:
-    def __init__(self, shape, own, rows, fan, total=None, lent=None):
-        self.total = jnp.zeros(shape, F32) if total is None else total
-        self.lent = jnp.zeros((shape[0], LANES), F32) if lent is None else lent
-        self.own, self.alone = own, 2 * rows - fan
-
-    def add(self, s, terms):
-        self.total = self.total + terms
-        if s >= self.alone:
-            self.lent = self.lent + jnp.where(self.own[s : s + 1] > 0.5, 0.0, terms[:, LANES:])
-
-    def done(self):
-        first, second = self.total[:, :LANES], self.total[:, LANES:]
-        return jnp.concatenate([first + self.lent, second - self.lent], axis=1)
+    units = spread.shape[0] // fan
+
+    def part(start, used):
+        place = pl.ds(start, used)
+        target[place, :] = silu_of_half(dot(spread[place, :], basis[...])).astype(BF16)
+
+    if isinstance(rows, int):
+        part(0, rows * units)
+    else:
+
+        def step(s, carry):
+            part(aligned(s * units, units), units)
+            return carry
+
+        lax.fori_loop(0, fan, step, 0)
+
+
+def add_terms(carry, own, s, terms, first):
+    total, lent = carry
+    if may_spill(s, first):
+        lent = lent + jnp.where(own[pl.ds(s, 1), :] > 0.5, 0.0, terms[:, LANES:])
+    return total + terms, lent
+
+
+def no_sums(chans, width):
+    return jnp.zeros((chans, width), F32), jnp.zeros((chans, LANES), F32)
+
+
+def summed_of(carry):
+    total, lent = carry
+    return jnp.concatenate([total[:, :LANES] + lent, total[:, LANES:] - lent], axis=1)
 
 
 def update_of(feats, summed, mix_half, fan):
@@ -192,25 +225,35 @@
 
 
 def first_block(rows, kinds, hid, own, seated, lo, width, weights):
-    embed_t, first, mix_half, spread = weights
+    embed_t, first, first_rest, mix_half, spread = weights
     fan = kinds.shape[0]
-    kinds_count = embed_t.shape[1]
     units = spread.shape[0] // fan
     species = first.shape[1] // units
-    kinds = kinds.astype(BF16)
     zero = jnp.zeros((), BF16)
-    sums = Sums((mix_half.shape[0], width), own, rows, fan)
-    for s in range(rows):
-        mine = hid[s * units : (s + 1) * units, :]
-        kind = jnp.broadcast_to(kinds[s : s + 1], (units, width))
+
+    def step(s, carry):
+        sums, whole, away = carry
+        mine = hid[pl.ds(s * units, units), :]
+        kind = jnp.broadcast_to(kinds[pl.ds(s, 1), :].astype(BF16), (units, width))
         sorted_out = [
             jnp.where(kind == jnp.full((), k, BF16), mine, zero) for k in range(species)
         ]
-        sums.add(s, dot(first[...], jnp.concatenate(sorted_out, axis=0)))
-    rows_of = lax.broadcasted_iota(I32, (kinds_count, width), 0).astype(F32)
+        sorted_out = jnp.concatenate(sorted_out, axis=0)
+        whole = whole + sorted_out
+        if may_spill(s, spill_from(rows, fan)):
+            mine = jnp.broadcast_to(own[pl.ds(s, 1), :].astype(BF16), away.shape)
+            away = away + jnp.where(mine > jnp.full((), 0.5, BF16), zero, sorted_out[:, LANES:])
+        sums = add_terms(sums, own, s, dot(first[...], sorted_out), spill_from(rows, fan))
+        return sums, whole, away
+
+    whole = jnp.zeros((species * units, width), BF16)
+    carry = no_sums(mix_half.shape[0], width), whole, whole[:, :LANES]
+    (total, lent), whole, away = over_rows(rows, step, carry)
+    sums = total + dot(first_rest[...], whole), lent + dot(first_rest[...], away)
+    rows_of = lax.broadcasted_iota(I32, (embed_t.shape[1], width), 0).astype(F32)
     same = rows_of == seated[SPECIES_ROW : SPECIES_ROW + 1, lo : lo + width]
     feats = dot(embed_t[...], jnp.where(same, 1.0, 0.0).astype(BF16))
-    return update_of(feats, sums.done(), mix_half[...], fan)
+    return update_of(feats, summed_of(sums), mix_half[...], fan)
 
 
 def turned(matrix):
@@ -223,7 +266,7 @@
     )
 
 
-def prepare(embed, rad_in, rad_out, mixing, embed_t, first, spread, out_t, mix_half):
+def prepare(embed, rad_in, rad_out, mixing, embed_t, first, first_rest, spread, out_t, mix_half):
     layers, count, units = rad_in.shape
     fan = spread.shape[1] // units
     for layer in range(layers):
@@ -245,6 +288,8 @@
     embed_t[...] = turned(padded.astype(BF16)).astype(BF16)
     scaled = jnp.concatenate([out * table[k : k + 1] for k in range(species)], axis=0)
     first[...] = turned(scaled.astype(BF16)).astype(BF16)
+    rest = scaled - scaled.astype(BF16).astype(F32)
+    first_rest[...] = turned(rest.astype(BF16)).astype(BF16)
 
 
 def seat_tile(width, pk, nbr, table, seated, edges, owns, depth, delta_out, basis_out, kinds_out, place_out, index):
@@ -255,13 +300,15 @@
     found = [seat_block(pk, index, b * width, width, seated) for b in range(blocks)]
     both = [counts[0] + counts[1] for _, _, counts in found]
     most = functools.reduce(jnp.maximum, both)
-    fits = jnp.max(most, axis=1, keepdims=True) <= float(2 * short_rows(nbr.shape[0]))
-    depth[...] = jnp.where(
-        jnp.broadcast_to(fits, depth.shape), float(short_rows(nbr.shape[0])), float(nbr.shape[0])
-    )
+    most = jnp.max(most, axis=1, keepdims=True)
+    fan = nbr.shape[0]
+    limit = jnp.full(most.shape, float(fan), F32)
+    for rows in depths(fan)[-2::-1]:
+        limit = jnp.where(most <= float(2 * rows), float(rows), limit)
+    depth[...] = jnp.broadcast_to(limit, depth.shape)
     for b, (seat, pieces, counts) in enumerate(found):
         table[SEAT_ROW : SEAT_ROW + 1, b * width : (b + 1) * width] = seat
-        edges[b], owns[b] = fill_rows(pieces, counts, fits)
+        edges[b], owns[b] = fill_rows(pieces, counts, limit)
     for part in halves(2 * width):
         wanted = jnp.broadcast_to(pk[SEND_ROW : SEND_ROW + 1, part].astype(I32), (PACK_ROWS, LANES))
         seats = lane_lookup([table[SEAT_ROW : SEAT_ROW + 1, p] for p in halves(atoms)], wanted)
@@ -276,9 +323,9 @@
         )
 
 
-def first_inner(width, ref_energy, pk, seated, owns, depth, basis, kinds, embed, rad_in, rad_out, mixing, w_in, feats_out, embed_t, first, spread, out_t, mix_half, w_row, ref_row, hid):
-    prepare(embed, rad_in, rad_out, mixing, embed_t, first, spread, out_t, mix_half)
-    weights = (embed_t, first, mix_half.at[0], spread.at[0])
+def first_inner(width, ref_energy, pk, seated, owns, depth, basis, kinds, embed, rad_in, rad_out, mixing, w_in, feats_out, embed_t, first, first_rest, spread, out_t, mix_half, w_row, ref_row, hid):
+    prepare(embed, rad_in, rad_out, mixing, embed_t, first, first_rest, spread, out_t, mix_half)
+    weights = (embed_t, first, first_rest, mix_half.at[0], spread.at[0])
     w_row[...] = w_in[...]
     kinds_row = pk[SPECIES_ROW : SPECIES_ROW + 1, :]
     energy = jnp.zeros(kinds_row.shape, F32)
@@ -287,26 +334,25 @@
     ref_row[...] = energy
     def run(rows):
         for i in range(kinds.shape[0]):
-            fill_hidden(hid.at[i], spread.at[0], basis[i], rows, kinds.shape[1])
+            fill_hidden(hid.at[i], spread.at[0], basis.at[i], rows, kinds.shape[1])
         for i in range(kinds.shape[0]):
             feats_out[:, i * width : (i + 1) * width] = first_block(
-                rows, kinds[i], hid.at[i], owns.at[i + 1], seated, (i + 1) * width, width, weights
+                rows, kinds.at[i], hid.at[i], owns.at[i + 1], seated, (i + 1) * width, width, weights
             )
 
     by_depth(depth, kinds.shape[1], run)
 
 
-def pack_halo(feats, table, core, width, to_mate, to_cross):
+def pack_halo(feats, table, start, width, out):
     atoms = feats.shape[1]
     rows = lax.broadcasted_iota(I32, (width, width), 0).astype(F32).astype(BF16)
     one, zero = jnp.ones((), BF16), jnp.zeros((), BF16)
-    for ref, start in ((to_mate, (1 - core) * width), (to_cross, core * width)):
-        wanted = table[SEND_ROW : SEND_ROW + 1, pl.ds(aligned(start, width), width)]
-        picks = []
-        for k in range(atoms // width):
-            place = jnp.clip(wanted - float(k * width), -1.0, float(width)).astype(BF16)
-            picks.append(jnp.where(rows == place, one, zero))
-        ref[...] = dot(feats[...], jnp.concatenate(picks, axis=0)).astype(BF16)
+    wanted = table[SEND_ROW : SEND_ROW + 1, pl.ds(aligned(start, width), width)]
+    picks = []
+    for k in range(atoms // width):
+        place = jnp.clip(wanted - float(k * width), -1.0, float(width)).astype(BF16)
+        picks.append(jnp.where(rows == place, one, zero))
+    out[...] = dot(feats[...], jnp.concatenate(picks, axis=0)).astype(BF16)
 
 
 def halo_places(core, atoms, width):
@@ -318,12 +364,12 @@
     return [(0, 0, 0), (1, blocks - 1, (blocks - 1) * width)]
 
 
-def first_outer(width, pk, own_table, seated, mate, cross, edges, owns, depth, embed_t, first, spread, mix_half, inner, delta_out, basis_out, place_out, feats_out, to_mate, to_cross, pair_out, table, kinds, hid):
+def first_outer(width, pk, own_table, seated, mate, cross, edges, owns, depth, embed_t, first, first_rest, spread, mix_half, inner, delta_out, basis_out, place_out, feats_out, to_mate, to_cross, pair_out, table, kinds, hid):
     core = core_index()
     atoms = pk.shape[1]
     blocks = atoms // width
     fan = edges.shape[1]
-    weights = (embed_t, first, mix_half.at[0], spread.at[0])
+    weights = (embed_t, first, first_rest, mix_half.at[0], spread.at[0])
     table[:, width : width + atoms] = own_table[...]
     at_mate, at_cross = halo_places(core, atoms, width)
     for ref, start, at in ((mate, core * width, at_mate), (cross, (1 - core) * width, at_cross)):
@@ -347,70 +393,77 @@
 
     def run(rows):
         for i in range(2):
-            fill_hidden(hid.at[i], spread.at[0], basis_out[i], rows, fan)
+            fill_hidden(hid.at[i], spread.at[0], basis_out.at[i], rows, fan)
         for i, b, lo in edge_blocks(blocks, width):
             feats_out[:, lo : lo + width] = first_block(
-                rows, kinds[i], hid.at[i], owns.at[b], seated, lo, width, weights
+                rows, kinds.at[i], hid.at[i], owns.at[b], seated, lo, width, weights
             )
 
     by_depth(depth, fan, run)
-    pack_halo(feats_out, own_table, core, width, to_mate, to_cross)
-
-
-def places_of(place, width, tiles=(0, 1, 2)):
-    return [jnp.clip(place - float(k * width), -1.0, float(width)).astype(BF16) for k in tiles]
-
-
-def fetch_rows(window, places, s, width):
-    rows = lax.broadcasted_iota(I32, (width, width), 0).astype(F32).astype(BF16)
-    one, zero = jnp.ones((), BF16), jnp.zeros((), BF16)
-    picks = [jnp.where(rows == place[s : s + 1], one, zero) for place in places]
-    return dot(window, jnp.concatenate(picks, axis=0))
-
-
-def layer_block(rows, window, place, own, hid, out_t, mix_half, feats):
-    fan, width = place.shape
-    places = places_of(place, width)
-    sums = Sums(feats.shape, own, rows, fan)
-    for s in range(rows):
-        far = fetch_rows(window, places, s, width)
-        sums.add(s, far * dot(out_t, hid(s)))
-    return update_of(feats, sums.done(), mix_half, fan)
-
-
-def stored(hid_edge, i, units):
-    return lambda s: hid_edge[i, s * units : (s + 1) * units, :]
+    pack_halo(feats_out, own_table, core * width, width, to_cross)
+    pack_halo(feats_out, own_table, (1 - core) * width, width, to_mate)
+
+
+class Places:
+    def __init__(self, place, width, tiles):
+        self.place, self.width, self.tiles = place, width, tiles
+        self.known = self.rows(place[...])
+
+    def rows(self, place):
+        width = float(self.width)
+        return [jnp.clip(place - k * width, -1.0, width).astype(BF16) for k in self.tiles]
+
+    def fetch(self, window, s):
+        if isinstance(s, int):
+            lines = [x[s : s + 1] for x in self.known]
+        else:
+            lines = self.rows(self.place[pl.ds(s, 1), :])
+        rows = lax.broadcasted_iota(I32, (self.width, self.width), 0).astype(F32).astype(BF16)
+        one, zero = jnp.ones((), BF16), jnp.zeros((), BF16)
+        return dot(window, jnp.concatenate([jnp.where(rows == x, one, zero) for x in lines], axis=0))
+
+
+def stored(hid, s, units):
+    return hid[pl.ds(s * units, units), :]
 
 
 def layer_inner(width, layer, owns, depth, spreads, outs_t, mixes, feats, basis, place, basis_edge, place_edge, pair, feats_out, field_edge, total_edge, lent_edge, pair_out, hid):
-    pair_out[...] = pair[...]
     spread, out_t, mix_half = spreads.at[layer], outs_t[layer], mixes[layer]
-    units = out_t.shape[1]
+    chans, units = out_t.shape
     fan = place.shape[1]
     inner = place.shape[0]
+    pair_out[...] = pair[...]
 
     def run(rows):
+        first = spill_from(rows, fan)
         for i in range(inner):
-            fill_hidden(hid.at[i], spread, basis[i], rows, fan)
+            fill_hidden(hid.at[i], spread, basis.at[i], rows, fan)
         for i in range(2):
-            fill_hidden(hid.at[inner + i], spread, basis_edge[i], rows, fan)
+            fill_hidden(hid.at[inner + i], spread, basis_edge.at[i], rows, fan)
         for i in range(inner):
             lo = (i + 1) * width
-            feats_out[:, lo - width : lo] = layer_block(
-                rows, feats[:, lo - width : lo + 2 * width], place[i], owns.at[i + 1],
-                stored(hid, i, units), out_t, mix_half, feats[:, lo : lo + width],
+            window = feats[:, lo - width : lo + 2 * width]
+            places = Places(place.at[i], width, (0, 1, 2))
+
+            def step(s, carry):
+                terms = places.fetch(window, s) * dot(out_t, stored(hid.at[i], s, units))
+                return add_terms(carry, owns.at[i + 1], s, terms, first)
+
+            sums = over_rows(rows, step, no_sums(chans, width))
+            feats_out[:, lo - width : lo] = update_of(
+                feats[:, lo : lo + width], summed_of(sums), mix_half, fan
             )
         for i, b, lo in edge_blocks(inner + 2, width):
-            near = max(lo - width, 0)
-            window = feats[:, near : near + 2 * width]
-            places = places_of(place_edge[i], width, (0, 1) if i else (1, 2))
-            sums = Sums(total_edge.shape[1:], owns.at[b], rows, fan)
-            for s in range(rows):
-                field = dot(out_t, stored(hid, inner + i, units)(s))
+            start = max(lo - width, 0)
+            window = feats[:, start : start + 2 * width]
+            places = Places(place_edge.at[i], width, (0, 1) if i else (1, 2))
+
+            def step(s, carry):
+                field = dot(out_t, stored(hid.at[inner + i], s, units))
                 field_edge[i, s] = field
-                sums.add(s, fetch_rows(window, places, s, width) * field)
-            total_edge[i] = sums.total
-            lent_edge[i] = sums.lent
+                return add_terms(carry, owns.at[b], s, places.fetch(window, s) * field, first)
+
+            total_edge[i], lent_edge[i] = over_rows(rows, step, no_sums(chans, width))
 
     by_depth(depth, fan, run)
 
@@ -430,29 +483,31 @@
     def run(rows):
         for i, b, lo in edge_blocks(atoms // width, width):
             halo = halo_of(i, core, mate, cross)
-            places = places_of(place[i], width, (2,) if i else (0,))
-            sums = Sums(None, owns.at[b], rows, fan, total_edge[i], lent_edge[i])
-            for s in range(rows):
-                sums.add(s, fetch_rows(halo, places, s, width) * field_edge[i, s])
+            places = Places(place.at[i], width, (2,) if i else (0,))
+
+            def step(s, carry):
+                terms = places.fetch(halo, s) * field_edge[i, s]
+                return add_terms(carry, owns.at[b], s, terms, spill_from(rows, fan))
+
+            sums = over_rows(rows, step, (total_edge[i], lent_edge[i]))
             feats_out[:, lo : lo + width] = update_of(
-                feats[:, lo : lo + width], sums.done(), mix_half, fan
+                feats[:, lo : lo + width], summed_of(sums), mix_half, fan
             )
 
     by_depth(depth, fan, run)
-    pack_halo(feats_out, own_table, core, width, to_mate, to_cross)
-
-
-def near_of(near, own, s, alone):
-    if s < alone:
+    pack_halo(feats_out, own_table, core * width, width, to_cross)
+    pack_halo(feats_out, own_table, (1 - core) * width, width, to_mate)
+
+
+def near_of(near, own, s, first):
+    if not may_spill(s, first):
         return near
-    lower = jnp.where(own[s : s + 1] > 0.5, near[:, LANES:], near[:, :LANES])
+    lower = jnp.where(own[pl.ds(s, 1), :] > 0.5, near[:, LANES:], near[:, :LANES])
     return jnp.concatenate([near[:, :LANES], lower], axis=1)
 
 
-def filled(pairs, fan):
-    if len(pairs) < fan:
-        pairs.append(jnp.zeros((fan - len(pairs), pairs[0].shape[1]), F32))
-    return jnp.concatenate(pairs, axis=0)
+def put_pair(pairs, s, terms):
+    pairs[pl.ds(s, 1), :] = jnp.sum(terms, axis=0, keepdims=True)
 
 
 def force_of(pair, own, delta, seat, chans):
@@ -485,46 +540,51 @@
     )
 
 
-def head_inner(width, layer, own_table, owns, depth, spreads, outs_t, feats, basis, place, delta, basis_edge, place_edge, force_out, field_edge, pair_edge, hid):
+def head_inner(width, layer, own_table, owns, depth, spreads, outs_t, feats, basis, place, delta, basis_edge, place_edge, force_out, field_edge, pair_edge, hid, pairs):
     spread, out_t = spreads.at[layer], outs_t[layer]
     chans, units = out_t.shape
     fan = place.shape[1]
     inner = place.shape[0]
+    pairs[...] = jnp.zeros(pairs.shape, F32)
+    pair_edge[...] = jnp.zeros(pair_edge.shape, F32)
 
     def run(rows):
+        first = spill_from(rows, fan)
         for i in range(inner):
-            fill_hidden(hid.at[i], spread, basis[i], rows, fan)
+            fill_hidden(hid.at[i], spread, basis.at[i], rows, fan)
         for i in range(2):
-            fill_hidden(hid.at[inner + i], spread, basis_edge[i], rows, fan)
-        alone = 2 * rows - fan
+            fill_hidden(hid.at[inner + i], spread, basis_edge.at[i], rows, fan)
         for i in range(inner):
             lo = (i + 1) * width
             window = feats[:, lo - width : lo + 2 * width]
             near = feats[:, lo : lo + width].astype(F32)
-            places = places_of(place[i], width)
-            pairs = []
-            for s in range(rows):
-                field = dot(out_t, stored(hid, i, units)(s))
-                field = field * near_of(near, owns.at[i + 1], s, alone)
-                terms = fetch_rows(window, places, s, width) * field
-                pairs.append(jnp.sum(terms, axis=0, keepdims=True))
+            places = Places(place.at[i], width, (0, 1, 2))
+
+            def step(s, carry):
+                field = dot(out_t, stored(hid.at[i], s, units))
+                field = field * near_of(near, owns.at[i + 1], s, first)
+                put_pair(pairs.at[i], s, places.fetch(window, s) * field)
+                return carry
+
+            over_rows(rows, step, 0)
             force_out[:, lo - width : lo] = force_of(
-                filled(pairs, fan), owns.at[i + 1], delta.at[i],
+                pairs[i], owns.at[i + 1], delta.at[i],
                 own_table[SEAT_ROW : SEAT_ROW + 1, lo : lo + width], chans,
             )
         for i, b, lo in edge_blocks(inner + 2, width):
             start = max(lo - width, 0)
             window = feats[:, start : start + 2 * width]
             near = feats[:, lo : lo + width].astype(F32)
-            places = places_of(place_edge[i], width, (0, 1) if i else (1, 2))
-            pairs = []
-            for s in range(rows):
-                field = dot(out_t, stored(hid, inner + i, units)(s))
-                field = field * near_of(near, owns.at[b], s, alone)
+            places = Places(place_edge.at[i], width, (0, 1) if i else (1, 2))
+
+            def step(s, carry):
+                field = dot(out_t, stored(hid.at[inner + i], s, units))
+                field = field * near_of(near, owns.at[b], s, first)
                 field_edge[i, s] = field
-                terms = fetch_rows(window, places, s, width) * field
-                pairs.append(jnp.sum(terms, axis=0, keepdims=True))
-            pair_edge[i] = filled(pairs, fan)
+                put_pair(pair_edge.at[i], s, places.fetch(window, s) * field)
+                return carry
+
+            over_rows(rows, step, 0)
 
     by_depth(depth, fan, run)
 
@@ -536,23 +596,26 @@
     return jnp.sum(total, axis=0, keepdims=True)
 
 
-def head_outer(width, own_table, owns, depth, place, delta, mate, cross, field_edge, pair_edge, inner, force_out):
+def head_outer(width, own_table, owns, depth, place, delta, mate, cross, field_edge, pair_edge, inner, force_out, pairs):
     core = core_index()
     chans = mate.shape[0]
     atoms = own_table.shape[1]
     fan = place.shape[1]
     force_out[:, width : atoms - width] = inner[...]
+    pairs[...] = jnp.zeros(pairs.shape, F32)
 
     def run(rows):
         for i, b, lo in edge_blocks(atoms // width, width):
             halo = halo_of(i, core, mate, cross)
-            places = places_of(place[i], width, (2,) if i else (0,))
-            pairs = []
-            for s in range(rows):
-                terms = fetch_rows(halo, places, s, width) * field_edge[i, s]
-                pairs.append(jnp.sum(terms, axis=0, keepdims=True))
+            places = Places(place.at[i], width, (2,) if i else (0,))
+
+            def step(s, carry):
+                put_pair(pairs.at[i], s, places.fetch(halo, s) * field_edge[i, s])
+                return carry
+
+            over_rows(rows, step, 0)
             force_out[:, lo : lo + width] = force_of(
-                pair_edge[i] + filled(pairs, fan), owns.at[b], delta.at[i],
+                pair_edge[i] + pairs[i], owns.at[b], delta.at[i],
                 own_table[SEAT_ROW : SEAT_ROW + 1, lo : lo + width], chans,
             )
 
@@ -685,12 +748,13 @@
         [((fan, atoms), F32)],
         flops=2**32,
     )
-    inner, embed_t, first, spread, out_t, mix_half, w_row, ref_row = call(
+    inner, embed_t, first, first_rest, spread, out_t, mix_half, w_row, ref_row = call(
         functools.partial(first_inner, width),
         (ref_energy[None], pk, seated, owns, depth, basis_in, kinds_in, embed, rad_in, rad_out, mixing, w_energy[None]),
         [
             ((chans, inner_atoms), BF16),
             ((chans, -(-embed.shape[0] // 16) * 16), BF16),
+            ((chans, embed.shape[0] * units), BF16),
             ((chans, embed.shape[0] * units), BF16),
             ((layers + 1, fan * units, fan * basis_count), BF16),
             ((layers + 1, chans, units), BF16),
@@ -703,7 +767,7 @@
     )
     delta_out, basis_out, place_out, feats, to_mate, to_cross, pair = call(
         functools.partial(first_outer, width),
-        (pk, own_table, seated, mate, cross, edges, owns, depth, embed_t, first, spread, mix_half, inner),
+        (pk, own_table, seated, mate, cross, edges, owns, depth, embed_t, first, first_rest, spread, mix_half, inner),
         block_outs(2) + [feats_type, halo_type, halo_type, pack_type],
         [((PACK_ROWS, atoms + 2 * width), F32), ((2, fan, width), F32), hid_type],
     )
@@ -735,7 +799,7 @@
         functools.partial(head_inner, width, layers),
         (own_table, owns, depth, spread, out_t, feats, basis_in, place_in, delta_in, basis_out, place_out),
         [((PACK_ROWS, inner_atoms), F32), ((2, fan, chans, width), F32), ((2, fan, width), F32)],
-        [((blocks, fan * units, width), BF16)],
+        [((blocks, fan * units, width), BF16), ((blocks - 2, fan, width), F32)],
         flops=2**32,
     )
     (late,) = call(pass_on, (received, inner), [pack_type])
@@ -744,6 +808,7 @@
         functools.partial(head_outer, width),
         (own_table, owns, depth, place_out, delta_out, mate, cross, field_edge, pair_edge, inner),
         [pack_type],
+        [((2, fan, width), F32)],
         flops=2**32,
     )
     band, sums = call(

time: 34.8 us -> 35.1 us (level)
  no operation moved by 1% of the time
where the time goes in v7:
time: 35.1 us; the launch traced here: 34.9 us
  Pallas kernels  15.1 us (43%)
  starting transfers between devices  14.4 us (41%)
  waiting for transfers between devices  3.59 us (10%)
  between operations  1.66 us (5%)
    pallas_call x12, Pallas kernels, call(): pl.pallas_call(body, out_shape=[jax.ShapeDtypeStruct(shape, dtype) for sh...  15.1 us
    ppermute x9, starting transfers between devices, swap(): return lax.ppermute(block, 'atom', swap_pairs(tiles, offset))  10.6 us
    ppermute x1, starting transfers between devices, on_device(): far = lax.ppermute(both, 'atom', [(i, i ^ 4) for i in range(tiles)])  2.26 us
    ppermute x9, waiting for transfers between devices, swap(): return lax.ppermute(block, 'atom', swap_pairs(tiles, offset))  2.17 us
    ppermute x1, starting transfers between devices, on_device(): received = lax.ppermute(pair, ('img', 'atom'), image_pairs(images, tiles))  1.55 us
    ppermute x1, waiting for transfers between devices, on_device(): lax.ppermute(both, 'atom', [(i, i ^ 2 if i % 2 == 0 else i ^ 6) for i in...  1.34 us
  transfers between devices with their start and end apart: 12, of which 5 were waited for; matrix products, arithmetic and copies ran while one was open for 0% of the time, Pallas kernels for 34%

profile of v7, /device:TPU:0, one launch (start us, length us, event | category | flops | bytes accessed | tf_op | source)
XLA Modules:
  0.0 34.9 jit_solution(11736754979053478127)
XLA Ops:
  0.7 0.0 copy-start.8
  0.7 0.0 copy-start.9
  0.7 0.0 copy-start.10
  0.7 0.0 copy-start.7
  0.7 0.0 copy-start
  1.5 0.1 select_select_fusion.pk
  1.6 0.0 copy-start.3
  1.6 0.0 copy-start.4
  1.7 4.6 %collective-permute-start.1 = (f32[8,1024]{1,0:T(8,128)S(1)}, f32[8,1024]{1,0:T(8,128)S(1)}, u32[]{:S(2)}, u32[]{:S(2)}) collective-permute-start(f32[8,1024]{1,0:T(8,128)S(1)} %select_select_fusion.pk), channel_id=1, source_target_pairs={{1,2},{2,1},{3,4},{4,3},{5,6},{6,5},{7,0},{0,7},{9,10},{10,9},{11,... | collective-permute-start | bytes 98312 | tf_op jit(solution)/shard_map/ppermute | solution.py:712
  6.2 1.4 %shard_map.132 = (f32[8,1024]{1,0:T(8,128)S(1)}, f32[8,1024]{1,0:T(8,128)S(1)}, f32[4,16,256]{2,1,0:T(8,128)S(1)}, f32[4,16,128]{2,1,0:T(8,128)S(1)}, f32[8,128]...) custom-call(f32[8,1024]{1,0:T(8,128)S(1)} %select_select_fusion.pk, ...), custom_call_target="tpu_custom_call" | custom-call | flops 4294967296 | bytes 1048576 | tf_op jit(solution)/shard_map/pallas_call | solution.py:701
  7.7 1.6 %shard_map.133 = (bf16[128,512]{1,0:T(8,128)(2,1)S(1)}, bf16[128,16]{1,0:T(8,128)(2,1)S(1)}, bf16[128,256]{1,0:T(8,128)(2,1)S(1)}, bf16[128,256]{1,0:T(8,128)(2,...) custom-call(f32[1,4]{1,0:T(1,128)S(1)} %bitcast.8, ...), custom_call_target="tpu_custom_call" | custom-call | flops 4294967296 | bytes 1048576 | tf_op jit(solution)/shard_map/pallas_call | solution.py:701
  9.4 2.3 %shard_map.134 = (f32[2,48,256]{2,1,0:T(8,128)S(1)}, bf16[2,128,256]{2,1,0:T(8,128)(2,1)S(1)}, f32[2,16,256]{2,1,0:T(8,128)S(1)}, bf16[128,1024]{1,0:T(8,128)(2,...) custom-call(f32[8,1024]{1,0:T(8,128)S(1)} %select_select_fusion.pk, ...), custom_call_target="tpu_custom_call" | custom-call | bytes 1048576 | tf_op jit(solution)/shard_map/pallas_call | solution.py:701
  11.6 0.6 %collective-permute-start.3 = (bf16[128,256]{1,0:T(8,128)(2,1)S(1)}, bf16[128,256]{1,0:T(8,128)(2,1)S(1)}, u32[]{:S(2)}, u32[]{:S(2)}) collective-permute-start(bf16[128,256]{1,0:T(8,128)(2,1)S(1)} %get-tuple-element.62), channel_id=1, source_target_pairs={{0,1},{1,0},{2,3},{3,2},{4,5},{5,4},{6,7},{7,6},{8,9},{9,8},{10,11... | collective-permute-start | bytes 196616 | tf_op jit(solution)/shard_map/ppermute | solution.py:712
  12.2 1.6 %collective-permute-start.4 = (bf16[128,256]{1,0:T(8,128)(2,1)S(1)}, bf16[128,256]{1,0:T(8,128)(2,1)S(1)}, u32[]{:S(2)}, u32[]{:S(2)}) collective-permute-start(bf16[128,256]{1,0:T(8,128)(2,1)S(1)} %get-tuple-element.63), channel_id=1, source_target_pairs={{1,2},{2,1},{3,4},{4,3},{5,6},{6,5},{7,0},{0,7},{9,10},{10,9},{11,... | collective-permute-start | bytes 196616 | tf_op jit(solution)/shard_map/ppermute | solution.py:712
  13.8 3.4 %shard_map.135 = (bf16[128,512]{1,0:T(8,128)(2,1)S(1)}, f32[2,16,128,256]{3,2,1,0:T(8,128)S(1)}, f32[2,128,256]{2,1,0:T(8,128)S(1)}, f32[2,128,128]{2,1,0:T(8,128)S(1)}, f32[8,1024]{1,0:T(8,128)S(1)}) custom-call(f32[4,16,128]{2,1,0:T(8,128)S(1)} %get-tuple-element.42.owns, f32[8,128]{1,0:T(8,128)S(1)} %get-tuple-element.43.depth, ...), custom_call_target="tpu_custom_call" | custom-call | flops 4294967296 | bytes 1048576 | tf_op jit(solution)/shard_map/pallas_call | solution.py:701
  17.2 1.6 %collective-permute-start.2 = (f32[8,1024]{1,0:T(8,128)S(1)}, f32[8,1024]{1,0:T(8,128)S(1)}, u32[]{:S(2)}, u32[]{:S(2)}) collective-permute-start(f32[8,1024]{1,0:T(8,128)S(1)} %get-tuple-element.61), channel_id=1, source_target_pairs={{0,8},{8,0},{16,24},{24,16},{9,17},{17,9},{25,1},{1,25},{2,10},{10... | collective-permute-start | bytes 98312 | tf_op jit(solution)/shard_map/ppermute | solution.py:795
  18.8 1.3 %shard_map.136 = (bf16[128,1024]{1,0:T(8,128)(2,1)S(1)}, bf16[128,256]{1,0:T(8,128)(2,1)S(1)}, bf16[128,256]{1,0:T(8,128)(2,1)S(1)}) custom-call(f32[8,1024]{1,0:T(8,128)S(1)} %get-tuple-element.50.own_table, f32[4,16,128]{2,1,0:T(8,128)S(1)} %get-tuple-element.42.owns, f32[8,128]{1,0:T(8,128)S(1)} %get-tuple-element.43.depth, ...), custom_call_target="tpu_custom_call" | custom-call | bytes 1048576 | tf_op jit(solution)/shard_map/pallas_call | solution.py:701
  20.1 0.1 collective-permute-start.6
  20.2 2.7 %collective-permute-start.7 = (bf16[128,256]{1,0:T(8,128)(2,1)S(1)}, bf16[128,256]{1,0:T(8,128)(2,1)S(1)}, u32[]{:S(2)}, u32[]{:S(2)}) collective-permute-start(bf16[128,256]{1,0:T(8,128)(2,1)S(1)} %get-tuple-element.75), channel_id=1, source_target_pairs={{1,2},{2,1},{3,4},{4,3},{5,6},{6,5},{7,0},{0,7},{9,10},{10,9},{11,... | collective-permute-start | bytes 196616 | tf_op jit(solution)/shard_map/ppermute | solution.py:712
  22.9 3.3 %shard_map.137 = (f32[8,512]{1,0:T(8,128)S(1)}, f32[2,16,128,256]{3,2,1,0:T(8,128)S(1)}, f32[2,16,256]{2,1,0:T(8,128)S(1)}) custom-call(f32[8,1024]{1,0:T(8,128)S(1)} %get-tuple-element.50.own_table, f32[4,16,128]{2,1,0:T(8,128)S(1)} %get-tuple-element.42.owns, f32[8,128]{1,0:T(8,128)S(1)} %get-tuple-element.43.depth, ...), custom_call_target="tpu_custom_call" | custom-call | flops 4294967296 | bytes 1048576 | tf_op jit(solution)/shard_map/pallas_call | solution.py:701
  26.3 0.1 collective-permute-start.5
  26.4 0.8 %shard_map.139.force_in.force = f32[8,1024]{1,0:T(8,128)S(1)} custom-call(f32[8,1024]{1,0:T(8,128)S(1)} %get-tuple-element.50.own_table, f32[4,16,128]{2,1,0:T(8,128)S(1)} %get-tuple-element.42.owns, f32[8,128]{1,0:T(8,128)S(1)} %get-tuple-element.43.depth, f32[2,16,256]{2,1,0:T(8,128)S(1)} %get-tuple-element.59.place_edge.place, ...), custom_call_target="tpu_custom_call" | custom-call | flops 4294967296 | bytes 1048576 | tf_op jit(solution)/shard_map/pallas_call | solution.py:701
  27.1 0.4 %collective-permute-done.5.relayed = f32[8,1024]{1,0:T(8,128)S(1)} collective-permute-done((f32[8,1024]{1,0:T(8,128)S(1)}, f32[8,1024]{1,0:T(8,128)S(1)}, u32[]{:S(2)}, u32[]{:S(2)}) %collective-permute-start.5) | collective-permute-done | bytes 32800 | tf_op jit(solution)/shard_map/ppermute | solution.py:712
  27.5 0.2 shard_map.140
  27.7 0.2 collective-permute-start.8
  27.9 1.0 %collective-permute-done.8.other = f32[8,128]{1,0:T(8,128)S(1)} collective-permute-done((f32[8,128]{1,0:T(8,128)S(1)}, f32[8,128]{1,0:T(8,128)S(1)}, u32[]{:S(2)}, u32[]{:S(2)}) %collective-permute-start.8) | collective-permute-done | bytes 4128 | tf_op jit(solution)/shard_map/ppermute | solution.py:712
  28.9 2.3 %collective-permute-start.10 = (f32[8,128]{1,0:T(8,128)S(1)}, f32[8,128]{1,0:T(8,128)S(1)}, u32[]{:S(2)}, u32[]{:S(2)}) collective-permute-start(f32[8,128]{1,0:T(8,128)S(1)} %shard_map.141.rest_0_), channel_id=1, source_target_pairs={{0,4},{1,5},{2,6},{3,7},{4,0},{5,1},{6,2},{7,3},{8,12},{9,13},{10,... | collective-permute-start | bytes 12296 | tf_op jit(solution)/shard_map/ppermute | solution.py:825
  31.2 1.3 %collective-permute-done.9.rest_1_ = f32[8,128]{1,0:T(8,128)S(1)} collective-permute-done((f32[8,128]{1,0:T(8,128)S(1)}, f32[8,128]{1,0:T(8,128)S(1)}, u32[]{:S(2)}, u32[]{:S(2)}) %collective-permute-start.9) | collective-permute-done | bytes 4128 | tf_op jit(solution)/shard_map/ppermute | solution.py:824
  32.5 0.8 %collective-permute-start.11 = (f32[8,128]{1,0:T(8,128)S(1)}, f32[8,128]{1,0:T(8,128)S(1)}, u32[]{:S(2)}, u32[]{:S(2)}) collective-permute-start(f32[8,128]{1,0:T(8,128)S(1)} %collective-permute-done.9.rest_1_), channel_id=1, source_target_pairs={{0,1},{1,0},{2,3},{3,2},{4,5},{5,4},{6,7},{7,6},{8,9},{9,8},{10,11... | collective-permute-start | bytes 12296 | tf_op jit(solution)/shard_map/ppermute | solution.py:712
  33.3 0.1 collective-permute-done.10.rest_2_
  33.4 0.7 %collective-permute-done.11.rest_3_ = f32[8,128]{1,0:T(8,128)S(1)} collective-permute-done((f32[8,128]{1,0:T(8,128)S(1)}, f32[8,128]{1,0:T(8,128)S(1)}, u32[]{:S(2)}, u32[]{:S(2)}) %collective-permute-start.11) | collective-permute-done | bytes 4128 | tf_op jit(solution)/shard_map/ppermute | solution.py:712
  34.2 0.8 %shard_map.142 = (f32[3,1,1024]{2,1,0:T(1,128)}, f32[1,1]{1,0:T(1,128)}) custom-call(f32[8,1024]{1,0:T(8,128)S(1)} %select_select_fusion.pk, f32[8,1024]{1,0:T(8,128)S(1)} %get-tuple-element.78.band, f32[8,1024]{1,0:T(8,128)S(1)} %shard_map.139.force_in.force, f32[8,128]{1,0:T(8,128)S(1)} %shard_map.141.rest_0_, ...), custom_call_target="tpu_custom_call" | custom-call | bytes 1048576 | tf_op jit(solution)/shard_map/pallas_call | solution.py:701
  (35 shorter events, 0.1 us)
Async XLA Ops:
  0.7 0.8 %copy-start.8 = (s32[1024]{0:T(1024)S(1)}, s32[1024]{0:T(1024)}, u32[]{:S(2)}) copy-start(s32[1024]{0:T(1024)} %param.13) | copy-start | bytes 12292
  0.7 0.8 %copy-start.9 = (s32[1024]{0:T(1024)S(1)}, s32[1024]{0:T(1024)}, u32[]{:S(2)}) copy-start(s32[1024]{0:T(1024)} %param.14) | copy-start | bytes 12292
  0.7 0.8 %copy-start.10 = (s32[512]{0:T(512)S(1)}, s32[512]{0:T(512)}, u32[]{:S(2)}) copy-start(s32[512]{0:T(512)} %param.16) | copy-start | bytes 6148
  0.7 0.8 %copy-start.7 = (f32[1,3,1024]{2,0,1:T(1,128)S(1)}, f32[1,3,1024]{2,0,1:T(1,128)}, u32[]{:S(2)}) copy-start(f32[1,3,1024]{2,0,1:T(1,128)} %param.12) | copy-start | bytes 36868
  0.7 5.5 %copy-start = (s32[16,1024]{1,0:T(8,128)S(1)}, s32[16,1024]{1,0:T(8,128)}, u32[]{:S(2)}) copy-start(s32[16,1024]{1,0:T(8,128)} %nbr.1) | copy-start | bytes 196612
  1.6 6.0 %copy-start.1 = (bf16[2,128,128]{2,1,0:T(8,128)(2,1)S(1)}, bf16[2,128,128]{2,1,0:T(8,128)(2,1)}, u32[]{:S(2)}) copy-start(bf16[2,128,128]{2,1,0:T(8,128)(2,1)} %mixing.1) | copy-start | bytes 196612
  1.6 6.0 %copy-start.2 = (bf16[3,64,128]{2,1,0:T(8,128)(2,1)S(1)}, bf16[3,64,128]{2,1,0:T(8,128)(2,1)}, u32[]{:S(2)}) copy-start(bf16[3,64,128]{2,1,0:T(8,128)(2,1)} %rad_out.1) | copy-start | bytes 147460
  1.6 6.0 %copy-start.3 = (bf16[3,8,64]{2,1,0:T(8,128)(2,1)S(1)}, bf16[3,8,64]{2,1,0:T(8,128)(2,1)}, u32[]{:S(2)}) copy-start(bf16[3,8,64]{2,1,0:T(8,128)(2,1)} %rad_in.1) | copy-start | bytes 9220
  1.6 6.0 %copy-start.4 = (bf16[4,128]{1,0:T(4,128)(2,1)S(1)}, bf16[4,128]{1,0:T(4,128)(2,1)}, u32[]{:S(2)}) copy-start(bf16[4,128]{1,0:T(4,128)(2,1)} %embed.1) | copy-start | bytes 3076
  1.7 6.0 %copy-start.5 = (f32[4]{0:T(128)S(1)}, f32[4]{0:T(128)}, u32[]{:S(2)}) copy-start(f32[4]{0:T(128)} %param.19) | copy-start | bytes 52
  1.7 6.0 %copy-start.6 = (bf16[128]{0:T(256)(128)(2,1)S(1)}, bf16[128]{0:T(256)(128)(2,1)}, u32[]{:S(2)}) copy-start(bf16[128]{0:T(256)(128)(2,1)} %param.23) | copy-start | bytes 772
  1.7 7.7 %collective-permute-start.1 = (f32[8,1024]{1,0:T(8,128)S(1)}, f32[8,1024]{1,0:T(8,128)S(1)}, u32[]{:S(2)}, u32[]{:S(2)}) collective-permute-start(f32[8,1024]{1,0:T(8,128)S(1)} %select_select_fusion.pk), channel_id=1, source_target_pairs={{1,2},{2,1},{3,4},{4,3},{5,6},{6,5},{7,0},{0,7},{9,10},{10,9},{11,... | collective-permute-start | bytes 98312 | tf_op jit(solution)/shard_map/ppermute | solution.py:712
  6.2 3.1 %collective-permute-start = (f32[8,1024]{1,0:T(8,128)S(1)}, f32[8,1024]{1,0:T(8,128)S(1)}, u32[]{:S(2)}, u32[]{:S(2)}) collective-permute-start(f32[8,1024]{1,0:T(8,128)S(1)} %select_select_fusion.pk), channel_id=1, source_target_pairs={{0,1},{1,0},{2,3},{3,2},{4,5},{5,4},{6,7},{7,6},{8,9},{9,8},{10,11... | collective-permute-start | bytes 98312 | tf_op jit(solution)/shard_map/ppermute | solution.py:712
  11.6 7.1 %collective-permute-start.3 = (bf16[128,256]{1,0:T(8,128)(2,1)S(1)}, bf16[128,256]{1,0:T(8,128)(2,1)S(1)}, u32[]{:S(2)}, u32[]{:S(2)}) collective-permute-start(bf16[128,256]{1,0:T(8,128)(2,1)S(1)} %get-tuple-element.62), channel_id=1, source_target_pairs={{0,1},{1,0},{2,3},{3,2},{4,5},{5,4},{6,7},{7,6},{8,9},{9,8},{10,11... | collective-permute-start | bytes 196616 | tf_op jit(solution)/shard_map/ppermute | solution.py:712
  12.2 6.6 %collective-permute-start.4 = (bf16[128,256]{1,0:T(8,128)(2,1)S(1)}, bf16[128,256]{1,0:T(8,128)(2,1)S(1)}, u32[]{:S(2)}, u32[]{:S(2)}) collective-permute-start(bf16[128,256]{1,0:T(8,128)(2,1)S(1)} %get-tuple-element.63), channel_id=1, source_target_pairs={{1,2},{2,1},{3,4},{4,3},{5,6},{6,5},{7,0},{0,7},{9,10},{10,9},{11,... | collective-permute-start | bytes 196616 | tf_op jit(solution)/shard_map/ppermute | solution.py:712
  17.2 9.0 %collective-permute-start.2 = (f32[8,1024]{1,0:T(8,128)S(1)}, f32[8,1024]{1,0:T(8,128)S(1)}, u32[]{:S(2)}, u32[]{:S(2)}) collective-permute-start(f32[8,1024]{1,0:T(8,128)S(1)} %get-tuple-element.61), channel_id=1, source_target_pairs={{0,8},{8,0},{16,24},{24,16},{9,17},{17,9},{25,1},{1,25},{2,10},{10... | collective-permute-start | bytes 98312 | tf_op jit(solution)/shard_map/ppermute | solution.py:795
  20.1 6.2 %collective-permute-start.6 = (bf16[128,256]{1,0:T(8,128)(2,1)S(1)}, bf16[128,256]{1,0:T(8,128)(2,1)S(1)}, u32[]{:S(2)}, u32[]{:S(2)}) collective-permute-start(bf16[128,256]{1,0:T(8,128)(2,1)S(1)} %get-tuple-element.74), channel_id=1, source_target_pairs={{0,1},{1,0},{2,3},{3,2},{4,5},{5,4},{6,7},{7,6},{8,9},{9,8},{10,11... | collective-permute-start | bytes 196616 | tf_op jit(solution)/shard_map/ppermute | solution.py:712
  20.2 6.2 %collective-permute-start.7 = (bf16[128,256]{1,0:T(8,128)(2,1)S(1)}, bf16[128,256]{1,0:T(8,128)(2,1)S(1)}, u32[]{:S(2)}, u32[]{:S(2)}) collective-permute-start(bf16[128,256]{1,0:T(8,128)(2,1)S(1)} %get-tuple-element.75), channel_id=1, source_target_pairs={{1,2},{2,1},{3,4},{4,3},{5,6},{6,5},{7,0},{0,7},{9,10},{10,9},{11,... | collective-permute-start | bytes 196616 | tf_op jit(solution)/shard_map/ppermute | solution.py:712
  26.3 1.3 %collective-permute-start.5 = (f32[8,1024]{1,0:T(8,128)S(1)}, f32[8,1024]{1,0:T(8,128)S(1)}, u32[]{:S(2)}, u32[]{:S(2)}) collective-permute-start(f32[8,1024]{1,0:T(8,128)S(1)} %shard_map.138), channel_id=1, source_target_pairs={{0,1},{1,0},{2,3},{3,2},{4,5},{5,4},{6,7},{7,6},{8,9},{9,8},{10,11... | collective-permute-start | bytes 98312 | tf_op jit(solution)/shard_map/ppermute | solution.py:712
  27.7 1.2 %collective-permute-start.8 = (f32[8,128]{1,0:T(8,128)S(1)}, f32[8,128]{1,0:T(8,128)S(1)}, u32[]{:S(2)}, u32[]{:S(2)}) collective-permute-start(f32[8,128]{1,0:T(8,128)S(1)} %get-tuple-element.79.mine), channel_id=1, source_target_pairs={{0,1},{1,0},{2,3},{3,2},{4,5},{5,4},{6,7},{7,6},{8,9},{9,8},{10,11... | collective-permute-start | bytes 12296 | tf_op jit(solution)/shard_map/ppermute | solution.py:712
  28.9 3.6 %collective-permute-start.9 = (f32[8,128]{1,0:T(8,128)S(1)}, f32[8,128]{1,0:T(8,128)S(1)}, u32[]{:S(2)}, u32[]{:S(2)}) collective-permute-start(f32[8,128]{1,0:T(8,128)S(1)} %shard_map.141.rest_0_), channel_id=1, source_target_pairs={{0,2},{1,7},{2,0},{3,5},{4,6},{5,3},{6,4},{7,1},{8,10},{9,15},{10,... | collective-permute-start | bytes 12296 | tf_op jit(solution)/shard_map/ppermute | solution.py:824
  28.9 4.5 %collective-permute-start.10 = (f32[8,128]{1,0:T(8,128)S(1)}, f32[8,128]{1,0:T(8,128)S(1)}, u32[]{:S(2)}, u32[]{:S(2)}) collective-permute-start(f32[8,128]{1,0:T(8,128)S(1)} %shard_map.141.rest_0_), channel_id=1, source_target_pairs={{0,4},{1,5},{2,6},{3,7},{4,0},{5,1},{6,2},{7,3},{8,12},{9,13},{10,... | collective-permute-start | bytes 12296 | tf_op jit(solution)/shard_map/ppermute | solution.py:825
  32.5 1.6 %collective-permute-start.11 = (f32[8,128]{1,0:T(8,128)S(1)}, f32[8,128]{1,0:T(8,128)S(1)}, u32[]{:S(2)}, u32[]{:S(2)}) collective-permute-start(f32[8,128]{1,0:T(8,128)S(1)} %collective-permute-done.9.rest_1_), channel_id=1, source_target_pairs={{0,1},{1,0},{2,3},{3,2},{4,5},{5,4},{6,7},{7,6},{8,9},{9,8},{10,11... | collective-permute-start | bytes 12296 | tf_op jit(solution)/shard_map/ppermute | solution.py:712

commit v8 on v7

--- a/solution.py
+++ b/solution.py
@@ -364,7 +364,7 @@
     return [(0, 0, 0), (1, blocks - 1, (blocks - 1) * width)]
 
 
-def first_outer(width, pk, own_table, seated, mate, cross, edges, owns, depth, embed_t, first, first_rest, spread, mix_half, inner, delta_out, basis_out, place_out, feats_out, to_mate, to_cross, pair_out, table, kinds, hid):
+def first_outer(width, pk, own_table, seated, mate, cross, edges, owns, depth, embed_t, first, first_rest, spread, mix_half, inner, delta_out, basis_out, place_out, feats_out, to_cross, pair_out, table, kinds, hid):
     core = core_index()
     atoms = pk.shape[1]
     blocks = atoms // width
@@ -401,7 +401,6 @@
 
     by_depth(depth, fan, run)
     pack_halo(feats_out, own_table, core * width, width, to_cross)
-    pack_halo(feats_out, own_table, (1 - core) * width, width, to_mate)
 
 
 class Places:
@@ -427,12 +426,13 @@
     return hid[pl.ds(s * units, units), :]
 
 
-def layer_inner(width, layer, owns, depth, spreads, outs_t, mixes, feats, basis, place, basis_edge, place_edge, pair, feats_out, field_edge, total_edge, lent_edge, pair_out, hid):
+def layer_inner(width, layer, owns, depth, spreads, outs_t, mixes, feats, basis, place, basis_edge, place_edge, pair, own_table, feats_out, field_edge, total_edge, lent_edge, pair_out, to_mate, hid):
     spread, out_t, mix_half = spreads.at[layer], outs_t[layer], mixes[layer]
     chans, units = out_t.shape
     fan = place.shape[1]
     inner = place.shape[0]
     pair_out[...] = pair[...]
+    pack_halo(feats, own_table, (1 - core_index()) * width, width, to_mate)
 
     def run(rows):
         first = spill_from(rows, fan)
@@ -596,7 +596,7 @@
     return jnp.sum(total, axis=0, keepdims=True)
 
 
-def head_outer(width, own_table, owns, depth, place, delta, mate, cross, field_edge, pair_edge, inner, force_out, pairs):
+def head_outer(width, own_table, owns, depth, place, delta, cross, mate, field_edge, pair_edge, inner, force_out, pairs):
     core = core_index()
     chans = mate.shape[0]
     atoms = own_table.shape[1]
@@ -765,36 +765,37 @@
         [hid_scratch],
         flops=2**32,
     )
-    delta_out, basis_out, place_out, feats, to_mate, to_cross, pair = call(
+    delta_out, basis_out, place_out, feats, to_cross, pair = call(
         functools.partial(first_outer, width),
         (pk, own_table, seated, mate, cross, edges, owns, depth, embed_t, first, first_rest, spread, mix_half, inner),
-        block_outs(2) + [feats_type, halo_type, halo_type, pack_type],
+        block_outs(2) + [feats_type, halo_type, pack_type],
         [((PACK_ROWS, atoms + 2 * width), F32), ((2, fan, width), F32), hid_type],
     )
     for layer in range(1, layers):
         cross = swap(to_cross, 1)
-        mate = swap(to_mate, 0)
-        inner, field_edge, total_edge, lent_edge, pair = call(
+        inner, field_edge, total_edge, lent_edge, pair, to_mate = call(
             functools.partial(layer_inner, width, layer),
-            (owns, depth, spread, out_t, mix_half, feats, basis_in, place_in, basis_out, place_out, pair),
+            (owns, depth, spread, out_t, mix_half, feats, basis_in, place_in, basis_out, place_out, pair, own_table),
             [
                 ((chans, inner_atoms), BF16),
                 ((2, fan, chans, width), F32),
                 ((2, chans, width), F32),
                 ((2, chans, LANES), F32),
                 pack_type,
+                halo_type,
             ],
             [((blocks, fan * units, width), BF16)],
             flops=2**32,
         )
+        mate = swap(to_mate, 0)
         feats, to_mate, to_cross = call(
             functools.partial(layer_outer, width, layer),
             (own_table, owns, depth, mix_half, feats, place_out, mate, cross, field_edge, total_edge, lent_edge, inner),
             [feats_type, halo_type, halo_type],
         )
     received = lax.ppermute(pair, ("img", "atom"), image_pairs(images, tiles))
+    mate = swap(to_mate, 0)
     cross = swap(to_cross, 1)
-    mate = swap(to_mate, 0)
     inner, field_edge, pair_edge = call(
         functools.partial(head_inner, width, layers),
         (own_table, owns, depth, spread, out_t, feats, basis_in, place_in, delta_in, basis_out, place_out),
@@ -806,7 +807,7 @@
     relayed = swap(late, 0)
     (force,) = call(
         functools.partial(head_outer, width),
-        (own_table, owns, depth, place_out, delta_out, mate, cross, field_edge, pair_edge, inner),
+        (own_table, owns, depth, place_out, delta_out, cross, mate, field_edge, pair_edge, inner),
         [pack_type],
         [((2, fan, width), F32)],
         flops=2**32,

time: 35.1 us -> 35 us (level)
  waiting for transfers between devices: 3.59 us -> 3.17 us
    ppermute x9, waiting for transfers between devices: 2.17 us -> 1.27 us  [swap(): return lax.ppermute(block, 'atom', swap_pairs(tiles, offset))]
    ppermute x1, starting transfers between devices: 2.26 us -> 1.62 us  [on_device(): far = lax.ppermute(both, 'atom', [(i, i ^ 4) for i in range(tiles)])]
    ppermute x1, starting transfers between devices: 0.01 us -> 0.52 us  [on_device(): lax.ppermute(both, 'atom', [(i, i ^ 2 if i % 2 == 0 else i ^ 6) for i in...]
    ppermute x9, starting transfers between devices: 10.6 us -> 11 us  [swap(): return lax.ppermute(block, 'atom', swap_pairs(tiles, offset))]
  transfers between devices with their start and end apart: 12 -> 12, of which waited for: 5 -> 4; matrix products, arithmetic and copies ran while one was open for 0% -> 0% of each run, Pallas kernels for 34% -> 35%
where the time goes in v8:
time: 35 us; the launch traced here: 34.8 us
  Pallas kernels  15.2 us (43%)
  starting transfers between devices  14.7 us (42%)
  waiting for transfers between devices  3.17 us (9%)
  between operations  1.63 us (5%)
    pallas_call x12, Pallas kernels, call(): pl.pallas_call(body, out_shape=[jax.ShapeDtypeStruct(shape, dtype) for sh...  15.2 us
    ppermute x9, starting transfers between devices, swap(): return lax.ppermute(block, 'atom', swap_pairs(tiles, offset))  11 us
    ppermute x1, starting transfers between devices, on_device(): far = lax.ppermute(both, 'atom', [(i, i ^ 4) for i in range(tiles)])  1.62 us
    ppermute x1, starting transfers between devices, on_device(): received = lax.ppermute(pair, ('img', 'atom'), image_pairs(images, tiles))  1.55 us
    ppermute x1, waiting for transfers between devices, on_device(): lax.ppermute(both, 'atom', [(i, i ^ 2 if i % 2 == 0 else i ^ 6) for i in...  1.46 us
    ppermute x9, waiting for transfers between devices, swap(): return lax.ppermute(block, 'atom', swap_pairs(tiles, offset))  1.27 us
  transfers between devices with their start and end apart: 12, of which 4 were waited for; matrix products, arithmetic and copies ran while one was open for 0% of the time, Pallas kernels for 35%

profile of v8, /device:TPU:0, one launch (start us, length us, event | category | flops | bytes accessed | tf_op | source)
XLA Modules:
  0.0 34.8 jit_solution(4575236754545231002)
XLA Ops:
  0.7 0.0 copy-start.8
  0.7 0.0 copy-start.9
  0.7 0.0 copy-start.10
  0.7 0.0 copy-start.7
  1.5 0.1 select_select_fusion.pk
  1.6 0.0 copy-start.2
  1.6 0.0 copy-start.3
  1.7 0.0 copy-start.6
  1.7 4.6 %collective-permute-start.1 = (f32[8,1024]{1,0:T(8,128)S(1)}, f32[8,1024]{1,0:T(8,128)S(1)}, u32[]{:S(2)}, u32[]{:S(2)}) collective-permute-start(f32[8,1024]{1,0:T(8,128)S(1)} %select_select_fusion.pk), channel_id=1, source_target_pairs={{1,2},{2,1},{3,4},{4,3},{5,6},{6,5},{7,0},{0,7},{9,10},{10,9},{11,... | collective-permute-start | bytes 98312 | tf_op jit(solution)/shard_map/ppermute | solution.py:712
  6.2 1.4 %shard_map.132 = (f32[8,1024]{1,0:T(8,128)S(1)}, f32[8,1024]{1,0:T(8,128)S(1)}, f32[4,16,256]{2,1,0:T(8,128)S(1)}, f32[4,16,128]{2,1,0:T(8,128)S(1)}, f32[8,128]...) custom-call(f32[8,1024]{1,0:T(8,128)S(1)} %select_select_fusion.pk, ...), custom_call_target="tpu_custom_call" | custom-call | flops 4294967296 | bytes 1048576 | tf_op jit(solution)/shard_map/pallas_call | solution.py:701
  7.7 1.6 %shard_map.133 = (bf16[128,512]{1,0:T(8,128)(2,1)S(1)}, bf16[128,16]{1,0:T(8,128)(2,1)S(1)}, bf16[128,256]{1,0:T(8,128)(2,1)S(1)}, bf16[128,256]{1,0:T(8,128)(2,...) custom-call(f32[1,4]{1,0:T(1,128)S(1)} %bitcast.8, ...), custom_call_target="tpu_custom_call" | custom-call | flops 4294967296 | bytes 1048576 | tf_op jit(solution)/shard_map/pallas_call | solution.py:701
  9.4 2.2 %shard_map.134 = (f32[2,48,256]{2,1,0:T(8,128)S(1)}, bf16[2,128,256]{2,1,0:T(8,128)(2,1)S(1)}, f32[2,16,256]{2,1,0:T(8,128)S(1)}, bf16[128,1024]{1,0:T(8,128)(2,...) custom-call(f32[8,1024]{1,0:T(8,128)S(1)} %select_select_fusion.pk, ...), custom_call_target="tpu_custom_call" | custom-call | bytes 1048576 | tf_op jit(solution)/shard_map/pallas_call | solution.py:701
  11.6 2.1 %collective-permute-start.4 = (bf16[128,256]{1,0:T(8,128)(2,1)S(1)}, bf16[128,256]{1,0:T(8,128)(2,1)S(1)}, u32[]{:S(2)}, u32[]{:S(2)}) collective-permute-start(bf16[128,256]{1,0:T(8,128)(2,1)S(1)} %get-tuple-element.63), channel_id=1, source_target_pairs={{1,2},{2,1},{3,4},{4,3},{5,6},{6,5},{7,0},{0,7},{9,10},{10,9},{11,... | collective-permute-start | bytes 196616 | tf_op jit(solution)/shard_map/ppermute | solution.py:712
  13.6 3.6 %shard_map.135 = (bf16[128,512]{1,0:T(8,128)(2,1)S(1)}, f32[2,16,128,256]{3,2,1,0:T(8,128)S(1)}, f32[2,128,256]{2,1,0:T(8,128)S(1)}, f32[2,128,128]{2,1,0:T(8,12...) custom-call(f32[4,16,128]{2,1,0:T(8,128)S(1)} %get-tuple-element.42.owns, ...), custom_call_target="tpu_custom_call" | custom-call | flops 4294967296 | bytes 1048576 | tf_op jit(solution)/shard_map/pallas_call | solution.py:701
  17.2 0.1 collective-permute-start.3
  17.3 1.6 %collective-permute-start.2 = (f32[8,1024]{1,0:T(8,128)S(1)}, f32[8,1024]{1,0:T(8,128)S(1)}, u32[]{:S(2)}, u32[]{:S(2)}) collective-permute-start(f32[8,1024]{1,0:T(8,128)S(1)} %get-tuple-element.61), channel_id=1, source_target_pairs={{0,8},{8,0},{16,24},{24,16},{9,17},{17,9},{25,1},{1,25},{2,10},{10... | collective-permute-start | bytes 98312 | tf_op jit(solution)/shard_map/ppermute | solution.py:796
  18.8 1.3 %shard_map.136 = (bf16[128,1024]{1,0:T(8,128)(2,1)S(1)}, bf16[128,256]{1,0:T(8,128)(2,1)S(1)}, bf16[128,256]{1,0:T(8,128)(2,1)S(1)}) custom-call(f32[8,1024]{1,0:T(8,128)S(1)} %get-tuple-element.50.own_table, f32[4,16,128]{2,1,0:T(8,128)S(1)} %get-tuple-element.42.owns, f32[8,128]{1,0:T(8,128)S(1)} %get-tuple-element.43.depth, ...), custom_call_target="tpu_custom_call" | custom-call | bytes 1048576 | tf_op jit(solution)/shard_map/pallas_call | solution.py:701
  20.2 2.3 %collective-permute-start.6 = (bf16[128,256]{1,0:T(8,128)(2,1)S(1)}, bf16[128,256]{1,0:T(8,128)(2,1)S(1)}, u32[]{:S(2)}, u32[]{:S(2)}) collective-permute-start(bf16[128,256]{1,0:T(8,128)(2,1)S(1)} %get-tuple-element.74), channel_id=1, source_target_pairs={{1,2},{2,1},{3,4},{4,3},{5,6},{6,5},{7,0},{0,7},{9,10},{10,9},{11,... | collective-permute-start | bytes 196616 | tf_op jit(solution)/shard_map/ppermute | solution.py:712
  22.5 3.3 %shard_map.137 = (f32[8,512]{1,0:T(8,128)S(1)}, f32[2,16,128,256]{3,2,1,0:T(8,128)S(1)}, f32[2,16,256]{2,1,0:T(8,128)S(1)}) custom-call(f32[8,1024]{1,0:T(8,128)S(1)} %get-tuple-element.50.own_table, f32[4,16,128]{2,1,0:T(8,128)S(1)} %get-tuple-element.42.owns, f32[8,128]{1,0:T(8,128)S(1)} %get-tuple-element.43.depth, ...), custom_call_target="tpu_custom_call" | custom-call | flops 4294967296 | bytes 1048576 | tf_op jit(solution)/shard_map/pallas_call | solution.py:701
  25.8 0.6 %collective-permute-start.5 = (f32[8,1024]{1,0:T(8,128)S(1)}, f32[8,1024]{1,0:T(8,128)S(1)}, u32[]{:S(2)}, u32[]{:S(2)}) collective-permute-start(f32[8,1024]{1,0:T(8,128)S(1)} %shard_map.138), channel_id=1, source_target_pairs={{0,1},{1,0},{2,3},{3,2},{4,5},{5,4},{6,7},{7,6},{8,9},{9,8},{10,11... | collective-permute-start | bytes 98312 | tf_op jit(solution)/shard_map/ppermute | solution.py:712
  26.4 0.8 %shard_map.139.force_in.force = f32[8,1024]{1,0:T(8,128)S(1)} custom-call(f32[8,1024]{1,0:T(8,128)S(1)} %get-tuple-element.50.own_table, f32[4,16,128]{2,1,0:T(8,128)S(1)} %get-tuple-element.42.owns, f32[8,128]{1,0:T(8,128)S(1)} %get-tuple-element.43.depth, f32[2,16,256]{2,1,0:T(8,128)S(1)} %get-tuple-element.59.place_edge.place, ...), custom_call_target="tpu_custom_call" | custom-call | flops 4294967296 | bytes 1048576 | tf_op jit(solution)/shard_map/pallas_call | solution.py:701
  27.2 0.0 collective-permute-done.5.relayed
  27.2 0.2 shard_map.140
  27.4 0.4 %collective-permute-start.8 = (f32[8,128]{1,0:T(8,128)S(1)}, f32[8,128]{1,0:T(8,128)S(1)}, u32[]{:S(2)}, u32[]{:S(2)}) collective-permute-start(f32[8,128]{1,0:T(8,128)S(1)} %get-tuple-element.79.mine), channel_id=1, source_target_pairs={{0,1},{1,0},{2,3},{3,2},{4,5},{5,4},{6,7},{7,6},{8,9},{9,8},{10,11... | collective-permute-start | bytes 12296 | tf_op jit(solution)/shard_map/ppermute | solution.py:712
  27.8 0.8 %collective-permute-done.8.other = f32[8,128]{1,0:T(8,128)S(1)} collective-permute-done((f32[8,128]{1,0:T(8,128)S(1)}, f32[8,128]{1,0:T(8,128)S(1)}, u32[]{:S(2)}, u32[]{:S(2)}) %collective-permute-start.8) | collective-permute-done | bytes 4128 | tf_op jit(solution)/shard_map/ppermute | solution.py:712
  28.6 0.5 %collective-permute-start.9 = (f32[8,128]{1,0:T(8,128)S(1)}, f32[8,128]{1,0:T(8,128)S(1)}, u32[]{:S(2)}, u32[]{:S(2)}) collective-permute-start(f32[8,128]{1,0:T(8,128)S(1)} %shard_map.141.rest_0_), channel_id=1, source_target_pairs={{0,2},{1,7},{2,0},{3,5},{4,6},{5,3},{6,4},{7,1},{8,10},{9,15},{10,... | collective-permute-start | bytes 12296 | tf_op jit(solution)/shard_map/ppermute | solution.py:825
  29.2 1.6 %collective-permute-start.10 = (f32[8,128]{1,0:T(8,128)S(1)}, f32[8,128]{1,0:T(8,128)S(1)}, u32[]{:S(2)}, u32[]{:S(2)}) collective-permute-start(f32[8,128]{1,0:T(8,128)S(1)} %shard_map.141.rest_0_), channel_id=1, source_target_pairs={{0,4},{1,5},{2,6},{3,7},{4,0},{5,1},{6,2},{7,3},{8,12},{9,13},{10,... | collective-permute-start | bytes 12296 | tf_op jit(solution)/shard_map/ppermute | solution.py:826
  30.8 1.5 %collective-permute-done.9.rest_1_ = f32[8,128]{1,0:T(8,128)S(1)} collective-permute-done((f32[8,128]{1,0:T(8,128)S(1)}, f32[8,128]{1,0:T(8,128)S(1)}, u32[]{:S(2)}, u32[]{:S(2)}) %collective-permute-start.9) | collective-permute-done | bytes 4128 | tf_op jit(solution)/shard_map/ppermute | solution.py:825
  32.2 1.0 %collective-permute-start.11 = (f32[8,128]{1,0:T(8,128)S(1)}, f32[8,128]{1,0:T(8,128)S(1)}, u32[]{:S(2)}, u32[]{:S(2)}) collective-permute-start(f32[8,128]{1,0:T(8,128)S(1)} %collective-permute-done.9.rest_1_), channel_id=1, source_target_pairs={{0,1},{1,0},{2,3},{3,2},{4,5},{5,4},{6,7},{7,6},{8,9},{9,8},{10,11... | collective-permute-start | bytes 12296 | tf_op jit(solution)/shard_map/ppermute | solution.py:712
  33.2 0.4 %collective-permute-done.10.rest_2_ = f32[8,128]{1,0:T(8,128)S(1)} collective-permute-done((f32[8,128]{1,0:T(8,128)S(1)}, f32[8,128]{1,0:T(8,128)S(1)}, u32[]{:S(2)}, u32[]{:S(2)}) %collective-permute-start.10) | collective-permute-done | bytes 4128 | tf_op jit(solution)/shard_map/ppermute | solution.py:826
  33.7 0.4 %collective-permute-done.11.rest_3_ = f32[8,128]{1,0:T(8,128)S(1)} collective-permute-done((f32[8,128]{1,0:T(8,128)S(1)}, f32[8,128]{1,0:T(8,128)S(1)}, u32[]{:S(2)}, u32[]{:S(2)}) %collective-permute-start.11) | collective-permute-done | bytes 4128 | tf_op jit(solution)/shard_map/ppermute | solution.py:712
  34.1 0.8 %shard_map.142 = (f32[3,1,1024]{2,1,0:T(1,128)}, f32[1,1]{1,0:T(1,128)}) custom-call(f32[8,1024]{1,0:T(8,128)S(1)} %select_select_fusion.pk, f32[8,1024]{1,0:T(8,128)S(1)} %get-tuple-element.78.band, f32[8,1024]{1,0:T(8,128)S(1)} %shard_map.139.force_in.force, f32[8,128]{1,0:T(8,128)S(1)} %shard_map.141.rest_0_, ...), custom_call_target="tpu_custom_call" | custom-call | bytes 1048576 | tf_op jit(solution)/shard_map/pallas_call | solution.py:701
  (35 shorter events, 0.1 us)
Async XLA Ops:
  0.7 0.8 %copy-start.8 = (s32[1024]{0:T(1024)S(1)}, s32[1024]{0:T(1024)}, u32[]{:S(2)}) copy-start(s32[1024]{0:T(1024)} %param.13) | copy-start | bytes 12292
  0.7 0.8 %copy-start.9 = (s32[1024]{0:T(1024)S(1)}, s32[1024]{0:T(1024)}, u32[]{:S(2)}) copy-start(s32[1024]{0:T(1024)} %param.14) | copy-start | bytes 12292
  0.7 0.8 %copy-start.10 = (s32[512]{0:T(512)S(1)}, s32[512]{0:T(512)}, u32[]{:S(2)}) copy-start(s32[512]{0:T(512)} %param.16) | copy-start | bytes 6148
  0.7 0.8 %copy-start.7 = (f32[1,3,1024]{2,0,1:T(1,128)S(1)}, f32[1,3,1024]{2,0,1:T(1,128)}, u32[]{:S(2)}) copy-start(f32[1,3,1024]{2,0,1:T(1,128)} %param.12) | copy-start | bytes 36868
  0.7 5.5 %copy-start = (s32[16,1024]{1,0:T(8,128)S(1)}, s32[16,1024]{1,0:T(8,128)}, u32[]{:S(2)}) copy-start(s32[16,1024]{1,0:T(8,128)} %nbr.1) | copy-start | bytes 196612
  1.6 6.0 %copy-start.1 = (bf16[2,128,128]{2,1,0:T(8,128)(2,1)S(1)}, bf16[2,128,128]{2,1,0:T(8,128)(2,1)}, u32[]{:S(2)}) copy-start(bf16[2,128,128]{2,1,0:T(8,128)(2,1)} %mixing.1) | copy-start | bytes 196612
  1.6 6.0 %copy-start.2 = (bf16[3,64,128]{2,1,0:T(8,128)(2,1)S(1)}, bf16[3,64,128]{2,1,0:T(8,128)(2,1)}, u32[]{:S(2)}) copy-start(bf16[3,64,128]{2,1,0:T(8,128)(2,1)} %rad_out.1) | copy-start | bytes 147460
  1.6 6.0 %copy-start.3 = (bf16[3,8,64]{2,1,0:T(8,128)(2,1)S(1)}, bf16[3,8,64]{2,1,0:T(8,128)(2,1)}, u32[]{:S(2)}) copy-start(bf16[3,8,64]{2,1,0:T(8,128)(2,1)} %rad_in.1) | copy-start | bytes 9220
  1.6 6.0 %copy-start.4 = (bf16[4,128]{1,0:T(4,128)(2,1)S(1)}, bf16[4,128]{1,0:T(4,128)(2,1)}, u32[]{:S(2)}) copy-start(bf16[4,128]{1,0:T(4,128)(2,1)} %embed.1) | copy-start | bytes 3076
  1.7 6.0 %copy-start.5 = (f32[4]{0:T(128)S(1)}, f32[4]{0:T(128)}, u32[]{:S(2)}) copy-start(f32[4]{0:T(128)} %param.19) | copy-start | bytes 52
  1.7 6.0 %copy-start.6 = (bf16[128]{0:T(256)(128)(2,1)S(1)}, bf16[128]{0:T(256)(128)(2,1)}, u32[]{:S(2)}) copy-start(bf16[128]{0:T(256)(128)(2,1)} %param.23) | copy-start | bytes 772
  1.7 7.7 %collective-permute-start.1 = (f32[8,1024]{1,0:T(8,128)S(1)}, f32[8,1024]{1,0:T(8,128)S(1)}, u32[]{:S(2)}, u32[]{:S(2)}) collective-permute-start(f32[8,1024]{1,0:T(8,128)S(1)} %select_select_fusion.pk), channel_id=1, source_target_pairs={{1,2},{2,1},{3,4},{4,3},{5,6},{6,5},{7,0},{0,7},{9,10},{10,9},{11,... | collective-permute-start | bytes 98312 | tf_op jit(solution)/shard_map/ppermute | solution.py:712
  6.2 3.1 %collective-permute-start = (f32[8,1024]{1,0:T(8,128)S(1)}, f32[8,1024]{1,0:T(8,128)S(1)}, u32[]{:S(2)}, u32[]{:S(2)}) collective-permute-start(f32[8,1024]{1,0:T(8,128)S(1)} %select_select_fusion.pk), channel_id=1, source_target_pairs={{0,1},{1,0},{2,3},{3,2},{4,5},{5,4},{6,7},{7,6},{8,9},{9,8},{10,11... | collective-permute-start | bytes 98312 | tf_op jit(solution)/shard_map/ppermute | solution.py:712
  11.6 7.3 %collective-permute-start.4 = (bf16[128,256]{1,0:T(8,128)(2,1)S(1)}, bf16[128,256]{1,0:T(8,128)(2,1)S(1)}, u32[]{:S(2)}, u32[]{:S(2)}) collective-permute-start(bf16[128,256]{1,0:T(8,128)(2,1)S(1)} %get-tuple-element.63), channel_id=1, source_target_pairs={{1,2},{2,1},{3,4},{4,3},{5,6},{6,5},{7,0},{0,7},{9,10},{10,9},{11,... | collective-permute-start | bytes 196616 | tf_op jit(solution)/shard_map/ppermute | solution.py:712
  17.2 1.6 %collective-permute-start.3 = (bf16[128,256]{1,0:T(8,128)(2,1)S(1)}, bf16[128,256]{1,0:T(8,128)(2,1)S(1)}, u32[]{:S(2)}, u32[]{:S(2)}) collective-permute-start(bf16[128,256]{1,0:T(8,128)(2,1)S(1)} %get-tuple-element.62), channel_id=1, source_target_pairs={{0,1},{1,0},{2,3},{3,2},{4,5},{5,4},{6,7},{7,6},{8,9},{9,8},{10,11... | collective-permute-start | bytes 196616 | tf_op jit(solution)/shard_map/ppermute | solution.py:712
  17.3 8.5 %collective-permute-start.2 = (f32[8,1024]{1,0:T(8,128)S(1)}, f32[8,1024]{1,0:T(8,128)S(1)}, u32[]{:S(2)}, u32[]{:S(2)}) collective-permute-start(f32[8,1024]{1,0:T(8,128)S(1)} %get-tuple-element.61), channel_id=1, source_target_pairs={{0,8},{8,0},{16,24},{24,16},{9,17},{17,9},{25,1},{1,25},{2,10},{10... | collective-permute-start | bytes 98312 | tf_op jit(solution)/shard_map/ppermute | solution.py:796
  20.2 6.2 %collective-permute-start.6 = (bf16[128,256]{1,0:T(8,128)(2,1)S(1)}, bf16[128,256]{1,0:T(8,128)(2,1)S(1)}, u32[]{:S(2)}, u32[]{:S(2)}) collective-permute-start(bf16[128,256]{1,0:T(8,128)(2,1)S(1)} %get-tuple-element.74), channel_id=1, source_target_pairs={{1,2},{2,1},{3,4},{4,3},{5,6},{6,5},{7,0},{0,7},{9,10},{10,9},{11,... | collective-permute-start | bytes 196616 | tf_op jit(solution)/shard_map/ppermute | solution.py:712
  22.5 3.9 %collective-permute-start.7 = (bf16[128,256]{1,0:T(8,128)(2,1)S(1)}, bf16[128,256]{1,0:T(8,128)(2,1)S(1)}, u32[]{:S(2)}, u32[]{:S(2)}) collective-permute-start(bf16[128,256]{1,0:T(8,128)(2,1)S(1)} %get-tuple-element.75), channel_id=1, source_target_pairs={{0,1},{1,0},{2,3},{3,2},{4,5},{5,4},{6,7},{7,6},{8,9},{9,8},{10,11... | collective-permute-start | bytes 196616 | tf_op jit(solution)/shard_map/ppermute | solution.py:712
  25.8 1.4 %collective-permute-start.5 = (f32[8,1024]{1,0:T(8,128)S(1)}, f32[8,1024]{1,0:T(8,128)S(1)}, u32[]{:S(2)}, u32[]{:S(2)}) collective-permute-start(f32[8,1024]{1,0:T(8,128)S(1)} %shard_map.138), channel_id=1, source_target_pairs={{0,1},{1,0},{2,3},{3,2},{4,5},{5,4},{6,7},{7,6},{8,9},{9,8},{10,11... | collective-permute-start | bytes 98312 | tf_op jit(solution)/shard_map/ppermute | solution.py:712
  27.4 1.2 %collective-permute-start.8 = (f32[8,128]{1,0:T(8,128)S(1)}, f32[8,128]{1,0:T(8,128)S(1)}, u32[]{:S(2)}, u32[]{:S(2)}) collective-permute-start(f32[8,128]{1,0:T(8,128)S(1)} %get-tuple-element.79.mine), channel_id=1, source_target_pairs={{0,1},{1,0},{2,3},{3,2},{4,5},{5,4},{6,7},{7,6},{8,9},{9,8},{10,11... | collective-permute-start | bytes 12296 | tf_op jit(solution)/shard_map/ppermute | solution.py:712
  28.6 3.6 %collective-permute-start.9 = (f32[8,128]{1,0:T(8,128)S(1)}, f32[8,128]{1,0:T(8,128)S(1)}, u32[]{:S(2)}, u32[]{:S(2)}) collective-permute-start(f32[8,128]{1,0:T(8,128)S(1)} %shard_map.141.rest_0_), channel_id=1, source_target_pairs={{0,2},{1,7},{2,0},{3,5},{4,6},{5,3},{6,4},{7,1},{8,10},{9,15},{10,... | collective-permute-start | bytes 12296 | tf_op jit(solution)/shard_map/ppermute | solution.py:825
  29.2 4.5 %collective-permute-start.10 = (f32[8,128]{1,0:T(8,128)S(1)}, f32[8,128]{1,0:T(8,128)S(1)}, u32[]{:S(2)}, u32[]{:S(2)}) collective-permute-start(f32[8,128]{1,0:T(8,128)S(1)} %shard_map.141.rest_0_), channel_id=1, source_target_pairs={{0,4},{1,5},{2,6},{3,7},{4,0},{5,1},{6,2},{7,3},{8,12},{9,13},{10,... | collective-permute-start | bytes 12296 | tf_op jit(solution)/shard_map/ppermute | solution.py:826
  32.2 1.8 %collective-permute-start.11 = (f32[8,128]{1,0:T(8,128)S(1)}, f32[8,128]{1,0:T(8,128)S(1)}, u32[]{:S(2)}, u32[]{:S(2)}) collective-permute-start(f32[8,128]{1,0:T(8,128)S(1)} %collective-permute-done.9.rest_1_), channel_id=1, source_target_pairs={{0,1},{1,0},{2,3},{3,2},{4,5},{5,4},{6,7},{7,6},{8,9},{9,8},{10,11... | collective-permute-start | bytes 12296 | tf_op jit(solution)/shard_map/ppermute | solution.py:712

commit v9 on v8

--- a/solution.py
+++ b/solution.py
@@ -18,6 +18,8 @@
 SEND_ROW = 5
 SEAT_ROW = 6
 CLIMB_ROW = 7
+CODE_ROW = 7
+KIND_STEP = 1024.0
 PACK_ROWS = 8
 SUM_ROWS = 8
 REDUCE_CHIPS = 4
@@ -166,9 +168,11 @@
             if part.start > 0:
                 here = jnp.where(mine, here, home[c : c + 1, :LANES])
             values.append(fetch(c) - here)
-        values.append(jnp.where(live, fetch(SPECIES_ROW), -1.0))
+        code = fetch(CODE_ROW)
+        seat = jnp.floor(code * (1.0 / KIND_STEP))
+        values.append(jnp.where(live, code - seat * KIND_STEP, -1.0))
         tile = (rel // width).astype(F32) * float(width)
-        values.append(jnp.where(live, fetch(SEAT_ROW) + tile, -1.0))
+        values.append(jnp.where(live, seat + tile, -1.0))
         parts.append(values)
     joined = [jnp.concatenate(list(piece), axis=1) for piece in zip(*parts)]
     for c in range(3):
@@ -307,7 +311,9 @@
         limit = jnp.where(most <= float(2 * rows), float(rows), limit)
     depth[...] = jnp.broadcast_to(limit, depth.shape)
     for b, (seat, pieces, counts) in enumerate(found):
-        table[SEAT_ROW : SEAT_ROW + 1, b * width : (b + 1) * width] = seat
+        here = slice(b * width, (b + 1) * width)
+        table[SEAT_ROW : SEAT_ROW + 1, here] = seat
+        table[CODE_ROW : CODE_ROW + 1, here] = seat * KIND_STEP + pk[SPECIES_ROW : SPECIES_ROW + 1, here]
         edges[b], owns[b] = fill_rows(pieces, counts, limit)
     for part in halves(2 * width):
         wanted = jnp.broadcast_to(pk[SEND_ROW : SEND_ROW + 1, part].astype(I32), (PACK_ROWS, LANES))
@@ -380,7 +386,8 @@
             place = pl.ds(aligned(at + k * LANES, LANES), LANES)
             table[:, place] = lane_lookup(spans, wanted)
             lane = lax.broadcasted_iota(I32, (1, LANES), 1) + k * LANES
-            table[SEAT_ROW : SEAT_ROW + 1, place] = lane.astype(F32)
+            kind = table[SPECIES_ROW : SPECIES_ROW + 1, place]
+            table[CODE_ROW : CODE_ROW + 1, place] = lane.astype(F32) * KIND_STEP + kind
     feats_out[:, width : atoms - width] = inner[...]
     pair_out[0:4, :] = pk[0:4, :]
     pair_out[4:8, :] = mate[0:4, :]

time: 35 us -> 34.9 us (level)
  transfers between devices with their start and end apart: 12 -> 12, of which waited for: 4 -> 4; matrix products, arithmetic and copies ran while one was open for 0% -> 0% of each run, Pallas kernels for 35% -> 34%
where the time goes in v9:
time: 34.9 us; the launch traced here: 34.7 us
  Pallas kernels  15 us (43%)
  starting transfers between devices  14.7 us (42%)
  waiting for transfers between devices  3.12 us (9%)
  between operations  1.64 us (5%)
    pallas_call x12, Pallas kernels, call(): pl.pallas_call(body, out_shape=[jax.ShapeDtypeStruct(shape, dtype) for sh...  15 us
    ppermute x9, starting transfers between devices, swap(): return lax.ppermute(block, 'atom', swap_pairs(tiles, offset))  10.9 us
    ppermute x1, starting transfers between devices, on_device(): far = lax.ppermute(both, 'atom', [(i, i ^ 4) for i in range(tiles)])  1.58 us
    ppermute x1, starting transfers between devices, on_device(): received = lax.ppermute(pair, ('img', 'atom'), image_pairs(images, tiles))  1.56 us
    ppermute x1, waiting for transfers between devices, on_device(): lax.ppermute(both, 'atom', [(i, i ^ 2 if i % 2 == 0 else i ^ 6) for i in...  1.41 us
    ppermute x9, waiting for transfers between devices, swap(): return lax.ppermute(block, 'atom', swap_pairs(tiles, offset))  1.19 us
  transfers between devices with their start and end apart: 12, of which 4 were waited for; matrix products, arithmetic and copies ran while one was open for 0% of the time, Pallas kernels for 34%

profile of v9, /device:TPU:0, one launch (start us, length us, event | category | flops | bytes accessed | tf_op | source)
XLA Modules:
  0.0 34.7 jit_solution(866048642000748919)
XLA Ops:
  0.7 0.0 copy-start.8
  0.7 0.0 copy-start.9
  0.7 0.0 copy-start.10
  0.7 0.0 copy-start.7
  1.5 0.1 select_select_fusion.pk
  1.6 0.0 copy-start.2
  1.6 0.0 copy-start.3
  1.7 0.0 copy-start.6
  1.7 4.6 %collective-permute-start.1 = (f32[8,1024]{1,0:T(8,128)S(1)}, f32[8,1024]{1,0:T(8,128)S(1)}, u32[]{:S(2)}, u32[]{:S(2)}) collective-permute-start(f32[8,1024]{1,0:T(8,128)S(1)} %select_select_fusion.pk), channel_id=1, source_target_pairs={{1,2},{2,1},{3,4},{4,3},{5,6},{6,5},{7,0},{0,7},{9,10},{10,9},{11,... | collective-permute-start | bytes 98312 | tf_op jit(solution)/shard_map/ppermute | solution.py:719
  6.2 1.3 %shard_map.132 = (f32[8,1024]{1,0:T(8,128)S(1)}, f32[8,1024]{1,0:T(8,128)S(1)}, f32[4,16,256]{2,1,0:T(8,128)S(1)}, f32[4,16,128]{2,1,0:T(8,128)S(1)}, f32[8,128]...) custom-call(f32[8,1024]{1,0:T(8,128)S(1)} %select_select_fusion.pk, ...), custom_call_target="tpu_custom_call" | custom-call | flops 4294967296 | bytes 1048576 | tf_op jit(solution)/shard_map/pallas_call | solution.py:708
  7.6 1.7 %shard_map.133 = (bf16[128,512]{1,0:T(8,128)(2,1)S(1)}, bf16[128,16]{1,0:T(8,128)(2,1)S(1)}, bf16[128,256]{1,0:T(8,128)(2,1)S(1)}, bf16[128,256]{1,0:T(8,128)(2,...) custom-call(f32[1,4]{1,0:T(1,128)S(1)} %bitcast.8, ...), custom_call_target="tpu_custom_call" | custom-call | flops 4294967296 | bytes 1048576 | tf_op jit(solution)/shard_map/pallas_call | solution.py:708
  9.3 2.1 %shard_map.134 = (f32[2,48,256]{2,1,0:T(8,128)S(1)}, bf16[2,128,256]{2,1,0:T(8,128)(2,1)S(1)}, f32[2,16,256]{2,1,0:T(8,128)S(1)}, bf16[128,1024]{1,0:T(8,128)(2,...) custom-call(f32[8,1024]{1,0:T(8,128)S(1)} %select_select_fusion.pk, ...), custom_call_target="tpu_custom_call" | custom-call | bytes 1048576 | tf_op jit(solution)/shard_map/pallas_call | solution.py:708
  11.4 2.2 %collective-permute-start.4 = (bf16[128,256]{1,0:T(8,128)(2,1)S(1)}, bf16[128,256]{1,0:T(8,128)(2,1)S(1)}, u32[]{:S(2)}, u32[]{:S(2)}) collective-permute-start(bf16[128,256]{1,0:T(8,128)(2,1)S(1)} %get-tuple-element.63), channel_id=1, source_target_pairs={{1,2},{2,1},{3,4},{4,3},{5,6},{6,5},{7,0},{0,7},{9,10},{10,9},{11,... | collective-permute-start | bytes 196616 | tf_op jit(solution)/shard_map/ppermute | solution.py:719
  13.6 3.6 %shard_map.135 = (bf16[128,512]{1,0:T(8,128)(2,1)S(1)}, f32[2,16,128,256]{3,2,1,0:T(8,128)S(1)}, f32[2,128,256]{2,1,0:T(8,128)S(1)}, f32[2,128,128]{2,1,0:T(8,12...) custom-call(f32[4,16,128]{2,1,0:T(8,128)S(1)} %get-tuple-element.42.owns, ...), custom_call_target="tpu_custom_call" | custom-call | flops 4294967296 | bytes 1048576 | tf_op jit(solution)/shard_map/pallas_call | solution.py:708
  17.1 0.1 collective-permute-start.3
  17.2 1.6 %collective-permute-start.2 = (f32[8,1024]{1,0:T(8,128)S(1)}, f32[8,1024]{1,0:T(8,128)S(1)}, u32[]{:S(2)}, u32[]{:S(2)}) collective-permute-start(f32[8,1024]{1,0:T(8,128)S(1)} %get-tuple-element.61), channel_id=1, source_target_pairs={{0,8},{8,0},{16,24},{24,16},{9,17},{17,9},{25,1},{1,25},{2,10},{10... | collective-permute-start | bytes 98312 | tf_op jit(solution)/shard_map/ppermute | solution.py:803
  18.8 1.3 %shard_map.136 = (bf16[128,1024]{1,0:T(8,128)(2,1)S(1)}, bf16[128,256]{1,0:T(8,128)(2,1)S(1)}, bf16[128,256]{1,0:T(8,128)(2,1)S(1)}) custom-call(f32[8,1024]{1,0:T(8,128)S(1)} %get-tuple-element.50.own_table, f32[4,16,128]{2,1,0:T(8,128)S(1)} %get-tuple-element.42.owns, f32[8,128]{1,0:T(8,128)S(1)} %get-tuple-element.43.depth, ...), custom_call_target="tpu_custom_call" | custom-call | bytes 1048576 | tf_op jit(solution)/shard_map/pallas_call | solution.py:708
  20.1 2.2 %collective-permute-start.6 = (bf16[128,256]{1,0:T(8,128)(2,1)S(1)}, bf16[128,256]{1,0:T(8,128)(2,1)S(1)}, u32[]{:S(2)}, u32[]{:S(2)}) collective-permute-start(bf16[128,256]{1,0:T(8,128)(2,1)S(1)} %get-tuple-element.74), channel_id=1, source_target_pairs={{1,2},{2,1},{3,4},{4,3},{5,6},{6,5},{7,0},{0,7},{9,10},{10,9},{11,... | collective-permute-start | bytes 196616 | tf_op jit(solution)/shard_map/ppermute | solution.py:719
  22.3 3.3 %shard_map.137 = (f32[8,512]{1,0:T(8,128)S(1)}, f32[2,16,128,256]{3,2,1,0:T(8,128)S(1)}, f32[2,16,256]{2,1,0:T(8,128)S(1)}) custom-call(f32[8,1024]{1,0:T(8,128)S(1)} %get-tuple-element.50.own_table, f32[4,16,128]{2,1,0:T(8,128)S(1)} %get-tuple-element.42.owns, f32[8,128]{1,0:T(8,128)S(1)} %get-tuple-element.43.depth, ...), custom_call_target="tpu_custom_call" | custom-call | flops 4294967296 | bytes 1048576 | tf_op jit(solution)/shard_map/pallas_call | solution.py:708
  25.7 0.6 %collective-permute-start.5 = (f32[8,1024]{1,0:T(8,128)S(1)}, f32[8,1024]{1,0:T(8,128)S(1)}, u32[]{:S(2)}, u32[]{:S(2)}) collective-permute-start(f32[8,1024]{1,0:T(8,128)S(1)} %shard_map.138), channel_id=1, source_target_pairs={{0,1},{1,0},{2,3},{3,2},{4,5},{5,4},{6,7},{7,6},{8,9},{9,8},{10,11... | collective-permute-start | bytes 98312 | tf_op jit(solution)/shard_map/ppermute | solution.py:719
  26.2 0.8 %shard_map.139.force_in.force = f32[8,1024]{1,0:T(8,128)S(1)} custom-call(f32[8,1024]{1,0:T(8,128)S(1)} %get-tuple-element.50.own_table, f32[4,16,128]{2,1,0:T(8,128)S(1)} %get-tuple-element.42.owns, f32[8,128]{1,0:T(8,128)S(1)} %get-tuple-element.43.depth, f32[2,16,256]{2,1,0:T(8,128)S(1)} %get-tuple-element.59.place_edge.place, ...), custom_call_target="tpu_custom_call" | custom-call | flops 4294967296 | bytes 1048576 | tf_op jit(solution)/shard_map/pallas_call | solution.py:708
  27.0 0.0 collective-permute-done.5.relayed
  27.1 0.2 shard_map.140
  27.3 0.4 %collective-permute-start.8 = (f32[8,128]{1,0:T(8,128)S(1)}, f32[8,128]{1,0:T(8,128)S(1)}, u32[]{:S(2)}, u32[]{:S(2)}) collective-permute-start(f32[8,128]{1,0:T(8,128)S(1)} %get-tuple-element.79.mine), channel_id=1, source_target_pairs={{0,1},{1,0},{2,3},{3,2},{4,5},{5,4},{6,7},{7,6},{8,9},{9,8},{10,11... | collective-permute-start | bytes 12296 | tf_op jit(solution)/shard_map/ppermute | solution.py:719
  27.7 0.8 %collective-permute-done.8.other = f32[8,128]{1,0:T(8,128)S(1)} collective-permute-done((f32[8,128]{1,0:T(8,128)S(1)}, f32[8,128]{1,0:T(8,128)S(1)}, u32[]{:S(2)}, u32[]{:S(2)}) %collective-permute-start.8) | collective-permute-done | bytes 4128 | tf_op jit(solution)/shard_map/ppermute | solution.py:719
  28.5 0.6 %collective-permute-start.9 = (f32[8,128]{1,0:T(8,128)S(1)}, f32[8,128]{1,0:T(8,128)S(1)}, u32[]{:S(2)}, u32[]{:S(2)}) collective-permute-start(f32[8,128]{1,0:T(8,128)S(1)} %shard_map.141.rest_0_), channel_id=1, source_target_pairs={{0,2},{1,7},{2,0},{3,5},{4,6},{5,3},{6,4},{7,1},{8,10},{9,15},{10,... | collective-permute-start | bytes 12296 | tf_op jit(solution)/shard_map/ppermute | solution.py:832
  29.1 1.6 %collective-permute-start.10 = (f32[8,128]{1,0:T(8,128)S(1)}, f32[8,128]{1,0:T(8,128)S(1)}, u32[]{:S(2)}, u32[]{:S(2)}) collective-permute-start(f32[8,128]{1,0:T(8,128)S(1)} %shard_map.141.rest_0_), channel_id=1, source_target_pairs={{0,4},{1,5},{2,6},{3,7},{4,0},{5,1},{6,2},{7,3},{8,12},{9,13},{10,... | collective-permute-start | bytes 12296 | tf_op jit(solution)/shard_map/ppermute | solution.py:833
  30.7 1.4 %collective-permute-done.9.rest_1_ = f32[8,128]{1,0:T(8,128)S(1)} collective-permute-done((f32[8,128]{1,0:T(8,128)S(1)}, f32[8,128]{1,0:T(8,128)S(1)}, u32[]{:S(2)}, u32[]{:S(2)}) %collective-permute-start.9) | collective-permute-done | bytes 4128 | tf_op jit(solution)/shard_map/ppermute | solution.py:832
  32.1 1.0 %collective-permute-start.11 = (f32[8,128]{1,0:T(8,128)S(1)}, f32[8,128]{1,0:T(8,128)S(1)}, u32[]{:S(2)}, u32[]{:S(2)}) collective-permute-start(f32[8,128]{1,0:T(8,128)S(1)} %collective-permute-done.9.rest_1_), channel_id=1, source_target_pairs={{0,1},{1,0},{2,3},{3,2},{4,5},{5,4},{6,7},{7,6},{8,9},{9,8},{10,11... | collective-permute-start | bytes 12296 | tf_op jit(solution)/shard_map/ppermute | solution.py:719
  33.1 0.5 %collective-permute-done.10.rest_2_ = f32[8,128]{1,0:T(8,128)S(1)} collective-permute-done((f32[8,128]{1,0:T(8,128)S(1)}, f32[8,128]{1,0:T(8,128)S(1)}, u32[]{:S(2)}, u32[]{:S(2)}) %collective-permute-start.10) | collective-permute-done | bytes 4128 | tf_op jit(solution)/shard_map/ppermute | solution.py:833
  33.6 0.3 collective-permute-done.11.rest_3_
  33.9 0.8 %shard_map.142 = (f32[3,1,1024]{2,1,0:T(1,128)}, f32[1,1]{1,0:T(1,128)}) custom-call(f32[8,1024]{1,0:T(8,128)S(1)} %select_select_fusion.pk, f32[8,1024]{1,0:T(8,128)S(1)} %get-tuple-element.78.band, f32[8,1024]{1,0:T(8,128)S(1)} %shard_map.139.force_in.force, f32[8,128]{1,0:T(8,128)S(1)} %shard_map.141.rest_0_, ...), custom_call_target="tpu_custom_call" | custom-call | bytes 1048576 | tf_op jit(solution)/shard_map/pallas_call | solution.py:708
  (35 shorter events, 0.1 us)
Async XLA Ops:
  0.7 0.8 %copy-start.8 = (s32[1024]{0:T(1024)S(1)}, s32[1024]{0:T(1024)}, u32[]{:S(2)}) copy-start(s32[1024]{0:T(1024)} %param.13) | copy-start | bytes 12292
  0.7 0.8 %copy-start.9 = (s32[1024]{0:T(1024)S(1)}, s32[1024]{0:T(1024)}, u32[]{:S(2)}) copy-start(s32[1024]{0:T(1024)} %param.14) | copy-start | bytes 12292
  0.7 0.8 %copy-start.10 = (s32[512]{0:T(512)S(1)}, s32[512]{0:T(512)}, u32[]{:S(2)}) copy-start(s32[512]{0:T(512)} %param.16) | copy-start | bytes 6148
  0.7 0.8 %copy-start.7 = (f32[1,3,1024]{2,0,1:T(1,128)S(1)}, f32[1,3,1024]{2,0,1:T(1,128)}, u32[]{:S(2)}) copy-start(f32[1,3,1024]{2,0,1:T(1,128)} %param.12) | copy-start | bytes 36868
  0.7 5.5 %copy-start = (s32[16,1024]{1,0:T(8,128)S(1)}, s32[16,1024]{1,0:T(8,128)}, u32[]{:S(2)}) copy-start(s32[16,1024]{1,0:T(8,128)} %nbr.1) | copy-start | bytes 196612
  1.6 5.9 %copy-start.1 = (bf16[2,128,128]{2,1,0:T(8,128)(2,1)S(1)}, bf16[2,128,128]{2,1,0:T(8,128)(2,1)}, u32[]{:S(2)}) copy-start(bf16[2,128,128]{2,1,0:T(8,128)(2,1)} %mixing.1) | copy-start | bytes 196612
  1.6 5.9 %copy-start.2 = (bf16[3,64,128]{2,1,0:T(8,128)(2,1)S(1)}, bf16[3,64,128]{2,1,0:T(8,128)(2,1)}, u32[]{:S(2)}) copy-start(bf16[3,64,128]{2,1,0:T(8,128)(2,1)} %rad_out.1) | copy-start | bytes 147460
  1.6 5.9 %copy-start.3 = (bf16[3,8,64]{2,1,0:T(8,128)(2,1)S(1)}, bf16[3,8,64]{2,1,0:T(8,128)(2,1)}, u32[]{:S(2)}) copy-start(bf16[3,8,64]{2,1,0:T(8,128)(2,1)} %rad_in.1) | copy-start | bytes 9220
  1.6 5.9 %copy-start.4 = (bf16[4,128]{1,0:T(4,128)(2,1)S(1)}, bf16[4,128]{1,0:T(4,128)(2,1)}, u32[]{:S(2)}) copy-start(bf16[4,128]{1,0:T(4,128)(2,1)} %embed.1) | copy-start | bytes 3076
  1.7 5.9 %copy-start.5 = (f32[4]{0:T(128)S(1)}, f32[4]{0:T(128)}, u32[]{:S(2)}) copy-start(f32[4]{0:T(128)} %param.19) | copy-start | bytes 52
  1.7 5.9 %copy-start.6 = (bf16[128]{0:T(256)(128)(2,1)S(1)}, bf16[128]{0:T(256)(128)(2,1)}, u32[]{:S(2)}) copy-start(bf16[128]{0:T(256)(128)(2,1)} %param.23) | copy-start | bytes 772
  1.7 7.6 %collective-permute-start.1 = (f32[8,1024]{1,0:T(8,128)S(1)}, f32[8,1024]{1,0:T(8,128)S(1)}, u32[]{:S(2)}, u32[]{:S(2)}) collective-permute-start(f32[8,1024]{1,0:T(8,128)S(1)} %select_select_fusion.pk), channel_id=1, source_target_pairs={{1,2},{2,1},{3,4},{4,3},{5,6},{6,5},{7,0},{0,7},{9,10},{10,9},{11,... | collective-permute-start | bytes 98312 | tf_op jit(solution)/shard_map/ppermute | solution.py:719
  6.2 3.0 %collective-permute-start = (f32[8,1024]{1,0:T(8,128)S(1)}, f32[8,1024]{1,0:T(8,128)S(1)}, u32[]{:S(2)}, u32[]{:S(2)}) collective-permute-start(f32[8,1024]{1,0:T(8,128)S(1)} %select_select_fusion.pk), channel_id=1, source_target_pairs={{0,1},{1,0},{2,3},{3,2},{4,5},{5,4},{6,7},{7,6},{8,9},{9,8},{10,11... | collective-permute-start | bytes 98312 | tf_op jit(solution)/shard_map/ppermute | solution.py:719
  11.4 7.4 %collective-permute-start.4 = (bf16[128,256]{1,0:T(8,128)(2,1)S(1)}, bf16[128,256]{1,0:T(8,128)(2,1)S(1)}, u32[]{:S(2)}, u32[]{:S(2)}) collective-permute-start(bf16[128,256]{1,0:T(8,128)(2,1)S(1)} %get-tuple-element.63), channel_id=1, source_target_pairs={{1,2},{2,1},{3,4},{4,3},{5,6},{6,5},{7,0},{0,7},{9,10},{10,9},{11,... | collective-permute-start | bytes 196616 | tf_op jit(solution)/shard_map/ppermute | solution.py:719
  17.1 1.6 %collective-permute-start.3 = (bf16[128,256]{1,0:T(8,128)(2,1)S(1)}, bf16[128,256]{1,0:T(8,128)(2,1)S(1)}, u32[]{:S(2)}, u32[]{:S(2)}) collective-permute-start(bf16[128,256]{1,0:T(8,128)(2,1)S(1)} %get-tuple-element.62), channel_id=1, source_target_pairs={{0,1},{1,0},{2,3},{3,2},{4,5},{5,4},{6,7},{7,6},{8,9},{9,8},{10,11... | collective-permute-start | bytes 196616 | tf_op jit(solution)/shard_map/ppermute | solution.py:719
  17.2 8.4 %collective-permute-start.2 = (f32[8,1024]{1,0:T(8,128)S(1)}, f32[8,1024]{1,0:T(8,128)S(1)}, u32[]{:S(2)}, u32[]{:S(2)}) collective-permute-start(f32[8,1024]{1,0:T(8,128)S(1)} %get-tuple-element.61), channel_id=1, source_target_pairs={{0,8},{8,0},{16,24},{24,16},{9,17},{17,9},{25,1},{1,25},{2,10},{10... | collective-permute-start | bytes 98312 | tf_op jit(solution)/shard_map/ppermute | solution.py:803
  20.1 6.1 %collective-permute-start.6 = (bf16[128,256]{1,0:T(8,128)(2,1)S(1)}, bf16[128,256]{1,0:T(8,128)(2,1)S(1)}, u32[]{:S(2)}, u32[]{:S(2)}) collective-permute-start(bf16[128,256]{1,0:T(8,128)(2,1)S(1)} %get-tuple-element.74), channel_id=1, source_target_pairs={{1,2},{2,1},{3,4},{4,3},{5,6},{6,5},{7,0},{0,7},{9,10},{10,9},{11,... | collective-permute-start | bytes 196616 | tf_op jit(solution)/shard_map/ppermute | solution.py:719
  22.3 3.9 %collective-permute-start.7 = (bf16[128,256]{1,0:T(8,128)(2,1)S(1)}, bf16[128,256]{1,0:T(8,128)(2,1)S(1)}, u32[]{:S(2)}, u32[]{:S(2)}) collective-permute-start(bf16[128,256]{1,0:T(8,128)(2,1)S(1)} %get-tuple-element.75), channel_id=1, source_target_pairs={{0,1},{1,0},{2,3},{3,2},{4,5},{5,4},{6,7},{7,6},{8,9},{9,8},{10,11... | collective-permute-start | bytes 196616 | tf_op jit(solution)/shard_map/ppermute | solution.py:719
  25.7 1.4 %collective-permute-start.5 = (f32[8,1024]{1,0:T(8,128)S(1)}, f32[8,1024]{1,0:T(8,128)S(1)}, u32[]{:S(2)}, u32[]{:S(2)}) collective-permute-start(f32[8,1024]{1,0:T(8,128)S(1)} %shard_map.138), channel_id=1, source_target_pairs={{0,1},{1,0},{2,3},{3,2},{4,5},{5,4},{6,7},{7,6},{8,9},{9,8},{10,11... | collective-permute-start | bytes 98312 | tf_op jit(solution)/shard_map/ppermute | solution.py:719
  27.3 1.2 %collective-permute-start.8 = (f32[8,128]{1,0:T(8,128)S(1)}, f32[8,128]{1,0:T(8,128)S(1)}, u32[]{:S(2)}, u32[]{:S(2)}) collective-permute-start(f32[8,128]{1,0:T(8,128)S(1)} %get-tuple-element.79.mine), channel_id=1, source_target_pairs={{0,1},{1,0},{2,3},{3,2},{4,5},{5,4},{6,7},{7,6},{8,9},{9,8},{10,11... | collective-permute-start | bytes 12296 | tf_op jit(solution)/shard_map/ppermute | solution.py:719
  28.5 3.6 %collective-permute-start.9 = (f32[8,128]{1,0:T(8,128)S(1)}, f32[8,128]{1,0:T(8,128)S(1)}, u32[]{:S(2)}, u32[]{:S(2)}) collective-permute-start(f32[8,128]{1,0:T(8,128)S(1)} %shard_map.141.rest_0_), channel_id=1, source_target_pairs={{0,2},{1,7},{2,0},{3,5},{4,6},{5,3},{6,4},{7,1},{8,10},{9,15},{10,... | collective-permute-start | bytes 12296 | tf_op jit(solution)/shard_map/ppermute | solution.py:832
  29.1 4.5 %collective-permute-start.10 = (f32[8,128]{1,0:T(8,128)S(1)}, f32[8,128]{1,0:T(8,128)S(1)}, u32[]{:S(2)}, u32[]{:S(2)}) collective-permute-start(f32[8,128]{1,0:T(8,128)S(1)} %shard_map.141.rest_0_), channel_id=1, source_target_pairs={{0,4},{1,5},{2,6},{3,7},{4,0},{5,1},{6,2},{7,3},{8,12},{9,13},{10,... | collective-permute-start | bytes 12296 | tf_op jit(solution)/shard_map/ppermute | solution.py:833
  32.1 1.8 %collective-permute-start.11 = (f32[8,128]{1,0:T(8,128)S(1)}, f32[8,128]{1,0:T(8,128)S(1)}, u32[]{:S(2)}, u32[]{:S(2)}) collective-permute-start(f32[8,128]{1,0:T(8,128)S(1)} %collective-permute-done.9.rest_1_), channel_id=1, source_target_pairs={{0,1},{1,0},{2,3},{3,2},{4,5},{5,4},{6,7},{7,6},{8,9},{9,8},{10,11... | collective-permute-start | bytes 12296 | tf_op jit(solution)/shard_map/ppermute | solution.py:719
